TPU v7x, 32 devices: a whole 2x2x4 slice. The times are simulated.
32 devices in a mesh: view: 4 (over z), space: 8 (over y, x, core).
Axes of the slice: x: 2, y: 2, z: 4, core: 2. Of those that a mesh axis runs over, the one named last changes fastest.
Arguments:
- prior: float32 [128, 64, 256], P('space'), may hold values from 0.5 to 2
- data: float32 [8, 128, 64, 256], P('view', 'space'), may hold values from 0.1 to 10
- taps: float32 [8, 3, 32], P('view'), may hold values from 0.03 to 8.3
- offsets: int32 [8], P('view'), may hold values from 0 to 7
- coverage: int32 [8, 128], P('view', 'space'), may hold values from 0 to 1, as said below
Outputs:
- estimate: float32 [128, 64, 256], P('space')
Inputs may be any that keep to these rules, and one draw needn't show every extreme that they name: `coverage`: every plane of the first dimension is covered by at least one view.
All inputs are finite; a program needn't handle non-finite values.
Results may differ from a plain program's by a relative error of at most 0.000098.
Values sent between devices are 32-bit elements; how exact they have to be, the bound alone decides.
No kernel may reach another device: no remote copies, remote signals or barrier semaphores. Data moves between devices by JAX's collectives and lax.ppermute only.
A program may use at most 64 MiB of HBM per device.

v0:
```python
import jax
import jax.numpy as jnp
from jax import lax
from jax.sharding import PartitionSpec as P

ITERS = 2


HIGH = lax.Precision.HIGHEST


def from_behind(value, axis, steps):
    count = lax.axis_size(axis)
    pairs = [(source, (source + steps) % count) for source in range(count)]
    return lax.ppermute(value, axis, pairs)


def with_halo(cells, sides, width):
    for axis, dim in sides:
        count = lax.axis_size(axis)
        head = lax.slice_in_dim(cells, 0, width, axis=dim)
        tail = lax.slice_in_dim(cells, cells.shape[dim] - width, cells.shape[dim], axis=dim)
        cells = jnp.concatenate(
            [
                lax.ppermute(tail, axis, [(i, (i + 1) % count) for i in range(count)]),
                cells,
                lax.ppermute(head, axis, [((i + 1) % count, i) for i in range(count)]),
            ],
            axis=dim,
        )
    return cells


def band(kern, rows, cols, sign, offset):
    spread = sign * (jnp.arange(cols)[None, :] - jnp.arange(rows)[:, None]) + offset
    hit = spread[:, :, None] == jnp.arange(kern.shape[-1])[None, None, :]
    return jnp.sum(jnp.where(hit[None], kern[:, None, None, :], 0.0), axis=-1)


def across(field, along_y, along_z):
    inner = jnp.einsum("vxyz,vwz->vxyw", field, along_z, precision=HIGH)
    return jnp.einsum("vxyz,vwy->vxwz", inner, along_y, precision=HIGH)


def finish(rimmed, along_x):
    return jnp.einsum("vkyz,vik->viyz", rimmed, along_x, precision=HIGH)


def turn_ahead(field, amount, bits):
    for bit in range(bits):
        moved = from_behind(field, "space", 1 << bit)
        pick = amount >> bit & 1 == 1
        field = jnp.where(pick[:, None, None, None], moved, field)
    return field


def turn_home(field, amount, bits):
    for bit in range(bits):
        moved = from_behind(field, "space", 1 << bit)
        pick = amount >> bit & 1 == 1
        field = jnp.where(pick[:, None, None, None], moved, field)
    return field


def clear_edges(rimmed, slab, nspace, radius):
    planes = jnp.arange(rimmed.shape[1])[None, :]
    lower = (planes < radius) & (slab == 0)[:, None]
    upper = (planes >= rimmed.shape[1] - radius) & (slab == nspace - 1)[:, None]
    return jnp.where((lower | upper)[:, :, None, None], 0.0, rimmed)


def body(prior, data, taps, offsets, coverage):
    kern = taps / jnp.sum(taps, axis=-1, keepdims=True)
    width, rows_y, rows_z = prior.shape
    radius = taps.shape[-1] // 2
    ahead_x = band(kern[:, 0], width, width + 2 * radius, 1, 0)
    back_x = band(kern[:, 0], width, width + 2 * radius, -1, 2 * radius)
    ahead_y = band(kern[:, 1], rows_y, rows_y, 1, radius)
    back_y = band(kern[:, 1], rows_y, rows_y, -1, radius)
    ahead_z = band(kern[:, 2], rows_z, rows_z, 1, radius)
    back_z = band(kern[:, 2], rows_z, rows_z, -1, radius)
    weight = coverage.astype(jnp.float32)
    count = lax.psum(jnp.sum(weight, axis=0), "view")
    nspace = lax.axis_size("space")
    bits = (nspace - 1).bit_length()
    stacked_shape = (data.shape[0],) + prior.shape
    slab = (lax.axis_index("space") - offsets) % nspace
    estimate = prior
    for step in range(ITERS):
        local = jnp.broadcast_to(estimate, stacked_shape)
        moved = turn_ahead(local, offsets % nspace, bits)
        partial_value = across(moved, ahead_y, ahead_z)
        rimmed = with_halo(partial_value, (("space", 1),), radius)
        rimmed = clear_edges(rimmed, slab, nspace, radius)
        ratio = data / finish(rimmed, ahead_x)
        partial_value = across(ratio, back_y, back_z)
        rimmed = with_halo(partial_value, (("space", 1),), radius)
        rimmed = clear_edges(rimmed, slab, nspace, radius)
        correction = turn_home(finish(rimmed, back_x), (nspace - offsets) % nspace, bits)
        weighted = jnp.sum(weight[:, :, None, None] * correction, axis=0)
        total = lax.psum(weighted, "view")
        estimate = estimate * total / count[:, None, None]
    return estimate


def solution(mesh):
    return jax.shard_map(
        body,
        mesh=mesh,
        in_specs=(
            P("space", None, None),
            P("view", "space", None, None),
            P("view", None, None),
            P("view"),
            P("view", "space"),
        ),
        out_specs=P("space", None, None),
        check_vma=False,
    )
```

profile of v0, /device:TPU:8, one launch (start us, length us, event | category | flops | bytes accessed | tf_op | source)
XLA Modules:
  0.0 849.0 jit_solution(4607361514802551493)
XLA Ops:
  6.5 2.9 broadcast_in_dim.255
  9.5 26.5 %collective-permute-done = f32[2,16,64,256]{3,2,1,0:T(8,128)S(1)} collective-permute-done((f32[2,16,64,256]{3,2,1,0:T(8,128)}, f32[2,16,64,256]{3,2,1,0:T(8,128)S(1)}, u32[]{:S(2)}, u32[]{:S(2)}) %collective-permute-start) | collective-permute-done | bytes 2097184 | tf_op jit(solution)/shard_map/ppermute | solution.py:15
  36.0 1.7 broadcast_select_fusion.1
  38.9 46.0 %collective-permute-done.1 = f32[2,16,64,256]{3,2,1,0:T(8,128)} collective-permute-done((f32[2,16,64,256]{3,2,1,0:T(8,128)}, f32[2,16,64,256]{3,2,1,0:T(8,128)}, u32[]{:S(2)}, u32[]{:S(2)}) %collective-permute-start.1) | collective-permute-done | bytes 2097184 | tf_op jit(solution)/shard_map/ppermute | solution.py:15
  84.8 2.1 broadcast_select_fusion.3
  86.9 1.6 collective-permute-start.2
  88.5 1.1 select_reduce_fusion.3
  89.6 2.2 iota_compare_fusion
  91.8 10.7 %select_reduce_fusion = (f32[2,256,256]{2,1,0:T(8,128)S(1)}, f32[2,256,256]{2,1,0:T(8,128)S(1)}) fusion(f32[2,32]{1,0:T(2,128)S(1)} %get-tuple-element.18, pred[256,256,32]{1,2,0:T(8,128)(4,1)S(1)} %get-tuple-element.28, pred[256,256,32]{1,2,0:T(8,128)(4,1)S(1)} %get-tuple-element.29), kind=kLoop, calls=%fused_computation | loop fusion | flops 16515072 | bytes 5243136 | tf_op jit(solution)/shard_map/reduce_sum | solution.py:37
  102.5 29.4 %collective-permute-done.2 = f32[2,16,64,256]{3,2,1,0:T(8,128)S(1)} collective-permute-done((f32[2,16,64,256]{3,2,1,0:T(8,128)S(1)}, f32[2,16,64,256]{3,2,1,0:T(8,128)S(1)}, u32[]{:S(2)}, u32[]{:S(2)}) %collective-permute-start.2) | collective-permute-done | bytes 2097184 | tf_op jit(solution)/shard_map/ppermute | solution.py:15
  131.9 2.1 fusion.14
  134.0 1.9 convolution_bitcast_fusion.3
  136.9 44.1 %collective-permute-done.4 = f32[2,16,64,256]{3,2,1,0:T(8,128)S(1)} collective-permute-done((f32[2,16,64,256]{3,2,1,0:T(8,128)S(1)}, f32[2,16,64,256]{3,2,1,0:T(8,128)S(1)}, u32[]{:S(2)}, u32[]{:S(2)}) %collective-permute-start.4) | collective-permute-done | bytes 2097184 | tf_op jit(solution)/shard_map/ppermute | solution.py:27
  181.0 2.6 collective-permute-done.3
  184.7 7.6 copy_divide_fusion.1
  192.3 3.2 fusion.10
  195.6 2.1 convolution_bitcast_fusion.2
  198.3 45.4 %collective-permute-done.6 = f32[2,16,64,256]{3,2,1,0:T(8,128)S(1)} collective-permute-done((f32[2,16,64,256]{3,2,1,0:T(8,128)S(1)}, f32[2,16,64,256]{3,2,1,0:T(8,128)S(1)}, u32[]{:S(2)}, u32[]{:S(2)}) %collective-permute-start.6) | collective-permute-done | bytes 2097184 | tf_op jit(solution)/shard_map/ppermute | solution.py:27
  243.7 2.0 collective-permute-done.5
  246.2 6.5 fusion.4
  252.9 26.3 %collective-permute-done.7 = f32[2,16,64,256]{3,1,2,0:T(8,128)S(1)} collective-permute-done((f32[2,16,64,256]{3,1,2,0:T(8,128)S(1)}, f32[2,16,64,256]{3,1,2,0:T(8,128)S(1)}, u32[]{:S(2)}, u32[]{:S(2)}) %collective-permute-start.7) | collective-permute-done | bytes 2097184 | tf_op jit(solution)/shard_map/ppermute | solution.py:15
  279.8 45.9 %collective-permute-done.8 = f32[2,16,64,256]{3,1,2,0:T(8,128)S(1)} collective-permute-done((f32[2,16,64,256]{3,1,2,0:T(8,128)S(1)}, f32[2,16,64,256]{3,1,2,0:T(8,128)S(1)}, u32[]{:S(2)}, u32[]{:S(2)}) %collective-permute-start.8) | collective-permute-done | bytes 2097184 | tf_op jit(solution)/shard_map/ppermute | solution.py:15
  326.9 43.7 %collective-permute-done.9 = f32[2,16,64,256]{3,1,2,0:T(8,128)S(1)} collective-permute-done((f32[2,16,64,256]{3,1,2,0:T(8,128)S(1)}, f32[2,16,64,256]{3,1,2,0:T(8,128)S(1)}, u32[]{:S(2)}, u32[]{:S(2)}) %collective-permute-start.9) | collective-permute-done | bytes 2097184 | tf_op jit(solution)/shard_map/ppermute | solution.py:15
  370.7 1.6 multiply_reduce_fusion.1
  372.4 9.6 %psum.22 = f32[16]{0:T(128)S(1)} all-reduce(f32[16]{0:T(128)S(1)} %convert_reduce_fusion), channel_id=1, replica_groups=mesh['view'=4,'space'=8] {'view'}, use_global_device_ids=true, to_apply=%region_10.11 | all-reduce | flops 16 | bytes 128 | tf_op jit(solution)/shard_map/psum | solution.py:83
  382.0 43.5 %all-reduce.3.cloned.1.call-done = f32[16,64,256]{2,0,1:T(8,128)} async-done(((f32[16,64,256]{2,0,1:T(8,128)}), f32[16,64,256]{2,0,1:T(8,128)}) %all-reduce.3.cloned.1.call-update) | async-done | bytes 1048592 | tf_op jit(solution)/shard_map/psum | solution.py:101
  425.5 1.9 fusion.20
  428.3 26.3 %collective-permute-done.10 = f32[2,16,64,256]{3,2,1,0:T(8,128)S(1)} collective-permute-done((f32[2,16,64,256]{3,2,1,0:T(8,128)S(1)}, f32[2,16,64,256]{3,2,1,0:T(8,128)S(1)}, u32[]{:S(2)}, u32[]{:S(2)}) %collective-permute-start.10) | collective-permute-done | bytes 2097184 | tf_op jit(solution)/shard_map/ppermute | solution.py:15
  455.6 46.1 %collective-permute-done.11 = f32[2,16,64,256]{3,2,1,0:T(8,128)S(1)} collective-permute-done((f32[2,16,64,256]{3,2,1,0:T(8,128)S(1)}, f32[2,16,64,256]{3,2,1,0:T(8,128)S(1)}, u32[]{:S(2)}, u32[]{:S(2)}) %collective-permute-start.11) | collective-permute-done | bytes 2097184 | tf_op jit(solution)/shard_map/ppermute | solution.py:15
  502.2 1.5 collective-permute-start.12
  503.7 43.3 %collective-permute-done.12 = f32[2,16,64,256]{3,2,1,0:T(8,128)S(1)} collective-permute-done((f32[2,16,64,256]{3,2,1,0:T(8,128)S(1)}, f32[2,16,64,256]{3,2,1,0:T(8,128)S(1)}, u32[]{:S(2)}, u32[]{:S(2)}) %collective-permute-start.12) | collective-permute-done | bytes 2097184 | tf_op jit(solution)/shard_map/ppermute | solution.py:15
  547.0 2.1 fusion.12
  549.1 1.9 convolution_bitcast_fusion.1
  551.6 44.6 %collective-permute-done.14 = f32[2,16,64,256]{3,2,1,0:T(8,128)S(1)} collective-permute-done((f32[2,16,64,256]{3,2,1,0:T(8,128)S(1)}, f32[2,16,64,256]{3,2,1,0:T(8,128)S(1)}, u32[]{:S(2)}, u32[]{:S(2)}) %collective-permute-start.14) | collective-permute-done | bytes 2097184 | tf_op jit(solution)/shard_map/ppermute | solution.py:27
  596.2 2.6 collective-permute-done.13
  599.8 7.6 copy_divide_fusion
  607.4 3.2 fusion.8
  610.6 2.1 convolution_bitcast_fusion
  613.3 45.4 %collective-permute-done.16 = f32[2,16,64,256]{3,2,1,0:T(8,128)S(1)} collective-permute-done((f32[2,16,64,256]{3,2,1,0:T(8,128)S(1)}, f32[2,16,64,256]{3,2,1,0:T(8,128)S(1)}, u32[]{:S(2)}, u32[]{:S(2)}) %collective-permute-start.16) | collective-permute-done | bytes 2097184 | tf_op jit(solution)/shard_map/ppermute | solution.py:27
  658.8 1.9 collective-permute-done.15
  661.2 6.5 fusion
  667.9 26.3 %collective-permute-done.17 = f32[2,16,64,256]{3,1,2,0:T(8,128)S(1)} collective-permute-done((f32[2,16,64,256]{3,1,2,0:T(8,128)S(1)}, f32[2,16,64,256]{3,1,2,0:T(8,128)S(1)}, u32[]{:S(2)}, u32[]{:S(2)}) %collective-permute-start.17) | collective-permute-done | bytes 2097184 | tf_op jit(solution)/shard_map/ppermute | solution.py:15
  694.8 46.0 %collective-permute-done.18 = f32[2,16,64,256]{3,1,2,0:T(8,128)S(1)} collective-permute-done((f32[2,16,64,256]{3,1,2,0:T(8,128)S(1)}, f32[2,16,64,256]{3,1,2,0:T(8,128)S(1)}, u32[]{:S(2)}, u32[]{:S(2)}) %collective-permute-start.18) | collective-permute-done | bytes 2097184 | tf_op jit(solution)/shard_map/ppermute | solution.py:15
  742.0 43.8 %collective-permute-done.19 = f32[2,16,64,256]{3,1,2,0:T(8,128)S(1)} collective-permute-done((f32[2,16,64,256]{3,1,2,0:T(8,128)S(1)}, f32[2,16,64,256]{3,1,2,0:T(8,128)S(1)}, u32[]{:S(2)}, u32[]{:S(2)}) %collective-permute-start.19) | collective-permute-done | bytes 2097184 | tf_op jit(solution)/shard_map/ppermute | solution.py:15
  785.8 1.6 multiply_reduce_fusion
  787.4 51.5 %all-reduce.5.cloned.1.call-done = f32[16,64,256]{2,0,1:T(8,128)} async-done(((f32[16,64,256]{2,0,1:T(8,128)}), f32[16,64,256]{2,0,1:T(8,128)}) %all-reduce.5.cloned.1.call-update) | async-done | bytes 1048592 | tf_op jit(solution)/shard_map/psum | solution.py:101
  838.9 1.5 multiply_divide_fusion
  840.4 1.6 copy.23
  (66 shorter events, 13.1 us)
Async XLA Ops:
  6.5 29.5 %copy-start = (f32[16,64,256]{2,1,0:T(8,128)S(1)}, f32[16,64,256]{2,1,0:T(8,128)}, u32[]{:S(2)}) copy-start(f32[16,64,256]{2,1,0:T(8,128)} %param.5) | copy-start | bytes 3145732
  6.5 2.9 copy-start.5
  6.5 418.9 %all-reduce.3.cloned.1.call-start = ((), (), s32[]{:S(2)}) async-start(), calls=%async_computation | async-start | bytes 2097152 | tf_op jit(solution)/shard_map/psum | solution.py:101
  9.5 26.6 %collective-permute-start = (f32[2,16,64,256]{3,2,1,0:T(8,128)}, f32[2,16,64,256]{3,2,1,0:T(8,128)S(1)}, u32[]{:S(2)}, u32[]{:S(2)}) collective-permute-start(f32[2,16,64,256]{3,2,1,0:T(8,128)} %broadcast_in_dim.255), channel_id=1, source_target_pairs={{0,1},{1,2},{2,3},{3,4},{4,5},{5,6},{6,7},{7,0},{8,9},{9,10},{10,1... | collective-permute-start | bytes 6291464 | tf_op jit(solution)/shard_map/ppermute | solution.py:15
  36.0 2.3 copy-start.3
  37.8 47.1 %collective-permute-start.1 = (f32[2,16,64,256]{3,2,1,0:T(8,128)}, f32[2,16,64,256]{3,2,1,0:T(8,128)}, u32[]{:S(2)}, u32[]{:S(2)}) collective-permute-start(f32[2,16,64,256]{3,2,1,0:T(8,128)} %broadcast_select_fusion.1), channel_id=1, source_target_pairs={{0,2},{1,3},{2,4},{3,5},{4,6},{5,7},{6,0},{7,1},{8,10},{9,11},{10,... | collective-permute-start | bytes 6291464 | tf_op jit(solution)/shard_map/ppermute | solution.py:15
  86.9 45.0 %collective-permute-start.2 = (f32[2,16,64,256]{3,2,1,0:T(8,128)S(1)}, f32[2,16,64,256]{3,2,1,0:T(8,128)S(1)}, u32[]{:S(2)}, u32[]{:S(2)}) collective-permute-start(f32[2,16,64,256]{3,2,1,0:T(8,128)S(1)} %broadcast_select_fusion.3), channel_id=1, source_target_pairs={{0,4},{1,5},{2,6},{3,7},{4,0},{5,1},{6,2},{7,3},{8,12},{9,13},{10,... | collective-permute-start | bytes 6291464 | tf_op jit(solution)/shard_map/ppermute | solution.py:15
  135.9 45.1 %collective-permute-start.4 = (f32[2,16,64,256]{3,2,1,0:T(8,128)S(1)}, f32[2,16,64,256]{3,2,1,0:T(8,128)S(1)}, u32[]{:S(2)}, u32[]{:S(2)}) collective-permute-start(f32[2,16,64,256]{3,2,1,0:T(8,128)S(1)} %convolution_bitcast_fusion.3), channel_id=1, source_target_pairs={{1,0},{2,1},{3,2},{4,3},{5,4},{6,5},{7,6},{0,7},{9,8},{10,9},{11,1... | collective-permute-start | bytes 6291464 | tf_op jit(solution)/shard_map/ppermute | solution.py:27
  136.0 47.7 %collective-permute-start.3 = (f32[2,16,64,256]{3,2,1,0:T(8,128)S(1)}, f32[2,16,64,256]{3,2,1,0:T(8,128)S(1)}, u32[]{:S(2)}, u32[]{:S(2)}) collective-permute-start(f32[2,16,64,256]{3,2,1,0:T(8,128)S(1)} %convolution_bitcast_fusion.3), channel_id=1, source_target_pairs={{0,1},{1,2},{2,3},{3,4},{4,5},{5,6},{6,7},{7,0},{8,9},{9,10},{10,1... | collective-permute-start | bytes 6291464 | tf_op jit(solution)/shard_map/ppermute | solution.py:25
  136.9 47.8 %copy-start.1 = (f32[2,16,64,256]{3,2,1,0:T(8,128)S(1)}, f32[2,16,64,256]{3,2,1,0:T(8,128)}, u32[]{:S(2)}) copy-start(f32[2,16,64,256]{3,2,1,0:T(8,128)} %param.6) | copy-start | bytes 6291460
  197.7 45.9 %collective-permute-start.6 = (f32[2,16,64,256]{3,2,1,0:T(8,128)S(1)}, f32[2,16,64,256]{3,2,1,0:T(8,128)S(1)}, u32[]{:S(2)}, u32[]{:S(2)}) collective-permute-start(f32[2,16,64,256]{3,2,1,0:T(8,128)S(1)} %convolution_bitcast_fusion.2), channel_id=1, source_target_pairs={{1,0},{2,1},{3,2},{4,3},{5,4},{6,5},{7,6},{0,7},{9,8},{10,9},{11,1... | collective-permute-start | bytes 6291464 | tf_op jit(solution)/shard_map/ppermute | solution.py:27
  197.9 47.7 %collective-permute-start.5 = (f32[2,16,64,256]{3,2,1,0:T(8,128)S(1)}, f32[2,16,64,256]{3,2,1,0:T(8,128)S(1)}, u32[]{:S(2)}, u32[]{:S(2)}) collective-permute-start(f32[2,16,64,256]{3,2,1,0:T(8,128)S(1)} %convolution_bitcast_fusion.2), channel_id=1, source_target_pairs={{0,1},{1,2},{2,3},{3,4},{4,5},{5,6},{6,7},{7,0},{8,9},{9,10},{10,1... | collective-permute-start | bytes 6291464 | tf_op jit(solution)/shard_map/ppermute | solution.py:25
  252.8 26.4 %collective-permute-start.7 = (f32[2,16,64,256]{3,1,2,0:T(8,128)S(1)}, f32[2,16,64,256]{3,1,2,0:T(8,128)S(1)}, u32[]{:S(2)}, u32[]{:S(2)}) collective-permute-start(f32[2,16,64,256]{3,1,2,0:T(8,128)S(1)} %fusion.4), channel_id=1, source_target_pairs={{0,1},{1,2},{2,3},{3,4},{4,5},{5,6},{6,7},{7,0},{8,9},{9,10},{10,1... | collective-permute-start | bytes 6291464 | tf_op jit(solution)/shard_map/ppermute | solution.py:15
  279.7 46.0 %collective-permute-start.8 = (f32[2,16,64,256]{3,1,2,0:T(8,128)S(1)}, f32[2,16,64,256]{3,1,2,0:T(8,128)S(1)}, u32[]{:S(2)}, u32[]{:S(2)}) collective-permute-start(f32[2,16,64,256]{3,1,2,0:T(8,128)S(1)} %broadcast_select_fusion.5), channel_id=1, source_target_pairs={{0,2},{1,3},{2,4},{3,5},{4,6},{5,7},{6,0},{7,1},{8,10},{9,11},{10,... | collective-permute-start | bytes 6291464 | tf_op jit(solution)/shard_map/ppermute | solution.py:15
  325.7 1.2 copy-start.4
  326.3 44.4 %collective-permute-start.9 = (f32[2,16,64,256]{3,1,2,0:T(8,128)S(1)}, f32[2,16,64,256]{3,1,2,0:T(8,128)S(1)}, u32[]{:S(2)}, u32[]{:S(2)}) collective-permute-start(f32[2,16,64,256]{3,1,2,0:T(8,128)S(1)} %broadcast_select_fusion.7), channel_id=1, source_target_pairs={{0,4},{1,5},{2,6},{3,7},{4,0},{5,1},{6,2},{7,3},{8,12},{9,13},{10,... | collective-permute-start | bytes 6291464 | tf_op jit(solution)/shard_map/ppermute | solution.py:15
  372.3 466.6 %all-reduce.5.cloned.1.call-start = ((), (), s32[]{:S(2)}) async-start(), calls=%async_computation.1 | async-start | bytes 2097152 | tf_op jit(solution)/shard_map/psum | solution.py:101
  428.2 26.4 %collective-permute-start.10 = (f32[2,16,64,256]{3,2,1,0:T(8,128)S(1)}, f32[2,16,64,256]{3,2,1,0:T(8,128)S(1)}, u32[]{:S(2)}, u32[]{:S(2)}) collective-permute-start(f32[2,16,64,256]{3,2,1,0:T(8,128)S(1)} %broadcast_in_dim.261), channel_id=1, source_target_pairs={{0,1},{1,2},{2,3},{3,4},{4,5},{5,6},{6,7},{7,0},{8,9},{9,10},{10,1... | collective-permute-start | bytes 6291464 | tf_op jit(solution)/shard_map/ppermute | solution.py:15
  454.9 46.7 %collective-permute-start.11 = (f32[2,16,64,256]{3,2,1,0:T(8,128)S(1)}, f32[2,16,64,256]{3,2,1,0:T(8,128)S(1)}, u32[]{:S(2)}, u32[]{:S(2)}) collective-permute-start(f32[2,16,64,256]{3,2,1,0:T(8,128)S(1)} %broadcast_select_fusion), channel_id=1, source_target_pairs={{0,2},{1,3},{2,4},{3,5},{4,6},{5,7},{6,0},{7,1},{8,10},{9,11},{10,... | collective-permute-start | bytes 6291464 | tf_op jit(solution)/shard_map/ppermute | solution.py:15
  502.2 44.9 %collective-permute-start.12 = (f32[2,16,64,256]{3,2,1,0:T(8,128)S(1)}, f32[2,16,64,256]{3,2,1,0:T(8,128)S(1)}, u32[]{:S(2)}, u32[]{:S(2)}) collective-permute-start(f32[2,16,64,256]{3,2,1,0:T(8,128)S(1)} %broadcast_select_fusion.2), channel_id=1, source_target_pairs={{0,4},{1,5},{2,6},{3,7},{4,0},{5,1},{6,2},{7,3},{8,12},{9,13},{10,... | collective-permute-start | bytes 6291464 | tf_op jit(solution)/shard_map/ppermute | solution.py:15
  551.0 48.7 %copy-start.2 = (f32[2,16,64,256]{3,2,1,0:T(8,128)S(1)}, f32[2,16,64,256]{3,2,1,0:T(8,128)}, u32[]{:S(2)}) copy-start(f32[2,16,64,256]{3,2,1,0:T(8,128)} %param.6) | copy-start | bytes 6291460
  551.0 45.1 %collective-permute-start.14 = (f32[2,16,64,256]{3,2,1,0:T(8,128)S(1)}, f32[2,16,64,256]{3,2,1,0:T(8,128)S(1)}, u32[]{:S(2)}, u32[]{:S(2)}) collective-permute-start(f32[2,16,64,256]{3,2,1,0:T(8,128)S(1)} %convolution_bitcast_fusion.1), channel_id=1, source_target_pairs={{1,0},{2,1},{3,2},{4,3},{5,4},{6,5},{7,6},{0,7},{9,8},{10,9},{11,1... | collective-permute-start | bytes 6291464 | tf_op jit(solution)/shard_map/ppermute | solution.py:27
  551.1 47.7 %collective-permute-start.13 = (f32[2,16,64,256]{3,2,1,0:T(8,128)S(1)}, f32[2,16,64,256]{3,2,1,0:T(8,128)S(1)}, u32[]{:S(2)}, u32[]{:S(2)}) collective-permute-start(f32[2,16,64,256]{3,2,1,0:T(8,128)S(1)} %convolution_bitcast_fusion.1), channel_id=1, source_target_pairs={{0,1},{1,2},{2,3},{3,4},{4,5},{5,6},{6,7},{7,0},{8,9},{9,10},{10,1... | collective-permute-start | bytes 6291464 | tf_op jit(solution)/shard_map/ppermute | solution.py:25
  612.7 46.0 %collective-permute-start.16 = (f32[2,16,64,256]{3,2,1,0:T(8,128)S(1)}, f32[2,16,64,256]{3,2,1,0:T(8,128)S(1)}, u32[]{:S(2)}, u32[]{:S(2)}) collective-permute-start(f32[2,16,64,256]{3,2,1,0:T(8,128)S(1)} %convolution_bitcast_fusion), channel_id=1, source_target_pairs={{1,0},{2,1},{3,2},{4,3},{5,4},{6,5},{7,6},{0,7},{9,8},{10,9},{11,1... | collective-permute-start | bytes 6291464 | tf_op jit(solution)/shard_map/ppermute | solution.py:27
  613.0 47.6 %collective-permute-start.15 = (f32[2,16,64,256]{3,2,1,0:T(8,128)S(1)}, f32[2,16,64,256]{3,2,1,0:T(8,128)S(1)}, u32[]{:S(2)}, u32[]{:S(2)}) collective-permute-start(f32[2,16,64,256]{3,2,1,0:T(8,128)S(1)} %convolution_bitcast_fusion), channel_id=1, source_target_pairs={{0,1},{1,2},{2,3},{3,4},{4,5},{5,6},{6,7},{7,0},{8,9},{9,10},{10,1... | collective-permute-start | bytes 6291464 | tf_op jit(solution)/shard_map/ppermute | solution.py:25
  667.8 26.4 %collective-permute-start.17 = (f32[2,16,64,256]{3,1,2,0:T(8,128)S(1)}, f32[2,16,64,256]{3,1,2,0:T(8,128)S(1)}, u32[]{:S(2)}, u32[]{:S(2)}) collective-permute-start(f32[2,16,64,256]{3,1,2,0:T(8,128)S(1)} %fusion), channel_id=1, source_target_pairs={{0,1},{1,2},{2,3},{3,4},{4,5},{5,6},{6,7},{7,0},{8,9},{9,10},{10,1... | collective-permute-start | bytes 6291464 | tf_op jit(solution)/shard_map/ppermute | solution.py:15
  694.7 46.1 %collective-permute-start.18 = (f32[2,16,64,256]{3,1,2,0:T(8,128)S(1)}, f32[2,16,64,256]{3,1,2,0:T(8,128)S(1)}, u32[]{:S(2)}, u32[]{:S(2)}) collective-permute-start(f32[2,16,64,256]{3,1,2,0:T(8,128)S(1)} %broadcast_select_fusion.4), channel_id=1, source_target_pairs={{0,2},{1,3},{2,4},{3,5},{4,6},{5,7},{6,0},{7,1},{8,10},{9,11},{10,... | collective-permute-start | bytes 6291464 | tf_op jit(solution)/shard_map/ppermute | solution.py:15
  741.4 44.4 %collective-permute-start.19 = (f32[2,16,64,256]{3,1,2,0:T(8,128)S(1)}, f32[2,16,64,256]{3,1,2,0:T(8,128)S(1)}, u32[]{:S(2)}, u32[]{:S(2)}) collective-permute-start(f32[2,16,64,256]{3,1,2,0:T(8,128)S(1)} %broadcast_select_fusion.6), channel_id=1, source_target_pairs={{0,4},{1,5},{2,6},{3,7},{4,0},{5,1},{6,2},{7,3},{8,12},{9,13},{10,... | collective-permute-start | bytes 6291464 | tf_op jit(solution)/shard_map/ppermute | solution.py:15
Sparse Core Ops, SparseCore 0:
  372.4 53.0 all-reduce.2
  787.5 51.2 all-reduce.4
where the time goes:
time: 859 us; the launch traced here: 849 us
  waiting for transfers between devices  733 us (85%)
  matrix products  47 us (5%)
  other arithmetic  31.4 us (4%)
  between operations  14 us (2%)
  blocking collectives  9.63 us (1%)
    ppermute x12, waiting for transfers between devices, from_behind(): return lax.ppermute(value, axis, pairs)  450 us
    ppermute x4, waiting for transfers between devices, with_halo(): lax.ppermute(head, axis, [((i + 1) % count, i) for i in range(count)])  179 us
    psum x2, waiting for transfers between devices, body(): total = lax.psum(weighted, 'view')  94.9 us
    dot_general x4, matrix products, finish(): return jnp.einsum('vkyz,vik->viyz', rimmed, along_x, precision=HIGH)  28.3 us
  transfers between devices with their start and end apart: 22, of which 22 were waited for; matrix products, arithmetic and copies ran while one was open for 2% of the time, Pallas kernels for 0%

commit v1 on v0

v1 whole, which is shorter than its diff:
```python
import jax
import jax.numpy as jnp
from jax import lax
from jax.sharding import PartitionSpec as P

ITERS = 2
HIGH = lax.Precision.HIGH


def swap(value, axis, mask):
    count = lax.axis_size(axis)
    return lax.ppermute(value, axis, [(i, i ^ mask) for i in range(count)])


def pick(kern, index):
    hit = index[..., None] == jnp.arange(kern.shape[-1])
    lead = kern.reshape(kern.shape[:1] + (1,) * (index.ndim - 1) + kern.shape[1:])
    return jnp.sum(jnp.where(hit, lead, 0.0), axis=-1)


def pack(edge):
    rows, planes, cells = edge.shape
    group = 128 // cells
    edge = edge.reshape(rows // group, group, planes, cells)
    return edge.transpose(0, 2, 1, 3).reshape(rows // group, planes, 128)


def unpack(packed, cells):
    lead = packed.shape[:-2]
    octets, planes, lanes = packed.shape[-3], packed.shape[-2], packed.shape[-1]
    del octets
    group = lanes // cells
    parts = packed.reshape(packed.shape[:-1] + (group, cells))
    parts = jnp.swapaxes(parts, -3, -2)
    return parts.reshape(lead[:-1] + (lead[-1] * group, planes, cells))


def halve(blocks, mask):
    order = blocks.shape[0]
    split = blocks.reshape((order // (2 * mask), 2, mask) + blocks.shape[1:])
    kept = split[:, 0] + swap(split[:, 1], "space", mask)
    return kept.reshape((order // 2,) + blocks.shape[1:])


def scatter_sum(blocks):
    bits = blocks.shape[0].bit_length() - 1
    blocks = halve(blocks, 1)
    middle = blocks.shape[1] // 2
    shift = (bits - 1) // 2
    out = []
    for part, turned in ((blocks[:, :middle], 0), (blocks[:, middle:], shift)):
        left = list(range(1, bits))
        for bit in [1 + (k + turned) % (bits - 1) for k in range(bits - 1)]:
            at = left.index(bit)
            order = part.shape[0]
            low = 1 << at
            split = part.reshape((order // (2 * low), 2, low) + part.shape[1:])
            part = split[:, 0] + swap(split[:, 1], "space", 1 << bit)
            part = part.reshape((order // 2,) + part.shape[2:])
            left.remove(bit)
        out.append(part[0])
    return jnp.concatenate(out, axis=0)


def body(prior, data, taps, offsets, coverage):
    nview, nspace = lax.axis_size("view"), lax.axis_size("space")
    g, j = lax.axis_index("view"), lax.axis_index("space")
    zh, yh = g >> 1, (g ^ (g >> 1)) & 1
    local, width, ny, nz = data.shape
    ntaps = taps.shape[-1]
    rad = ntaps // 2
    hy, hz = ny // 2, nz // 2
    wy = hy + rad

    def quadrant(owner):
        oz, oy = owner >> 1, (owner ^ (owner >> 1)) & 1
        return lax.dynamic_slice(data, (0, 0, oy * hy, oz * hz), (local, width, hy, hz))

    pieces = [quadrant(g)] + [swap(quadrant(g ^ r), "view", r) for r in range(1, nview)]

    flat = jnp.concatenate(
        [
            taps.reshape(local, -1),
            offsets.astype(jnp.float32)[:, None],
            coverage.astype(jnp.float32),
        ],
        axis=1,
    )
    used = flat.shape[1]
    flat = jnp.pad(flat, ((0, 0), (0, -used % 128)))
    every = lax.all_gather(flat, ("view", "space"))
    every = every.reshape((nview, nspace) + flat.shape)
    every = jnp.concatenate(
        [lax.dynamic_slice_in_dim(every, g ^ r, 1, axis=0) for r in range(nview)], axis=0
    )
    nviews = nview * local
    shared = every[:, 0].reshape(nviews, -1)
    kern = shared[:, : 3 * ntaps].reshape(nviews, 3, ntaps)
    kern = kern / jnp.sum(kern, axis=-1, keepdims=True)
    turn = shared[:, 3 * ntaps].astype(jnp.int32)
    cover = every[..., 3 * ntaps + 1 : used].transpose(0, 2, 1, 3).reshape(nviews, nspace, width)
    count = lax.dynamic_index_in_dim(jnp.sum(cover, axis=0), j, 0, keepdims=False)

    slab = (j - turn) % nspace
    place = slab[:, None] * width + jnp.arange(width)
    planes = jnp.arange(nspace * width).reshape(nspace, width)
    band_x = pick(kern[:, 0], planes - place[:, :, None, None] + rad)
    relative = j ^ jnp.arange(nspace)
    planes_r = relative[:, None] * width + jnp.arange(width)
    band_xt = pick(kern[:, 0], planes_r - place[:, :, None, None] + rad)
    cover_r = jnp.concatenate(
        [lax.dynamic_slice_in_dim(cover, j ^ r, 1, axis=1) for r in range(nspace)], axis=1
    )
    band_xt = band_xt * cover_r[:, None]
    rows = jnp.arange(wy) + rad * yh
    band_y = pick(kern[:, 1], (rows - (jnp.arange(hy)[:, None] + hy * yh) + rad)[None])
    cells = jnp.concatenate([jnp.arange(hz) + hz * zh, jnp.arange(rad) + jnp.where(zh == 0, hz, hz - rad)])
    band_z = pick(kern[:, 2], (cells - (jnp.arange(hz)[:, None] + hz * zh) + rad)[None])

    window = lax.dynamic_slice_in_dim(prior, rad * yh, wy, axis=1).transpose(1, 0, 2)
    main = lax.dynamic_slice_in_dim(window, hz * zh, hz, axis=2)
    rim = lax.dynamic_slice_in_dim(window, jnp.where(zh == 0, hz, hz - rad), rad, axis=2)
    estimate = jnp.concatenate([main, pack(rim)], axis=0)

    observed = jnp.concatenate(pieces, axis=0).transpose(0, 2, 1, 3)

    for step in range(ITERS):
        wide = lax.all_gather(estimate, "space")
        wide = jnp.concatenate([wide[:, :wy], unpack(wide[:, wy:], rad)], axis=-1)
        inner = jnp.einsum("vibx,byxz->vyiz", band_x, wide, precision=HIGH)
        inner = jnp.einsum("vyiz,vwz->vyiw", inner, band_z, precision=HIGH)
        blurred = jnp.einsum("vyiw,voy->voiw", inner, band_y, precision=HIGH)
        ratio = observed / blurred
        inner = jnp.einsum("voiw,voy->vyiw", ratio, band_y, precision=HIGH)
        inner = jnp.einsum("vyiw,vwz->vyiz", inner, band_z, precision=HIGH)
        total = jnp.einsum("vibx,vyiz->byxz", band_xt, inner, precision=HIGH)
        rim = jax.vmap(pack)(total[..., hz:])
        total = jnp.concatenate([total[..., :hz], rim], axis=1)
        total = scatter_sum(total)
        main, rim = total[:wy], unpack(total[wy:], rad)
        start = jnp.where(yh == 0, wy - hy, 0)
        edge = jnp.where(zh == 0, main[..., hz - rad :], main[..., :rad])

        def overlap(value):
            return lax.dynamic_slice_in_dim(value, start, hy, axis=0)

        from_y = swap(jnp.concatenate([overlap(main), pack(overlap(rim))], axis=0), "view", 1)
        from_z = swap(jnp.concatenate([pack(rim), pack(edge)], axis=0), "view", 3)
        from_c = swap(jnp.concatenate([pack(overlap(rim)), pack(overlap(edge))], axis=0), "view", 2)
        z_edge, z_rim = jnp.split(unpack(from_z, rad), 2, axis=0)
        c_edge, c_rim = jnp.split(unpack(from_c, rad), 2, axis=0)

        def spread(value):
            return lax.dynamic_update_slice_in_dim(jnp.zeros((wy,) + value.shape[1:], value.dtype), value, start, 0)

        def widen(value):
            empty = jnp.zeros(value.shape[:-1] + (hz - rad,), value.dtype)
            return jnp.where(
                zh == 0,
                jnp.concatenate([empty, value], axis=-1),
                jnp.concatenate([value, empty], axis=-1),
            )

        main = main + spread(from_y[:hy]) + widen(z_edge + spread(c_edge))
        rim = rim + spread(unpack(from_y[hy:], rad)) + z_rim + spread(c_rim)
        total = jnp.concatenate([main, pack(rim)], axis=0)
        estimate = estimate * total / count[None, :, None]

    own = lax.dynamic_slice_in_dim(estimate, rad * yh, hy, axis=0)
    parts = lax.all_gather(own, "view")
    low = jnp.concatenate([parts[0], parts[1]], axis=0)
    high = jnp.concatenate([parts[3], parts[2]], axis=0)
    return jnp.concatenate([low, high], axis=-1).transpose(1, 0, 2)


def solution(mesh):
    return jax.shard_map(
        body,
        mesh=mesh,
        in_specs=(
            P("space", None, None),
            P("view", "space", None, None),
            P("view", None, None),
            P("view"),
            P("view", "space"),
        ),
        out_specs=P("space", None, None),
        check_vma=False,
    )
```

time: 859 us -> 348 us (0.41)
  waiting for transfers between devices: 733 us -> 111 us
  blocking collectives: 9.63 us -> 67.8 us
  local copies, waits for them, and re-layouts: 5.37 us -> 55.4 us
  starting transfers between devices: 8.22 us -> 25.8 us
    ppermute x20 -> x19, waiting for transfers between devices: 638 us -> 47.4 us  [swap(): return lax.ppermute(value, axis, [(i, i ^ mask) for i in range(count)])]
    psum x2 -> x0, waiting for transfers between devices: 94.9 us -> none  [body(): total = lax.psum(weighted, 'view')]
    all_gather x0 -> x1, blocking collectives: none -> 67.8 us  [body(): every = lax.all_gather(flat, ('view', 'space'))]
    all_gather x0 -> x3, waiting for transfers between devices: none -> 63.2 us  [the longest x2 34.3 us: body(): wide = lax.all_gather(estimate, 'space')]
    ppermute x20 -> x19, starting transfers between devices: 8.18 us -> 25.5 us  [swap(): return lax.ppermute(value, axis, [(i, i ^ mask) for i in range(count)])]
    reshape x0 -> x29, local copies, waits for them, and re-layouts: none -> 15.6 us  [the longest x4 7.29 us: pack(): edge = edge.reshape(rows // group, group, planes, cells)]
    slice x0 -> x20, local copies, waits for them, and re-layouts: none -> 11.8 us  [the longest x2 4.11 us: body(): total = jnp.concatenate([total[..., :hz], rim], axis=1)]
    psum x1 -> x0, blocking collectives: 9.63 us -> none  [body(): count = lax.psum(jnp.sum(weight, axis=0), 'view')]
  transfers between devices with their start and end apart: 22 -> 22, of which waited for: 22 -> 15; matrix products, arithmetic and copies ran while one was open for 2% -> 14% of each run, Pallas kernels for 0% -> 0%
where the time goes in v1:
time: 348 us; the launch traced here: 343 us
  waiting for transfers between devices  111 us (32%)
  blocking collectives  67.8 us (19%)
  local copies, waits for them, and re-layouts  55.4 us (16%)
  matrix products  40.3 us (12%)
  other arithmetic  28.6 us (8%)
  starting transfers between devices  25.8 us (7%)
  between operations  14.5 us (4%)
    all_gather x1, blocking collectives, body(): every = lax.all_gather(flat, ('view', 'space'))  67.8 us
    ppermute x19, waiting for transfers between devices, swap(): return lax.ppermute(value, axis, [(i, i ^ mask) for i in range(count)])  47.4 us
    all_gather x2, waiting for transfers between devices, body(): wide = lax.all_gather(estimate, 'space')  34.3 us
    all_gather x1, waiting for transfers between devices, body(): parts = lax.all_gather(own, 'view')  28.9 us
    ppermute x19, starting transfers between devices, swap(): return lax.ppermute(value, axis, [(i, i ^ mask) for i in range(count)])  25.5 us
    reduce_sum x3, other arithmetic, pick(): return jnp.sum(jnp.where(hit, lead, 0.0), axis=-1)  16 us
    dot_general x2, matrix products, body(): inner = jnp.einsum('vyiz,vwz->vyiw', inner, band_z, precision=HIGH)  13.1 us
    reshape x4, local copies, waits for them, and re-layouts, pack(): edge = edge.reshape(rows // group, group, planes, cells)  7.29 us
  transfers between devices with their start and end apart: 22, of which 15 were waited for; matrix products, arithmetic and copies ran while one was open for 14% of the time, Pallas kernels for 0%

profile of v1, /device:TPU:8, one launch (start us, length us, event | category | flops | bytes accessed | tf_op | source)
XLA Modules:
  0.0 342.9 jit_solution(11404941799546216654)
XLA Ops:
  9.4 2.8 constant_dynamic-slice_fusion.18
  12.2 3.1 collective-permute-start.2
  16.9 67.8 %all-gather.3 = f32[32,2,128]{2,1,0:T(2,128)S(1)} all-gather(f32[1,2,128]{2,1,0:T(2,128)S(1)} %fusion.85), channel_id=2, replica_groups=mesh['view'=4,'space'=8] {'view','space'}, dimensions={0}, use_global_device_ids=true | all-gather | bytes 33792 | tf_op jit(solution)/shard_map/all_gather | solution.py:91
  85.6 11.5 %select_reduce_fusion.1 = (f32[8,16,8,16]{3,2,1,0:T(8,128)S(1)}, f32[8,16,8,16]{3,2,1,0:T(8,128)}) fusion(s32[8,16,8,16]{3,2,1,0:T(8,128)S(1)} %get-tuple-element.47, f32[8,32]{1,0:T(8,128)S(1)} %bitcast.410, s32[8,16,8,16]{3,2,1,0:T(8,128)S(1)} %get-tuple-element.46), kind=kLoop, calls=%fused_computation.1 | loop fusion | flops 3112960 | bytes 263168 | tf_op jit(solution)/shard_map/reduce_sum | solution.py:18
  99.8 3.7 %select_reduce_fusion = f32[8,128,144]{1,2,0:T(8,128)S(1)} fusion(f32[8,32]{1,0:T(8,128)S(1)} %bitcast.408, pred[128,144,32]{0,2,1:T(8,128)(4,1)S(1)} %iota_compare_fusion.2), kind=kLoop, calls=%fused_computation | loop fusion | flops 9289728 | bytes 1180672 | tf_op jit(solution)/shard_map/reduce_sum | solution.py:18
  104.5 2.6 reshape.393
  107.1 2.6 copy.156
  110.2 3.1 fusion.25
  113.4 6.8 %fusion.12 = f32[8,48,16,128]{3,1,2,0:T(8,128)S(1)} fusion(f32[8,48,16,144]{3,2,0,1:T(8,128)S(1)} %fusion.25, f32[8,128,144]{1,2,0:T(8,128)S(1)} %select_reduce_fusion), kind=kOutput, calls=%fused_computation.19 | convolution fusion | flops 679477248 | bytes 7274496 | tf_op jit(solution)/shard_map/vyiz,vwz->vyiw/dot_general | solution.py:131
  121.4 2.8 fusion.28
  124.3 3.2 fusion.16
  127.5 3.3 fusion.18
  131.2 2.1 slice.257
  133.2 3.5 %copy.258 = f32[8,6,8,16,16]{4,2,3,1,0:T(8,128)} copy(f32[8,6,8,16,16]{4,3,0,2,1:T(8,128)S(1)} %bitcast.355) | data formatting | bytes 786432 | tf_op jit(solution)/shard_map/vmap()/reshape | solution.py:24
  136.8 2.4 concatenate.125
  139.2 2.2 copy_dynamic-update-slice_fusion.1
  141.9 3.4 collective-permute-done.3
  146.5 1.6 collective-permute-start.6
  148.3 2.7 collective-permute-start.4
  151.0 8.2 %collective-permute-done.6 = f32[1,2,27,16,128]{4,3,2,1,0:T(8,128)} collective-permute-done((f32[1,2,27,16,128]{4,3,2,1,0:T(8,128)}, f32[1,2,27,16,128]{4,3,2,1,0:T(8,128)}, u32[]{:S(2)}, u32[]{:S(2)}) %collective-permute-start.6) | collective-permute-done | bytes 442400 | tf_op jit(solution)/shard_map/ppermute | solution.py:12
  160.3 2.5 collective-permute-start.7
  162.9 1.8 collective-permute-start.5
  164.7 3.5 %collective-permute-done.7 = f32[1,1,27,16,128]{4,3,2,1,0:T(8,128)S(1)} collective-permute-done((f32[1,1,27,16,128]{4,3,2,1,0:T(8,128)S(1)}, f32[1,1,27,16,128]{4,3,2,1,0:T(8,128)S(1)}, u32[]{:S(2)}, u32[]{:S(2)}) %collective-permute-start.7) | collective-permute-done | bytes 221216 | tf_op jit(solution)/shard_map/ppermute | solution.py:12
  168.2 1.6 collective-permute-done.5
  170.7 2.4 collective-permute-start.9
  175.8 3.7 %collective-permute-done.10 = f32[8,16,128]{2,1,0:T(8,128)S(1)} collective-permute-done((f32[8,16,128]{2,1,0:T(8,128)S(1)}, f32[8,16,128]{2,1,0:T(8,128)S(1)}, u32[]{:S(2)}, u32[]{:S(2)}) %collective-permute-start.10) | collective-permute-done | bytes 65568 | tf_op jit(solution)/shard_map/ppermute | solution.py:12
  187.6 34.3 %all-gather.8.cloned.1.call-done = f32[8,54,16,128]{3,2,0,1:T(8,128)} async-done(((f32[1,54,16,128]{3,2,0,1:T(8,128)}), f32[8,54,16,128]{3,2,0,1:T(8,128)}) %all-gather.8.cloned.1.call-update) | async-done | bytes 3538960 | tf_op jit(solution)/shard_map/all_gather | solution.py:128
  223.0 2.6 reshape.414
  225.6 2.4 copy.181
  228.0 1.9 slice-done
  230.0 3.1 fusion.24
  233.1 6.3 %fusion.10 = f32[8,48,16,128]{3,1,2,0:T(8,128)S(1)} fusion(f32[8,48,16,144]{3,2,0,1:T(8,128)S(1)} %fusion.24, f32[8,128,144]{1,2,0:T(8,128)S(1)} %select_reduce_fusion), kind=kOutput, calls=%fused_computation.17 | convolution fusion | flops 679477248 | bytes 7274496 | tf_op jit(solution)/shard_map/vyiz,vwz->vyiw/dot_general | solution.py:131
  240.6 3.2 fusion.26
  243.9 3.1 fusion.14
  247.0 2.9 fusion.21
  250.3 2.1 slice.280
  252.4 3.5 %copy.257 = f32[8,6,8,16,16]{4,2,3,1,0:T(8,128)} copy(f32[8,6,8,16,16]{4,3,0,2,1:T(8,128)S(1)} %bitcast.356) | data formatting | bytes 786432 | tf_op jit(solution)/shard_map/vmap()/reshape | solution.py:24
  255.9 2.6 concatenate.142
  258.5 2.2 copy_dynamic-update-slice_fusion
  261.1 3.4 %collective-permute-done.11 = f32[4,1,54,16,128]{4,3,2,0,1:T(8,128)S(1)} collective-permute-done((f32[4,1,54,16,128]{4,3,2,0,1:T(8,128)S(1)}, f32[4,1,54,16,128]{4,3,2,0,1:T(8,128)S(1)}, u32[]{:S(2)}, u32[]{:S(2)}) %collective-permute-start.11) | collective-permute-done | bytes 1769504 | tf_op jit(solution)/shard_map/ppermute | solution.py:12
  267.3 10.2 %collective-permute-done.14 = f32[1,2,27,16,128]{4,3,2,1,0:T(8,128)} collective-permute-done((f32[1,2,27,16,128]{4,3,2,1,0:T(8,128)S(1)}, f32[1,2,27,16,128]{4,3,2,1,0:T(8,128)}, u32[]{:S(2)}, u32[]{:S(2)}) %collective-permute-start.14) | collective-permute-done | bytes 442400 | tf_op jit(solution)/shard_map/ppermute | solution.py:12
  278.6 1.5 collective-permute-start.15
  280.8 4.6 %collective-permute-done.15 = f32[1,1,27,16,128]{4,3,2,1,0:T(8,128)S(1)} collective-permute-done((f32[1,1,27,16,128]{4,3,2,1,0:T(8,128)S(1)}, f32[1,1,27,16,128]{4,3,2,1,0:T(8,128)S(1)}, u32[]{:S(2)}, u32[]{:S(2)}) %collective-permute-start.15) | collective-permute-done | bytes 221216 | tf_op jit(solution)/shard_map/ppermute | solution.py:12
  287.8 2.5 collective-permute-start.18
  294.1 3.5 %collective-permute-done.17 = f32[12,16,128]{2,1,0:T(8,128)S(1)} collective-permute-done((f32[12,16,128]{2,1,0:T(8,128)S(1)}, f32[12,16,128]{2,1,0:T(8,128)S(1)}, u32[]{:S(2)}, u32[]{:S(2)}) %collective-permute-start.17) | collective-permute-done | bytes 98336 | tf_op jit(solution)/shard_map/ppermute | solution.py:12
  298.1 1.9 collective-permute-done.16
  303.5 28.9 %all-gather.12.cloned.1.call-done = f32[128,16,128]{2,1,0:T(8,128)} async-done(((f32[32,16,128]{2,1,0:T(8,128)}), f32[128,16,128]{2,1,0:T(8,128)}) %all-gather.12.cloned.1.call-update) | async-done | bytes 1048592 | tf_op jit(solution)/shard_map/all_gather | solution.py:170
  334.6 1.6 copy.201
  (208 shorter events, 45.6 us)
Async XLA Ops:
  6.5 1.2 copy-start
  6.5 96.9 %all-gather.10.cloned.1.call-start = ((), (), s32[]{:S(2)}) async-start(), calls=%async_computation.1 | async-start | bytes 3981312 | tf_op jit(solution)/shard_map/all_gather | solution.py:128
  8.3 8.3 %copy-start.14 = (s32[2]{0:T(128)S(1)}, s32[2]{0:T(128)}, u32[]{:S(2)}) copy-start(s32[2]{0:T(128)} %param.8) | copy-start | bytes 28
  8.3 8.4 %copy-start.13 = (s32[2,16]{1,0:T(2,128)S(1)}, s32[2,16]{1,0:T(2,128)}, u32[]{:S(2)}) copy-start(s32[2,16]{1,0:T(2,128)} %param.9) | copy-start | bytes 388
  8.3 8.4 %copy-start.12 = (f32[2,3,32]{2,0,1:T(2,128)S(1)}, f32[2,3,32]{2,0,1:T(2,128)}, u32[]{:S(2)}) copy-start(f32[2,3,32]{2,0,1:T(2,128)} %param.7) | copy-start | bytes 2308
  9.3 212.6 %all-gather.8.cloned.1.call-start = ((), (), s32[]{:S(2)}) async-start(), calls=%async_computation | async-start | bytes 3981312 | tf_op jit(solution)/shard_map/all_gather | solution.py:128
  12.2 109.2 %copy-start.5 = (f32[2,16,32,128]{3,2,1,0:T(8,128)}, f32[2,16,32,128]{3,2,1,0:T(8,128)S(1)}, u32[]{:S(2)}) copy-start(f32[2,16,32,128]{3,2,1,0:T(8,128)S(1)} %get-tuple-element.7) | copy-start | bytes 1572868
  12.2 109.2 %collective-permute-start = (f32[2,16,32,128]{3,2,1,0:T(8,128)}, f32[2,16,32,128]{3,2,1,0:T(8,128)}, u32[]{:S(2)}, u32[]{:S(2)}) collective-permute-start(f32[2,16,32,128]{3,2,1,0:T(8,128)} %get-tuple-element.8), channel_id=1, source_target_pairs={{0,8},{8,0},{16,24},{24,16},{1,9},{9,1},{17,25},{25,17},{2,10},{10... | collective-permute-start | bytes 1572872 | tf_op jit(solution)/shard_map/ppermute | solution.py:12
  12.2 109.2 %collective-permute-start.2 = (f32[2,16,32,128]{3,2,1,0:T(8,128)}, f32[2,16,32,128]{3,2,1,0:T(8,128)}, u32[]{:S(2)}, u32[]{:S(2)}) collective-permute-start(f32[2,16,32,128]{3,2,1,0:T(8,128)} %get-tuple-element.9), channel_id=1, source_target_pairs={{0,24},{8,16},{16,8},{24,0},{1,25},{9,17},{17,9},{25,1},{2,26},{10... | collective-permute-start | bytes 1572872 | tf_op jit(solution)/shard_map/ppermute | solution.py:12
  15.3 106.1 %collective-permute-start.1 = (f32[2,16,32,128]{3,2,1,0:T(8,128)S(1)}, f32[2,16,32,128]{3,2,1,0:T(8,128)}, u32[]{:S(2)}, u32[]{:S(2)}) collective-permute-start(f32[2,16,32,128]{3,2,1,0:T(8,128)S(1)} %get-tuple-element.10), channel_id=1, source_target_pairs={{0,16},{8,24},{16,0},{24,8},{1,17},{9,25},{17,1},{25,9},{2,18},{10... | collective-permute-start | bytes 1572872 | tf_op jit(solution)/shard_map/ppermute | solution.py:12
  107.1 2.6 copy-start.9
  107.1 3.1 copy-start.11
  124.3 3.2 copy-start.7
  141.5 3.8 %collective-permute-start.3 = (f32[4,1,54,16,128]{4,3,2,0,1:T(8,128)S(1)}, f32[4,1,54,16,128]{4,3,2,0,1:T(8,128)S(1)}, u32[]{:S(2)}, u32[]{:S(2)}) collective-permute-start(f32[4,1,54,16,128]{4,3,2,0,1:T(8,128)S(1)} %slice_bitcast_fusion.2), channel_id=1, source_target_pairs={{0,1},{1,0},{2,3},{3,2},{4,5},{5,4},{6,7},{7,6},{8,9},{9,8},{10,11... | collective-permute-start | bytes 5308424 | tf_op jit(solution)/shard_map/ppermute | solution.py:12
  146.5 12.7 %collective-permute-start.6 = (f32[1,2,27,16,128]{4,3,2,1,0:T(8,128)}, f32[1,2,27,16,128]{4,3,2,1,0:T(8,128)}, u32[]{:S(2)}, u32[]{:S(2)}) collective-permute-start(f32[1,2,27,16,128]{4,3,2,1,0:T(8,128)} %slice_bitcast_fusion.8), channel_id=1, source_target_pairs={{0,4},{1,5},{2,6},{3,7},{4,0},{5,1},{6,2},{7,3},{8,12},{9,13},{10,... | collective-permute-start | bytes 1327112 | tf_op jit(solution)/shard_map/ppermute | solution.py:12
  148.3 14.5 %collective-permute-start.4 = (f32[2,1,27,16,128]{4,3,2,0,1:T(8,128)S(1)}, f32[2,1,27,16,128]{4,3,2,0,1:T(8,128)S(1)}, u32[]{:S(2)}, u32[]{:S(2)}) collective-permute-start(f32[2,1,27,16,128]{4,3,2,0,1:T(8,128)S(1)} %slice_bitcast_fusion.10), channel_id=1, source_target_pairs={{0,2},{1,3},{2,0},{3,1},{4,6},{5,7},{6,4},{7,5},{8,10},{9,11},{10,... | collective-permute-start | bytes 1327112 | tf_op jit(solution)/shard_map/ppermute | solution.py:12
  160.3 7.9 %collective-permute-start.7 = (f32[1,1,27,16,128]{4,3,2,1,0:T(8,128)S(1)}, f32[1,1,27,16,128]{4,3,2,1,0:T(8,128)S(1)}, u32[]{:S(2)}, u32[]{:S(2)}) collective-permute-start(f32[1,1,27,16,128]{4,3,2,1,0:T(8,128)S(1)} %slice_bitcast_fusion.16), channel_id=1, source_target_pairs={{0,2},{1,3},{2,0},{3,1},{4,6},{5,7},{6,4},{7,5},{8,10},{9,11},{10,... | collective-permute-start | bytes 663560 | tf_op jit(solution)/shard_map/ppermute | solution.py:12
  162.9 7.0 %collective-permute-start.5 = (f32[1,1,27,16,128]{4,3,2,1,0:T(8,128)S(1)}, f32[1,1,27,16,128]{4,3,2,1,0:T(8,128)S(1)}, u32[]{:S(2)}, u32[]{:S(2)}) collective-permute-start(f32[1,1,27,16,128]{4,3,2,1,0:T(8,128)S(1)} %slice_bitcast_fusion.18), channel_id=1, source_target_pairs={{0,4},{1,5},{2,6},{3,7},{4,0},{5,1},{6,2},{7,3},{8,12},{9,13},{10,... | collective-permute-start | bytes 663560 | tf_op jit(solution)/shard_map/ppermute | solution.py:12
  170.7 10.0 %collective-permute-start.9 = (f32[12,16,128]{2,1,0:T(8,128)S(1)}, f32[12,16,128]{2,1,0:T(8,128)S(1)}, u32[]{:S(2)}, u32[]{:S(2)}) collective-permute-start(f32[12,16,128]{2,1,0:T(8,128)S(1)} %pad_maximum_fusion.5), channel_id=1, source_target_pairs={{0,24},{8,16},{16,8},{24,0},{1,25},{9,17},{17,9},{25,1},{2,26},{10... | collective-permute-start | bytes 294920 | tf_op jit(solution)/shard_map/ppermute | solution.py:12
  173.5 6.0 %collective-permute-start.10 = (f32[8,16,128]{2,1,0:T(8,128)S(1)}, f32[8,16,128]{2,1,0:T(8,128)S(1)}, u32[]{:S(2)}, u32[]{:S(2)}) collective-permute-start(f32[8,16,128]{2,1,0:T(8,128)S(1)} %pad_maximum_fusion.7), channel_id=1, source_target_pairs={{0,16},{8,24},{16,0},{24,8},{1,17},{9,25},{17,1},{25,9},{2,18},{10... | collective-permute-start | bytes 196616 | tf_op jit(solution)/shard_map/ppermute | solution.py:12
  174.4 8.5 %collective-permute-start.8 = (f32[36,16,128]{2,1,0:T(8,128)}, f32[36,16,128]{2,1,0:T(8,128)}, u32[]{:S(2)}, u32[]{:S(2)}) collective-permute-start(f32[36,16,128]{2,1,0:T(8,128)} %pad_maximum_fusion.3), channel_id=1, source_target_pairs={{0,8},{8,0},{16,24},{24,16},{1,9},{9,1},{17,25},{25,17},{2,10},{10... | collective-permute-start | bytes 884744 | tf_op jit(solution)/shard_map/ppermute | solution.py:12
  180.9 1.0 copy-start.4
  186.4 39.1 %copy-start.2 = (f32[48,16,128]{2,1,0:T(8,128)}, f32[48,16,128]{2,1,0:T(8,128)S(1)}, u32[]{:S(2)}) copy-start(f32[48,16,128]{2,1,0:T(8,128)S(1)} %select_add_fusion.1) | copy-start | bytes 1179652
  187.4 145.0 %all-gather.12.cloned.1.call-start = ((), (), s32[]{:S(2)}) async-start(), calls=%async_computation.2 | async-start | bytes 1310720 | tf_op jit(solution)/shard_map/all_gather | solution.py:170
  228.0 1.9 slice-start
  228.0 2.0 copy-start.10
  239.4 1.2 copy-start.6
  243.9 3.1 copy-start.8
  260.8 3.8 %collective-permute-start.11 = (f32[4,1,54,16,128]{4,3,2,0,1:T(8,128)S(1)}, f32[4,1,54,16,128]{4,3,2,0,1:T(8,128)S(1)}, u32[]{:S(2)}, u32[]{:S(2)}) collective-permute-start(f32[4,1,54,16,128]{4,3,2,0,1:T(8,128)S(1)} %slice_bitcast_fusion), channel_id=1, source_target_pairs={{0,1},{1,0},{2,3},{3,2},{4,5},{5,4},{6,7},{7,6},{8,9},{9,8},{10,11... | collective-permute-start | bytes 5308424 | tf_op jit(solution)/shard_map/ppermute | solution.py:12
  265.0 12.5 %collective-permute-start.14 = (f32[1,2,27,16,128]{4,3,2,1,0:T(8,128)S(1)}, f32[1,2,27,16,128]{4,3,2,1,0:T(8,128)}, u32[]{:S(2)}, u32[]{:S(2)}) collective-permute-start(f32[1,2,27,16,128]{4,3,2,1,0:T(8,128)S(1)} %slice_bitcast_fusion.4), channel_id=1, source_target_pairs={{0,4},{1,5},{2,6},{3,7},{4,0},{5,1},{6,2},{7,3},{8,12},{9,13},{10,... | collective-permute-start | bytes 1327112 | tf_op jit(solution)/shard_map/ppermute | solution.py:12
  266.2 14.0 %collective-permute-start.12 = (f32[2,1,27,16,128]{4,3,2,0,1:T(8,128)S(1)}, f32[2,1,27,16,128]{4,3,2,0,1:T(8,128)S(1)}, u32[]{:S(2)}, u32[]{:S(2)}) collective-permute-start(f32[2,1,27,16,128]{4,3,2,0,1:T(8,128)S(1)} %slice_bitcast_fusion.6), channel_id=1, source_target_pairs={{0,2},{1,3},{2,0},{3,1},{4,6},{5,7},{6,4},{7,5},{8,10},{9,11},{10,... | collective-permute-start | bytes 1327112 | tf_op jit(solution)/shard_map/ppermute | solution.py:12
  278.6 6.8 %collective-permute-start.15 = (f32[1,1,27,16,128]{4,3,2,1,0:T(8,128)S(1)}, f32[1,1,27,16,128]{4,3,2,1,0:T(8,128)S(1)}, u32[]{:S(2)}, u32[]{:S(2)}) collective-permute-start(f32[1,1,27,16,128]{4,3,2,1,0:T(8,128)S(1)} %slice_bitcast_fusion.12), channel_id=1, source_target_pairs={{0,2},{1,3},{2,0},{3,1},{4,6},{5,7},{6,4},{7,5},{8,10},{9,11},{10,... | collective-permute-start | bytes 663560 | tf_op jit(solution)/shard_map/ppermute | solution.py:12
  280.2 6.6 %collective-permute-start.13 = (f32[1,1,27,16,128]{4,3,2,1,0:T(8,128)S(1)}, f32[1,1,27,16,128]{4,3,2,1,0:T(8,128)S(1)}, u32[]{:S(2)}, u32[]{:S(2)}) collective-permute-start(f32[1,1,27,16,128]{4,3,2,1,0:T(8,128)S(1)} %slice_bitcast_fusion.14), channel_id=1, source_target_pairs={{0,4},{1,5},{2,6},{3,7},{4,0},{5,1},{6,2},{7,3},{8,12},{9,13},{10,... | collective-permute-start | bytes 663560 | tf_op jit(solution)/shard_map/ppermute | solution.py:12
  287.8 6.0 %collective-permute-start.18 = (f32[8,16,128]{2,1,0:T(8,128)S(1)}, f32[8,16,128]{2,1,0:T(8,128)S(1)}, u32[]{:S(2)}, u32[]{:S(2)}) collective-permute-start(f32[8,16,128]{2,1,0:T(8,128)S(1)} %pad_maximum_fusion.8), channel_id=1, source_target_pairs={{0,16},{8,24},{16,0},{24,8},{1,17},{9,25},{17,1},{25,9},{2,18},{10... | collective-permute-start | bytes 196616 | tf_op jit(solution)/shard_map/ppermute | solution.py:12
  291.0 9.0 %collective-permute-start.16 = (f32[36,16,128]{2,1,0:T(8,128)}, f32[36,16,128]{2,1,0:T(8,128)}, u32[]{:S(2)}, u32[]{:S(2)}) collective-permute-start(f32[36,16,128]{2,1,0:T(8,128)} %pad_maximum_fusion.4), channel_id=1, source_target_pairs={{0,8},{8,0},{16,24},{24,16},{1,9},{9,1},{17,25},{25,17},{2,10},{10... | collective-permute-start | bytes 884744 | tf_op jit(solution)/shard_map/ppermute | solution.py:12
  291.9 5.7 %collective-permute-start.17 = (f32[12,16,128]{2,1,0:T(8,128)S(1)}, f32[12,16,128]{2,1,0:T(8,128)S(1)}, u32[]{:S(2)}, u32[]{:S(2)}) collective-permute-start(f32[12,16,128]{2,1,0:T(8,128)S(1)} %pad_maximum_fusion.6), channel_id=1, source_target_pairs={{0,24},{8,16},{16,8},{24,0},{1,25},{9,17},{17,9},{25,1},{2,26},{10... | collective-permute-start | bytes 294920 | tf_op jit(solution)/shard_map/ppermute | solution.py:12
  300.9 1.7 copy-start.3
  303.5 32.7 %copy-start.1 = (f32[16,64,256]{2,1,0:T(8,128)S(1)}, f32[16,64,256]{2,1,0:T(8,128)}, u32[]{:S(2)}) copy-start(f32[16,64,256]{2,1,0:T(8,128)} %param.5) | copy-start | bytes 3145732
Sparse Core Ops, SparseCore 0:
  9.4 35.1 all-gather.9
  187.5 34.3 all-gather.7
  303.6 28.7 all-gather.11

commit v2 on v1

v2 whole, which is shorter than its diff:
```python
import functools

import jax
import jax.numpy as jnp
from jax import lax
from jax.experimental import pallas as pl
from jax.experimental.pallas import tpu as pltpu
from jax.sharding import PartitionSpec as P

ITERS = 2
LANES = 128
BLOCK = 8
F32, BF16 = jnp.float32, jnp.bfloat16
PARAMS = pltpu.CompilerParams(vmem_limit_bytes=58 * 1024 * 1024)


def swap(value, axis, mask):
    count = lax.axis_size(axis)
    return lax.ppermute(value, axis, [(i, i ^ mask) for i in range(count)])


def pick(kern, index):
    hit = index[..., None] == jnp.arange(kern.shape[-1])
    lead = kern.reshape(kern.shape[:1] + (1,) * (index.ndim - 1) + kern.shape[1:])
    return jnp.sum(jnp.where(hit, lead, 0.0), axis=-1)


def orders(bits):
    shift = (bits - 1) // 2
    upper = list(range(1, bits))
    return upper, upper[shift:] + upper[:shift]


def scatter_sum(kept, sent):
    bits = lax.axis_size("space").bit_length() - 1
    blocks = kept + swap(sent, "space", 1)
    middle = blocks.shape[1] // 2
    out = []
    for part, order in zip((blocks[:, :middle], blocks[:, middle:]), orders(bits)):
        left = list(range(1, bits))
        for bit in order:
            low = 1 << left.index(bit)
            split = part.reshape((part.shape[0] // (2 * low), 2, low) + part.shape[1:])
            part = split[:, 0] + swap(split[:, 1], "space", 1 << bit)
            part = part.reshape((-1,) + part.shape[2:])
            left.remove(bit)
        out.append(part[0])
    return out


def gather(parts):
    bits = lax.axis_size("space").bit_length() - 1
    out = []
    for part, order in zip(parts, orders(bits)):
        part = part[None]
        have = []
        for bit in reversed(order):
            low = 1 << sum(other < bit for other in have)
            part = part.reshape((part.shape[0] // low, 1, low) + part.shape[1:])
            part = jnp.concatenate([part, swap(part, "space", 1 << bit)], axis=1)
            part = part.reshape((-1,) + part.shape[3:])
            have.append(bit)
        out += [part, swap(part, "space", 1)]
    return out


def split(value):
    high = value.astype(BF16)
    return high, (value - high.astype(F32)).astype(BF16)


def stack3(value):
    high, low = split(value)
    return jnp.concatenate([high, low, high], axis=0)


def mul(a, b):
    return jnp.dot(a, b, preferred_element_type=F32)


def mul3(value, high, low):
    a, b = split(value)
    return mul(a, high) + mul(b, high) + mul(a, low)


def lane_of(shape):
    return lax.broadcasted_iota(jnp.int32, shape, len(shape) - 1)


def ahead_kernel(rad, place, ky, wx, kzh, kzl, a0, a1, b0, b1, blurred, u, uh, zp):
    yh = place[0]
    wy, nvi, hz = u.shape
    hy = blurred.shape[0]
    width = a0.shape[2]
    nviews = nvi // width
    half, group = wy // 2, hz // rad
    for h, pair in enumerate(((a0, a1), (b0, b1))):

        def row(y):
            return jnp.concatenate([ref[k, y] for ref in pair for k in range(ref.shape[0])], axis=0)

        rims = half // group
        for k in range(rims):
            out = mul(wx[...], stack3(row(half + k)))
            for m in range(group):
                uh[h * half + k * group + m] = out if m == 0 else pltpu.roll(out, hz - rad * m, 1)

        def two(p, carry):
            out = mul(wx[...], stack3(jnp.concatenate([row(2 * p), row(2 * p + 1)], axis=1)))
            u[h * half + 2 * p] = out[:, :hz]
            u[h * half + 2 * p + 1] = out[:, hz:]
            return carry

        lax.fori_loop(0, half // 2, two, 0)

    lead = rad * (1 - yh)
    zp[pl.ds((wy) * yh, rad)] = jnp.zeros((rad, nvi, hz), F32)

    def one(v, carry):
        at = pl.ds(pl.multiple_of(v * width, width), width)
        for c in range(2):
            rows = pl.ds(c * half, half)
            value = jnp.concatenate([u[rows, at, :], uh[rows, at, :]], axis=-1)
            out = mul3(value.reshape(half * width, 2 * hz), kzh[v], kzl[v])
            zp[pl.ds(lead + c * half, half), at, :] = out.reshape(half, width, hz)
        return carry

    lax.fori_loop(0, nviews, one, 0)

    def tile(s, carry):
        v = s // (width // 8)
        at = pl.ds(pl.multiple_of(s * 8, 8), 8)
        tap = [ky[v, t] for t in range(2 * rad)]
        for first in range(0, hy, BLOCK):
            total = [None] * BLOCK
            for y in range(first, first + BLOCK + 2 * rad - 1):
                value = zp[y, at, :]
                for k in range(BLOCK):
                    t = y - first - k
                    if 0 <= t < 2 * rad:
                        term = tap[t] * value
                        total[k] = term if total[k] is None else total[k] + term
            for k in range(BLOCK):
                blurred[first + k, at, :] = total[k]
        return carry

    lax.fori_loop(0, nvi // 8, tile, 0)


def back_kernel(rad, npieces, place, ky, wxt, kzh, kzl, blurred, *refs):
    pieces, (kept, sent, r, yb, gm, gh) = refs[:npieces], refs[npieces:]
    yh = place[0]
    hy, nvi, hz = blurred.shape
    wy = gm.shape[0]
    local, width = pieces[0].shape[:2]
    nviews = nvi // width
    half, group = wy // 2, hz // rad
    rims = half // group
    for p, piece in enumerate(pieces):
        for k in range(local):
            first = (p * local + k) * width
            for y in range(hy):
                r[y, first : first + width, :] = piece[k, :, y, :] / blurred[y, first : first + width, :]

    def tile(s, carry):
        v = s // (width // 8)
        at = pl.ds(pl.multiple_of(s * 8, 8), 8)
        tap = [ky[v, t] for t in range(2 * rad)]
        for first in range(0, hy + 2 * rad, BLOCK):
            total = [None] * BLOCK
            for y in range(max(0, first - 2 * rad + 1), min(hy, first + BLOCK)):
                value = r[y, at, :]
                for k in range(BLOCK):
                    t = first + k - y
                    if 0 <= t < 2 * rad:
                        term = tap[t] * value
                        total[k] = term if total[k] is None else total[k] + term
            for k in range(BLOCK):
                yb[first + k, at, :] = jnp.zeros((8, hz), F32) if total[k] is None else total[k]
        return carry

    lax.fori_loop(0, nvi // 8, tile, 0)

    lead = rad * (1 - yh)

    def one(v, carry):
        at = pl.ds(pl.multiple_of(v * width, width), width)
        for c in range(2):
            value = yb[pl.ds(lead + c * half, half), at, :].reshape(half * width, hz)
            out = mul3(value, kzh[v], kzl[v]).reshape(half, width, 2 * hz)
            gm[pl.ds(c * half, half), at, :] = out[..., :hz]
            for k in range(rims):
                total = out[k * group, :, hz:]
                for m in range(1, group):
                    total = total + pltpu.roll(out[k * group + m, :, hz:], rad * m, 1)
                gh[c * rims + k, at, :] = total
        return carry

    lax.fori_loop(0, nviews, one, 0)

    def store(out, row):
        for c, ref in enumerate((kept, sent)):
            for k in range(ref.shape[0]):
                first = (c * ref.shape[0] + k) * width
                ref[k, row] = out[first : first + width]

    for c in range(2):
        for k in range(rims):
            store(mul(wxt[...], stack3(gh[c * rims + k])), c * (half + rims) + half + k)

        def two(p, carry):
            y = c * half + 2 * p
            out = mul(wxt[...], stack3(jnp.concatenate([gm[y], gm[y + 1]], axis=1)))
            row = c * (half + rims) + 2 * p
            store(out[:, :hz], row)
            store(out[:, hz:], row + 1)
            return carry

        lax.fori_loop(0, half // 2, two, 0)


def row_of(a, b, y, half):
    return a[y] if y < half else b[y - half]


def pack_kernel(rad, place, a, b, to_y, to_z, to_c, edge):
    yh, zh = place[0], place[1]
    rows, width, hz = a.shape
    group = hz // rad
    half = rows * group // (group + 1)
    rims, wy = half // group, 2 * half
    begin = (hz - rad) * (1 - zh)
    lane = lane_of((width, hz)) // rad
    for o in range(2 * rims):
        total = None
        for m in range(group):
            value = pltpu.roll(row_of(a, b, o * group + m, half), (rad * m - begin + hz) % hz, 1)
            total = value if m == 0 else jnp.where(lane == m, value, total)
        edge[o] = total
        to_z[2 * rims + o] = total
        to_z[o] = (a if o < rims else b)[half + o % rims]
    hy = wy - rad
    over = hy // group
    for y in range(wy):
        @pl.when(jnp.logical_and(y >= rad * (1 - yh), y < rad * (1 - yh) + hy))
        def _():
            to_y[y - rad * (1 - yh)] = row_of(a, b, y, half)
    skip = (rad // group) * (1 - yh)
    for k in range(over):
        to_y[hy + k] = to_z[skip + k]
        to_c[k] = to_z[skip + k]
        to_c[over + k] = edge[skip + k]


def update_kernel(rad, place, a, b, fy, fz, fc, old, count, new):
    yh, zh = place[0], place[1]
    rows, width, hz = a.shape
    group = hz // rad
    half = rows * group // (group + 1)
    rims, wy = half // group, 2 * half
    hy = wy - rad
    over = hy // group
    start, skip = rad * (1 - yh), (rad // group) * (1 - yh)
    begin = (hz - rad) * (1 - zh)
    zero = jnp.zeros((width, hz), F32)
    inside = (lane_of((width, hz)) >= begin) & (lane_of((width, hz)) < begin + rad)
    total = count[...]

    def part(ref, first, at, limit):
        ok = jnp.logical_and(at >= 0, at < limit)
        return jnp.where(ok, ref[first + jnp.clip(at, 0, limit - 1)], zero)

    for o in range(2 * rims):
        h, k = o // rims, o % rims
        row = h * rows + half + k
        rim = (a, b)[h][half + k] + fz[2 * rims + o]
        rim = rim + part(fy, hy, o - skip, over) + part(fc, over, o - skip, over)
        new[row] = old[row] * rim / total
        edge = fz[o] + part(fc, 0, o - skip, over)
        for m in range(group):
            y = o * group + m
            moved = jnp.where(inside, pltpu.roll(edge, (begin - rad * m + hz) % hz, 1), 0.0)
            value = row_of(a, b, y, half) + part(fy, 0, y - start, hy) + moved
            row = h * rows + y - h * half
            new[row] = old[row] * value / total


VMEM = pl.BlockSpec(memory_space=pltpu.VMEM)
SMEM = pl.BlockSpec(memory_space=pltpu.SMEM)


def call(kernel, shapes, scratch, smem, cost, *args):
    flops, moved = cost
    return pl.pallas_call(
        kernel,
        out_shape=[jax.ShapeDtypeStruct(shape, F32) for shape in shapes],
        in_specs=[SMEM] * smem + [VMEM] * (len(args) - smem),
        out_specs=[VMEM] * len(shapes),
        scratch_shapes=[pltpu.VMEM(shape, F32) for shape in scratch],
        compiler_params=PARAMS,
        cost_estimate=pl.CostEstimate(flops=flops, bytes_accessed=moved, transcendentals=0),
    )(*args)


def body(prior, data, taps, offsets, coverage):
    nview, nspace = lax.axis_size("view"), lax.axis_size("space")
    g, j = lax.axis_index("view"), lax.axis_index("space")
    zh, yh = g >> 1, (g ^ (g >> 1)) & 1
    place_yz = jnp.stack([yh, zh]).astype(jnp.int32)
    local, width, ny, nz = data.shape
    ntaps = taps.shape[-1]
    rad = ntaps // 2
    hy, hz = ny // 2, nz // 2
    wy = hy + rad
    group = hz // rad
    half, rims = wy // 2, wy // 2 // group
    rows = half + rims

    flat = jnp.concatenate(
        [
            taps.reshape(local, -1),
            offsets.astype(jnp.float32)[:, None],
            coverage.astype(jnp.float32),
        ],
        axis=1,
    )
    used = flat.shape[1]
    flat = jnp.pad(flat, ((0, 0), (0, -used % LANES)))
    shared = [flat] + [swap(flat, "view", r) for r in range(1, nview)]
    *shared, data = lax.optimization_barrier((*shared, data))
    shared = jnp.concatenate(shared, axis=0)

    def quadrant(owner):
        oz, oy = owner >> 1, (owner ^ (owner >> 1)) & 1
        return lax.dynamic_slice(data, (0, 0, oy * hy, oz * hz), (local, width, hy, hz))

    pieces = [quadrant(g)] + [swap(quadrant(g ^ r), "view", r) for r in range(1, nview)]

    nviews = nview * local
    nvi = nviews * width
    kern = shared[:, : 3 * ntaps].reshape(nviews, 3, ntaps)
    kern = kern / jnp.sum(kern, axis=-1, keepdims=True)
    turn = shared[:, 3 * ntaps].astype(jnp.int32)
    cover = shared[:, 3 * ntaps + 1 : used]
    count = jnp.broadcast_to(jnp.sum(cover, axis=0)[:, None], (width, hz))
    note = jnp.pad(cover.T, ((0, 0), (0, hz - nviews)))[None]

    window = lax.dynamic_slice_in_dim(prior, rad * yh, wy, axis=1).transpose(1, 0, 2)
    main = lax.dynamic_slice_in_dim(window, hz * zh, hz, axis=2)
    rim = lax.dynamic_slice_in_dim(window, jnp.where(zh == 0, hz, hz - rad), rad, axis=2)
    rim = rim.reshape(2 * rims, group, width, rad).transpose(0, 2, 1, 3).reshape(2 * rims, width, hz)
    parts = [main[:half], rim[:rims], main[half:], rim[rims:]]
    estimate = jnp.concatenate(parts, axis=0)
    wide = gather([jnp.concatenate(parts[:2] + [note], axis=0), jnp.concatenate(parts[2:], axis=0)])
    cover = jnp.stack([wide[0][:, -1], wide[1][:, -1]])[..., :nviews]
    cover = cover.transpose(3, 0, 1, 2).reshape(nviews, 1, nspace * width)

    slab = (j - turn) % nspace
    spot = slab[:, None] * width + jnp.arange(width)
    order = jnp.arange(nspace).reshape(nspace // 2, 2).T.reshape(-1)
    planes = ((j ^ order)[:, None] * width + jnp.arange(width)).reshape(-1)
    band_x = pick(kern[:, 0], planes - spot[:, :, None] + rad)
    band_xt = (band_x * cover).reshape(nvi, -1).T
    band_x = band_x.reshape(nvi, -1)

    def halves(value):
        high = lax.reduce_precision(value, 8, 7)
        return high.astype(BF16), (value - high).astype(BF16)

    def triple(value):
        high, low = halves(value)
        return jnp.concatenate([high, high, low], axis=1)

    wx, wxt = triple(band_x), triple(band_xt)
    cells = jnp.concatenate([jnp.arange(hz) + hz * zh, jnp.arange(hz) + jnp.where(zh == 0, hz, hz - rad)])
    real = jnp.arange(2 * hz) < hz + rad
    goal = jnp.arange(hz) + hz * zh
    index = jnp.where(real[:, None], cells[:, None] - goal + rad, -1)
    band_z = pick(kern[:, 2], index[None])
    kz = halves(band_z)
    kzt = halves(band_z.transpose(0, 2, 1))
    ky = kern[:, 1]

    plane = width * hz
    mxu = 2 * 3 * nvi * plane * 2 * rows * (nspace // 2)

    def ahead(wide):
        return call(
            functools.partial(ahead_kernel, rad),
            [(hy, nvi, hz)],
            [(wy, nvi, hz), (wy, nvi, hz), (wy + rad, nvi, hz)],
            2,
            (mxu, 4 * plane * (nspace * 2 * rows + hy * nviews)),
            place_yz, ky, wx, *kz, *wide,
        )[0]

    def back(blurred):
        return call(
            functools.partial(back_kernel, rad, nview),
            [(nspace // 2, 2 * rows, width, hz)] * 2,
            [(hy, nvi, hz), (hy + 2 * rad, nvi, hz), (wy, nvi, hz), (2 * rims, nvi, hz)],
            2,
            (mxu, 4 * plane * (nspace * 2 * rows + 2 * hy * nviews)),
            place_yz, ky, wxt, *kzt, blurred, *pieces,
        )

    over = hy // group
    for step in range(ITERS):
        if step:
            wide = gather([estimate[:rows], estimate[rows:]])
        a, b = scatter_sum(*back(ahead(wide)))
        to_y, to_z, to_c = call(
            functools.partial(pack_kernel, rad),
            [(hy + over, width, hz), (4 * rims, width, hz), (2 * over, width, hz)],
            [(2 * rims, width, hz)],
            1,
            (plane, 4 * plane * 4 * rows),
            place_yz, a, b,
        )
        estimate = call(
            functools.partial(update_kernel, rad),
            [(2 * rows, width, hz)],
            [],
            1,
            (plane, 4 * plane * 8 * rows),
            place_yz, a, b, swap(to_y, "view", 1), swap(to_z, "view", 3), swap(to_c, "view", 2), estimate, count,
        )[0]

    main = jnp.concatenate([estimate[:half], estimate[rows : rows + half]], axis=0)
    own = lax.dynamic_slice_in_dim(main, rad * yh, hy, axis=0)
    parts = lax.all_gather(own, "view")
    low = jnp.concatenate([parts[0], parts[1]], axis=0)
    high = jnp.concatenate([parts[3], parts[2]], axis=0)
    return jnp.concatenate([low, high], axis=-1).transpose(1, 0, 2)


def solution(mesh):
    return jax.shard_map(
        body,
        mesh=mesh,
        in_specs=(
            P("space", None, None),
            P("view", "space", None, None),
            P("view", None, None),
            P("view"),
            P("view", "space"),
        ),
        out_specs=P("space", None, None),
        check_vma=False,
    )
```

time: 348 us -> 289 us (0.83)
  Pallas kernels: 0 us -> 85.3 us
  blocking collectives: 67.8 us -> 0 us
  local copies, waits for them, and re-layouts: 55.4 us -> 14.6 us
  matrix products: 40.3 us -> 0 us
  starting transfers between devices: 25.8 us -> 37.8 us
    pallas_call x0 -> x8, Pallas kernels: none -> 85.3 us  [call(): pl.pallas_call(kernel, out_shape=[jax.ShapeDtypeStruct(shape, F32) for sh...]
    all_gather x1 -> x0, blocking collectives: 67.8 us -> none  [body(): every = lax.all_gather(flat, ('view', 'space'))]
    dot_general x12 -> x0, matrix products: 40.3 us -> none  [the longest x2 13.1 us: body(): inner = jnp.einsum('vyiz,vwz->vyiw', inner, band_z, precision=HIGH)]
    all_gather x2 -> x0, waiting for transfers between devices: 34.3 us -> none  [body(): wide = lax.all_gather(estimate, 'space')]
    ppermute x19 -> x34, waiting for transfers between devices: 47.4 us -> 80.6 us  [swap(): return lax.ppermute(value, axis, [(i, i ^ mask) for i in range(count)])]
    reshape x27 -> x0, local copies, waits for them, and re-layouts: 15.5 us -> none  [the longest x4 7.29 us: pack(): edge = edge.reshape(rows // group, group, planes, cells)]
    ppermute x19 -> x34, starting transfers between devices: 25.5 us -> 37.8 us  [swap(): return lax.ppermute(value, axis, [(i, i ^ mask) for i in range(count)])]
    slice x18 -> x5, local copies, waits for them, and re-layouts: 10.6 us -> 1.32 us  [the longest x1 1.05 us: body(): estimate[rows:rows + half]]
  transfers between devices with their start and end apart: 22 -> 35, of which waited for: 15 -> 22; matrix products, arithmetic and copies ran while one was open for 14% -> 9% of each run, Pallas kernels for 0% -> 6%
where the time goes in v2:
time: 289 us; the launch traced here: 287 us
  waiting for transfers between devices  108 us (37%)
  Pallas kernels  85.3 us (30%)
  starting transfers between devices  37.8 us (13%)
  other arithmetic  27.1 us (9%)
  local copies, waits for them, and re-layouts  14.6 us (5%)
  between operations  14 us (5%)
    pallas_call x8, Pallas kernels, call(): pl.pallas_call(kernel, out_shape=[jax.ShapeDtypeStruct(shape, F32) for sh...  85.3 us
    ppermute x34, waiting for transfers between devices, swap(): return lax.ppermute(value, axis, [(i, i ^ mask) for i in range(count)])  80.6 us
    ppermute x34, starting transfers between devices, swap(): return lax.ppermute(value, axis, [(i, i ^ mask) for i in range(count)])  37.8 us
    all_gather x1, waiting for transfers between devices, body(): parts = lax.all_gather(own, 'view')  27.6 us
    reduce_sum x2, other arithmetic, pick(): return jnp.sum(jnp.where(hit, lead, 0.0), axis=-1)  7.04 us
  transfers between devices with their start and end apart: 35, of which 22 were waited for; matrix products, arithmetic and copies ran while one was open for 9% of the time, Pallas kernels for 6%

profile of v2, /device:TPU:8, one launch (start us, length us, event | category | flops | bytes accessed | tf_op | source)
XLA Modules:
  0.0 286.9 jit_solution(1261936720578294641)
XLA Ops:
  8.9 3.0 %collective-permute-start.1 = (f32[2,128]{1,0:T(2,128)S(1)}, f32[2,128]{1,0:T(2,128)S(1)}, u32[]{:S(2)}, u32[]{:S(2)}) collective-permute-start(f32[2,128]{1,0:T(2,128)S(1)} %select_maximum_fusion), channel_id=1, source_target_pairs={{0,16},{8,24},{16,0},{24,8},{1,17},{9,25},{17,1},{25,9},{2,18},{10... | collective-permute-start | bytes 3080 | tf_op jit(solution)/shard_map/ppermute | solution.py:19
  13.2 1.6 collective-permute-start.6
  17.7 1.6 collective-permute-start.3
  19.3 6.5 %select_reduce_fusion = f32[8,256,128]{2,1,0:T(8,128)S(1)} fusion(f32[8,32]{1,0:T(8,128)S(1)} %get-tuple-element.61, pred[256,128,32]{1,2,0:T(8,128)(4,1)S(1)} %iota_compare_fusion), kind=kLoop, calls=%fused_computation | loop fusion | flops 16515072 | bytes 2098176 | tf_op jit(solution)/shard_map/reduce_sum | solution.py:25
  28.0 1.4 constant_dynamic-slice_fusion
  32.0 3.3 %collective-permute-start.9 = (f32[2,16,32,128]{3,2,1,0:T(8,128)}, f32[2,16,32,128]{3,2,1,0:T(8,128)S(1)}, u32[]{:S(2)}, u32[]{:S(2)}) collective-permute-start(f32[2,16,32,128]{3,2,1,0:T(8,128)} %get-tuple-element.37), channel_id=1, source_target_pairs={{0,8},{8,0},{16,24},{24,16},{1,9},{9,1},{17,25},{25,17},{2,10},{10... | collective-permute-start | bytes 1572872 | tf_op jit(solution)/shard_map/ppermute | solution.py:19
  35.5 1.3 collective-permute-start.11
  36.8 1.5 collective-permute-done.4
  39.6 1.2 collective-permute-done.7
  40.8 2.1 pad_maximum_fusion.1
  46.1 18.4 %shard_map.55.blurred = f32[32,128,128]{2,1,0:T(8,128)} custom-call(s32[2]{0:T(128)} %pad_add_fusion.1.place, f32[8,32]{1,0:T(8,128)} %get-tuple-element.63.ky, bf16[128,384]{1,0:T(8,128)(2,1)} %pad_maximum_fusion.6.wx, bf16[8,256,128]{2,1,0:T(8,128)(2,1)} %get-tuple-element.46.kzh, bf16[8,256,128]{2,1,0:T(8,128)(2,1)} %get-tuple-element.45.kzl, ...), custom_call_target="tpu_custom_call" | custom-call | flops 339738624 | bytes 5636096 | tf_op jit(solution)/shard_map/pallas_call | solution.py:294
  65.1 5.5 %collective-permute-done.10.refs_2_ = f32[2,16,32,128]{3,2,1,0:T(8,128)} collective-permute-done((f32[2,16,32,128]{3,2,1,0:T(8,128)}, f32[2,16,32,128]{3,2,1,0:T(8,128)}, u32[]{:S(2)}, u32[]{:S(2)}) %collective-permute-start.10) | collective-permute-done | bytes 524320 | tf_op jit(solution)/shard_map/ppermute | solution.py:19
  70.7 9.3 %collective-permute-done.11.refs_3_ = f32[2,16,32,128]{3,2,1,0:T(8,128)} collective-permute-done((f32[2,16,32,128]{3,2,1,0:T(8,128)}, f32[2,16,32,128]{3,2,1,0:T(8,128)}, u32[]{:S(2)}, u32[]{:S(2)}) %collective-permute-start.11) | collective-permute-done | bytes 524320 | tf_op jit(solution)/shard_map/ppermute | solution.py:19
  80.0 19.8 %shard_map.56 = (f32[4,54,16,128]{3,2,1,0:T(8,128)}, f32[4,54,16,128]{3,2,1,0:T(8,128)}) custom-call(s32[2]{0:T(128)} %pad_add_fusion.1.place, f32[8,32]{1,0:T(8,128)} %get-tuple-element.63.ky, bf16[128,384]{1,0:T(8,128)(2,1)} %pad_maximum_fusion.5.wxt, bf16[8,128,256]{2,1,0:T(8,128)(2,1)} %get-tuple-element.48.kzh, ...), custom_call_target="tpu_custom_call" | custom-call | flops 339738624 | bytes 7733248 | tf_op jit(solution)/shard_map/pallas_call | solution.py:294
  99.8 3.9 %collective-permute-done.12 = f32[4,54,16,128]{3,2,1,0:T(8,128)S(1)} collective-permute-done((f32[4,54,16,128]{3,2,1,0:T(8,128)}, f32[4,54,16,128]{3,2,1,0:T(8,128)S(1)}, u32[]{:S(2)}, u32[]{:S(2)}) %collective-permute-start.12) | collective-permute-done | bytes 1769504 | tf_op jit(solution)/shard_map/ppermute | solution.py:19
  103.7 1.8 add.187
  105.7 1.4 collective-permute-start.13
  107.1 1.6 collective-permute-start.15
  108.7 9.2 %collective-permute-done.13 = f32[2,1,27,16,128]{4,3,2,0,1:T(8,128)S(1)} collective-permute-done((f32[2,1,27,16,128]{4,3,2,0,1:T(8,128)S(1)}, f32[2,1,27,16,128]{4,3,2,0,1:T(8,128)S(1)}, u32[]{:S(2)}, u32[]{:S(2)}) %collective-permute-start.13) | collective-permute-done | bytes 442400 | tf_op jit(solution)/shard_map/ppermute | solution.py:19
  118.1 1.6 collective-permute-start.14
  119.7 1.4 collective-permute-start.16
  121.2 3.6 %collective-permute-done.14 = f32[1,1,27,16,128]{4,3,2,1,0:T(8,128)S(1)} collective-permute-done((f32[1,1,27,16,128]{4,3,2,1,0:T(8,128)S(1)}, f32[1,1,27,16,128]{4,3,2,1,0:T(8,128)S(1)}, u32[]{:S(2)}, u32[]{:S(2)}) %collective-permute-start.14) | collective-permute-done | bytes 221216 | tf_op jit(solution)/shard_map/ppermute | solution.py:19
  126.9 2.2 shard_map.57
  129.1 1.4 collective-permute-start.18
  130.6 3.0 %collective-permute-start.19 = (f32[8,16,128]{2,1,0:T(8,128)}, f32[8,16,128]{2,1,0:T(8,128)S(1)}, u32[]{:S(2)}, u32[]{:S(2)}) collective-permute-start(f32[8,16,128]{2,1,0:T(8,128)} %get-tuple-element.29), channel_id=1, source_target_pairs={{0,16},{8,24},{16,0},{24,8},{1,17},{9,25},{17,1},{25,9},{2,18},{10... | collective-permute-start | bytes 196616 | tf_op jit(solution)/shard_map/ppermute | solution.py:19
  134.3 6.4 %collective-permute-done.19.fc = f32[8,16,128]{2,1,0:T(8,128)S(1)} collective-permute-done((f32[8,16,128]{2,1,0:T(8,128)}, f32[8,16,128]{2,1,0:T(8,128)S(1)}, u32[]{:S(2)}, u32[]{:S(2)}) %collective-permute-start.19) | collective-permute-done | bytes 65568 | tf_op jit(solution)/shard_map/ppermute | solution.py:19
  141.5 2.4 shard_map.58.old
  146.2 1.4 collective-permute-start.23
  147.6 3.6 %collective-permute-done.20 = f32[1,1,1,27,16,128]{5,4,3,2,1,0:T(8,128)S(1)} collective-permute-done((f32[1,1,1,27,16,128]{5,4,3,2,1,0:T(8,128)S(1)}, f32[1,1,1,27,16,128]{5,4,3,2,1,0:T(8,128)S(1)}, u32[]{:S(2)}, u32[]{:S(2)}) %collective-permute-start.20) | collective-permute-done | bytes 221216 | tf_op jit(solution)/shard_map/ppermute | solution.py:19
  151.3 1.6 collective-permute-start.21
  152.9 1.6 collective-permute-done.23
  155.4 5.9 %collective-permute-done.21 = f32[2,1,1,27,16,128]{5,4,3,0,2,1:T(8,128)S(1)} collective-permute-done((f32[2,1,1,27,16,128]{5,4,3,0,2,1:T(8,128)S(1)}, f32[2,1,1,27,16,128]{5,4,3,0,2,1:T(8,128)S(1)}, u32[]{:S(2)}, u32[]{:S(2)}) %collective-permute-start.21) | collective-permute-done | bytes 442400 | tf_op jit(solution)/shard_map/ppermute | solution.py:19
  161.5 1.4 collective-permute-done.24
  163.9 1.5 collective-permute-done.25.b1
  166.4 18.1 %shard_map.59.blurred = f32[32,128,128]{2,1,0:T(8,128)} custom-call(s32[2]{0:T(128)} %pad_add_fusion.1.place, f32[8,32]{1,0:T(8,128)} %get-tuple-element.63.ky, bf16[128,384]{1,0:T(8,128)(2,1)} %pad_maximum_fusion.6.wx, bf16[8,256,128]{2,1,0:T(8,128)(2,1)} %get-tuple-element.46.kzh, bf16[8,256,128]{2,1,0:T(8,128)(2,1)} %get-tuple-element.45.kzl, ...), custom_call_target="tpu_custom_call" | custom-call | flops 339738624 | bytes 5636096 | tf_op jit(solution)/shard_map/pallas_call | solution.py:294
  184.5 19.8 %shard_map.60 = (f32[4,54,16,128]{3,2,1,0:T(8,128)}, f32[4,54,16,128]{3,2,1,0:T(8,128)}) custom-call(s32[2]{0:T(128)} %pad_add_fusion.1.place, f32[8,32]{1,0:T(8,128)} %get-tuple-element.63.ky, bf16[128,384]{1,0:T(8,128)(2,1)} %pad_maximum_fusion.5.wxt, bf16[8,128,256]{2,1,0:T(8,128)(2,1)} %get-tuple-element.48.kzh, ...), custom_call_target="tpu_custom_call" | custom-call | flops 339738624 | bytes 7733248 | tf_op jit(solution)/shard_map/pallas_call | solution.py:294
  204.5 3.8 %collective-permute-done.26 = f32[4,54,16,128]{3,2,1,0:T(8,128)S(1)} collective-permute-done((f32[4,54,16,128]{3,2,1,0:T(8,128)}, f32[4,54,16,128]{3,2,1,0:T(8,128)S(1)}, u32[]{:S(2)}, u32[]{:S(2)}) %collective-permute-start.26) | collective-permute-done | bytes 1769504 | tf_op jit(solution)/shard_map/ppermute | solution.py:19
  208.2 1.8 add.192
  210.2 1.5 collective-permute-start.27
  212.8 9.7 %collective-permute-done.27 = f32[2,1,27,16,128]{4,3,2,0,1:T(8,128)S(1)} collective-permute-done((f32[2,1,27,16,128]{4,3,2,0,1:T(8,128)S(1)}, f32[2,1,27,16,128]{4,3,2,0,1:T(8,128)S(1)}, u32[]{:S(2)}, u32[]{:S(2)}) %collective-permute-start.27) | collective-permute-done | bytes 442400 | tf_op jit(solution)/shard_map/ppermute | solution.py:19
  223.8 1.4 collective-permute-start.30
  225.3 4.1 %collective-permute-done.28 = f32[1,1,27,16,128]{4,3,2,1,0:T(8,128)S(1)} collective-permute-done((f32[1,1,27,16,128]{4,3,2,1,0:T(8,128)S(1)}, f32[1,1,27,16,128]{4,3,2,1,0:T(8,128)S(1)}, u32[]{:S(2)}, u32[]{:S(2)}) %collective-permute-start.28) | collective-permute-done | bytes 221216 | tf_op jit(solution)/shard_map/ppermute | solution.py:19
  230.9 2.2 shard_map.61
  234.4 3.1 %collective-permute-start.33 = (f32[8,16,128]{2,1,0:T(8,128)}, f32[8,16,128]{2,1,0:T(8,128)S(1)}, u32[]{:S(2)}, u32[]{:S(2)}) collective-permute-start(f32[8,16,128]{2,1,0:T(8,128)} %get-tuple-element.34), channel_id=1, source_target_pairs={{0,16},{8,24},{16,0},{24,8},{1,17},{9,25},{17,1},{25,9},{2,18},{10... | collective-permute-start | bytes 196616 | tf_op jit(solution)/shard_map/ppermute | solution.py:19
  237.5 6.5 %collective-permute-done.33.fc = f32[8,16,128]{2,1,0:T(8,128)S(1)} collective-permute-done((f32[8,16,128]{2,1,0:T(8,128)}, f32[8,16,128]{2,1,0:T(8,128)S(1)}, u32[]{:S(2)}, u32[]{:S(2)}) %collective-permute-start.33) | collective-permute-done | bytes 65568 | tf_op jit(solution)/shard_map/ppermute | solution.py:19
  245.4 2.4 shard_map.62
  249.6 27.6 %all-gather.3.cloned.1.call-done = f32[128,16,128]{2,1,0:T(8,128)} async-done(((f32[32,16,128]{2,1,0:T(8,128)}), f32[128,16,128]{2,1,0:T(8,128)}) %all-gather.3.cloned.1.call-update) | async-done | bytes 1048592 | tf_op jit(solution)/shard_map/all_gather | solution.py:431
  278.5 1.6 copy.103
  (173 shorter events, 35.8 us)
Async XLA Ops:
  6.5 5.9 %copy-start = (f32[16,64,256]{2,1,0:T(8,128)S(1)}, f32[16,64,256]{2,1,0:T(8,128)}, u32[]{:S(2)}) copy-start(f32[16,64,256]{2,1,0:T(8,128)} %param.5) | copy-start | bytes 3145732
  6.5 270.7 %all-gather.3.cloned.1.call-start = ((), (), s32[]{:S(2)}) async-start(), calls=%async_computation | async-start | bytes 1310720 | tf_op jit(solution)/shard_map/all_gather | solution.py:431
  8.9 7.6 %collective-permute-start = (f32[2,128]{1,0:T(2,128)S(1)}, f32[2,128]{1,0:T(2,128)S(1)}, u32[]{:S(2)}, u32[]{:S(2)}) collective-permute-start(f32[2,128]{1,0:T(2,128)S(1)} %select_maximum_fusion), channel_id=1, source_target_pairs={{0,8},{8,0},{16,24},{24,16},{1,9},{9,1},{17,25},{25,17},{2,10},{10... | collective-permute-start | bytes 3080 | tf_op jit(solution)/shard_map/ppermute | solution.py:19
  8.9 7.6 %collective-permute-start.1 = (f32[2,128]{1,0:T(2,128)S(1)}, f32[2,128]{1,0:T(2,128)S(1)}, u32[]{:S(2)}, u32[]{:S(2)}) collective-permute-start(f32[2,128]{1,0:T(2,128)S(1)} %select_maximum_fusion), channel_id=1, source_target_pairs={{0,16},{8,24},{16,0},{24,8},{1,17},{9,25},{17,1},{25,9},{2,18},{10... | collective-permute-start | bytes 3080 | tf_op jit(solution)/shard_map/ppermute | solution.py:19
  12.0 4.6 %collective-permute-start.2 = (f32[2,128]{1,0:T(2,128)S(1)}, f32[2,128]{1,0:T(2,128)S(1)}, u32[]{:S(2)}, u32[]{:S(2)}) collective-permute-start(f32[2,128]{1,0:T(2,128)S(1)} %select_maximum_fusion), channel_id=1, source_target_pairs={{0,24},{8,16},{16,8},{24,0},{1,25},{9,17},{17,9},{25,1},{2,26},{10... | collective-permute-start | bytes 3080 | tf_op jit(solution)/shard_map/ppermute | solution.py:19
  13.0 6.3 %copy-start.9 = (f32[24,16,128]{2,1,0:T(8,128)}, f32[24,16,128]{2,1,0:T(8,128)S(1)}, u32[]{:S(2)}) copy-start(f32[24,16,128]{2,1,0:T(8,128)S(1)} %get-tuple-element.54) | copy-start | bytes 589828
  13.2 16.3 %collective-permute-start.6 = (f32[1,1,1,27,16,128]{5,4,3,2,1,0:T(8,128)S(1)}, f32[1,1,1,27,16,128]{5,4,3,2,1,0:T(8,128)S(1)}, u32[]{:S(2)}, u32[]{:S(2)}) collective-permute-start(f32[1,1,1,27,16,128]{5,4,3,2,1,0:T(8,128)S(1)} %maximum_bitcast_fusion.6), channel_id=1, source_target_pairs={{0,2},{1,3},{2,0},{3,1},{4,6},{5,7},{6,4},{7,5},{8,10},{9,11},{10,... | collective-permute-start | bytes 663560 | tf_op jit(solution)/shard_map/ppermute | solution.py:19
  16.5 2.8 copy-start.16
  17.7 9.6 %collective-permute-start.3 = (f32[1,1,1,28,16,128]{5,4,3,2,1,0:T(8,128)S(1)}, f32[1,1,1,28,16,128]{5,4,3,2,1,0:T(8,128)S(1)}, u32[]{:S(2)}, u32[]{:S(2)}) collective-permute-start(f32[1,1,1,28,16,128]{5,4,3,2,1,0:T(8,128)S(1)} %maximum_bitcast_fusion.5), channel_id=1, source_target_pairs={{0,4},{1,5},{2,6},{3,7},{4,0},{5,1},{6,2},{7,3},{8,12},{9,13},{10,... | collective-permute-start | bytes 688136 | tf_op jit(solution)/shard_map/ppermute | solution.py:19
  19.2 8.7 %copy-start.6 = (f32[2,16,64,256]{3,2,1,0:T(8,128)S(1)}, f32[2,16,64,256]{3,2,1,0:T(8,128)}, u32[]{:S(2)}) copy-start(f32[2,16,64,256]{3,2,1,0:T(8,128)} %param.6) | copy-start | bytes 6291460
  27.3 11.0 %collective-permute-start.4 = (f32[2,1,1,28,16,128]{5,4,3,0,2,1:T(8,128)S(1)}, f32[2,1,1,28,16,128]{5,4,3,0,2,1:T(8,128)}, u32[]{:S(2)}, u32[]{:S(2)}) collective-permute-start(f32[2,1,1,28,16,128]{5,4,3,0,2,1:T(8,128)S(1)} %maximum_bitcast_fusion.1), channel_id=1, source_target_pairs={{0,2},{1,3},{2,0},{3,1},{4,6},{5,7},{6,4},{7,5},{8,10},{9,11},{10,... | collective-permute-start | bytes 1376264 | tf_op jit(solution)/shard_map/ppermute | solution.py:19
  30.2 10.6 %collective-permute-start.7 = (f32[1,1,2,27,16,128]{5,4,3,2,1,0:T(8,128)}, f32[1,1,2,27,16,128]{5,4,3,2,1,0:T(8,128)}, u32[]{:S(2)}, u32[]{:S(2)}) collective-permute-start(f32[1,1,2,27,16,128]{5,4,3,2,1,0:T(8,128)} %maximum_bitcast_fusion.2), channel_id=1, source_target_pairs={{0,4},{1,5},{2,6},{3,7},{4,0},{5,1},{6,2},{7,3},{8,12},{9,13},{10,... | collective-permute-start | bytes 1327112 | tf_op jit(solution)/shard_map/ppermute | solution.py:19
  32.0 33.1 %collective-permute-start.9 = (f32[2,16,32,128]{3,2,1,0:T(8,128)}, f32[2,16,32,128]{3,2,1,0:T(8,128)S(1)}, u32[]{:S(2)}, u32[]{:S(2)}) collective-permute-start(f32[2,16,32,128]{3,2,1,0:T(8,128)} %get-tuple-element.37), channel_id=1, source_target_pairs={{0,8},{8,0},{16,24},{24,16},{1,9},{9,1},{17,25},{25,17},{2,10},{10... | collective-permute-start | bytes 1572872 | tf_op jit(solution)/shard_map/ppermute | solution.py:19
  35.3 35.3 %collective-permute-start.10 = (f32[2,16,32,128]{3,2,1,0:T(8,128)}, f32[2,16,32,128]{3,2,1,0:T(8,128)}, u32[]{:S(2)}, u32[]{:S(2)}) collective-permute-start(f32[2,16,32,128]{3,2,1,0:T(8,128)} %get-tuple-element.36), channel_id=1, source_target_pairs={{0,16},{8,24},{16,0},{24,8},{1,17},{9,25},{17,1},{25,9},{2,18},{10... | collective-permute-start | bytes 1572872 | tf_op jit(solution)/shard_map/ppermute | solution.py:19
  35.5 44.5 %collective-permute-start.11 = (f32[2,16,32,128]{3,2,1,0:T(8,128)}, f32[2,16,32,128]{3,2,1,0:T(8,128)}, u32[]{:S(2)}, u32[]{:S(2)}) collective-permute-start(f32[2,16,32,128]{3,2,1,0:T(8,128)} %get-tuple-element.35), channel_id=1, source_target_pairs={{0,24},{8,16},{16,8},{24,0},{1,25},{9,17},{17,9},{25,1},{2,26},{10... | collective-permute-start | bytes 1572872 | tf_op jit(solution)/shard_map/ppermute | solution.py:19
  39.5 5.6 %copy-start.2 = (f32[2,2,1,28,16,128]{5,4,3,1,0,2:T(8,128)}, f32[2,2,1,28,16,128]{5,4,3,1,0,2:T(8,128)S(1)}, u32[]{:S(2)}) copy-start(f32[2,2,1,28,16,128]{5,4,3,1,0,2:T(8,128)S(1)} %copy.92) | copy-start | bytes 2752516
  39.5 5.6 %collective-permute-start.5 = (f32[4,28,16,128]{3,2,1,0:T(8,128)S(1)}, f32[4,28,16,128]{3,2,1,0:T(8,128)}, u32[]{:S(2)}, u32[]{:S(2)}) collective-permute-start(f32[4,28,16,128]{3,2,1,0:T(8,128)S(1)} %bitcast.161), channel_id=1, source_target_pairs={{0,1},{1,0},{2,3},{3,2},{4,5},{5,4},{6,7},{7,6},{8,9},{9,8},{10,11... | collective-permute-start | bytes 2752520 | tf_op jit(solution)/shard_map/ppermute | solution.py:19
  43.0 3.1 %collective-permute-start.8 = (f32[4,27,16,128]{3,2,1,0:T(8,128)}, f32[4,27,16,128]{3,2,1,0:T(8,128)}, u32[]{:S(2)}, u32[]{:S(2)}) collective-permute-start(f32[4,27,16,128]{3,2,1,0:T(8,128)} %bitcast.25.b0), channel_id=1, source_target_pairs={{0,1},{1,0},{2,3},{3,2},{4,5},{5,4},{6,7},{7,6},{8,9},{9,8},{10,11... | collective-permute-start | bytes 2654216 | tf_op jit(solution)/shard_map/ppermute | solution.py:19
  46.1 18.4 %copy-start.15 = (f32[128,128]{0,1:T(8,128)S(1)}, f32[128,128]{0,1:T(8,128)}, u32[]{:S(2)}) copy-start(f32[128,128]{0,1:T(8,128)} %copy.95) | copy-start | bytes 196612
  65.1 14.8 %copy-start.5 = (f32[2,16,32,128]{3,2,1,0:T(8,128)}, f32[2,16,32,128]{3,2,1,0:T(8,128)S(1)}, u32[]{:S(2)}) copy-start(f32[2,16,32,128]{3,2,1,0:T(8,128)S(1)} %collective-permute-done.9.refs_1_) | copy-start | bytes 1572868
  99.8 3.9 %collective-permute-start.12 = (f32[4,54,16,128]{3,2,1,0:T(8,128)}, f32[4,54,16,128]{3,2,1,0:T(8,128)S(1)}, u32[]{:S(2)}, u32[]{:S(2)}) collective-permute-start(f32[4,54,16,128]{3,2,1,0:T(8,128)} %get-tuple-element.26), channel_id=1, source_target_pairs={{0,1},{1,0},{2,3},{3,2},{4,5},{5,4},{6,7},{7,6},{8,9},{9,8},{10,11... | collective-permute-start | bytes 5308424 | tf_op jit(solution)/shard_map/ppermute | solution.py:19
  105.7 12.3 %collective-permute-start.13 = (f32[2,1,27,16,128]{4,3,2,0,1:T(8,128)S(1)}, f32[2,1,27,16,128]{4,3,2,0,1:T(8,128)S(1)}, u32[]{:S(2)}, u32[]{:S(2)}) collective-permute-start(f32[2,1,27,16,128]{4,3,2,0,1:T(8,128)S(1)} %slice_bitcast_fusion.6), channel_id=1, source_target_pairs={{0,2},{1,3},{2,0},{3,1},{4,6},{5,7},{6,4},{7,5},{8,10},{9,11},{10,... | collective-permute-start | bytes 1327112 | tf_op jit(solution)/shard_map/ppermute | solution.py:19
  107.1 12.6 %collective-permute-start.15 = (f32[1,2,27,16,128]{4,3,2,1,0:T(8,128)S(1)}, f32[1,2,27,16,128]{4,3,2,1,0:T(8,128)S(1)}, u32[]{:S(2)}, u32[]{:S(2)}) collective-permute-start(f32[1,2,27,16,128]{4,3,2,1,0:T(8,128)S(1)} %slice_bitcast_fusion.4), channel_id=1, source_target_pairs={{0,4},{1,5},{2,6},{3,7},{4,0},{5,1},{6,2},{7,3},{8,12},{9,13},{10,... | collective-permute-start | bytes 1327112 | tf_op jit(solution)/shard_map/ppermute | solution.py:19
  118.0 15.5 %copy-start.8 = (f32[24,16,128]{2,1,0:T(8,128)S(1)}, f32[24,16,128]{2,1,0:T(8,128)}, u32[]{:S(2)}) copy-start(f32[24,16,128]{2,1,0:T(8,128)} %copy-done.7) | copy-start | bytes 589828
  118.0 15.5 %copy-start.10 = (f32[24,16,128]{2,1,0:T(8,128)S(1)}, f32[24,16,128]{2,1,0:T(8,128)}, u32[]{:S(2)}) copy-start(f32[24,16,128]{2,1,0:T(8,128)} %copy-done.9) | copy-start | bytes 589828
  118.1 15.5 %copy-start.17 = (f32[3,16,128]{2,1,0:T(8,128)S(1)}, f32[3,16,128]{2,1,0:T(8,128)}, u32[]{:S(2)}) copy-start(f32[3,16,128]{2,1,0:T(8,128)} %copy-done.16) | copy-start | bytes 73732
  118.1 15.5 %copy-start.19 = (f32[3,16,128]{2,1,0:T(8,128)S(1)}, f32[3,16,128]{2,1,0:T(8,128)}, u32[]{:S(2)}) copy-start(f32[3,16,128]{2,1,0:T(8,128)} %copy-done.18) | copy-start | bytes 73732
  118.1 6.7 %collective-permute-start.14 = (f32[1,1,27,16,128]{4,3,2,1,0:T(8,128)S(1)}, f32[1,1,27,16,128]{4,3,2,1,0:T(8,128)S(1)}, u32[]{:S(2)}, u32[]{:S(2)}) collective-permute-start(f32[1,1,27,16,128]{4,3,2,1,0:T(8,128)S(1)} %slice_bitcast_fusion.16), channel_id=1, source_target_pairs={{0,4},{1,5},{2,6},{3,7},{4,0},{5,1},{6,2},{7,3},{8,12},{9,13},{10,... | collective-permute-start | bytes 663560 | tf_op jit(solution)/shard_map/ppermute | solution.py:19
  119.7 6.4 %collective-permute-start.16 = (f32[1,1,27,16,128]{4,3,2,1,0:T(8,128)S(1)}, f32[1,1,27,16,128]{4,3,2,1,0:T(8,128)S(1)}, u32[]{:S(2)}, u32[]{:S(2)}) collective-permute-start(f32[1,1,27,16,128]{4,3,2,1,0:T(8,128)S(1)} %slice_bitcast_fusion.14), channel_id=1, source_target_pairs={{0,2},{1,3},{2,0},{3,1},{4,6},{5,7},{6,4},{7,5},{8,10},{9,11},{10,... | collective-permute-start | bytes 663560 | tf_op jit(solution)/shard_map/ppermute | solution.py:19
  129.1 11.6 %collective-permute-start.17 = (f32[36,16,128]{2,1,0:T(8,128)}, f32[36,16,128]{2,1,0:T(8,128)S(1)}, u32[]{:S(2)}, u32[]{:S(2)}) collective-permute-start(f32[36,16,128]{2,1,0:T(8,128)} %get-tuple-element.27), channel_id=1, source_target_pairs={{0,8},{8,0},{16,24},{24,16},{1,9},{9,1},{17,25},{25,17},{2,10},{10... | collective-permute-start | bytes 884744 | tf_op jit(solution)/shard_map/ppermute | solution.py:19
  129.1 11.6 %collective-permute-start.18 = (f32[12,16,128]{2,1,0:T(8,128)}, f32[12,16,128]{2,1,0:T(8,128)S(1)}, u32[]{:S(2)}, u32[]{:S(2)}) collective-permute-start(f32[12,16,128]{2,1,0:T(8,128)} %get-tuple-element.28), channel_id=1, source_target_pairs={{0,24},{8,16},{16,8},{24,0},{1,25},{9,17},{17,9},{25,1},{2,26},{10... | collective-permute-start | bytes 294920 | tf_op jit(solution)/shard_map/ppermute | solution.py:19
  130.6 10.2 %collective-permute-start.19 = (f32[8,16,128]{2,1,0:T(8,128)}, f32[8,16,128]{2,1,0:T(8,128)S(1)}, u32[]{:S(2)}, u32[]{:S(2)}) collective-permute-start(f32[8,16,128]{2,1,0:T(8,128)} %get-tuple-element.29), channel_id=1, source_target_pairs={{0,16},{8,24},{16,0},{24,8},{1,17},{9,25},{17,1},{25,9},{2,18},{10... | collective-permute-start | bytes 196616 | tf_op jit(solution)/shard_map/ppermute | solution.py:19
  145.0 6.2 %collective-permute-start.20 = (f32[1,1,1,27,16,128]{5,4,3,2,1,0:T(8,128)S(1)}, f32[1,1,1,27,16,128]{5,4,3,2,1,0:T(8,128)S(1)}, u32[]{:S(2)}, u32[]{:S(2)}) collective-permute-start(f32[1,1,1,27,16,128]{5,4,3,2,1,0:T(8,128)S(1)} %get-tuple-element.52), channel_id=1, source_target_pairs={{0,4},{1,5},{2,6},{3,7},{4,0},{5,1},{6,2},{7,3},{8,12},{9,13},{10,... | collective-permute-start | bytes 663560 | tf_op jit(solution)/shard_map/ppermute | solution.py:19
  146.2 8.3 %collective-permute-start.23 = (f32[1,1,1,27,16,128]{5,4,3,2,1,0:T(8,128)S(1)}, f32[1,1,1,27,16,128]{5,4,3,2,1,0:T(8,128)S(1)}, u32[]{:S(2)}, u32[]{:S(2)}) collective-permute-start(f32[1,1,1,27,16,128]{5,4,3,2,1,0:T(8,128)S(1)} %get-tuple-element.51), channel_id=1, source_target_pairs={{0,2},{1,3},{2,0},{3,1},{4,6},{5,7},{6,4},{7,5},{8,10},{9,11},{10,... | collective-permute-start | bytes 663560 | tf_op jit(solution)/shard_map/ppermute | solution.py:19
  151.3 10.0 %collective-permute-start.21 = (f32[2,1,1,27,16,128]{5,4,3,0,2,1:T(8,128)S(1)}, f32[2,1,1,27,16,128]{5,4,3,0,2,1:T(8,128)S(1)}, u32[]{:S(2)}, u32[]{:S(2)}) collective-permute-start(f32[2,1,1,27,16,128]{5,4,3,0,2,1:T(8,128)S(1)} %maximum_bitcast_fusion.3), channel_id=1, source_target_pairs={{0,2},{1,3},{2,0},{3,1},{4,6},{5,7},{6,4},{7,5},{8,10},{9,11},{10,... | collective-permute-start | bytes 1327112 | tf_op jit(solution)/shard_map/ppermute | solution.py:19
  154.5 8.4 %collective-permute-start.24 = (f32[1,1,2,27,16,128]{5,4,3,2,1,0:T(8,128)S(1)}, f32[1,1,2,27,16,128]{5,4,3,2,1,0:T(8,128)S(1)}, u32[]{:S(2)}, u32[]{:S(2)}) collective-permute-start(f32[1,1,2,27,16,128]{5,4,3,2,1,0:T(8,128)S(1)} %maximum_bitcast_fusion.4), channel_id=1, source_target_pairs={{0,4},{1,5},{2,6},{3,7},{4,0},{5,1},{6,2},{7,3},{8,12},{9,13},{10,... | collective-permute-start | bytes 1327112 | tf_op jit(solution)/shard_map/ppermute | solution.py:19
  161.4 4.0 %copy-start.3 = (f32[2,2,1,27,16,128]{5,4,3,1,0,2:T(8,128)}, f32[2,2,1,27,16,128]{5,4,3,1,0,2:T(8,128)S(1)}, u32[]{:S(2)}) copy-start(f32[2,2,1,27,16,128]{5,4,3,1,0,2:T(8,128)S(1)} %copy.100) | copy-start | bytes 2654212
  161.5 2.5 collective-permute-start.22
  162.9 2.5 copy-start.4
  163.0 2.5 collective-permute-start.25
  204.3 3.9 %collective-permute-start.26 = (f32[4,54,16,128]{3,2,1,0:T(8,128)}, f32[4,54,16,128]{3,2,1,0:T(8,128)S(1)}, u32[]{:S(2)}, u32[]{:S(2)}) collective-permute-start(f32[4,54,16,128]{3,2,1,0:T(8,128)} %get-tuple-element.31), channel_id=1, source_target_pairs={{0,1},{1,0},{2,3},{3,2},{4,5},{5,4},{6,7},{7,6},{8,9},{9,8},{10,11... | collective-permute-start | bytes 5308424 | tf_op jit(solution)/shard_map/ppermute | solution.py:19
  210.2 12.3 %collective-permute-start.27 = (f32[2,1,27,16,128]{4,3,2,0,1:T(8,128)S(1)}, f32[2,1,27,16,128]{4,3,2,0,1:T(8,128)S(1)}, u32[]{:S(2)}, u32[]{:S(2)}) collective-permute-start(f32[2,1,27,16,128]{4,3,2,0,1:T(8,128)S(1)} %slice_bitcast_fusion.2), channel_id=1, source_target_pairs={{0,2},{1,3},{2,0},{3,1},{4,6},{5,7},{6,4},{7,5},{8,10},{9,11},{10,... | collective-permute-start | bytes 1327112 | tf_op jit(solution)/shard_map/ppermute | solution.py:19
  211.7 12.0 %collective-permute-start.29 = (f32[1,2,27,16,128]{4,3,2,1,0:T(8,128)S(1)}, f32[1,2,27,16,128]{4,3,2,1,0:T(8,128)S(1)}, u32[]{:S(2)}, u32[]{:S(2)}) collective-permute-start(f32[1,2,27,16,128]{4,3,2,1,0:T(8,128)S(1)} %slice_bitcast_fusion), channel_id=1, source_target_pairs={{0,4},{1,5},{2,6},{3,7},{4,0},{5,1},{6,2},{7,3},{8,12},{9,13},{10,... | collective-permute-start | bytes 1327112 | tf_op jit(solution)/shard_map/ppermute | solution.py:19
  222.6 6.7 %collective-permute-start.28 = (f32[1,1,27,16,128]{4,3,2,1,0:T(8,128)S(1)}, f32[1,1,27,16,128]{4,3,2,1,0:T(8,128)S(1)}, u32[]{:S(2)}, u32[]{:S(2)}) collective-permute-start(f32[1,1,27,16,128]{4,3,2,1,0:T(8,128)S(1)} %slice_bitcast_fusion.10), channel_id=1, source_target_pairs={{0,4},{1,5},{2,6},{3,7},{4,0},{5,1},{6,2},{7,3},{8,12},{9,13},{10,... | collective-permute-start | bytes 663560 | tf_op jit(solution)/shard_map/ppermute | solution.py:19
  223.8 6.4 %collective-permute-start.30 = (f32[1,1,27,16,128]{4,3,2,1,0:T(8,128)S(1)}, f32[1,1,27,16,128]{4,3,2,1,0:T(8,128)S(1)}, u32[]{:S(2)}, u32[]{:S(2)}) collective-permute-start(f32[1,1,27,16,128]{4,3,2,1,0:T(8,128)S(1)} %slice_bitcast_fusion.8), channel_id=1, source_target_pairs={{0,2},{1,3},{2,0},{3,1},{4,6},{5,7},{6,4},{7,5},{8,10},{9,11},{10,... | collective-permute-start | bytes 663560 | tf_op jit(solution)/shard_map/ppermute | solution.py:19
  233.1 10.9 %collective-permute-start.31 = (f32[36,16,128]{2,1,0:T(8,128)}, f32[36,16,128]{2,1,0:T(8,128)S(1)}, u32[]{:S(2)}, u32[]{:S(2)}) collective-permute-start(f32[36,16,128]{2,1,0:T(8,128)} %get-tuple-element.32), channel_id=1, source_target_pairs={{0,8},{8,0},{16,24},{24,16},{1,9},{9,1},{17,25},{25,17},{2,10},{10... | collective-permute-start | bytes 884744 | tf_op jit(solution)/shard_map/ppermute | solution.py:19
  233.9 10.2 %collective-permute-start.32 = (f32[12,16,128]{2,1,0:T(8,128)}, f32[12,16,128]{2,1,0:T(8,128)S(1)}, u32[]{:S(2)}, u32[]{:S(2)}) collective-permute-start(f32[12,16,128]{2,1,0:T(8,128)} %get-tuple-element.33), channel_id=1, source_target_pairs={{0,24},{8,16},{16,8},{24,0},{1,25},{9,17},{17,9},{25,1},{2,26},{10... | collective-permute-start | bytes 294920 | tf_op jit(solution)/shard_map/ppermute | solution.py:19
  234.4 9.6 %collective-permute-start.33 = (f32[8,16,128]{2,1,0:T(8,128)}, f32[8,16,128]{2,1,0:T(8,128)S(1)}, u32[]{:S(2)}, u32[]{:S(2)}) collective-permute-start(f32[8,16,128]{2,1,0:T(8,128)} %get-tuple-element.34), channel_id=1, source_target_pairs={{0,16},{8,24},{16,0},{24,8},{1,17},{9,25},{17,1},{25,9},{2,18},{10... | collective-permute-start | bytes 196616 | tf_op jit(solution)/shard_map/ppermute | solution.py:19
  (12 other events, 13.4 us)
Sparse Core Ops, SparseCore 0:
  249.7 27.4 all-gather.2

commit v3 on v2

--- a/solution.py
+++ b/solution.py
@@ -78,32 +78,35 @@
     return jnp.dot(a, b, preferred_element_type=F32)
 
 
-def mul3(value, high, low):
-    a, b = split(value)
-    return mul(a, high) + mul(b, high) + mul(a, low)
-
-
 def lane_of(shape):
     return lax.broadcasted_iota(jnp.int32, shape, len(shape) - 1)
 
 
-def ahead_kernel(rad, place, ky, wx, kzh, kzl, a0, a1, b0, b1, blurred, u, uh, zp):
+def ahead_kernel(rad, place, ky, wx, kz, a0, a1, b0, b1, *refs):
+    blurred, u, uh, za, zb = refs[-5:]
     yh = place[0]
     wy, nvi, hz = u.shape
     hy = blurred.shape[0]
     width = a0.shape[2]
     nviews = nvi // width
     half, group = wy // 2, hz // rad
+    part = lane_of((nvi, hz)) // rad
     for h, pair in enumerate(((a0, a1), (b0, b1))):
 
         def row(y):
             return jnp.concatenate([ref[k, y] for ref in pair for k in range(ref.shape[0])], axis=0)
 
-        rims = half // group
-        for k in range(rims):
+        for k in range(half // group):
             out = mul(wx[...], stack3(row(half + k)))
+            high = out.astype(BF16).astype(F32)
+            low = out - high
             for m in range(group):
-                uh[h * half + k * group + m] = out if m == 0 else pltpu.roll(out, hz - rad * m, 1)
+                first, second, third = (
+                    pltpu.roll(value, (rad * (at - m)) % hz, 1) if at != m else value
+                    for at, value in enumerate((high, low, high))
+                )
+                value = jnp.where(part == 0, first, jnp.where(part == 1, second, jnp.where(part == 2, third, 0.0)))
+                uh[h * half + k * group + m] = value.astype(BF16)
 
         def two(p, carry):
             out = mul(wx[...], stack3(jnp.concatenate([row(2 * p), row(2 * p + 1)], axis=1)))
@@ -114,41 +117,44 @@
         lax.fori_loop(0, half // 2, two, 0)
 
     lead = rad * (1 - yh)
-    zp[pl.ds((wy) * yh, rad)] = jnp.zeros((rad, nvi, hz), F32)
-
-    def one(v, carry):
+    for z in (za, zb):
+        z[pl.ds(wy * yh, rad)] = jnp.zeros((rad, width, hz), F32)
+
+    def along_z(v, z):
         at = pl.ds(pl.multiple_of(v * width, width), width)
-        for c in range(2):
-            rows = pl.ds(c * half, half)
-            value = jnp.concatenate([u[rows, at, :], uh[rows, at, :]], axis=-1)
-            out = mul3(value.reshape(half * width, 2 * hz), kzh[v], kzl[v])
-            zp[pl.ds(lead + c * half, half), at, :] = out.reshape(half, width, hz)
+        high, low = split(u[:, at, :].reshape(wy * width, hz))
+        value = jnp.concatenate([high, low, high, uh[:, at, :].reshape(wy * width, hz)], axis=1)
+        z[pl.ds(lead, wy)] = mul(value, kz[v]).reshape(wy, width, hz)
+
+    def along_y(v, z):
+        tap = [ky[v, t] for t in range(2 * rad)]
+        for s in range(0, width, 8):
+            for first in range(0, hy, BLOCK):
+                total = [None] * BLOCK
+                for y in range(first, first + BLOCK + 2 * rad - 1):
+                    value = z[y, s : s + 8, :]
+                    for k in range(BLOCK):
+                        t = y - first - k
+                        if 0 <= t < 2 * rad:
+                            term = tap[t] * value
+                            total[k] = term if total[k] is None else total[k] + term
+                for k in range(BLOCK):
+                    blurred[first + k, pl.ds(pl.multiple_of(v * width + s, 8), 8), :] = total[k]
+
+    along_z(0, za)
+
+    def views(p, carry):
+        along_z(2 * p + 1, zb)
+        along_y(2 * p, za)
+        along_z(jnp.minimum(2 * p + 2, nviews - 1), za)
+        along_y(2 * p + 1, zb)
         return carry
 
-    lax.fori_loop(0, nviews, one, 0)
-
-    def tile(s, carry):
-        v = s // (width // 8)
-        at = pl.ds(pl.multiple_of(s * 8, 8), 8)
-        tap = [ky[v, t] for t in range(2 * rad)]
-        for first in range(0, hy, BLOCK):
-            total = [None] * BLOCK
-            for y in range(first, first + BLOCK + 2 * rad - 1):
-                value = zp[y, at, :]
-                for k in range(BLOCK):
-                    t = y - first - k
-                    if 0 <= t < 2 * rad:
-                        term = tap[t] * value
-                        total[k] = term if total[k] is None else total[k] + term
-            for k in range(BLOCK):
-                blurred[first + k, at, :] = total[k]
-        return carry
-
-    lax.fori_loop(0, nvi // 8, tile, 0)
-
-
-def back_kernel(rad, npieces, place, ky, wxt, kzh, kzl, blurred, *refs):
-    pieces, (kept, sent, r, yb, gm, gh) = refs[:npieces], refs[npieces:]
+    lax.fori_loop(0, nviews // 2, views, 0)
+
+
+def back_kernel(rad, npieces, place, ky, wxt, kz, blurred, *refs):
+    pieces, (kept, sent, r, ya, yb, gm, gh) = refs[:npieces], refs[npieces:]
     yh = place[0]
     hy, nvi, hz = blurred.shape
     wy = gm.shape[0]
@@ -162,41 +168,45 @@
             for y in range(hy):
                 r[y, first : first + width, :] = piece[k, :, y, :] / blurred[y, first : first + width, :]
 
-    def tile(s, carry):
-        v = s // (width // 8)
-        at = pl.ds(pl.multiple_of(s * 8, 8), 8)
+    lead = rad * (1 - yh)
+
+    def along_y(v, out):
         tap = [ky[v, t] for t in range(2 * rad)]
-        for first in range(0, hy + 2 * rad, BLOCK):
-            total = [None] * BLOCK
-            for y in range(max(0, first - 2 * rad + 1), min(hy, first + BLOCK)):
-                value = r[y, at, :]
+        for s in range(0, width, 8):
+            at = pl.ds(pl.multiple_of(v * width + s, 8), 8)
+            for first in range(0, hy + 2 * rad, BLOCK):
+                total = [None] * BLOCK
+                for y in range(max(0, first - 2 * rad + 1), min(hy, first + BLOCK)):
+                    value = r[y, at, :]
+                    for k in range(BLOCK):
+                        t = first + k - y
+                        if 0 <= t < 2 * rad:
+                            term = tap[t] * value
+                            total[k] = term if total[k] is None else total[k] + term
                 for k in range(BLOCK):
-                    t = first + k - y
-                    if 0 <= t < 2 * rad:
-                        term = tap[t] * value
-                        total[k] = term if total[k] is None else total[k] + term
-            for k in range(BLOCK):
-                yb[first + k, at, :] = jnp.zeros((8, hz), F32) if total[k] is None else total[k]
+                    out[first + k, s : s + 8, :] = jnp.zeros((8, hz), F32) if total[k] is None else total[k]
+
+    def along_z(v, y):
+        at = pl.ds(pl.multiple_of(v * width, width), width)
+        high, low = split(y[pl.ds(lead, wy)].reshape(wy * width, hz))
+        out = mul(jnp.concatenate([high, low, high], axis=1), kz[v]).reshape(wy, width, 2 * hz)
+        gm[:, at, :] = out[..., :hz]
+        for o in range(2 * rims):
+            total = out[o * group, :, hz:]
+            for m in range(1, group):
+                total = total + pltpu.roll(out[o * group + m, :, hz:], rad * m, 1)
+            gh[o, at, :] = total
+
+    along_y(0, ya)
+
+    def views(p, carry):
+        along_y(2 * p + 1, yb)
+        along_z(2 * p, ya)
+        along_y(jnp.minimum(2 * p + 2, nviews - 1), ya)
+        along_z(2 * p + 1, yb)
         return carry
 
-    lax.fori_loop(0, nvi // 8, tile, 0)
-
-    lead = rad * (1 - yh)
-
-    def one(v, carry):
-        at = pl.ds(pl.multiple_of(v * width, width), width)
-        for c in range(2):
-            value = yb[pl.ds(lead + c * half, half), at, :].reshape(half * width, hz)
-            out = mul3(value, kzh[v], kzl[v]).reshape(half, width, 2 * hz)
-            gm[pl.ds(c * half, half), at, :] = out[..., :hz]
-            for k in range(rims):
-                total = out[k * group, :, hz:]
-                for m in range(1, group):
-                    total = total + pltpu.roll(out[k * group + m, :, hz:], rad * m, 1)
-                gh[c * rims + k, at, :] = total
-        return carry
-
-    lax.fori_loop(0, nviews, one, 0)
+    lax.fori_loop(0, nviews // 2, views, 0)
 
     def store(out, row):
         for c, ref in enumerate((kept, sent)):
@@ -285,21 +295,35 @@
             new[row] = old[row] * value / total
 
 
+def assemble_kernel(where, *refs):
+    pieces, out = refs[:-1], refs[-1]
+    hy, width, hz = pieces[0].shape
+    for r, piece in enumerate(pieces):
+        for owner in range(len(pieces)):
+            oz, oy = owner >> 1, (owner ^ (owner >> 1)) & 1
+
+            @pl.when(where[0] == owner ^ r)
+            def _():
+                for y in range(hy):
+                    out[:, oy * hy + y, oz * hz : (oz + 1) * hz] = piece[y]
+
+
 VMEM = pl.BlockSpec(memory_space=pltpu.VMEM)
+ANY = pl.BlockSpec(memory_space=pl.ANY)
 SMEM = pl.BlockSpec(memory_space=pltpu.SMEM)
 
 
-def call(kernel, shapes, scratch, smem, cost, *args):
+def call(kernel, shapes, scratch, smem, cost, *args, late=()):
     flops, moved = cost
     return pl.pallas_call(
         kernel,
         out_shape=[jax.ShapeDtypeStruct(shape, F32) for shape in shapes],
-        in_specs=[SMEM] * smem + [VMEM] * (len(args) - smem),
+        in_specs=[SMEM] * smem + [VMEM] * (len(args) - smem) + [ANY] * len(late),
         out_specs=[VMEM] * len(shapes),
-        scratch_shapes=[pltpu.VMEM(shape, F32) for shape in scratch],
+        scratch_shapes=[pltpu.VMEM(s, F32) if isinstance(s, tuple) else s for s in scratch],
         compiler_params=PARAMS,
         cost_estimate=pl.CostEstimate(flops=flops, bytes_accessed=moved, transcendentals=0),
-    )(*args)
+    )(*args, *late)
 
 
 def body(prior, data, taps, offsets, coverage):
@@ -327,7 +351,6 @@
     used = flat.shape[1]
     flat = jnp.pad(flat, ((0, 0), (0, -used % LANES)))
     shared = [flat] + [swap(flat, "view", r) for r in range(1, nview)]
-    *shared, data = lax.optimization_barrier((*shared, data))
     shared = jnp.concatenate(shared, axis=0)
 
     def quadrant(owner):
@@ -377,38 +400,44 @@
     goal = jnp.arange(hz) + hz * zh
     index = jnp.where(real[:, None], cells[:, None] - goal + rad, -1)
     band_z = pick(kern[:, 2], index[None])
-    kz = halves(band_z)
-    kzt = halves(band_z.transpose(0, 2, 1))
+    high, low = halves(band_z)
+    kz = [high[:, :hz], high[:, :hz], low[:, :hz]]
+    kz += [high[:, hz : hz + rad], high[:, hz : hz + rad], low[:, hz : hz + rad]]
+    kz = jnp.concatenate(kz + [jnp.zeros((nviews, hz - 3 * rad, hz), BF16)], axis=1)
+    high, low = halves(band_z.transpose(0, 2, 1))
+    kzt = jnp.concatenate([high, high, low], axis=1)
     ky = kern[:, 1]
 
     plane = width * hz
     mxu = 2 * 3 * nvi * plane * 2 * rows * (nspace // 2)
 
-    def ahead(wide):
+    def ahead(wide, late, cost):
         return call(
             functools.partial(ahead_kernel, rad),
             [(hy, nvi, hz)],
-            [(wy, nvi, hz), (wy, nvi, hz), (wy + rad, nvi, hz)],
+            [(wy, nvi, hz), pltpu.VMEM((wy, nvi, hz), BF16), (wy + rad, width, hz), (wy + rad, width, hz)],
             2,
-            (mxu, 4 * plane * (nspace * 2 * rows + hy * nviews)),
-            place_yz, ky, wx, *kz, *wide,
+            cost,
+            place_yz, ky, wx, kz, *wide,
+            late=late,
         )[0]
 
     def back(blurred):
         return call(
             functools.partial(back_kernel, rad, nview),
             [(nspace // 2, 2 * rows, width, hz)] * 2,
-            [(hy, nvi, hz), (hy + 2 * rad, nvi, hz), (wy, nvi, hz), (2 * rims, nvi, hz)],
+            [(hy, nvi, hz), (hy + 2 * rad, width, hz), (hy + 2 * rad, width, hz), (wy, nvi, hz), (2 * rims, nvi, hz)],
             2,
             (mxu, 4 * plane * (nspace * 2 * rows + 2 * hy * nviews)),
-            place_yz, ky, wxt, *kzt, blurred, *pieces,
+            place_yz, ky, wxt, kzt, blurred, *pieces,
         )
 
     over = hy // group
     for step in range(ITERS):
         if step:
             wide = gather([estimate[:rows], estimate[rows:]])
-        a, b = scatter_sum(*back(ahead(wide)))
+        blurred = ahead(wide, () if step else tuple(pieces[1:3]), (mxu if step else 0, plane))
+        a, b = scatter_sum(*back(blurred))
         to_y, to_z, to_c = call(
             functools.partial(pack_kernel, rad),
             [(hy + over, width, hz), (4 * rims, width, hz), (2 * over, width, hz)],
@@ -428,10 +457,15 @@
 
     main = jnp.concatenate([estimate[:half], estimate[rows : rows + half]], axis=0)
     own = lax.dynamic_slice_in_dim(main, rad * yh, hy, axis=0)
-    parts = lax.all_gather(own, "view")
-    low = jnp.concatenate([parts[0], parts[1]], axis=0)
-    high = jnp.concatenate([parts[3], parts[2]], axis=0)
-    return jnp.concatenate([low, high], axis=-1).transpose(1, 0, 2)
+    parts = [own] + [swap(own, "view", r) for r in range(1, nview)]
+    return call(
+        assemble_kernel,
+        [(width, ny, nz)],
+        [],
+        1,
+        (plane, 16 * plane * ny),
+        g.astype(jnp.int32)[None], *parts,
+    )[0]
 
 
 def solution(mesh):

time: 289 us -> 266 us (0.920)
  waiting for transfers between devices: 108 us -> 93.7 us
  between operations: 14 us -> 0.64 us
  starting transfers between devices: 37.8 us -> 41.8 us
  local copies, waits for them, and re-layouts: 14.6 us -> 18.1 us
    all_gather x1 -> x0, waiting for transfers between devices: 27.6 us -> none  [body(): parts = lax.all_gather(own, 'view')]
    ppermute x34 -> x37, waiting for transfers between devices: 80.6 us -> 93.7 us  [swap(): return lax.ppermute(value, axis, [(i, i ^ mask) for i in range(count)])]
    unnamed x51 -> x75, local copies, waits for them, and re-layouts: 3.26 us -> 8.63 us
    ppermute x34 -> x37, starting transfers between devices: 37.8 us -> 41.8 us  [swap(): return lax.ppermute(value, axis, [(i, i ^ mask) for i in range(count)])]
    pallas_call x8 -> x9, Pallas kernels: 85.3 us -> 82.8 us  [call(): pl.pallas_call(kernel, out_shape=[jax.ShapeDtypeStruct(shape, F32) for sh...]
  transfers between devices with their start and end apart: 35 -> 37, of which waited for: 22 -> 23; matrix products, arithmetic and copies ran while one was open for 9% -> 12% of each run, Pallas kernels for 6% -> 6%
where the time goes in v3:
time: 266 us; the launch traced here: 265 us
  waiting for transfers between devices  93.7 us (35%)
  Pallas kernels  82.8 us (31%)
  starting transfers between devices  41.8 us (16%)
  other arithmetic  27.9 us (10%)
  local copies, waits for them, and re-layouts  18.1 us (7%)
    ppermute x37, waiting for transfers between devices, swap(): return lax.ppermute(value, axis, [(i, i ^ mask) for i in range(count)])  93.7 us
    pallas_call x9, Pallas kernels, call(): pl.pallas_call(kernel, out_shape=[jax.ShapeDtypeStruct(shape, F32) for sh...  82.8 us
    ppermute x37, starting transfers between devices, swap(): return lax.ppermute(value, axis, [(i, i ^ mask) for i in range(count)])  41.8 us
    unnamed x75, local copies, waits for them, and re-layouts  8.63 us
    reduce_sum x2, other arithmetic, pick(): return jnp.sum(jnp.where(hit, lead, 0.0), axis=-1)  7.04 us
  transfers between devices with their start and end apart: 37, of which 23 were waited for; matrix products, arithmetic and copies ran while one was open for 12% of the time, Pallas kernels for 6%

profile of v3, /device:TPU:8, one launch (start us, length us, event | category | flops | bytes accessed | tf_op | source)
XLA Modules:
  0.0 264.9 jit_solution(10286932504834756225)
XLA Ops:
  2.4 3.0 %collective-permute-start.1 = (f32[2,128]{1,0:T(2,128)S(1)}, f32[2,128]{1,0:T(2,128)S(1)}, u32[]{:S(2)}, u32[]{:S(2)}) collective-permute-start(f32[2,128]{1,0:T(2,128)S(1)} %select_maximum_fusion), channel_id=1, source_target_pairs={{0,16},{8,24},{16,0},{24,8},{1,17},{9,25},{17,1},{25,9},{2,18},{10... | collective-permute-start | bytes 3080 | tf_op jit(solution)/shard_map/ppermute | solution.py:19
  7.3 1.5 collective-permute-start.6
  8.8 1.4 constant_dynamic-slice_fusion
  10.2 3.5 %collective-permute-start.10 = (f32[2,16,32,128]{3,2,1,0:T(8,128)}, f32[2,16,32,128]{3,2,1,0:T(8,128)S(1)}, u32[]{:S(2)}, u32[]{:S(2)}) collective-permute-start(f32[2,16,32,128]{3,2,1,0:T(8,128)} %get-tuple-element.26), channel_id=1, source_target_pairs={{0,16},{8,24},{16,0},{24,8},{1,17},{9,25},{17,1},{25,9},{2,18},{10... | collective-permute-start | bytes 1572872 | tf_op jit(solution)/shard_map/ppermute | solution.py:19
  17.3 6.5 %select_reduce_fusion = f32[8,256,128]{2,1,0:T(8,128)S(1)} fusion(f32[8,32]{1,0:T(8,128)S(1)} %get-tuple-element.49, pred[256,128,32]{1,2,0:T(8,128)(4,1)S(1)} %iota_compare_fusion), kind=kLoop, calls=%fused_computation | loop fusion | flops 16515072 | bytes 2098176 | tf_op jit(solution)/shard_map/reduce_sum | solution.py:25
  27.4 1.6 collective-permute-start.3
  31.0 2.5 collective-permute-done.3
  36.0 1.6 collective-permute-start.7
  38.4 5.0 %collective-permute-done.4 = f32[2,1,1,28,16,128]{5,4,3,0,2,1:T(8,128)S(1)} collective-permute-done((f32[2,1,1,28,16,128]{5,4,3,0,2,1:T(8,128)S(1)}, f32[2,1,1,28,16,128]{5,4,3,0,2,1:T(8,128)S(1)}, u32[]{:S(2)}, u32[]{:S(2)}) %collective-permute-start.4) | collective-permute-done | bytes 458784 | tf_op jit(solution)/shard_map/ppermute | solution.py:19
  43.6 1.9 collective-permute-done.7
  47.2 1.6 copy.83
  48.9 2.7 %pad_maximum_fusion.kz = bf16[8,384,256]{2,1,0:T(8,128)(2,1)} fusion(bf16[8,128,256]{2,1,0:T(8,128)(2,1)} %get-tuple-element.36, bf16[8,128,256]{2,1,0:T(8,128)(2,1)S(1)} %copy-done.9), kind=kLoop, calls=%fused_computation.4 | loop fusion | flops 4718592 | bytes 2621440 | tf_op jit(solution)/shard_map/concatenate | solution.py:408
  53.6 17.1 %shard_map.55.blurred = f32[32,128,128]{2,1,0:T(8,128)} custom-call(s32[2]{0:T(128)} %pad_add_fusion.1.place, f32[8,32]{1,0:T(8,128)} %get-tuple-element.51.ky, bf16[128,384]{1,0:T(8,128)(2,1)} %pad_maximum_fusion.7.wx, bf16[8,512,128]{2,1,0:T(8,128)(2,1)} %copy-done.2, f32[4,28,16,128]{3,2,1,0:T(8,128)} %bitcast.162, ...), custom_call_target="tpu_custom_call" | custom-call | bytes 2048 | tf_op jit(solution)/shard_map/pallas_call | solution.py:318
  71.3 18.2 %shard_map.56 = (f32[4,54,16,128]{3,2,1,0:T(8,128)}, f32[4,54,16,128]{3,2,1,0:T(8,128)}) custom-call(s32[2]{0:T(128)} %pad_add_fusion.1.place, f32[8,32]{1,0:T(8,128)} %get-tuple-element.51.ky, bf16[128,384]{1,0:T(8,128)(2,1)} %pad_maximum_fusion.6.wxt, bf16[8,384,256]{2,1,0:T(8,128)(2,1)} %pad_maximum_fusion.kz, f32[32,128,128]{2,1,0:T(8,128)} %shard_map.55.blurred, ...), custom_call_target="tpu_custom_call" | custom-call | flops 339738624 | bytes 7733248 | tf_op jit(solution)/shard_map/pallas_call | solution.py:318
  90.0 3.5 %collective-permute-done.12 = f32[4,54,16,128]{3,2,1,0:T(8,128)S(1)} collective-permute-done((f32[4,54,16,128]{3,2,1,0:T(8,128)}, f32[4,54,16,128]{3,2,1,0:T(8,128)S(1)}, u32[]{:S(2)}, u32[]{:S(2)}) %collective-permute-start.12) | collective-permute-done | bytes 1769504 | tf_op jit(solution)/shard_map/ppermute | solution.py:19
  93.5 1.8 add.187
  95.5 1.6 collective-permute-start.15
  98.3 9.6 %collective-permute-done.15 = f32[1,2,27,16,128]{4,3,2,1,0:T(8,128)S(1)} collective-permute-done((f32[1,2,27,16,128]{4,3,2,1,0:T(8,128)S(1)}, f32[1,2,27,16,128]{4,3,2,1,0:T(8,128)S(1)}, u32[]{:S(2)}, u32[]{:S(2)}) %collective-permute-start.15) | collective-permute-done | bytes 442400 | tf_op jit(solution)/shard_map/ppermute | solution.py:19
  109.5 1.6 collective-permute-start.14
  111.1 4.0 %collective-permute-done.16 = f32[1,1,27,16,128]{4,3,2,1,0:T(8,128)S(1)} collective-permute-done((f32[1,1,27,16,128]{4,3,2,1,0:T(8,128)S(1)}, f32[1,1,27,16,128]{4,3,2,1,0:T(8,128)S(1)}, u32[]{:S(2)}, u32[]{:S(2)}) %collective-permute-start.16) | collective-permute-done | bytes 221216 | tf_op jit(solution)/shard_map/ppermute | solution.py:19
  116.9 2.5 shard_map.57
  119.3 1.4 collective-permute-start.17
  120.8 2.6 collective-permute-start.18
  124.6 7.5 %collective-permute-done.19.fc = f32[8,16,128]{2,1,0:T(8,128)S(1)} collective-permute-done((f32[8,16,128]{2,1,0:T(8,128)}, f32[8,16,128]{2,1,0:T(8,128)S(1)}, u32[]{:S(2)}, u32[]{:S(2)}) %collective-permute-start.19) | collective-permute-done | bytes 65568 | tf_op jit(solution)/shard_map/ppermute | solution.py:19
  132.9 2.4 shard_map.58.old
  137.6 1.5 collective-permute-start.20
  139.1 3.3 %collective-permute-done.23 = f32[1,1,1,27,16,128]{5,4,3,2,1,0:T(8,128)S(1)} collective-permute-done((f32[1,1,1,27,16,128]{5,4,3,2,1,0:T(8,128)S(1)}, f32[1,1,1,27,16,128]{5,4,3,2,1,0:T(8,128)S(1)}, u32[]{:S(2)}, u32[]{:S(2)}) %collective-permute-start.23) | collective-permute-done | bytes 221216 | tf_op jit(solution)/shard_map/ppermute | solution.py:19
  142.4 1.6 collective-permute-start.24
  144.0 1.6 collective-permute-done.20
  146.6 6.4 %collective-permute-done.24 = f32[1,1,2,27,16,128]{5,4,3,2,1,0:T(8,128)S(1)} collective-permute-done((f32[1,1,2,27,16,128]{5,4,3,2,1,0:T(8,128)S(1)}, f32[1,1,2,27,16,128]{5,4,3,2,1,0:T(8,128)S(1)}, u32[]{:S(2)}, u32[]{:S(2)}) %collective-permute-start.24) | collective-permute-done | bytes 442400 | tf_op jit(solution)/shard_map/ppermute | solution.py:19
  157.8 16.8 %shard_map.59.blurred = f32[32,128,128]{2,1,0:T(8,128)} custom-call(s32[2]{0:T(128)} %pad_add_fusion.1.place, f32[8,32]{1,0:T(8,128)} %get-tuple-element.51.ky, bf16[128,384]{1,0:T(8,128)(2,1)} %pad_maximum_fusion.7.wx, bf16[8,512,128]{2,1,0:T(8,128)(2,1)} %copy-done.2, f32[4,27,16,128]{3,2,1,0:T(8,128)} %bitcast.174, f32[4,27,16,128]{3,2,1,0:T(8,128)} %copy-done.17, ...), custom_call_target="tpu_custom_call" | custom-call | flops 339738624 | bytes 2048 | tf_op jit(solution)/shard_map/pallas_call | solution.py:318
  174.7 18.2 %shard_map.60 = (f32[4,54,16,128]{3,2,1,0:T(8,128)}, f32[4,54,16,128]{3,2,1,0:T(8,128)}) custom-call(s32[2]{0:T(128)} %pad_add_fusion.1.place, f32[8,32]{1,0:T(8,128)} %get-tuple-element.51.ky, bf16[128,384]{1,0:T(8,128)(2,1)} %pad_maximum_fusion.6.wxt, bf16[8,384,256]{2,1,0:T(8,128)(2,1)} %pad_maximum_fusion.kz, f32[32,128,128]{2,1,0:T(8,128)} %shard_map.59.blurred, ...), custom_call_target="tpu_custom_call" | custom-call | flops 339738624 | bytes 7733248 | tf_op jit(solution)/shard_map/pallas_call | solution.py:318
  193.0 3.8 %collective-permute-done.26 = f32[4,54,16,128]{3,2,1,0:T(8,128)S(1)} collective-permute-done((f32[4,54,16,128]{3,2,1,0:T(8,128)}, f32[4,54,16,128]{3,2,1,0:T(8,128)S(1)}, u32[]{:S(2)}, u32[]{:S(2)}) %collective-permute-start.26) | collective-permute-done | bytes 1769504 | tf_op jit(solution)/shard_map/ppermute | solution.py:19
  196.8 1.8 add.192
  198.8 1.6 collective-permute-start.29
  201.4 9.7 %collective-permute-done.29 = f32[1,2,27,16,128]{4,3,2,1,0:T(8,128)S(1)} collective-permute-done((f32[1,2,27,16,128]{4,3,2,1,0:T(8,128)S(1)}, f32[1,2,27,16,128]{4,3,2,1,0:T(8,128)S(1)}, u32[]{:S(2)}, u32[]{:S(2)}) %collective-permute-start.29) | collective-permute-done | bytes 442400 | tf_op jit(solution)/shard_map/ppermute | solution.py:19
  212.5 1.3 collective-permute-start.28
  213.8 4.0 %collective-permute-done.30 = f32[1,1,27,16,128]{4,3,2,1,0:T(8,128)S(1)} collective-permute-done((f32[1,1,27,16,128]{4,3,2,1,0:T(8,128)S(1)}, f32[1,1,27,16,128]{4,3,2,1,0:T(8,128)S(1)}, u32[]{:S(2)}, u32[]{:S(2)}) %collective-permute-start.30) | collective-permute-done | bytes 221216 | tf_op jit(solution)/shard_map/ppermute | solution.py:19
  219.6 2.2 shard_map.61
  222.6 1.6 collective-permute-start.32
  224.2 2.0 collective-permute-start.33
  226.2 6.4 %collective-permute-done.33.fc = f32[8,16,128]{2,1,0:T(8,128)S(1)} collective-permute-done((f32[8,16,128]{2,1,0:T(8,128)}, f32[8,16,128]{2,1,0:T(8,128)S(1)}, u32[]{:S(2)}, u32[]{:S(2)}) %collective-permute-start.33) | collective-permute-done | bytes 65568 | tf_op jit(solution)/shard_map/ppermute | solution.py:19
  234.0 2.4 shard_map.62
  238.4 2.1 collective-permute-start.35
  241.2 5.8 %collective-permute-done.34.refs_1_ = f32[32,16,128]{2,1,0:T(8,128)S(1)} collective-permute-done((f32[32,16,128]{2,1,0:T(8,128)S(1)}, f32[32,16,128]{2,1,0:T(8,128)S(1)}, u32[]{:S(2)}, u32[]{:S(2)}) %collective-permute-start.34) | collective-permute-done | bytes 262176 | tf_op jit(solution)/shard_map/ppermute | solution.py:19
  246.9 9.9 %collective-permute-done.35.refs_2_ = f32[32,16,128]{2,1,0:T(8,128)S(1)} collective-permute-done((f32[32,16,128]{2,1,0:T(8,128)S(1)}, f32[32,16,128]{2,1,0:T(8,128)S(1)}, u32[]{:S(2)}, u32[]{:S(2)}) %collective-permute-start.35) | collective-permute-done | bytes 262176 | tf_op jit(solution)/shard_map/ppermute | solution.py:19
  256.8 4.3 %collective-permute-done.36.refs_3_ = f32[32,16,128]{2,1,0:T(8,128)S(1)} collective-permute-done((f32[32,16,128]{2,1,0:T(8,128)S(1)}, f32[32,16,128]{2,1,0:T(8,128)S(1)}, u32[]{:S(2)}, u32[]{:S(2)}) %collective-permute-start.36) | collective-permute-done | bytes 262176 | tf_op jit(solution)/shard_map/ppermute | solution.py:19
  261.9 3.0 %shard_map.63 = f32[16,64,256]{2,1,0:T(8,128)} custom-call(s32[1]{0:T(128)} %bitcast.where, f32[32,16,128]{2,1,0:T(8,128)} %copy-done.15, f32[32,16,128]{2,1,0:T(8,128)} %copy-done.21, f32[32,16,128]{2,1,0:T(8,128)} %copy-done.22, f32[32,16,128]{2,1,0:T(8,128)} %copy-done.23), custom_call_target="tpu_custom_call" | custom-call | flops 2048 | bytes 2097152 | tf_op jit(solution)/shard_map/pallas_call | solution.py:318
  (198 shorter events, 46.2 us)
Async XLA Ops:
  2.4 13.1 %collective-permute-start = (f32[2,128]{1,0:T(2,128)S(1)}, f32[2,128]{1,0:T(2,128)S(1)}, u32[]{:S(2)}, u32[]{:S(2)}) collective-permute-start(f32[2,128]{1,0:T(2,128)S(1)} %select_maximum_fusion), channel_id=1, source_target_pairs={{0,8},{8,0},{16,24},{24,16},{1,9},{9,1},{17,25},{25,17},{2,10},{10... | collective-permute-start | bytes 3080 | tf_op jit(solution)/shard_map/ppermute | solution.py:19
  2.4 13.1 %collective-permute-start.1 = (f32[2,128]{1,0:T(2,128)S(1)}, f32[2,128]{1,0:T(2,128)S(1)}, u32[]{:S(2)}, u32[]{:S(2)}) collective-permute-start(f32[2,128]{1,0:T(2,128)S(1)} %select_maximum_fusion), channel_id=1, source_target_pairs={{0,16},{8,24},{16,0},{24,8},{1,17},{9,25},{17,1},{25,9},{2,18},{10... | collective-permute-start | bytes 3080 | tf_op jit(solution)/shard_map/ppermute | solution.py:19
  5.4 10.7 %collective-permute-start.2 = (f32[2,128]{1,0:T(2,128)S(1)}, f32[2,128]{1,0:T(2,128)S(1)}, u32[]{:S(2)}, u32[]{:S(2)}) collective-permute-start(f32[2,128]{1,0:T(2,128)S(1)} %select_maximum_fusion), channel_id=1, source_target_pairs={{0,24},{8,16},{16,8},{24,0},{1,25},{9,17},{17,9},{25,1},{2,26},{10... | collective-permute-start | bytes 3080 | tf_op jit(solution)/shard_map/ppermute | solution.py:19
  6.2 21.2 %copy-start.12 = (f32[24,16,128]{2,1,0:T(8,128)}, f32[24,16,128]{2,1,0:T(8,128)S(1)}, u32[]{:S(2)}) copy-start(f32[24,16,128]{2,1,0:T(8,128)S(1)} %get-tuple-element.42) | copy-start | bytes 589828
  7.3 27.7 %collective-permute-start.6 = (f32[1,1,1,27,16,128]{5,4,3,2,1,0:T(8,128)}, f32[1,1,1,27,16,128]{5,4,3,2,1,0:T(8,128)}, u32[]{:S(2)}, u32[]{:S(2)}) collective-permute-start(f32[1,1,1,27,16,128]{5,4,3,2,1,0:T(8,128)} %maximum_bitcast_fusion.5), channel_id=1, source_target_pairs={{0,2},{1,3},{2,0},{3,1},{4,6},{5,7},{6,4},{7,5},{8,10},{9,11},{10,... | collective-permute-start | bytes 663560 | tf_op jit(solution)/shard_map/ppermute | solution.py:19
  10.2 42.4 %collective-permute-start.10 = (f32[2,16,32,128]{3,2,1,0:T(8,128)}, f32[2,16,32,128]{3,2,1,0:T(8,128)S(1)}, u32[]{:S(2)}, u32[]{:S(2)}) collective-permute-start(f32[2,16,32,128]{3,2,1,0:T(8,128)} %get-tuple-element.26), channel_id=1, source_target_pairs={{0,16},{8,24},{16,0},{24,8},{1,17},{9,25},{17,1},{25,9},{2,18},{10... | collective-permute-start | bytes 1572872 | tf_op jit(solution)/shard_map/ppermute | solution.py:19
  15.3 12.1 %copy-start.25 = (f32[3,16,128]{2,1,0:T(8,128)}, f32[3,16,128]{2,1,0:T(8,128)S(1)}, u32[]{:S(2)}) copy-start(f32[3,16,128]{2,1,0:T(8,128)S(1)} %slice.137) | copy-start | bytes 73732
  15.4 37.2 %collective-permute-start.9 = (f32[2,16,32,128]{3,2,1,0:T(8,128)}, f32[2,16,32,128]{3,2,1,0:T(8,128)S(1)}, u32[]{:S(2)}, u32[]{:S(2)}) collective-permute-start(f32[2,16,32,128]{3,2,1,0:T(8,128)} %get-tuple-element.27), channel_id=1, source_target_pairs={{0,8},{8,0},{16,24},{24,16},{1,9},{9,1},{17,25},{25,17},{2,10},{10... | collective-permute-start | bytes 1572872 | tf_op jit(solution)/shard_map/ppermute | solution.py:19
  15.5 55.8 %collective-permute-start.11 = (f32[2,16,32,128]{3,2,1,0:T(8,128)}, f32[2,16,32,128]{3,2,1,0:T(8,128)}, u32[]{:S(2)}, u32[]{:S(2)}) collective-permute-start(f32[2,16,32,128]{3,2,1,0:T(8,128)} %get-tuple-element.25), channel_id=1, source_target_pairs={{0,24},{8,16},{16,8},{24,0},{1,25},{9,17},{17,9},{25,1},{2,26},{10... | collective-permute-start | bytes 1572872 | tf_op jit(solution)/shard_map/ppermute | solution.py:19
  27.4 6.1 %collective-permute-start.3 = (f32[1,1,1,28,16,128]{5,4,3,2,1,0:T(8,128)S(1)}, f32[1,1,1,28,16,128]{5,4,3,2,1,0:T(8,128)S(1)}, u32[]{:S(2)}, u32[]{:S(2)}) collective-permute-start(f32[1,1,1,28,16,128]{5,4,3,2,1,0:T(8,128)S(1)} %maximum_bitcast_fusion.4), channel_id=1, source_target_pairs={{0,4},{1,5},{2,6},{3,7},{4,0},{5,1},{6,2},{7,3},{8,12},{9,13},{10,... | collective-permute-start | bytes 688136 | tf_op jit(solution)/shard_map/ppermute | solution.py:19
  31.0 12.6 %copy-start.18 = (f32[8,16,128]{2,1,0:T(8,128)}, f32[8,16,128]{2,1,0:T(8,128)S(1)}, u32[]{:S(2)}) copy-start(f32[8,16,128]{2,1,0:T(8,128)S(1)} %select_reduce_fusion.1) | copy-start | bytes 196612
  33.6 9.8 %collective-permute-start.4 = (f32[2,1,1,28,16,128]{5,4,3,0,2,1:T(8,128)S(1)}, f32[2,1,1,28,16,128]{5,4,3,0,2,1:T(8,128)S(1)}, u32[]{:S(2)}, u32[]{:S(2)}) collective-permute-start(f32[2,1,1,28,16,128]{5,4,3,0,2,1:T(8,128)S(1)} %maximum_bitcast_fusion), channel_id=1, source_target_pairs={{0,2},{1,3},{2,0},{3,1},{4,6},{5,7},{6,4},{7,5},{8,10},{9,11},{10,... | collective-permute-start | bytes 1376264 | tf_op jit(solution)/shard_map/ppermute | solution.py:19
  36.0 9.4 %collective-permute-start.7 = (f32[1,1,2,27,16,128]{5,4,3,2,1,0:T(8,128)S(1)}, f32[1,1,2,27,16,128]{5,4,3,2,1,0:T(8,128)S(1)}, u32[]{:S(2)}, u32[]{:S(2)}) collective-permute-start(f32[1,1,2,27,16,128]{5,4,3,2,1,0:T(8,128)S(1)} %maximum_bitcast_fusion.1), channel_id=1, source_target_pairs={{0,4},{1,5},{2,6},{3,7},{4,0},{5,1},{6,2},{7,3},{8,12},{9,13},{10,... | collective-permute-start | bytes 1327112 | tf_op jit(solution)/shard_map/ppermute | solution.py:19
  43.5 8.1 %collective-permute-start.5 = (f32[4,28,16,128]{3,2,1,0:T(8,128)S(1)}, f32[4,28,16,128]{3,2,1,0:T(8,128)}, u32[]{:S(2)}, u32[]{:S(2)}) collective-permute-start(f32[4,28,16,128]{3,2,1,0:T(8,128)S(1)} %bitcast.160), channel_id=1, source_target_pairs={{0,1},{1,0},{2,3},{3,2},{4,5},{5,4},{6,7},{7,6},{8,9},{9,8},{10,11... | collective-permute-start | bytes 2752520 | tf_op jit(solution)/shard_map/ppermute | solution.py:19
  46.6 6.0 %collective-permute-start.8 = (f32[4,27,16,128]{3,2,1,0:T(8,128)}, f32[4,27,16,128]{3,2,1,0:T(8,128)}, u32[]{:S(2)}, u32[]{:S(2)}) collective-permute-start(f32[4,27,16,128]{3,2,1,0:T(8,128)} %bitcast.26.b0), channel_id=1, source_target_pairs={{0,1},{1,0},{2,3},{3,2},{4,5},{5,4},{6,7},{7,6},{8,9},{9,8},{10,11... | collective-permute-start | bytes 2654216 | tf_op jit(solution)/shard_map/ppermute | solution.py:19
  53.5 17.1 %copy-start.24 = (f32[128,128]{0,1:T(8,128)S(1)}, f32[128,128]{0,1:T(8,128)}, u32[]{:S(2)}) copy-start(f32[128,128]{0,1:T(8,128)} %copy.83) | copy-start | bytes 196612
  89.4 4.0 %collective-permute-start.12 = (f32[4,54,16,128]{3,2,1,0:T(8,128)}, f32[4,54,16,128]{3,2,1,0:T(8,128)S(1)}, u32[]{:S(2)}, u32[]{:S(2)}) collective-permute-start(f32[4,54,16,128]{3,2,1,0:T(8,128)} %get-tuple-element.16), channel_id=1, source_target_pairs={{0,1},{1,0},{2,3},{3,2},{4,5},{5,4},{6,7},{7,6},{8,9},{9,8},{10,11... | collective-permute-start | bytes 5308424 | tf_op jit(solution)/shard_map/ppermute | solution.py:19
  95.5 12.5 %collective-permute-start.15 = (f32[1,2,27,16,128]{4,3,2,1,0:T(8,128)S(1)}, f32[1,2,27,16,128]{4,3,2,1,0:T(8,128)S(1)}, u32[]{:S(2)}, u32[]{:S(2)}) collective-permute-start(f32[1,2,27,16,128]{4,3,2,1,0:T(8,128)S(1)} %slice_bitcast_fusion.4), channel_id=1, source_target_pairs={{0,4},{1,5},{2,6},{3,7},{4,0},{5,1},{6,2},{7,3},{8,12},{9,13},{10,... | collective-permute-start | bytes 1327112 | tf_op jit(solution)/shard_map/ppermute | solution.py:19
  97.1 12.3 %collective-permute-start.13 = (f32[2,1,27,16,128]{4,3,2,0,1:T(8,128)S(1)}, f32[2,1,27,16,128]{4,3,2,0,1:T(8,128)S(1)}, u32[]{:S(2)}, u32[]{:S(2)}) collective-permute-start(f32[2,1,27,16,128]{4,3,2,0,1:T(8,128)S(1)} %slice_bitcast_fusion.6), channel_id=1, source_target_pairs={{0,2},{1,3},{2,0},{3,1},{4,6},{5,7},{6,4},{7,5},{8,10},{9,11},{10,... | collective-permute-start | bytes 1327112 | tf_op jit(solution)/shard_map/ppermute | solution.py:19
  108.0 15.7 %copy-start.11 = (f32[24,16,128]{2,1,0:T(8,128)S(1)}, f32[24,16,128]{2,1,0:T(8,128)}, u32[]{:S(2)}) copy-start(f32[24,16,128]{2,1,0:T(8,128)} %copy-done.10) | copy-start | bytes 589828
  108.1 15.7 %copy-start.13 = (f32[24,16,128]{2,1,0:T(8,128)S(1)}, f32[24,16,128]{2,1,0:T(8,128)}, u32[]{:S(2)}) copy-start(f32[24,16,128]{2,1,0:T(8,128)} %copy-done.12) | copy-start | bytes 589828
  108.1 15.7 %copy-start.26 = (f32[3,16,128]{2,1,0:T(8,128)S(1)}, f32[3,16,128]{2,1,0:T(8,128)}, u32[]{:S(2)}) copy-start(f32[3,16,128]{2,1,0:T(8,128)} %copy-done.25) | copy-start | bytes 73732
  108.1 15.7 %copy-start.28 = (f32[3,16,128]{2,1,0:T(8,128)S(1)}, f32[3,16,128]{2,1,0:T(8,128)}, u32[]{:S(2)}) copy-start(f32[3,16,128]{2,1,0:T(8,128)} %copy-done.27) | copy-start | bytes 73732
  108.1 7.0 %collective-permute-start.16 = (f32[1,1,27,16,128]{4,3,2,1,0:T(8,128)S(1)}, f32[1,1,27,16,128]{4,3,2,1,0:T(8,128)S(1)}, u32[]{:S(2)}, u32[]{:S(2)}) collective-permute-start(f32[1,1,27,16,128]{4,3,2,1,0:T(8,128)S(1)} %slice_bitcast_fusion.14), channel_id=1, source_target_pairs={{0,2},{1,3},{2,0},{3,1},{4,6},{5,7},{6,4},{7,5},{8,10},{9,11},{10,... | collective-permute-start | bytes 663560 | tf_op jit(solution)/shard_map/ppermute | solution.py:19
  109.5 6.7 %collective-permute-start.14 = (f32[1,1,27,16,128]{4,3,2,1,0:T(8,128)S(1)}, f32[1,1,27,16,128]{4,3,2,1,0:T(8,128)S(1)}, u32[]{:S(2)}, u32[]{:S(2)}) collective-permute-start(f32[1,1,27,16,128]{4,3,2,1,0:T(8,128)S(1)} %slice_bitcast_fusion.16), channel_id=1, source_target_pairs={{0,4},{1,5},{2,6},{3,7},{4,0},{5,1},{6,2},{7,3},{8,12},{9,13},{10,... | collective-permute-start | bytes 663560 | tf_op jit(solution)/shard_map/ppermute | solution.py:19
  119.3 12.8 %collective-permute-start.17 = (f32[36,16,128]{2,1,0:T(8,128)}, f32[36,16,128]{2,1,0:T(8,128)S(1)}, u32[]{:S(2)}, u32[]{:S(2)}) collective-permute-start(f32[36,16,128]{2,1,0:T(8,128)} %get-tuple-element.17), channel_id=1, source_target_pairs={{0,8},{8,0},{16,24},{24,16},{1,9},{9,1},{17,25},{25,17},{2,10},{10... | collective-permute-start | bytes 884744 | tf_op jit(solution)/shard_map/ppermute | solution.py:19
  120.8 11.3 %collective-permute-start.18 = (f32[12,16,128]{2,1,0:T(8,128)}, f32[12,16,128]{2,1,0:T(8,128)S(1)}, u32[]{:S(2)}, u32[]{:S(2)}) collective-permute-start(f32[12,16,128]{2,1,0:T(8,128)} %get-tuple-element.18), channel_id=1, source_target_pairs={{0,24},{8,16},{16,8},{24,0},{1,25},{9,17},{17,9},{25,1},{2,26},{10... | collective-permute-start | bytes 294920 | tf_op jit(solution)/shard_map/ppermute | solution.py:19
  123.4 8.7 %collective-permute-start.19 = (f32[8,16,128]{2,1,0:T(8,128)}, f32[8,16,128]{2,1,0:T(8,128)S(1)}, u32[]{:S(2)}, u32[]{:S(2)}) collective-permute-start(f32[8,16,128]{2,1,0:T(8,128)} %get-tuple-element.19), channel_id=1, source_target_pairs={{0,16},{8,24},{16,0},{24,8},{1,17},{9,25},{17,1},{25,9},{2,18},{10... | collective-permute-start | bytes 196616 | tf_op jit(solution)/shard_map/ppermute | solution.py:19
  136.4 6.0 %collective-permute-start.23 = (f32[1,1,1,27,16,128]{5,4,3,2,1,0:T(8,128)S(1)}, f32[1,1,1,27,16,128]{5,4,3,2,1,0:T(8,128)S(1)}, u32[]{:S(2)}, u32[]{:S(2)}) collective-permute-start(f32[1,1,1,27,16,128]{5,4,3,2,1,0:T(8,128)S(1)} %get-tuple-element.39), channel_id=1, source_target_pairs={{0,2},{1,3},{2,0},{3,1},{4,6},{5,7},{6,4},{7,5},{8,10},{9,11},{10,... | collective-permute-start | bytes 663560 | tf_op jit(solution)/shard_map/ppermute | solution.py:19
  137.6 8.1 %collective-permute-start.20 = (f32[1,1,1,27,16,128]{5,4,3,2,1,0:T(8,128)S(1)}, f32[1,1,1,27,16,128]{5,4,3,2,1,0:T(8,128)S(1)}, u32[]{:S(2)}, u32[]{:S(2)}) collective-permute-start(f32[1,1,1,27,16,128]{5,4,3,2,1,0:T(8,128)S(1)} %get-tuple-element.40), channel_id=1, source_target_pairs={{0,4},{1,5},{2,6},{3,7},{4,0},{5,1},{6,2},{7,3},{8,12},{9,13},{10,... | collective-permute-start | bytes 663560 | tf_op jit(solution)/shard_map/ppermute | solution.py:19
  142.4 10.5 %collective-permute-start.24 = (f32[1,1,2,27,16,128]{5,4,3,2,1,0:T(8,128)S(1)}, f32[1,1,2,27,16,128]{5,4,3,2,1,0:T(8,128)S(1)}, u32[]{:S(2)}, u32[]{:S(2)}) collective-permute-start(f32[1,1,2,27,16,128]{5,4,3,2,1,0:T(8,128)S(1)} %maximum_bitcast_fusion.3), channel_id=1, source_target_pairs={{0,4},{1,5},{2,6},{3,7},{4,0},{5,1},{6,2},{7,3},{8,12},{9,13},{10,... | collective-permute-start | bytes 1327112 | tf_op jit(solution)/shard_map/ppermute | solution.py:19
  145.7 8.4 %collective-permute-start.21 = (f32[2,1,1,27,16,128]{5,4,3,0,2,1:T(8,128)S(1)}, f32[2,1,1,27,16,128]{5,4,3,0,2,1:T(8,128)S(1)}, u32[]{:S(2)}, u32[]{:S(2)}) collective-permute-start(f32[2,1,1,27,16,128]{5,4,3,0,2,1:T(8,128)S(1)} %maximum_bitcast_fusion.2), channel_id=1, source_target_pairs={{0,2},{1,3},{2,0},{3,1},{4,6},{5,7},{6,4},{7,5},{8,10},{9,11},{10,... | collective-permute-start | bytes 1327112 | tf_op jit(solution)/shard_map/ppermute | solution.py:19
  153.0 2.5 collective-permute-start.25
  154.2 2.6 collective-permute-start.22
  192.9 3.9 %collective-permute-start.26 = (f32[4,54,16,128]{3,2,1,0:T(8,128)}, f32[4,54,16,128]{3,2,1,0:T(8,128)S(1)}, u32[]{:S(2)}, u32[]{:S(2)}) collective-permute-start(f32[4,54,16,128]{3,2,1,0:T(8,128)} %get-tuple-element.21), channel_id=1, source_target_pairs={{0,1},{1,0},{2,3},{3,2},{4,5},{5,4},{6,7},{7,6},{8,9},{9,8},{10,11... | collective-permute-start | bytes 5308424 | tf_op jit(solution)/shard_map/ppermute | solution.py:19
  198.8 12.3 %collective-permute-start.29 = (f32[1,2,27,16,128]{4,3,2,1,0:T(8,128)S(1)}, f32[1,2,27,16,128]{4,3,2,1,0:T(8,128)S(1)}, u32[]{:S(2)}, u32[]{:S(2)}) collective-permute-start(f32[1,2,27,16,128]{4,3,2,1,0:T(8,128)S(1)} %slice_bitcast_fusion), channel_id=1, source_target_pairs={{0,4},{1,5},{2,6},{3,7},{4,0},{5,1},{6,2},{7,3},{8,12},{9,13},{10,... | collective-permute-start | bytes 1327112 | tf_op jit(solution)/shard_map/ppermute | solution.py:19
  200.4 12.0 %collective-permute-start.27 = (f32[2,1,27,16,128]{4,3,2,0,1:T(8,128)S(1)}, f32[2,1,27,16,128]{4,3,2,0,1:T(8,128)S(1)}, u32[]{:S(2)}, u32[]{:S(2)}) collective-permute-start(f32[2,1,27,16,128]{4,3,2,0,1:T(8,128)S(1)} %slice_bitcast_fusion.2), channel_id=1, source_target_pairs={{0,2},{1,3},{2,0},{3,1},{4,6},{5,7},{6,4},{7,5},{8,10},{9,11},{10,... | collective-permute-start | bytes 1327112 | tf_op jit(solution)/shard_map/ppermute | solution.py:19
  211.1 6.7 %collective-permute-start.30 = (f32[1,1,27,16,128]{4,3,2,1,0:T(8,128)S(1)}, f32[1,1,27,16,128]{4,3,2,1,0:T(8,128)S(1)}, u32[]{:S(2)}, u32[]{:S(2)}) collective-permute-start(f32[1,1,27,16,128]{4,3,2,1,0:T(8,128)S(1)} %slice_bitcast_fusion.8), channel_id=1, source_target_pairs={{0,2},{1,3},{2,0},{3,1},{4,6},{5,7},{6,4},{7,5},{8,10},{9,11},{10,... | collective-permute-start | bytes 663560 | tf_op jit(solution)/shard_map/ppermute | solution.py:19
  212.5 6.4 %collective-permute-start.28 = (f32[1,1,27,16,128]{4,3,2,1,0:T(8,128)S(1)}, f32[1,1,27,16,128]{4,3,2,1,0:T(8,128)S(1)}, u32[]{:S(2)}, u32[]{:S(2)}) collective-permute-start(f32[1,1,27,16,128]{4,3,2,1,0:T(8,128)S(1)} %slice_bitcast_fusion.10), channel_id=1, source_target_pairs={{0,4},{1,5},{2,6},{3,7},{4,0},{5,1},{6,2},{7,3},{8,12},{9,13},{10,... | collective-permute-start | bytes 663560 | tf_op jit(solution)/shard_map/ppermute | solution.py:19
  221.8 10.8 %collective-permute-start.31 = (f32[36,16,128]{2,1,0:T(8,128)}, f32[36,16,128]{2,1,0:T(8,128)S(1)}, u32[]{:S(2)}, u32[]{:S(2)}) collective-permute-start(f32[36,16,128]{2,1,0:T(8,128)} %get-tuple-element.22), channel_id=1, source_target_pairs={{0,8},{8,0},{16,24},{24,16},{1,9},{9,1},{17,25},{25,17},{2,10},{10... | collective-permute-start | bytes 884744 | tf_op jit(solution)/shard_map/ppermute | solution.py:19
  222.6 10.0 %collective-permute-start.32 = (f32[12,16,128]{2,1,0:T(8,128)}, f32[12,16,128]{2,1,0:T(8,128)S(1)}, u32[]{:S(2)}, u32[]{:S(2)}) collective-permute-start(f32[12,16,128]{2,1,0:T(8,128)} %get-tuple-element.23), channel_id=1, source_target_pairs={{0,24},{8,16},{16,8},{24,0},{1,25},{9,17},{17,9},{25,1},{2,26},{10... | collective-permute-start | bytes 294920 | tf_op jit(solution)/shard_map/ppermute | solution.py:19
  224.2 8.4 %collective-permute-start.33 = (f32[8,16,128]{2,1,0:T(8,128)}, f32[8,16,128]{2,1,0:T(8,128)S(1)}, u32[]{:S(2)}, u32[]{:S(2)}) collective-permute-start(f32[8,16,128]{2,1,0:T(8,128)} %get-tuple-element.24), channel_id=1, source_target_pairs={{0,16},{8,24},{16,0},{24,8},{1,17},{9,25},{17,1},{25,9},{2,18},{10... | collective-permute-start | bytes 196616 | tf_op jit(solution)/shard_map/ppermute | solution.py:19
  234.0 30.8 %copy-start.1 = (f32[16,64,256]{2,1,0:T(8,128)S(1)}, f32[16,64,256]{2,1,0:T(8,128)}, u32[]{:S(2)}) copy-start(f32[16,64,256]{2,1,0:T(8,128)} %param.5) | copy-start | bytes 3145732
  237.6 23.5 %copy-start.15 = (f32[32,16,128]{2,1,0:T(8,128)}, f32[32,16,128]{2,1,0:T(8,128)S(1)}, u32[]{:S(2)}) copy-start(f32[32,16,128]{2,1,0:T(8,128)S(1)} %fusion.10.refs_0_) | copy-start | bytes 786436
  237.6 9.3 %collective-permute-start.34 = (f32[32,16,128]{2,1,0:T(8,128)S(1)}, f32[32,16,128]{2,1,0:T(8,128)S(1)}, u32[]{:S(2)}, u32[]{:S(2)}) collective-permute-start(f32[32,16,128]{2,1,0:T(8,128)S(1)} %fusion.10.refs_0_), channel_id=1, source_target_pairs={{0,8},{8,0},{16,24},{24,16},{1,9},{9,1},{17,25},{25,17},{2,10},{10... | collective-permute-start | bytes 786440 | tf_op jit(solution)/shard_map/ppermute | solution.py:19
  238.4 18.4 %collective-permute-start.35 = (f32[32,16,128]{2,1,0:T(8,128)S(1)}, f32[32,16,128]{2,1,0:T(8,128)S(1)}, u32[]{:S(2)}, u32[]{:S(2)}) collective-permute-start(f32[32,16,128]{2,1,0:T(8,128)S(1)} %fusion.10.refs_0_), channel_id=1, source_target_pairs={{0,16},{8,24},{16,0},{24,8},{1,17},{9,25},{17,1},{25,9},{2,18},{10... | collective-permute-start | bytes 786440 | tf_op jit(solution)/shard_map/ppermute | solution.py:19
  240.5 20.6 %collective-permute-start.36 = (f32[32,16,128]{2,1,0:T(8,128)S(1)}, f32[32,16,128]{2,1,0:T(8,128)S(1)}, u32[]{:S(2)}, u32[]{:S(2)}) collective-permute-start(f32[32,16,128]{2,1,0:T(8,128)S(1)} %fusion.10.refs_0_), channel_id=1, source_target_pairs={{0,24},{8,16},{16,8},{24,0},{1,25},{9,17},{17,9},{25,1},{2,26},{10... | collective-permute-start | bytes 786440 | tf_op jit(solution)/shard_map/ppermute | solution.py:19
  246.9 14.2 %copy-start.21 = (f32[32,16,128]{2,1,0:T(8,128)}, f32[32,16,128]{2,1,0:T(8,128)S(1)}, u32[]{:S(2)}) copy-start(f32[32,16,128]{2,1,0:T(8,128)S(1)} %collective-permute-done.34.refs_1_) | copy-start | bytes 786436
  (22 other events, 56.1 us)

commit v4 on v3

--- a/solution.py
+++ b/solution.py
@@ -108,13 +108,10 @@
                 value = jnp.where(part == 0, first, jnp.where(part == 1, second, jnp.where(part == 2, third, 0.0)))
                 uh[h * half + k * group + m] = value.astype(BF16)
 
-        def two(p, carry):
-            out = mul(wx[...], stack3(jnp.concatenate([row(2 * p), row(2 * p + 1)], axis=1)))
-            u[h * half + 2 * p] = out[:, :hz]
-            u[h * half + 2 * p + 1] = out[:, hz:]
-            return carry
-
-        lax.fori_loop(0, half // 2, two, 0)
+        for y in range(0, half, 2):
+            out = mul(wx[...], stack3(jnp.concatenate([row(y), row(y + 1)], axis=1)))
+            u[h * half + y] = out[:, :hz]
+            u[h * half + y + 1] = out[:, hz:]
 
     lead = rad * (1 - yh)
     for z in (za, zb):
@@ -218,15 +215,10 @@
         for k in range(rims):
             store(mul(wxt[...], stack3(gh[c * rims + k])), c * (half + rims) + half + k)
 
-        def two(p, carry):
-            y = c * half + 2 * p
+        for y in range(c * half, (c + 1) * half, 2):
             out = mul(wxt[...], stack3(jnp.concatenate([gm[y], gm[y + 1]], axis=1)))
-            row = c * (half + rims) + 2 * p
-            store(out[:, :hz], row)
-            store(out[:, hz:], row + 1)
-            return carry
-
-        lax.fori_loop(0, half // 2, two, 0)
+            store(out[:, :hz], c * rims + y)
+            store(out[:, hz:], c * rims + y + 1)
 
 
 def row_of(a, b, y, half):
@@ -374,9 +366,9 @@
     rim = rim.reshape(2 * rims, group, width, rad).transpose(0, 2, 1, 3).reshape(2 * rims, width, hz)
     parts = [main[:half], rim[:rims], main[half:], rim[rims:]]
     estimate = jnp.concatenate(parts, axis=0)
-    wide = gather([jnp.concatenate(parts[:2] + [note], axis=0), jnp.concatenate(parts[2:], axis=0)])
-    cover = jnp.stack([wide[0][:, -1], wide[1][:, -1]])[..., :nviews]
-    cover = cover.transpose(3, 0, 1, 2).reshape(nviews, 1, nspace * width)
+    wide = gather([jnp.concatenate(parts[:2], axis=0), jnp.concatenate(parts[2:], axis=0)])
+    cover = jnp.concatenate(gather([note]), axis=1)[..., :nviews]
+    cover = cover.transpose(3, 1, 0, 2).reshape(nviews, 1, nspace * width)
 
     slab = (j - turn) % nspace
     spot = slab[:, None] * width + jnp.arange(width)

time: 266 us -> 273 us (1.026); the launches traced: 265 us -> 269 us
  local copies, waits for them, and re-layouts: 18.1 us -> 25.1 us
  Pallas kernels: 82.8 us -> 76.2 us
  other arithmetic: 27.9 us -> 33.9 us
  waiting for transfers between devices: 93.7 us -> 87.7 us
  starting transfers between devices: 41.8 us -> 44.9 us
    pallas_call x9, Pallas kernels: 82.8 us -> 76.2 us  [call(): pl.pallas_call(kernel, out_shape=[jax.ShapeDtypeStruct(shape, F32) for sh...]
    ppermute x37 -> x40, waiting for transfers between devices: 93.7 us -> 87.7 us  [swap(): return lax.ppermute(value, axis, [(i, i ^ mask) for i in range(count)])]
    mul x3, local copies, waits for them, and re-layouts: 0.17 us -> 4.35 us  [body(): band_xt = (band_x * cover).reshape(nvi, -1).T]
    another operation x6 -> x7, other arithmetic: 1.91 us -> 5.14 us  [gather(): part = part.reshape((part.shape[0] // low, 1, low) + part.shape[1:])]
    ppermute x37 -> x40, starting transfers between devices: 41.8 us -> 44.9 us  [swap(): return lax.ppermute(value, axis, [(i, i ^ mask) for i in range(count)])]
    unnamed x75 -> x72, local copies, waits for them, and re-layouts: 8.63 us -> 6.45 us
  transfers between devices with their start and end apart: 37 -> 40, of which waited for: 23 -> 23; matrix products, arithmetic and copies ran while one was open for 12% -> 16% of each run, Pallas kernels for 6% -> 5%
where the time goes in v4:
time: 273 us; the launch traced here: 269 us
  waiting for transfers between devices  87.7 us (32%)
  Pallas kernels  76.2 us (28%)
  starting transfers between devices  44.9 us (16%)
  other arithmetic  33.9 us (12%)
  local copies, waits for them, and re-layouts  25.1 us (9%)
    ppermute x40, waiting for transfers between devices, swap(): return lax.ppermute(value, axis, [(i, i ^ mask) for i in range(count)])  87.7 us
    pallas_call x9, Pallas kernels, call(): pl.pallas_call(kernel, out_shape=[jax.ShapeDtypeStruct(shape, F32) for sh...  76.2 us
    ppermute x40, starting transfers between devices, swap(): return lax.ppermute(value, axis, [(i, i ^ mask) for i in range(count)])  44.9 us
    reduce_sum x2, other arithmetic, pick(): return jnp.sum(jnp.where(hit, lead, 0.0), axis=-1)  7.04 us
    unnamed x72, local copies, waits for them, and re-layouts  6.45 us
  transfers between devices with their start and end apart: 40, of which 23 were waited for; matrix products, arithmetic and copies ran while one was open for 16% of the time, Pallas kernels for 5%

profile of v4, /device:TPU:8, one launch (start us, length us, event | category | flops | bytes accessed | tf_op | source)
XLA Modules:
  0.0 268.7 jit_solution(17985307103245934571)
XLA Ops:
  2.4 1.6 collective-permute-start.2
  7.9 1.5 collective-permute-start.6
  12.7 3.1 %constant_dynamic-slice_fusion = (f32[2,16,32,128]{3,2,1,0:T(8,128)}, f32[2,16,32,128]{3,2,1,0:T(8,128)}, f32[2,16,32,128]{3,2,1,0:T(8,128)}, f32[2,16,32,128]{3,2,1,0:T(8,128)}) fusion(f32[2,16,64,256]{3,2,1,0:T(8,128)} %param.6, s32[]{:T(128)S(6)} %select_n.82, s32[]{:T(128)S(6)} %select_n.83, s32[]{:T(128)S(6)} %select_n.79, s32[]{:T(128)S(6)} %select_n.80, ...), kind=kLoop, calls=%fused_computation.100 | loop fusion | bytes 4194336 | tf_op jit(solution)/shard_map/dynamic_slice | solution.py:350
  17.7 2.2 collective-permute-start.13
  21.7 6.5 %select_reduce_fusion = f32[8,256,128]{2,1,0:T(8,128)S(1)} fusion(f32[8,32]{1,0:T(8,128)S(1)} %get-tuple-element.51, pred[256,128,32]{1,2,0:T(8,128)(4,1)S(1)} %iota_compare_fusion), kind=kLoop, calls=%fused_computation | loop fusion | flops 16515072 | bytes 2098176 | tf_op jit(solution)/shard_map/reduce_sum | solution.py:25
  34.1 1.8 maximum_bitcast_fusion.1
  36.0 1.5 collective-permute-start.10
  43.9 2.0 collective-permute-done.10
  45.9 2.1 pad_maximum_fusion.2
  50.0 1.6 copy.78
  58.7 1.6 copy.79
  62.8 12.5 %shard_map.55.blurred = f32[32,128,128]{2,1,0:T(8,128)} custom-call(s32[2]{0:T(128)} %pad_add_fusion.1.place, f32[8,32]{1,0:T(8,128)} %get-tuple-element.53.ky, bf16[128,384]{1,0:T(8,128)(2,1)} %pad_maximum_fusion.7.wx, bf16[8,512,128]{2,1,0:T(8,128)(2,1)} %copy-done.2, f32[4,27,16,128]{3,2,1,0:T(8,128)} %bitcast.163, ...), custom_call_target="tpu_custom_call" | custom-call | bytes 2048 | tf_op jit(solution)/shard_map/pallas_call | solution.py:310
  75.3 2.6 collective-permute-done.14.refs_3_
  78.7 14.4 %shard_map.56 = (f32[4,54,16,128]{3,2,1,0:T(8,128)}, f32[4,54,16,128]{3,2,1,0:T(8,128)}) custom-call(s32[2]{0:T(128)} %pad_add_fusion.1.place, f32[8,32]{1,0:T(8,128)} %get-tuple-element.53.ky, bf16[128,384]{1,0:T(8,128)(2,1)} %pad_maximum_fusion.6.wxt, bf16[8,384,256]{2,1,0:T(8,128)(2,1)} %pad_maximum_fusion.kz, f32[32,128,128]{2,1,0:T(8,128)} %shard_map.55.blurred, ...), custom_call_target="tpu_custom_call" | custom-call | flops 339738624 | bytes 7733248 | tf_op jit(solution)/shard_map/pallas_call | solution.py:310
  93.1 3.9 %collective-permute-done.15 = f32[4,54,16,128]{3,2,1,0:T(8,128)S(1)} collective-permute-done((f32[4,54,16,128]{3,2,1,0:T(8,128)}, f32[4,54,16,128]{3,2,1,0:T(8,128)S(1)}, u32[]{:S(2)}, u32[]{:S(2)}) %collective-permute-start.15) | collective-permute-done | bytes 1769504 | tf_op jit(solution)/shard_map/ppermute | solution.py:19
  97.0 1.8 add.187
  98.9 1.6 collective-permute-start.16
  100.5 1.6 collective-permute-start.18
  102.1 9.1 %collective-permute-done.16 = f32[2,1,27,16,128]{4,3,2,0,1:T(8,128)S(1)} collective-permute-done((f32[2,1,27,16,128]{4,3,2,0,1:T(8,128)S(1)}, f32[2,1,27,16,128]{4,3,2,0,1:T(8,128)S(1)}, u32[]{:S(2)}, u32[]{:S(2)}) %collective-permute-start.16) | collective-permute-done | bytes 442400 | tf_op jit(solution)/shard_map/ppermute | solution.py:19
  111.4 1.6 collective-permute-start.17
  113.1 1.6 collective-permute-start.19
  114.6 3.5 %collective-permute-done.17 = f32[1,1,27,16,128]{4,3,2,1,0:T(8,128)S(1)} collective-permute-done((f32[1,1,27,16,128]{4,3,2,1,0:T(8,128)S(1)}, f32[1,1,27,16,128]{4,3,2,1,0:T(8,128)S(1)}, u32[]{:S(2)}, u32[]{:S(2)}) %collective-permute-start.17) | collective-permute-done | bytes 221216 | tf_op jit(solution)/shard_map/ppermute | solution.py:19
  120.2 12.4 %shard_map.57 = (f32[36,16,128]{2,1,0:T(8,128)}, f32[12,16,128]{2,1,0:T(8,128)}, f32[8,16,128]{2,1,0:T(8,128)}) custom-call(s32[2]{0:T(128)} %pad_add_fusion.1.place, f32[27,16,128]{2,1,0:T(8,128)} %fusion.18.a, f32[27,16,128]{2,1,0:T(8,128)} %fusion.16.b), custom_call_target="tpu_custom_call" | custom-call | flops 2048 | bytes 884736 | tf_op jit(solution)/shard_map/pallas_call | solution.py:310
  132.6 1.5 collective-permute-start.21
  134.2 2.9 %collective-permute-start.22 = (f32[8,16,128]{2,1,0:T(8,128)}, f32[8,16,128]{2,1,0:T(8,128)S(1)}, u32[]{:S(2)}, u32[]{:S(2)}) collective-permute-start(f32[8,16,128]{2,1,0:T(8,128)} %get-tuple-element.19), channel_id=1, source_target_pairs={{0,16},{8,24},{16,0},{24,8},{1,17},{9,25},{17,1},{25,9},{2,18},{10... | collective-permute-start | bytes 196616 | tf_op jit(solution)/shard_map/ppermute | solution.py:19
  137.8 5.5 %collective-permute-done.22.fc = f32[8,16,128]{2,1,0:T(8,128)S(1)} collective-permute-done((f32[8,16,128]{2,1,0:T(8,128)}, f32[8,16,128]{2,1,0:T(8,128)S(1)}, u32[]{:S(2)}, u32[]{:S(2)}) %collective-permute-start.22) | collective-permute-done | bytes 65568 | tf_op jit(solution)/shard_map/ppermute | solution.py:19
  144.1 2.4 shard_map.58.old
  150.2 3.5 %collective-permute-done.23 = f32[1,1,1,27,16,128]{5,4,3,2,1,0:T(8,128)S(1)} collective-permute-done((f32[1,1,1,27,16,128]{5,4,3,2,1,0:T(8,128)S(1)}, f32[1,1,1,27,16,128]{5,4,3,2,1,0:T(8,128)S(1)}, u32[]{:S(2)}, u32[]{:S(2)}) %collective-permute-start.23) | collective-permute-done | bytes 221216 | tf_op jit(solution)/shard_map/ppermute | solution.py:19
  153.8 1.7 collective-permute-start.24
  155.5 1.5 collective-permute-done.26
  158.0 5.8 %collective-permute-done.24 = f32[2,1,1,27,16,128]{5,4,3,0,2,1:T(8,128)S(1)} collective-permute-done((f32[2,1,1,27,16,128]{5,4,3,0,2,1:T(8,128)S(1)}, f32[2,1,1,27,16,128]{5,4,3,0,2,1:T(8,128)S(1)}, u32[]{:S(2)}, u32[]{:S(2)}) %collective-permute-start.24) | collective-permute-done | bytes 442400 | tf_op jit(solution)/shard_map/ppermute | solution.py:19
  169.0 12.5 %shard_map.59.blurred = f32[32,128,128]{2,1,0:T(8,128)} custom-call(s32[2]{0:T(128)} %pad_add_fusion.1.place, f32[8,32]{1,0:T(8,128)} %get-tuple-element.53.ky, bf16[128,384]{1,0:T(8,128)(2,1)} %pad_maximum_fusion.7.wx, bf16[8,512,128]{2,1,0:T(8,128)(2,1)} %copy-done.2, f32[4,27,16,128]{3,2,1,0:T(8,128)} %bitcast.173, f32[4,27,16,128]{3,2,1,0:T(8,128)} %copy-done.15, ...), custom_call_target="tpu_custom_call" | custom-call | flops 339738624 | bytes 2048 | tf_op jit(solution)/shard_map/pallas_call | solution.py:310
  181.4 14.4 %shard_map.60 = (f32[4,54,16,128]{3,2,1,0:T(8,128)}, f32[4,54,16,128]{3,2,1,0:T(8,128)}) custom-call(s32[2]{0:T(128)} %pad_add_fusion.1.place, f32[8,32]{1,0:T(8,128)} %get-tuple-element.53.ky, bf16[128,384]{1,0:T(8,128)(2,1)} %pad_maximum_fusion.6.wxt, bf16[8,384,256]{2,1,0:T(8,128)(2,1)} %pad_maximum_fusion.kz, f32[32,128,128]{2,1,0:T(8,128)} %shard_map.59.blurred, ...), custom_call_target="tpu_custom_call" | custom-call | flops 339738624 | bytes 7733248 | tf_op jit(solution)/shard_map/pallas_call | solution.py:310
  196.0 3.8 %collective-permute-done.29 = f32[4,54,16,128]{3,2,1,0:T(8,128)S(1)} collective-permute-done((f32[4,54,16,128]{3,2,1,0:T(8,128)}, f32[4,54,16,128]{3,2,1,0:T(8,128)S(1)}, u32[]{:S(2)}, u32[]{:S(2)}) %collective-permute-start.29) | collective-permute-done | bytes 1769504 | tf_op jit(solution)/shard_map/ppermute | solution.py:19
  199.8 1.8 add.192
  201.7 1.6 collective-permute-start.30
  204.4 9.6 %collective-permute-done.30 = f32[2,1,27,16,128]{4,3,2,0,1:T(8,128)S(1)} collective-permute-done((f32[2,1,27,16,128]{4,3,2,0,1:T(8,128)S(1)}, f32[2,1,27,16,128]{4,3,2,0,1:T(8,128)S(1)}, u32[]{:S(2)}, u32[]{:S(2)}) %collective-permute-start.30) | collective-permute-done | bytes 442400 | tf_op jit(solution)/shard_map/ppermute | solution.py:19
  216.8 4.0 %collective-permute-done.31 = f32[1,1,27,16,128]{4,3,2,1,0:T(8,128)S(1)} collective-permute-done((f32[1,1,27,16,128]{4,3,2,1,0:T(8,128)S(1)}, f32[1,1,27,16,128]{4,3,2,1,0:T(8,128)S(1)}, u32[]{:S(2)}, u32[]{:S(2)}) %collective-permute-start.31) | collective-permute-done | bytes 221216 | tf_op jit(solution)/shard_map/ppermute | solution.py:19
  222.5 2.2 shard_map.61
  225.5 1.5 collective-permute-start.35
  227.0 2.1 collective-permute-start.36
  229.1 7.4 %collective-permute-done.36.fc = f32[8,16,128]{2,1,0:T(8,128)S(1)} collective-permute-done((f32[8,16,128]{2,1,0:T(8,128)}, f32[8,16,128]{2,1,0:T(8,128)S(1)}, u32[]{:S(2)}, u32[]{:S(2)}) %collective-permute-start.36) | collective-permute-done | bytes 65568 | tf_op jit(solution)/shard_map/ppermute | solution.py:19
  237.9 2.4 shard_map.62
  243.5 1.5 collective-permute-start.39
  245.0 5.8 %collective-permute-done.37.refs_1_ = f32[32,16,128]{2,1,0:T(8,128)S(1)} collective-permute-done((f32[32,16,128]{2,1,0:T(8,128)S(1)}, f32[32,16,128]{2,1,0:T(8,128)S(1)}, u32[]{:S(2)}, u32[]{:S(2)}) %collective-permute-start.37) | collective-permute-done | bytes 262176 | tf_op jit(solution)/shard_map/ppermute | solution.py:19
  250.8 9.3 %collective-permute-done.38.refs_2_ = f32[32,16,128]{2,1,0:T(8,128)S(1)} collective-permute-done((f32[32,16,128]{2,1,0:T(8,128)S(1)}, f32[32,16,128]{2,1,0:T(8,128)S(1)}, u32[]{:S(2)}, u32[]{:S(2)}) %collective-permute-start.38) | collective-permute-done | bytes 262176 | tf_op jit(solution)/shard_map/ppermute | solution.py:19
  260.1 4.7 %collective-permute-done.39.refs_3_ = f32[32,16,128]{2,1,0:T(8,128)S(1)} collective-permute-done((f32[32,16,128]{2,1,0:T(8,128)S(1)}, f32[32,16,128]{2,1,0:T(8,128)S(1)}, u32[]{:S(2)}, u32[]{:S(2)}) %collective-permute-start.39) | collective-permute-done | bytes 262176 | tf_op jit(solution)/shard_map/ppermute | solution.py:19
  265.5 3.0 %shard_map.63 = f32[16,64,256]{2,1,0:T(8,128)} custom-call(s32[1]{0:T(128)} %bitcast.where, f32[32,16,128]{2,1,0:T(8,128)} %copy-done.14, f32[32,16,128]{2,1,0:T(8,128)} %copy-done.20, f32[32,16,128]{2,1,0:T(8,128)} %copy-done.21, f32[32,16,128]{2,1,0:T(8,128)} %copy-done.22), custom_call_target="tpu_custom_call" | custom-call | flops 2048 | bytes 2097152 | tf_op jit(solution)/shard_map/pallas_call | solution.py:310
  (203 shorter events, 63.5 us)
Async XLA Ops:
  2.4 14.6 %collective-permute-start.2 = (f32[2,128]{1,0:T(2,128)S(1)}, f32[2,128]{1,0:T(2,128)S(1)}, u32[]{:S(2)}, u32[]{:S(2)}) collective-permute-start(f32[2,128]{1,0:T(2,128)S(1)} %select_maximum_fusion), channel_id=1, source_target_pairs={{0,24},{8,16},{16,8},{24,0},{1,25},{9,17},{17,9},{25,1},{2,26},{10... | collective-permute-start | bytes 3080 | tf_op jit(solution)/shard_map/ppermute | solution.py:19
  4.0 13.8 %collective-permute-start.1 = (f32[2,128]{1,0:T(2,128)S(1)}, f32[2,128]{1,0:T(2,128)S(1)}, u32[]{:S(2)}, u32[]{:S(2)}) collective-permute-start(f32[2,128]{1,0:T(2,128)S(1)} %select_maximum_fusion), channel_id=1, source_target_pairs={{0,16},{8,24},{16,0},{24,8},{1,17},{9,25},{17,1},{25,9},{2,18},{10... | collective-permute-start | bytes 3080 | tf_op jit(solution)/shard_map/ppermute | solution.py:19
  5.0 14.9 %collective-permute-start = (f32[2,128]{1,0:T(2,128)S(1)}, f32[2,128]{1,0:T(2,128)S(1)}, u32[]{:S(2)}, u32[]{:S(2)}) collective-permute-start(f32[2,128]{1,0:T(2,128)S(1)} %select_maximum_fusion), channel_id=1, source_target_pairs={{0,8},{8,0},{16,24},{24,16},{1,9},{9,1},{17,25},{25,17},{2,10},{10... | collective-permute-start | bytes 3080 | tf_op jit(solution)/shard_map/ppermute | solution.py:19
  7.1 8.6 %copy-start.10 = (f32[24,16,128]{2,1,0:T(8,128)}, f32[24,16,128]{2,1,0:T(8,128)S(1)}, u32[]{:S(2)}) copy-start(f32[24,16,128]{2,1,0:T(8,128)S(1)} %get-tuple-element.41) | copy-start | bytes 589828
  7.9 24.5 %collective-permute-start.6 = (f32[1,1,1,27,16,128]{5,4,3,2,1,0:T(8,128)}, f32[1,1,1,27,16,128]{5,4,3,2,1,0:T(8,128)}, u32[]{:S(2)}, u32[]{:S(2)}) collective-permute-start(f32[1,1,1,27,16,128]{5,4,3,2,1,0:T(8,128)} %maximum_bitcast_fusion.4), channel_id=1, source_target_pairs={{0,4},{1,5},{2,6},{3,7},{4,0},{5,1},{6,2},{7,3},{8,12},{9,13},{10,... | collective-permute-start | bytes 663560 | tf_op jit(solution)/shard_map/ppermute | solution.py:19
  10.2 23.9 %collective-permute-start.9 = (f32[1,1,1,27,16,128]{5,4,3,2,1,0:T(8,128)}, f32[1,1,1,27,16,128]{5,4,3,2,1,0:T(8,128)}, u32[]{:S(2)}, u32[]{:S(2)}) collective-permute-start(f32[1,1,1,27,16,128]{5,4,3,2,1,0:T(8,128)} %maximum_bitcast_fusion.5), channel_id=1, source_target_pairs={{0,2},{1,3},{2,0},{3,1},{4,6},{5,7},{6,4},{7,5},{8,10},{9,11},{10,... | collective-permute-start | bytes 663560 | tf_op jit(solution)/shard_map/ppermute | solution.py:19
  16.9 44.9 %collective-permute-start.12 = (f32[2,16,32,128]{3,2,1,0:T(8,128)}, f32[2,16,32,128]{3,2,1,0:T(8,128)S(1)}, u32[]{:S(2)}, u32[]{:S(2)}) collective-permute-start(f32[2,16,32,128]{3,2,1,0:T(8,128)} %get-tuple-element.27), channel_id=1, source_target_pairs={{0,8},{8,0},{16,24},{24,16},{1,9},{9,1},{17,25},{25,17},{2,10},{10... | collective-permute-start | bytes 1572872 | tf_op jit(solution)/shard_map/ppermute | solution.py:19
  17.7 44.1 %collective-permute-start.13 = (f32[2,16,32,128]{3,2,1,0:T(8,128)}, f32[2,16,32,128]{3,2,1,0:T(8,128)S(1)}, u32[]{:S(2)}, u32[]{:S(2)}) collective-permute-start(f32[2,16,32,128]{3,2,1,0:T(8,128)} %get-tuple-element.26), channel_id=1, source_target_pairs={{0,16},{8,24},{16,0},{24,8},{1,17},{9,25},{17,1},{25,9},{2,18},{10... | collective-permute-start | bytes 1572872 | tf_op jit(solution)/shard_map/ppermute | solution.py:19
  29.5 9.5 %collective-permute-start.3 = (f32[1,1,1,1,16,128]{4,5,3,2,1,0:T(8,128)}, f32[1,1,1,1,16,128]{4,5,3,2,1,0:T(8,128)}, u32[]{:S(2)}, u32[]{:S(2)}) collective-permute-start(f32[1,1,1,1,16,128]{4,5,3,2,1,0:T(8,128)} %pad_bitcast_fusion), channel_id=1, source_target_pairs={{0,4},{1,5},{2,6},{3,7},{4,0},{5,1},{6,2},{7,3},{8,12},{9,13},{10,... | collective-permute-start | bytes 24584 | tf_op jit(solution)/shard_map/ppermute | solution.py:19
  33.5 10.2 %collective-permute-start.7 = (f32[2,1,1,27,16,128]{5,4,3,0,2,1:T(8,128)S(1)}, f32[2,1,1,27,16,128]{5,4,3,0,2,1:T(8,128)S(1)}, u32[]{:S(2)}, u32[]{:S(2)}) collective-permute-start(f32[2,1,1,27,16,128]{5,4,3,0,2,1:T(8,128)S(1)} %maximum_bitcast_fusion), channel_id=1, source_target_pairs={{0,2},{1,3},{2,0},{3,1},{4,6},{5,7},{6,4},{7,5},{8,10},{9,11},{10,... | collective-permute-start | bytes 1327112 | tf_op jit(solution)/shard_map/ppermute | solution.py:19
  36.0 10.0 %collective-permute-start.10 = (f32[1,1,2,27,16,128]{5,4,3,2,1,0:T(8,128)}, f32[1,1,2,27,16,128]{5,4,3,2,1,0:T(8,128)}, u32[]{:S(2)}, u32[]{:S(2)}) collective-permute-start(f32[1,1,2,27,16,128]{5,4,3,2,1,0:T(8,128)} %maximum_bitcast_fusion.1), channel_id=1, source_target_pairs={{0,4},{1,5},{2,6},{3,7},{4,0},{5,1},{6,2},{7,3},{8,12},{9,13},{10,... | collective-permute-start | bytes 1327112 | tf_op jit(solution)/shard_map/ppermute | solution.py:19
  41.2 8.2 %collective-permute-start.4 = (f32[2,1,1,1,16,128]{5,4,0,3,2,1:T(8,128)S(1)}, f32[2,1,1,1,16,128]{5,4,0,3,2,1:T(8,128)S(1)}, u32[]{:S(2)}, u32[]{:S(2)}) collective-permute-start(f32[2,1,1,1,16,128]{5,4,0,3,2,1:T(8,128)S(1)} %get-tuple-element.50), channel_id=1, source_target_pairs={{0,2},{1,3},{2,0},{3,1},{4,6},{5,7},{6,4},{7,5},{8,10},{9,11},{10,... | collective-permute-start | bytes 49160 | tf_op jit(solution)/shard_map/ppermute | solution.py:19
  43.9 18.0 %collective-permute-start.8 = (f32[4,27,16,128]{3,2,1,0:T(8,128)S(1)}, f32[4,27,16,128]{3,2,1,0:T(8,128)}, u32[]{:S(2)}, u32[]{:S(2)}) collective-permute-start(f32[4,27,16,128]{3,2,1,0:T(8,128)S(1)} %bitcast.162), channel_id=1, source_target_pairs={{0,1},{1,0},{2,3},{3,2},{4,5},{5,4},{6,7},{7,6},{8,9},{9,8},{10,11... | collective-permute-start | bytes 2654216 | tf_op jit(solution)/shard_map/ppermute | solution.py:19
  48.1 13.8 %collective-permute-start.11 = (f32[4,27,16,128]{3,2,1,0:T(8,128)}, f32[4,27,16,128]{3,2,1,0:T(8,128)}, u32[]{:S(2)}, u32[]{:S(2)}) collective-permute-start(f32[4,27,16,128]{3,2,1,0:T(8,128)} %bitcast.28.b0), channel_id=1, source_target_pairs={{0,1},{1,0},{2,3},{3,2},{4,5},{5,4},{6,7},{7,6},{8,9},{9,8},{10,11... | collective-permute-start | bytes 2654216 | tf_op jit(solution)/shard_map/ppermute | solution.py:19
  49.4 2.3 collective-permute-start.5
  50.0 11.9 %copy-start.2 = (bf16[8,512,128]{2,1,0:T(8,128)(2,1)}, bf16[8,512,128]{2,1,0:T(8,128)(2,1)S(1)}, u32[]{:S(2)}) copy-start(bf16[8,512,128]{2,1,0:T(8,128)(2,1)S(1)} %broadcast_dynamic-update-slice_fusion.kz) | copy-start | bytes 3145732
  52.3 25.5 %collective-permute-start.14 = (f32[2,16,32,128]{3,2,1,0:T(8,128)}, f32[2,16,32,128]{3,2,1,0:T(8,128)S(1)}, u32[]{:S(2)}, u32[]{:S(2)}) collective-permute-start(f32[2,16,32,128]{3,2,1,0:T(8,128)} %get-tuple-element.25), channel_id=1, source_target_pairs={{0,24},{8,16},{16,8},{24,0},{1,25},{9,17},{17,9},{25,1},{2,26},{10... | collective-permute-start | bytes 1572872 | tf_op jit(solution)/shard_map/ppermute | solution.py:19
  93.1 3.9 %collective-permute-start.15 = (f32[4,54,16,128]{3,2,1,0:T(8,128)}, f32[4,54,16,128]{3,2,1,0:T(8,128)S(1)}, u32[]{:S(2)}, u32[]{:S(2)}) collective-permute-start(f32[4,54,16,128]{3,2,1,0:T(8,128)} %get-tuple-element.16), channel_id=1, source_target_pairs={{0,1},{1,0},{2,3},{3,2},{4,5},{5,4},{6,7},{7,6},{8,9},{9,8},{10,11... | collective-permute-start | bytes 5308424 | tf_op jit(solution)/shard_map/ppermute | solution.py:19
  98.9 12.3 %collective-permute-start.16 = (f32[2,1,27,16,128]{4,3,2,0,1:T(8,128)S(1)}, f32[2,1,27,16,128]{4,3,2,0,1:T(8,128)S(1)}, u32[]{:S(2)}, u32[]{:S(2)}) collective-permute-start(f32[2,1,27,16,128]{4,3,2,0,1:T(8,128)S(1)} %slice_bitcast_fusion.6), channel_id=1, source_target_pairs={{0,2},{1,3},{2,0},{3,1},{4,6},{5,7},{6,4},{7,5},{8,10},{9,11},{10,... | collective-permute-start | bytes 1327112 | tf_op jit(solution)/shard_map/ppermute | solution.py:19
  100.5 12.4 %collective-permute-start.18 = (f32[1,2,27,16,128]{4,3,2,1,0:T(8,128)S(1)}, f32[1,2,27,16,128]{4,3,2,1,0:T(8,128)S(1)}, u32[]{:S(2)}, u32[]{:S(2)}) collective-permute-start(f32[1,2,27,16,128]{4,3,2,1,0:T(8,128)S(1)} %slice_bitcast_fusion.4), channel_id=1, source_target_pairs={{0,4},{1,5},{2,6},{3,7},{4,0},{5,1},{6,2},{7,3},{8,12},{9,13},{10,... | collective-permute-start | bytes 1327112 | tf_op jit(solution)/shard_map/ppermute | solution.py:19
  111.3 25.7 %copy-start.11 = (f32[24,16,128]{2,1,0:T(8,128)S(1)}, f32[24,16,128]{2,1,0:T(8,128)}, u32[]{:S(2)}) copy-start(f32[24,16,128]{2,1,0:T(8,128)} %copy-done.10) | copy-start | bytes 589828
  111.3 25.7 %copy-start.13 = (f32[24,16,128]{2,1,0:T(8,128)S(1)}, f32[24,16,128]{2,1,0:T(8,128)}, u32[]{:S(2)}) copy-start(f32[24,16,128]{2,1,0:T(8,128)} %copy-done.12) | copy-start | bytes 589828
  111.4 32.0 %copy-start.31 = (f32[16]{0:T(128)S(1)}, f32[16]{0:T(128)}, u32[]{:S(2)}) copy-start(f32[16]{0:T(128)} %get-tuple-element.54) | copy-start | bytes 196
  111.4 6.7 %collective-permute-start.17 = (f32[1,1,27,16,128]{4,3,2,1,0:T(8,128)S(1)}, f32[1,1,27,16,128]{4,3,2,1,0:T(8,128)S(1)}, u32[]{:S(2)}, u32[]{:S(2)}) collective-permute-start(f32[1,1,27,16,128]{4,3,2,1,0:T(8,128)S(1)} %slice_bitcast_fusion.16), channel_id=1, source_target_pairs={{0,4},{1,5},{2,6},{3,7},{4,0},{5,1},{6,2},{7,3},{8,12},{9,13},{10,... | collective-permute-start | bytes 663560 | tf_op jit(solution)/shard_map/ppermute | solution.py:19
  113.1 6.4 %collective-permute-start.19 = (f32[1,1,27,16,128]{4,3,2,1,0:T(8,128)S(1)}, f32[1,1,27,16,128]{4,3,2,1,0:T(8,128)S(1)}, u32[]{:S(2)}, u32[]{:S(2)}) collective-permute-start(f32[1,1,27,16,128]{4,3,2,1,0:T(8,128)S(1)} %slice_bitcast_fusion.14), channel_id=1, source_target_pairs={{0,2},{1,3},{2,0},{3,1},{4,6},{5,7},{6,4},{7,5},{8,10},{9,11},{10,... | collective-permute-start | bytes 663560 | tf_op jit(solution)/shard_map/ppermute | solution.py:19
  132.6 10.7 %collective-permute-start.20 = (f32[36,16,128]{2,1,0:T(8,128)}, f32[36,16,128]{2,1,0:T(8,128)S(1)}, u32[]{:S(2)}, u32[]{:S(2)}) collective-permute-start(f32[36,16,128]{2,1,0:T(8,128)} %get-tuple-element.17), channel_id=1, source_target_pairs={{0,8},{8,0},{16,24},{24,16},{1,9},{9,1},{17,25},{25,17},{2,10},{10... | collective-permute-start | bytes 884744 | tf_op jit(solution)/shard_map/ppermute | solution.py:19
  132.6 10.7 %collective-permute-start.21 = (f32[12,16,128]{2,1,0:T(8,128)}, f32[12,16,128]{2,1,0:T(8,128)S(1)}, u32[]{:S(2)}, u32[]{:S(2)}) collective-permute-start(f32[12,16,128]{2,1,0:T(8,128)} %get-tuple-element.18), channel_id=1, source_target_pairs={{0,24},{8,16},{16,8},{24,0},{1,25},{9,17},{17,9},{25,1},{2,26},{10... | collective-permute-start | bytes 294920 | tf_op jit(solution)/shard_map/ppermute | solution.py:19
  134.2 9.1 %collective-permute-start.22 = (f32[8,16,128]{2,1,0:T(8,128)}, f32[8,16,128]{2,1,0:T(8,128)S(1)}, u32[]{:S(2)}, u32[]{:S(2)}) collective-permute-start(f32[8,16,128]{2,1,0:T(8,128)} %get-tuple-element.19), channel_id=1, source_target_pairs={{0,16},{8,24},{16,0},{24,8},{1,17},{9,25},{17,1},{25,9},{2,18},{10... | collective-permute-start | bytes 196616 | tf_op jit(solution)/shard_map/ppermute | solution.py:19
  147.5 6.2 %collective-permute-start.23 = (f32[1,1,1,27,16,128]{5,4,3,2,1,0:T(8,128)S(1)}, f32[1,1,1,27,16,128]{5,4,3,2,1,0:T(8,128)S(1)}, u32[]{:S(2)}, u32[]{:S(2)}) collective-permute-start(f32[1,1,1,27,16,128]{5,4,3,2,1,0:T(8,128)S(1)} %get-tuple-element.40), channel_id=1, source_target_pairs={{0,4},{1,5},{2,6},{3,7},{4,0},{5,1},{6,2},{7,3},{8,12},{9,13},{10,... | collective-permute-start | bytes 663560 | tf_op jit(solution)/shard_map/ppermute | solution.py:19
  148.7 8.3 %collective-permute-start.26 = (f32[1,1,1,27,16,128]{5,4,3,2,1,0:T(8,128)S(1)}, f32[1,1,1,27,16,128]{5,4,3,2,1,0:T(8,128)S(1)}, u32[]{:S(2)}, u32[]{:S(2)}) collective-permute-start(f32[1,1,1,27,16,128]{5,4,3,2,1,0:T(8,128)S(1)} %get-tuple-element.39), channel_id=1, source_target_pairs={{0,2},{1,3},{2,0},{3,1},{4,6},{5,7},{6,4},{7,5},{8,10},{9,11},{10,... | collective-permute-start | bytes 663560 | tf_op jit(solution)/shard_map/ppermute | solution.py:19
  153.8 10.1 %collective-permute-start.24 = (f32[2,1,1,27,16,128]{5,4,3,0,2,1:T(8,128)S(1)}, f32[2,1,1,27,16,128]{5,4,3,0,2,1:T(8,128)S(1)}, u32[]{:S(2)}, u32[]{:S(2)}) collective-permute-start(f32[2,1,1,27,16,128]{5,4,3,0,2,1:T(8,128)S(1)} %maximum_bitcast_fusion.2), channel_id=1, source_target_pairs={{0,2},{1,3},{2,0},{3,1},{4,6},{5,7},{6,4},{7,5},{8,10},{9,11},{10,... | collective-permute-start | bytes 1327112 | tf_op jit(solution)/shard_map/ppermute | solution.py:19
  157.1 8.4 %collective-permute-start.27 = (f32[1,1,2,27,16,128]{5,4,3,2,1,0:T(8,128)S(1)}, f32[1,1,2,27,16,128]{5,4,3,2,1,0:T(8,128)S(1)}, u32[]{:S(2)}, u32[]{:S(2)}) collective-permute-start(f32[1,1,2,27,16,128]{5,4,3,2,1,0:T(8,128)S(1)} %maximum_bitcast_fusion.3), channel_id=1, source_target_pairs={{0,4},{1,5},{2,6},{3,7},{4,0},{5,1},{6,2},{7,3},{8,12},{9,13},{10,... | collective-permute-start | bytes 1327112 | tf_op jit(solution)/shard_map/ppermute | solution.py:19
  164.0 2.5 collective-permute-start.25
  165.5 2.5 collective-permute-start.28
  195.9 3.9 %collective-permute-start.29 = (f32[4,54,16,128]{3,2,1,0:T(8,128)}, f32[4,54,16,128]{3,2,1,0:T(8,128)S(1)}, u32[]{:S(2)}, u32[]{:S(2)}) collective-permute-start(f32[4,54,16,128]{3,2,1,0:T(8,128)} %get-tuple-element.21), channel_id=1, source_target_pairs={{0,1},{1,0},{2,3},{3,2},{4,5},{5,4},{6,7},{7,6},{8,9},{9,8},{10,11... | collective-permute-start | bytes 5308424 | tf_op jit(solution)/shard_map/ppermute | solution.py:19
  201.7 12.3 %collective-permute-start.30 = (f32[2,1,27,16,128]{4,3,2,0,1:T(8,128)S(1)}, f32[2,1,27,16,128]{4,3,2,0,1:T(8,128)S(1)}, u32[]{:S(2)}, u32[]{:S(2)}) collective-permute-start(f32[2,1,27,16,128]{4,3,2,0,1:T(8,128)S(1)} %slice_bitcast_fusion.2), channel_id=1, source_target_pairs={{0,2},{1,3},{2,0},{3,1},{4,6},{5,7},{6,4},{7,5},{8,10},{9,11},{10,... | collective-permute-start | bytes 1327112 | tf_op jit(solution)/shard_map/ppermute | solution.py:19
  203.3 12.0 %collective-permute-start.32 = (f32[1,2,27,16,128]{4,3,2,1,0:T(8,128)S(1)}, f32[1,2,27,16,128]{4,3,2,1,0:T(8,128)S(1)}, u32[]{:S(2)}, u32[]{:S(2)}) collective-permute-start(f32[1,2,27,16,128]{4,3,2,1,0:T(8,128)S(1)} %slice_bitcast_fusion), channel_id=1, source_target_pairs={{0,4},{1,5},{2,6},{3,7},{4,0},{5,1},{6,2},{7,3},{8,12},{9,13},{10,... | collective-permute-start | bytes 1327112 | tf_op jit(solution)/shard_map/ppermute | solution.py:19
  214.1 6.7 %collective-permute-start.31 = (f32[1,1,27,16,128]{4,3,2,1,0:T(8,128)S(1)}, f32[1,1,27,16,128]{4,3,2,1,0:T(8,128)S(1)}, u32[]{:S(2)}, u32[]{:S(2)}) collective-permute-start(f32[1,1,27,16,128]{4,3,2,1,0:T(8,128)S(1)} %slice_bitcast_fusion.10), channel_id=1, source_target_pairs={{0,4},{1,5},{2,6},{3,7},{4,0},{5,1},{6,2},{7,3},{8,12},{9,13},{10,... | collective-permute-start | bytes 663560 | tf_op jit(solution)/shard_map/ppermute | solution.py:19
  215.4 6.4 %collective-permute-start.33 = (f32[1,1,27,16,128]{4,3,2,1,0:T(8,128)S(1)}, f32[1,1,27,16,128]{4,3,2,1,0:T(8,128)S(1)}, u32[]{:S(2)}, u32[]{:S(2)}) collective-permute-start(f32[1,1,27,16,128]{4,3,2,1,0:T(8,128)S(1)} %slice_bitcast_fusion.8), channel_id=1, source_target_pairs={{0,2},{1,3},{2,0},{3,1},{4,6},{5,7},{6,4},{7,5},{8,10},{9,11},{10,... | collective-permute-start | bytes 663560 | tf_op jit(solution)/shard_map/ppermute | solution.py:19
  224.7 11.8 %collective-permute-start.34 = (f32[36,16,128]{2,1,0:T(8,128)}, f32[36,16,128]{2,1,0:T(8,128)S(1)}, u32[]{:S(2)}, u32[]{:S(2)}) collective-permute-start(f32[36,16,128]{2,1,0:T(8,128)} %get-tuple-element.22), channel_id=1, source_target_pairs={{0,8},{8,0},{16,24},{24,16},{1,9},{9,1},{17,25},{25,17},{2,10},{10... | collective-permute-start | bytes 884744 | tf_op jit(solution)/shard_map/ppermute | solution.py:19
  225.5 11.0 %collective-permute-start.35 = (f32[12,16,128]{2,1,0:T(8,128)}, f32[12,16,128]{2,1,0:T(8,128)S(1)}, u32[]{:S(2)}, u32[]{:S(2)}) collective-permute-start(f32[12,16,128]{2,1,0:T(8,128)} %get-tuple-element.23), channel_id=1, source_target_pairs={{0,24},{8,16},{16,8},{24,0},{1,25},{9,17},{17,9},{25,1},{2,26},{10... | collective-permute-start | bytes 294920 | tf_op jit(solution)/shard_map/ppermute | solution.py:19
  227.0 9.5 %collective-permute-start.36 = (f32[8,16,128]{2,1,0:T(8,128)}, f32[8,16,128]{2,1,0:T(8,128)S(1)}, u32[]{:S(2)}, u32[]{:S(2)}) collective-permute-start(f32[8,16,128]{2,1,0:T(8,128)} %get-tuple-element.24), channel_id=1, source_target_pairs={{0,16},{8,24},{16,0},{24,8},{1,17},{9,25},{17,1},{25,9},{2,18},{10... | collective-permute-start | bytes 196616 | tf_op jit(solution)/shard_map/ppermute | solution.py:19
  237.9 30.6 %copy-start.1 = (f32[16,64,256]{2,1,0:T(8,128)S(1)}, f32[16,64,256]{2,1,0:T(8,128)}, u32[]{:S(2)}) copy-start(f32[16,64,256]{2,1,0:T(8,128)} %param.5) | copy-start | bytes 3145732
  241.5 23.3 %copy-start.14 = (f32[32,16,128]{2,1,0:T(8,128)}, f32[32,16,128]{2,1,0:T(8,128)S(1)}, u32[]{:S(2)}) copy-start(f32[32,16,128]{2,1,0:T(8,128)S(1)} %fusion.10.refs_0_) | copy-start | bytes 786436
  241.5 9.3 %collective-permute-start.37 = (f32[32,16,128]{2,1,0:T(8,128)S(1)}, f32[32,16,128]{2,1,0:T(8,128)S(1)}, u32[]{:S(2)}, u32[]{:S(2)}) collective-permute-start(f32[32,16,128]{2,1,0:T(8,128)S(1)} %fusion.10.refs_0_), channel_id=1, source_target_pairs={{0,8},{8,0},{16,24},{24,16},{1,9},{9,1},{17,25},{25,17},{2,10},{10... | collective-permute-start | bytes 786440 | tf_op jit(solution)/shard_map/ppermute | solution.py:19
  242.3 17.8 %collective-permute-start.38 = (f32[32,16,128]{2,1,0:T(8,128)S(1)}, f32[32,16,128]{2,1,0:T(8,128)S(1)}, u32[]{:S(2)}, u32[]{:S(2)}) collective-permute-start(f32[32,16,128]{2,1,0:T(8,128)S(1)} %fusion.10.refs_0_), channel_id=1, source_target_pairs={{0,16},{8,24},{16,0},{24,8},{1,17},{9,25},{17,1},{25,9},{2,18},{10... | collective-permute-start | bytes 786440 | tf_op jit(solution)/shard_map/ppermute | solution.py:19
  243.5 21.3 %collective-permute-start.39 = (f32[32,16,128]{2,1,0:T(8,128)S(1)}, f32[32,16,128]{2,1,0:T(8,128)S(1)}, u32[]{:S(2)}, u32[]{:S(2)}) collective-permute-start(f32[32,16,128]{2,1,0:T(8,128)S(1)} %fusion.10.refs_0_), channel_id=1, source_target_pairs={{0,24},{8,16},{16,8},{24,0},{1,25},{9,17},{17,9},{25,1},{2,26},{10... | collective-permute-start | bytes 786440 | tf_op jit(solution)/shard_map/ppermute | solution.py:19
  250.8 14.0 %copy-start.20 = (f32[32,16,128]{2,1,0:T(8,128)}, f32[32,16,128]{2,1,0:T(8,128)S(1)}, u32[]{:S(2)}) copy-start(f32[32,16,128]{2,1,0:T(8,128)S(1)} %collective-permute-done.37.refs_1_) | copy-start | bytes 786436
  (24 other events, 58.4 us)

commit v5 on v4

--- a/solution.py
+++ b/solution.py
@@ -17,12 +17,6 @@
 def swap(value, axis, mask):
     count = lax.axis_size(axis)
     return lax.ppermute(value, axis, [(i, i ^ mask) for i in range(count)])
-
-
-def pick(kern, index):
-    hit = index[..., None] == jnp.arange(kern.shape[-1])
-    lead = kern.reshape(kern.shape[:1] + (1,) * (index.ndim - 1) + kern.shape[1:])
-    return jnp.sum(jnp.where(hit, lead, 0.0), axis=-1)
 
 
 def orders(bits):
@@ -82,6 +76,52 @@
     return lax.broadcasted_iota(jnp.int32, shape, len(shape) - 1)
 
 
+def bands_kernel(rad, place, slab, kern, wx, bxt, kz, kzt):
+    zh, j = place[1], place[2]
+    nx, nvi = bxt.shape
+    nviews, _, hz = kz.shape
+    width = nvi // nviews
+    taps = 2 * rad
+
+    def taken(v, axis, index):
+        total = jnp.zeros(index.shape, F32)
+        for t in range(taps):
+            total = jnp.where(index == t, kern[v, axis * taps + t], total)
+        return total
+
+    shape = (width, nx)
+    lane, row = lane_of(shape), lax.broadcasted_iota(jnp.int32, shape, 0)
+    block = lane // width
+    blocks = nx // width // 2
+    block = jnp.bitwise_xor(2 * (block % blocks) + block // blocks, jnp.full(shape, j, jnp.int32))
+    cell = block * width + lane % width - row + rad
+    for v in range(nviews):
+        value = taken(v, 0, cell - slab[v] * width)
+        high, low = split(value)
+        at = pl.ds(v * width, width)
+        wx[at, :nx] = high
+        wx[at, nx : 2 * nx] = high
+        wx[at, 2 * nx :] = low
+        bxt[:, v * width : (v + 1) * width] = value.T
+    shape = (hz, hz)
+    middle = lax.broadcasted_iota(jnp.int32, shape, 0) - lane_of(shape) + rad
+    shape = (rad, hz)
+    outer = lax.broadcasted_iota(jnp.int32, shape, 0) - lane_of(shape) + (hz + rad) * (1 - zh)
+
+    def one(v, carry):
+        main, rim = taken(v, 2, middle), taken(v, 2, outer)
+        high, low = split(main)
+        rim_high, rim_low = split(rim)
+        rest = jnp.zeros((hz - 3 * rad, hz), BF16)
+        kz[v] = jnp.concatenate([high, high, low, rim_high, rim_high, rim_low, rest], axis=0)
+        rim = jnp.concatenate([rim, jnp.zeros((hz - rad, hz), F32)], axis=0)
+        high, low = split(jnp.concatenate([main.T, rim.T], axis=1))
+        kzt[v] = jnp.concatenate([high, high, low], axis=0)
+        return carry
+
+    lax.fori_loop(0, nviews, one, 0)
+
+
 def ahead_kernel(rad, place, ky, wx, kz, a0, a1, b0, b1, *refs):
     blurred, u, uh, za, zb = refs[-5:]
     yh = place[0]
@@ -150,8 +190,8 @@
     lax.fori_loop(0, nviews // 2, views, 0)
 
 
-def back_kernel(rad, npieces, place, ky, wxt, kz, blurred, *refs):
-    pieces, (kept, sent, r, ya, yb, gm, gh) = refs[:npieces], refs[npieces:]
+def back_kernel(rad, npieces, place, ky, bxt, note0, note1, kz, blurred, *refs):
+    pieces, (kept, sent, r, ya, yb, gm, gh, wxt) = refs[:npieces], refs[npieces:]
     yh = place[0]
     hy, nvi, hz = blurred.shape
     wy = gm.shape[0]
@@ -159,6 +199,11 @@
     nviews = nvi // width
     half, group = wy // 2, hz // rad
     rims = half // group
+    cover = jnp.concatenate([ref[k, 0] for ref in (note0, note1) for k in range(ref.shape[0])], axis=0)
+    shape = (hz, nvi)
+    spread = jnp.where(lane_of(shape) // width == lax.broadcasted_iota(jnp.int32, shape, 0), 1.0, 0.0)
+    high, low = split(bxt[...] * mul(cover.astype(BF16), spread.astype(BF16)))
+    wxt[...] = jnp.concatenate([high, high, low], axis=1)
     for p, piece in enumerate(pieces):
         for k in range(local):
             first = (p * local + k) * width
@@ -322,7 +367,7 @@
     nview, nspace = lax.axis_size("view"), lax.axis_size("space")
     g, j = lax.axis_index("view"), lax.axis_index("space")
     zh, yh = g >> 1, (g ^ (g >> 1)) & 1
-    place_yz = jnp.stack([yh, zh]).astype(jnp.int32)
+    place_yz = jnp.stack([yh, zh, j]).astype(jnp.int32)
     local, width, ny, nz = data.shape
     ntaps = taps.shape[-1]
     rad = ntaps // 2
@@ -367,37 +412,22 @@
     parts = [main[:half], rim[:rims], main[half:], rim[rims:]]
     estimate = jnp.concatenate(parts, axis=0)
     wide = gather([jnp.concatenate(parts[:2], axis=0), jnp.concatenate(parts[2:], axis=0)])
-    cover = jnp.concatenate(gather([note]), axis=1)[..., :nviews]
-    cover = cover.transpose(3, 1, 0, 2).reshape(nviews, 1, nspace * width)
-
-    slab = (j - turn) % nspace
-    spot = slab[:, None] * width + jnp.arange(width)
-    order = jnp.arange(nspace).reshape(nspace // 2, 2).T.reshape(-1)
-    planes = ((j ^ order)[:, None] * width + jnp.arange(width)).reshape(-1)
-    band_x = pick(kern[:, 0], planes - spot[:, :, None] + rad)
-    band_xt = (band_x * cover).reshape(nvi, -1).T
-    band_x = band_x.reshape(nvi, -1)
-
-    def halves(value):
-        high = lax.reduce_precision(value, 8, 7)
-        return high.astype(BF16), (value - high).astype(BF16)
-
-    def triple(value):
-        high, low = halves(value)
-        return jnp.concatenate([high, high, low], axis=1)
-
-    wx, wxt = triple(band_x), triple(band_xt)
-    cells = jnp.concatenate([jnp.arange(hz) + hz * zh, jnp.arange(hz) + jnp.where(zh == 0, hz, hz - rad)])
-    real = jnp.arange(2 * hz) < hz + rad
-    goal = jnp.arange(hz) + hz * zh
-    index = jnp.where(real[:, None], cells[:, None] - goal + rad, -1)
-    band_z = pick(kern[:, 2], index[None])
-    high, low = halves(band_z)
-    kz = [high[:, :hz], high[:, :hz], low[:, :hz]]
-    kz += [high[:, hz : hz + rad], high[:, hz : hz + rad], low[:, hz : hz + rad]]
-    kz = jnp.concatenate(kz + [jnp.zeros((nviews, hz - 3 * rad, hz), BF16)], axis=1)
-    high, low = halves(band_z.transpose(0, 2, 1))
-    kzt = jnp.concatenate([high, high, low], axis=1)
+    notes = gather([note])
+
+    nx = nspace * width
+    wx, bxt, kz, kzt = pl.pallas_call(
+        functools.partial(bands_kernel, rad),
+        out_shape=[
+            jax.ShapeDtypeStruct((nvi, 3 * nx), BF16),
+            jax.ShapeDtypeStruct((nx, nvi), F32),
+            jax.ShapeDtypeStruct((nviews, 4 * hz, hz), BF16),
+            jax.ShapeDtypeStruct((nviews, 3 * hz, 2 * hz), BF16),
+        ],
+        in_specs=[SMEM] * 3,
+        out_specs=[VMEM] * 4,
+        compiler_params=PARAMS,
+        cost_estimate=pl.CostEstimate(flops=nviews * hz * hz * 32, bytes_accessed=nviews * hz * hz * 16, transcendentals=0),
+    )(place_yz, (j - turn) % nspace, kern.reshape(nviews, -1))
     ky = kern[:, 1]
 
     plane = width * hz
@@ -418,10 +448,10 @@
         return call(
             functools.partial(back_kernel, rad, nview),
             [(nspace // 2, 2 * rows, width, hz)] * 2,
-            [(hy, nvi, hz), (hy + 2 * rad, width, hz), (hy + 2 * rad, width, hz), (wy, nvi, hz), (2 * rims, nvi, hz)],
+            [(hy, nvi, hz), (hy + 2 * rad, width, hz), (hy + 2 * rad, width, hz), (wy, nvi, hz), (2 * rims, nvi, hz), pltpu.VMEM((nx, 3 * nvi), BF16)],
             2,
             (mxu, 4 * plane * (nspace * 2 * rows + 2 * hy * nviews)),
-            place_yz, ky, wxt, kzt, blurred, *pieces,
+            place_yz, ky, bxt, *notes, kzt, blurred, *pieces,
         )
 
     over = hy // group

time: 273 us -> 249 us (0.912); the launches traced: 269 us -> 249 us
  waiting for transfers between devices: 87.7 us -> 105 us
  other arithmetic: 33.9 us -> 17.7 us
  local copies, waits for them, and re-layouts: 25.1 us -> 14.8 us
  starting transfers between devices: 44.9 us -> 38.9 us
  Pallas kernels: 76.2 us -> 71.6 us
    ppermute x40, waiting for transfers between devices: 87.7 us -> 105 us  [swap(): return lax.ppermute(value, axis, [(i, i ^ mask) for i in range(count)])]
    pallas_call x9, Pallas kernels: 76.2 us -> 66.3 us  [call(): pl.pallas_call(kernel, out_shape=[jax.ShapeDtypeStruct(shape, F32) for sh...]
    reduce_sum x2 -> x0, other arithmetic: 7.04 us -> none  [pick(): return jnp.sum(jnp.where(hit, lead, 0.0), axis=-1)]
    ppermute x40, starting transfers between devices: 44.9 us -> 38.9 us  [swap(): return lax.ppermute(value, axis, [(i, i ^ mask) for i in range(count)])]
    pallas_call x0 -> x1, Pallas kernels: none -> 5.21 us  [body(): pl.pallas_call(functools.partial(bands_kernel, rad), out_shape=[jax.Shape...]
    concatenate x5 -> x0, other arithmetic: 4.84 us -> none  [the longest x2 2.14 us: triple(): return jnp.concatenate([high, high, low], axis=1)]
    mul x4 -> x0, local copies, waits for them, and re-layouts: 4.44 us -> none  [the longest x3 4.35 us: body(): band_xt = (band_x * cover).reshape(nvi, -1).T]
    slice x4, local copies, waits for them, and re-layouts: 0.27 us -> 3.1 us  [body(): parts = [main[:half], rim[:rims], main[half:], rim[rims:]]]
  transfers between devices with their start and end apart: 40 -> 40, of which waited for: 23 -> 22; matrix products, arithmetic and copies ran while one was open for 16% -> 7% of each run, Pallas kernels for 5% -> 7%
where the time goes in v5:
time: 249 us
  waiting for transfers between devices  105 us (42%)
  Pallas kernels  71.6 us (29%)
  starting transfers between devices  38.9 us (16%)
  other arithmetic  17.7 us (7%)
  local copies, waits for them, and re-layouts  14.8 us (6%)
    ppermute x40, waiting for transfers between devices, swap(): return lax.ppermute(value, axis, [(i, i ^ mask) for i in range(count)])  105 us
    pallas_call x9, Pallas kernels, call(): pl.pallas_call(kernel, out_shape=[jax.ShapeDtypeStruct(shape, F32) for sh...  66.3 us
    ppermute x40, starting transfers between devices, swap(): return lax.ppermute(value, axis, [(i, i ^ mask) for i in range(count)])  38.9 us
    unnamed x53, local copies, waits for them, and re-layouts  5.91 us
    pallas_call x1, Pallas kernels, body(): pl.pallas_call(functools.partial(bands_kernel, rad), out_shape=[jax.Shape...  5.21 us
  transfers between devices with their start and end apart: 40, of which 22 were waited for; matrix products, arithmetic and copies ran while one was open for 7% of the time, Pallas kernels for 7%

profile of v5, /device:TPU:8, one launch (start us, length us, event | category | flops | bytes accessed | tf_op | source)
XLA Modules:
  0.0 248.6 jit_solution(12487577907271857389)
XLA Ops:
  2.4 1.6 collective-permute-start.2
  5.0 1.4 collective-permute-start
  9.5 1.5 collective-permute-start.6
  11.0 1.7 slice.111
  12.7 1.4 maximum_bitcast_fusion.5
  14.1 1.5 collective-permute-start.9
  15.6 1.4 constant_dynamic-slice_fusion
  18.4 2.2 collective-permute-start.13
  24.4 1.6 collective-permute-start.3
  26.0 6.4 %collective-permute-done.7 = f32[2,1,1,27,16,128]{5,4,3,0,2,1:T(8,128)S(1)} collective-permute-done((f32[2,1,1,27,16,128]{5,4,3,0,2,1:T(8,128)S(1)}, f32[2,1,1,27,16,128]{5,4,3,0,2,1:T(8,128)S(1)}, u32[]{:S(2)}, u32[]{:S(2)}) %collective-permute-start.7) | collective-permute-done | bytes 442400 | tf_op jit(solution)/shard_map/ppermute | solution.py:19
  32.6 1.9 collective-permute-done.10
  36.2 1.5 collective-permute-start.4
  38.1 1.9 collective-permute-done.4
  41.9 5.2 %shard_map.55 = (bf16[128,384]{1,0:T(8,128)(2,1)}, f32[128,128]{1,0:T(8,128)}, bf16[8,512,128]{2,1,0:T(8,128)(2,1)}, bf16[8,384,256]{2,1,0:T(8,128)(2,1)}) custom-call(s32[3]{0:T(128)} %pad_add_fusion.place, s32[8]{0:T(128)} %and_select_fusion.slab, f32[8,96]{1,0:T(8,128)} %slice_divide_fusion.kern), custom_call_target="tpu_custom_call" | custom-call | flops 4194304 | bytes 2097152 | tf_op jit(solution)/shard_map/pallas_call | solution.py:418
  47.1 7.3 %collective-permute-done.13.refs_1_.refs_2_ = f32[2,16,32,128]{3,2,1,0:T(8,128)S(1)} collective-permute-done((f32[2,16,32,128]{3,2,1,0:T(8,128)}, f32[2,16,32,128]{3,2,1,0:T(8,128)S(1)}, u32[]{:S(2)}, u32[]{:S(2)}) %collective-permute-start.13) | collective-permute-done | bytes 524320 | tf_op jit(solution)/shard_map/ppermute | solution.py:19
  55.2 12.5 %shard_map.56.blurred = f32[32,128,128]{2,1,0:T(8,128)} custom-call(s32[3]{0:T(128)} %pad_add_fusion.place, f32[8,32]{1,0:T(8,128)} %fusion.19.ky, bf16[128,384]{1,0:T(8,128)(2,1)} %get-tuple-element.21.wx, bf16[8,512,128]{2,1,0:T(8,128)(2,1)} %get-tuple-element.22.kz, f32[4,27,16,128]{3,2,1,0:T(8,128)} %bitcast.147, ...), custom_call_target="tpu_custom_call" | custom-call | bytes 2048 | tf_op jit(solution)/shard_map/pallas_call | solution.py:355
  68.5 14.5 %shard_map.57 = (f32[4,54,16,128]{3,2,1,0:T(8,128)}, f32[4,54,16,128]{3,2,1,0:T(8,128)}) custom-call(s32[3]{0:T(128)} %pad_add_fusion.place, f32[8,32]{1,0:T(8,128)} %fusion.19.ky, f32[128,128]{1,0:T(8,128)} %get-tuple-element.19.bxt, f32[4,1,16,128]{3,2,1,0:T(8,128)} %bitcast.162, f32[4,1,16,128]{3,2,1,0:T(8,128)} %copy-done.20, ...), custom_call_target="tpu_custom_call" | custom-call | flops 339738624 | bytes 7733248 | tf_op jit(solution)/shard_map/pallas_call | solution.py:355
  82.9 3.9 %collective-permute-done.15 = f32[4,54,16,128]{3,2,1,0:T(8,128)S(1)} collective-permute-done((f32[4,54,16,128]{3,2,1,0:T(8,128)}, f32[4,54,16,128]{3,2,1,0:T(8,128)S(1)}, u32[]{:S(2)}, u32[]{:S(2)}) %collective-permute-start.15) | collective-permute-done | bytes 1769504 | tf_op jit(solution)/shard_map/ppermute | solution.py:19
  86.8 1.8 add.88
  89.5 11.6 %collective-permute-done.16 = f32[2,1,27,16,128]{4,3,2,0,1:T(8,128)S(1)} collective-permute-done((f32[2,1,27,16,128]{4,3,2,0,1:T(8,128)S(1)}, f32[2,1,27,16,128]{4,3,2,0,1:T(8,128)S(1)}, u32[]{:S(2)}, u32[]{:S(2)}) %collective-permute-start.16) | collective-permute-done | bytes 442400 | tf_op jit(solution)/shard_map/ppermute | solution.py:19
  103.1 4.9 %collective-permute-done.17 = f32[1,1,27,16,128]{4,3,2,1,0:T(8,128)S(1)} collective-permute-done((f32[1,1,27,16,128]{4,3,2,1,0:T(8,128)S(1)}, f32[1,1,27,16,128]{4,3,2,1,0:T(8,128)S(1)}, u32[]{:S(2)}, u32[]{:S(2)}) %collective-permute-start.17) | collective-permute-done | bytes 221216 | tf_op jit(solution)/shard_map/ppermute | solution.py:19
  109.4 2.5 shard_map.58
  111.9 3.8 %collective-permute-start.21 = (f32[12,16,128]{2,1,0:T(8,128)}, f32[12,16,128]{2,1,0:T(8,128)S(1)}, u32[]{:S(2)}, u32[]{:S(2)}) collective-permute-start(f32[12,16,128]{2,1,0:T(8,128)} %get-tuple-element.26), channel_id=1, source_target_pairs={{0,24},{8,16},{16,8},{24,0},{1,25},{9,17},{17,9},{25,1},{2,26},{10... | collective-permute-start | bytes 294920 | tf_op jit(solution)/shard_map/ppermute | solution.py:19
  117.1 7.3 %collective-permute-done.22.fc = f32[8,16,128]{2,1,0:T(8,128)S(1)} collective-permute-done((f32[8,16,128]{2,1,0:T(8,128)}, f32[8,16,128]{2,1,0:T(8,128)S(1)}, u32[]{:S(2)}, u32[]{:S(2)}) %collective-permute-start.22) | collective-permute-done | bytes 65568 | tf_op jit(solution)/shard_map/ppermute | solution.py:19
  125.2 2.4 shard_map.59.old
  130.6 4.1 %collective-permute-done.23 = f32[1,1,1,27,16,128]{5,4,3,2,1,0:T(8,128)S(1)} collective-permute-done((f32[1,1,1,27,16,128]{5,4,3,2,1,0:T(8,128)S(1)}, f32[1,1,1,27,16,128]{5,4,3,2,1,0:T(8,128)S(1)}, u32[]{:S(2)}, u32[]{:S(2)}) %collective-permute-start.23) | collective-permute-done | bytes 221216 | tf_op jit(solution)/shard_map/ppermute | solution.py:19
  135.8 1.8 collective-permute-done.26
  137.6 1.6 collective-permute-start.27
  139.2 5.9 %collective-permute-done.24 = f32[2,1,1,27,16,128]{5,4,3,0,2,1:T(8,128)S(1)} collective-permute-done((f32[2,1,1,27,16,128]{5,4,3,0,2,1:T(8,128)S(1)}, f32[2,1,1,27,16,128]{5,4,3,0,2,1:T(8,128)S(1)}, u32[]{:S(2)}, u32[]{:S(2)}) %collective-permute-start.24) | collective-permute-done | bytes 442400 | tf_op jit(solution)/shard_map/ppermute | solution.py:19
  146.1 1.6 collective-permute-done.25.a1
  147.7 1.3 collective-permute-done.28.b1
  149.9 12.5 %shard_map.60.blurred = f32[32,128,128]{2,1,0:T(8,128)} custom-call(s32[3]{0:T(128)} %pad_add_fusion.place, f32[8,32]{1,0:T(8,128)} %fusion.19.ky, bf16[128,384]{1,0:T(8,128)(2,1)} %get-tuple-element.21.wx, bf16[8,512,128]{2,1,0:T(8,128)(2,1)} %get-tuple-element.22.kz, f32[4,27,16,128]{3,2,1,0:T(8,128)} %bitcast.157, f32[4,27,16,128]{3,2,1,0:T(8,128)} %copy-done.9, ...), custom_call_target="tpu_custom_call" | custom-call | flops 339738624 | bytes 2048 | tf_op jit(solution)/shard_map/pallas_call | solution.py:355
  162.4 14.5 %shard_map.61 = (f32[4,54,16,128]{3,2,1,0:T(8,128)}, f32[4,54,16,128]{3,2,1,0:T(8,128)}) custom-call(s32[3]{0:T(128)} %pad_add_fusion.place, f32[8,32]{1,0:T(8,128)} %fusion.19.ky, f32[128,128]{1,0:T(8,128)} %get-tuple-element.19.bxt, f32[4,1,16,128]{3,2,1,0:T(8,128)} %bitcast.163, f32[4,1,16,128]{3,2,1,0:T(8,128)} %copy-done.20, ...), custom_call_target="tpu_custom_call" | custom-call | flops 339738624 | bytes 7733248 | tf_op jit(solution)/shard_map/pallas_call | solution.py:355
  177.0 3.8 %collective-permute-done.29 = f32[4,54,16,128]{3,2,1,0:T(8,128)S(1)} collective-permute-done((f32[4,54,16,128]{3,2,1,0:T(8,128)}, f32[4,54,16,128]{3,2,1,0:T(8,128)S(1)}, u32[]{:S(2)}, u32[]{:S(2)}) %collective-permute-start.29) | collective-permute-done | bytes 1769504 | tf_op jit(solution)/shard_map/ppermute | solution.py:19
  180.8 1.8 add.93
  183.8 1.2 collective-permute-start.32
  185.0 10.0 %collective-permute-done.30 = f32[2,1,27,16,128]{4,3,2,0,1:T(8,128)S(1)} collective-permute-done((f32[2,1,27,16,128]{4,3,2,0,1:T(8,128)S(1)}, f32[2,1,27,16,128]{4,3,2,0,1:T(8,128)S(1)}, u32[]{:S(2)}, u32[]{:S(2)}) %collective-permute-start.30) | collective-permute-done | bytes 442400 | tf_op jit(solution)/shard_map/ppermute | solution.py:19
  197.5 4.4 %collective-permute-done.31 = f32[1,1,27,16,128]{4,3,2,1,0:T(8,128)S(1)} collective-permute-done((f32[1,1,27,16,128]{4,3,2,1,0:T(8,128)S(1)}, f32[1,1,27,16,128]{4,3,2,1,0:T(8,128)S(1)}, u32[]{:S(2)}, u32[]{:S(2)}) %collective-permute-start.31) | collective-permute-done | bytes 221216 | tf_op jit(solution)/shard_map/ppermute | solution.py:19
  203.6 2.2 shard_map.62
  206.5 1.6 collective-permute-start.35
  208.0 2.1 collective-permute-start.36
  210.2 6.3 %collective-permute-done.36.fc = f32[8,16,128]{2,1,0:T(8,128)S(1)} collective-permute-done((f32[8,16,128]{2,1,0:T(8,128)}, f32[8,16,128]{2,1,0:T(8,128)S(1)}, u32[]{:S(2)}, u32[]{:S(2)}) %collective-permute-start.36) | collective-permute-done | bytes 65568 | tf_op jit(solution)/shard_map/ppermute | solution.py:19
  217.9 2.4 shard_map.63
  222.2 2.3 collective-permute-start.38
  224.9 5.8 %collective-permute-done.37.refs_1_ = f32[32,16,128]{2,1,0:T(8,128)S(1)} collective-permute-done((f32[32,16,128]{2,1,0:T(8,128)S(1)}, f32[32,16,128]{2,1,0:T(8,128)S(1)}, u32[]{:S(2)}, u32[]{:S(2)}) %collective-permute-start.37) | collective-permute-done | bytes 262176 | tf_op jit(solution)/shard_map/ppermute | solution.py:19
  230.7 10.0 %collective-permute-done.38.refs_2_ = f32[32,16,128]{2,1,0:T(8,128)S(1)} collective-permute-done((f32[32,16,128]{2,1,0:T(8,128)S(1)}, f32[32,16,128]{2,1,0:T(8,128)S(1)}, u32[]{:S(2)}, u32[]{:S(2)}) %collective-permute-start.38) | collective-permute-done | bytes 262176 | tf_op jit(solution)/shard_map/ppermute | solution.py:19
  240.7 4.2 %collective-permute-done.39.refs_3_ = f32[32,16,128]{2,1,0:T(8,128)S(1)} collective-permute-done((f32[32,16,128]{2,1,0:T(8,128)S(1)}, f32[32,16,128]{2,1,0:T(8,128)S(1)}, u32[]{:S(2)}, u32[]{:S(2)}) %collective-permute-start.39) | collective-permute-done | bytes 262176 | tf_op jit(solution)/shard_map/ppermute | solution.py:19
  245.6 3.0 %shard_map.64 = f32[16,64,256]{2,1,0:T(8,128)} custom-call(s32[1]{0:T(128)} %bitcast.where, f32[32,16,128]{2,1,0:T(8,128)} %copy-done.8, f32[32,16,128]{2,1,0:T(8,128)} %copy-done.14, f32[32,16,128]{2,1,0:T(8,128)} %copy-done.15, f32[32,16,128]{2,1,0:T(8,128)} %copy-done.16), custom_call_target="tpu_custom_call" | custom-call | flops 2048 | bytes 2097152 | tf_op jit(solution)/shard_map/pallas_call | solution.py:355
  (162 shorter events, 40.4 us)
Async XLA Ops:
  2.4 15.2 %collective-permute-start.2 = (f32[2,128]{1,0:T(2,128)S(1)}, f32[2,128]{1,0:T(2,128)S(1)}, u32[]{:S(2)}, u32[]{:S(2)}) collective-permute-start(f32[2,128]{1,0:T(2,128)S(1)} %select_maximum_fusion), channel_id=1, source_target_pairs={{0,24},{8,16},{16,8},{24,0},{1,25},{9,17},{17,9},{25,1},{2,26},{10... | collective-permute-start | bytes 3080 | tf_op jit(solution)/shard_map/ppermute | solution.py:19
  4.0 14.5 %collective-permute-start.1 = (f32[2,128]{1,0:T(2,128)S(1)}, f32[2,128]{1,0:T(2,128)S(1)}, u32[]{:S(2)}, u32[]{:S(2)}) collective-permute-start(f32[2,128]{1,0:T(2,128)S(1)} %select_maximum_fusion), channel_id=1, source_target_pairs={{0,16},{8,24},{16,0},{24,8},{1,17},{9,25},{17,1},{25,9},{2,18},{10... | collective-permute-start | bytes 3080 | tf_op jit(solution)/shard_map/ppermute | solution.py:19
  5.0 15.6 %collective-permute-start = (f32[2,128]{1,0:T(2,128)S(1)}, f32[2,128]{1,0:T(2,128)S(1)}, u32[]{:S(2)}, u32[]{:S(2)}) collective-permute-start(f32[2,128]{1,0:T(2,128)S(1)} %select_maximum_fusion), channel_id=1, source_target_pairs={{0,8},{8,0},{16,24},{24,16},{1,9},{9,1},{17,25},{25,17},{2,10},{10... | collective-permute-start | bytes 3080 | tf_op jit(solution)/shard_map/ppermute | solution.py:19
  8.0 7.5 %copy-start.6 = (f32[2,16,64,256]{3,2,1,0:T(8,128)S(1)}, f32[2,16,64,256]{3,2,1,0:T(8,128)}, u32[]{:S(2)}) copy-start(f32[2,16,64,256]{3,2,1,0:T(8,128)} %param.6) | copy-start | bytes 6291460
  9.5 11.5 %collective-permute-start.6 = (f32[1,1,1,27,16,128]{5,4,3,2,1,0:T(8,128)}, f32[1,1,1,27,16,128]{5,4,3,2,1,0:T(8,128)}, u32[]{:S(2)}, u32[]{:S(2)}) collective-permute-start(f32[1,1,1,27,16,128]{5,4,3,2,1,0:T(8,128)} %maximum_bitcast_fusion.4), channel_id=1, source_target_pairs={{0,4},{1,5},{2,6},{3,7},{4,0},{5,1},{6,2},{7,3},{8,12},{9,13},{10,... | collective-permute-start | bytes 663560 | tf_op jit(solution)/shard_map/ppermute | solution.py:19
  14.1 8.6 %collective-permute-start.9 = (f32[1,1,1,27,16,128]{5,4,3,2,1,0:T(8,128)}, f32[1,1,1,27,16,128]{5,4,3,2,1,0:T(8,128)}, u32[]{:S(2)}, u32[]{:S(2)}) collective-permute-start(f32[1,1,1,27,16,128]{5,4,3,2,1,0:T(8,128)} %maximum_bitcast_fusion.5), channel_id=1, source_target_pairs={{0,2},{1,3},{2,0},{3,1},{4,6},{5,7},{6,4},{7,5},{8,10},{9,11},{10,... | collective-permute-start | bytes 663560 | tf_op jit(solution)/shard_map/ppermute | solution.py:19
  17.6 23.5 %collective-permute-start.12 = (f32[2,16,32,128]{3,2,1,0:T(8,128)}, f32[2,16,32,128]{3,2,1,0:T(8,128)S(1)}, u32[]{:S(2)}, u32[]{:S(2)}) collective-permute-start(f32[2,16,32,128]{3,2,1,0:T(8,128)} %get-tuple-element.35), channel_id=1, source_target_pairs={{0,8},{8,0},{16,24},{24,16},{1,9},{9,1},{17,25},{25,17},{2,10},{10... | collective-permute-start | bytes 1572872 | tf_op jit(solution)/shard_map/ppermute | solution.py:19
  18.4 36.0 %collective-permute-start.13 = (f32[2,16,32,128]{3,2,1,0:T(8,128)}, f32[2,16,32,128]{3,2,1,0:T(8,128)S(1)}, u32[]{:S(2)}, u32[]{:S(2)}) collective-permute-start(f32[2,16,32,128]{3,2,1,0:T(8,128)} %get-tuple-element.34), channel_id=1, source_target_pairs={{0,16},{8,24},{16,0},{24,8},{1,17},{9,25},{17,1},{25,9},{2,18},{10... | collective-permute-start | bytes 1572872 | tf_op jit(solution)/shard_map/ppermute | solution.py:19
  22.0 10.3 %collective-permute-start.7 = (f32[2,1,1,27,16,128]{5,4,3,0,2,1:T(8,128)S(1)}, f32[2,1,1,27,16,128]{5,4,3,0,2,1:T(8,128)S(1)}, u32[]{:S(2)}, u32[]{:S(2)}) collective-permute-start(f32[2,1,1,27,16,128]{5,4,3,0,2,1:T(8,128)S(1)} %maximum_bitcast_fusion), channel_id=1, source_target_pairs={{0,2},{1,3},{2,0},{3,1},{4,6},{5,7},{6,4},{7,5},{8,10},{9,11},{10,... | collective-permute-start | bytes 1327112 | tf_op jit(solution)/shard_map/ppermute | solution.py:19
  23.7 10.7 %collective-permute-start.10 = (f32[1,1,2,27,16,128]{5,4,3,2,1,0:T(8,128)S(1)}, f32[1,1,2,27,16,128]{5,4,3,2,1,0:T(8,128)S(1)}, u32[]{:S(2)}, u32[]{:S(2)}) collective-permute-start(f32[1,1,2,27,16,128]{5,4,3,2,1,0:T(8,128)S(1)} %maximum_bitcast_fusion.1), channel_id=1, source_target_pairs={{0,4},{1,5},{2,6},{3,7},{4,0},{5,1},{6,2},{7,3},{8,12},{9,13},{10,... | collective-permute-start | bytes 1327112 | tf_op jit(solution)/shard_map/ppermute | solution.py:19
  24.4 11.7 %collective-permute-start.3 = (f32[1,1,1,1,16,128]{4,5,3,2,1,0:T(8,128)S(1)}, f32[1,1,1,1,16,128]{4,5,3,2,1,0:T(8,128)S(1)}, u32[]{:S(2)}, u32[]{:S(2)}) collective-permute-start(f32[1,1,1,1,16,128]{4,5,3,2,1,0:T(8,128)S(1)} %pad_bitcast_fusion), channel_id=1, source_target_pairs={{0,4},{1,5},{2,6},{3,7},{4,0},{5,1},{6,2},{7,3},{8,12},{9,13},{10,... | collective-permute-start | bytes 24584 | tf_op jit(solution)/shard_map/ppermute | solution.py:19
  32.5 21.9 %copy-start.3 = (f32[2,2,1,27,16,128]{5,4,3,1,0,2:T(8,128)}, f32[2,2,1,27,16,128]{5,4,3,1,0,2:T(8,128)S(1)}, u32[]{:S(2)}) copy-start(f32[2,2,1,27,16,128]{5,4,3,1,0,2:T(8,128)S(1)} %copy.36) | copy-start | bytes 2654212
  32.5 21.9 %collective-permute-start.8 = (f32[4,27,16,128]{3,2,1,0:T(8,128)S(1)}, f32[4,27,16,128]{3,2,1,0:T(8,128)}, u32[]{:S(2)}, u32[]{:S(2)}) collective-permute-start(f32[4,27,16,128]{3,2,1,0:T(8,128)S(1)} %bitcast.146), channel_id=1, source_target_pairs={{0,1},{1,0},{2,3},{3,2},{4,5},{5,4},{6,7},{7,6},{8,9},{9,8},{10,11... | collective-permute-start | bytes 2654216 | tf_op jit(solution)/shard_map/ppermute | solution.py:19
  35.5 18.9 %collective-permute-start.11 = (f32[4,27,16,128]{3,2,1,0:T(8,128)}, f32[4,27,16,128]{3,2,1,0:T(8,128)}, u32[]{:S(2)}, u32[]{:S(2)}) collective-permute-start(f32[4,27,16,128]{3,2,1,0:T(8,128)} %bitcast.21.b0), channel_id=1, source_target_pairs={{0,1},{1,0},{2,3},{3,2},{4,5},{5,4},{6,7},{7,6},{8,9},{9,8},{10,11... | collective-permute-start | bytes 2654216 | tf_op jit(solution)/shard_map/ppermute | solution.py:19
  36.2 3.8 %collective-permute-start.4 = (f32[2,1,1,1,16,128]{5,4,0,3,2,1:T(8,128)S(1)}, f32[2,1,1,1,16,128]{5,4,0,3,2,1:T(8,128)S(1)}, u32[]{:S(2)}, u32[]{:S(2)}) collective-permute-start(f32[2,1,1,1,16,128]{5,4,0,3,2,1:T(8,128)S(1)} %get-tuple-element.50), channel_id=1, source_target_pairs={{0,2},{1,3},{2,0},{3,1},{4,6},{5,7},{6,4},{7,5},{8,10},{9,11},{10,... | collective-permute-start | bytes 49160 | tf_op jit(solution)/shard_map/ppermute | solution.py:19
  40.0 27.7 %collective-permute-start.14 = (f32[2,16,32,128]{3,2,1,0:T(8,128)}, f32[2,16,32,128]{3,2,1,0:T(8,128)S(1)}, u32[]{:S(2)}, u32[]{:S(2)}) collective-permute-start(f32[2,16,32,128]{3,2,1,0:T(8,128)} %get-tuple-element.33), channel_id=1, source_target_pairs={{0,24},{8,16},{16,8},{24,0},{1,25},{9,17},{17,9},{25,1},{2,26},{10... | collective-permute-start | bytes 1572872 | tf_op jit(solution)/shard_map/ppermute | solution.py:19
  41.1 26.6 %copy-start.11 = (f32[2,2,1,1,16,128]{5,4,3,2,1,0:T(8,128)}, f32[2,2,1,1,16,128]{5,4,3,2,1,0:T(8,128)S(1)}, u32[]{:S(2)}) copy-start(f32[2,2,1,1,16,128]{5,4,3,2,1,0:T(8,128)S(1)} %pad_maximum_fusion.5) | copy-start | bytes 98308
  41.1 13.2 %copy-start.1 = (f32[2,16,32,128]{3,2,1,0:T(8,128)}, f32[2,16,32,128]{3,2,1,0:T(8,128)S(1)}, u32[]{:S(2)}) copy-start(f32[2,16,32,128]{3,2,1,0:T(8,128)S(1)} %collective-permute-done.12.refs_0_.refs_1_) | copy-start | bytes 1572868
  41.2 26.5 %collective-permute-start.5 = (f32[4,1,16,128]{3,2,1,0:T(8,128)S(1)}, f32[4,1,16,128]{3,2,1,0:T(8,128)S(1)}, u32[]{:S(2)}, u32[]{:S(2)}) collective-permute-start(f32[4,1,16,128]{3,2,1,0:T(8,128)S(1)} %bitcast.161), channel_id=1, source_target_pairs={{0,1},{1,0},{2,3},{3,2},{4,5},{5,4},{6,7},{7,6},{8,9},{9,8},{10,11... | collective-permute-start | bytes 98312 | tf_op jit(solution)/shard_map/ppermute | solution.py:19
  82.9 3.9 %collective-permute-start.15 = (f32[4,54,16,128]{3,2,1,0:T(8,128)}, f32[4,54,16,128]{3,2,1,0:T(8,128)S(1)}, u32[]{:S(2)}, u32[]{:S(2)}) collective-permute-start(f32[4,54,16,128]{3,2,1,0:T(8,128)} %get-tuple-element.24), channel_id=1, source_target_pairs={{0,1},{1,0},{2,3},{3,2},{4,5},{5,4},{6,7},{7,6},{8,9},{9,8},{10,11... | collective-permute-start | bytes 5308424 | tf_op jit(solution)/shard_map/ppermute | solution.py:19
  88.8 12.3 %collective-permute-start.16 = (f32[2,1,27,16,128]{4,3,2,0,1:T(8,128)S(1)}, f32[2,1,27,16,128]{4,3,2,0,1:T(8,128)S(1)}, u32[]{:S(2)}, u32[]{:S(2)}) collective-permute-start(f32[2,1,27,16,128]{4,3,2,0,1:T(8,128)S(1)} %slice_bitcast_fusion.6), channel_id=1, source_target_pairs={{0,2},{1,3},{2,0},{3,1},{4,6},{5,7},{6,4},{7,5},{8,10},{9,11},{10,... | collective-permute-start | bytes 1327112 | tf_op jit(solution)/shard_map/ppermute | solution.py:19
  88.9 12.9 %collective-permute-start.18 = (f32[1,2,27,16,128]{4,3,2,1,0:T(8,128)S(1)}, f32[1,2,27,16,128]{4,3,2,1,0:T(8,128)S(1)}, u32[]{:S(2)}, u32[]{:S(2)}) collective-permute-start(f32[1,2,27,16,128]{4,3,2,1,0:T(8,128)S(1)} %slice_bitcast_fusion.4), channel_id=1, source_target_pairs={{0,4},{1,5},{2,6},{3,7},{4,0},{5,1},{6,2},{7,3},{8,12},{9,13},{10,... | collective-permute-start | bytes 1327112 | tf_op jit(solution)/shard_map/ppermute | solution.py:19
  101.2 15.0 %copy-start.18 = (f32[3,16,128]{2,1,0:T(8,128)S(1)}, f32[3,16,128]{2,1,0:T(8,128)}, u32[]{:S(2)}) copy-start(f32[3,16,128]{2,1,0:T(8,128)} %slice.108) | copy-start | bytes 73732
  101.2 15.0 %copy-start.19 = (f32[3,16,128]{2,1,0:T(8,128)S(1)}, f32[3,16,128]{2,1,0:T(8,128)}, u32[]{:S(2)}) copy-start(f32[3,16,128]{2,1,0:T(8,128)} %slice.111) | copy-start | bytes 73732
  101.3 6.7 %collective-permute-start.17 = (f32[1,1,27,16,128]{4,3,2,1,0:T(8,128)S(1)}, f32[1,1,27,16,128]{4,3,2,1,0:T(8,128)S(1)}, u32[]{:S(2)}, u32[]{:S(2)}) collective-permute-start(f32[1,1,27,16,128]{4,3,2,1,0:T(8,128)S(1)} %slice_bitcast_fusion.16), channel_id=1, source_target_pairs={{0,4},{1,5},{2,6},{3,7},{4,0},{5,1},{6,2},{7,3},{8,12},{9,13},{10,... | collective-permute-start | bytes 663560 | tf_op jit(solution)/shard_map/ppermute | solution.py:19
  101.9 6.8 %collective-permute-start.19 = (f32[1,1,27,16,128]{4,3,2,1,0:T(8,128)S(1)}, f32[1,1,27,16,128]{4,3,2,1,0:T(8,128)S(1)}, u32[]{:S(2)}, u32[]{:S(2)}) collective-permute-start(f32[1,1,27,16,128]{4,3,2,1,0:T(8,128)S(1)} %slice_bitcast_fusion.14), channel_id=1, source_target_pairs={{0,2},{1,3},{2,0},{3,1},{4,6},{5,7},{6,4},{7,5},{8,10},{9,11},{10,... | collective-permute-start | bytes 663560 | tf_op jit(solution)/shard_map/ppermute | solution.py:19
  111.9 12.6 %collective-permute-start.20 = (f32[36,16,128]{2,1,0:T(8,128)}, f32[36,16,128]{2,1,0:T(8,128)S(1)}, u32[]{:S(2)}, u32[]{:S(2)}) collective-permute-start(f32[36,16,128]{2,1,0:T(8,128)} %get-tuple-element.25), channel_id=1, source_target_pairs={{0,8},{8,0},{16,24},{24,16},{1,9},{9,1},{17,25},{25,17},{2,10},{10... | collective-permute-start | bytes 884744 | tf_op jit(solution)/shard_map/ppermute | solution.py:19
  111.9 12.6 %collective-permute-start.21 = (f32[12,16,128]{2,1,0:T(8,128)}, f32[12,16,128]{2,1,0:T(8,128)S(1)}, u32[]{:S(2)}, u32[]{:S(2)}) collective-permute-start(f32[12,16,128]{2,1,0:T(8,128)} %get-tuple-element.26), channel_id=1, source_target_pairs={{0,24},{8,16},{16,8},{24,0},{1,25},{9,17},{17,9},{25,1},{2,26},{10... | collective-permute-start | bytes 294920 | tf_op jit(solution)/shard_map/ppermute | solution.py:19
  115.7 8.7 %collective-permute-start.22 = (f32[8,16,128]{2,1,0:T(8,128)}, f32[8,16,128]{2,1,0:T(8,128)S(1)}, u32[]{:S(2)}, u32[]{:S(2)}) collective-permute-start(f32[8,16,128]{2,1,0:T(8,128)} %get-tuple-element.27), channel_id=1, source_target_pairs={{0,16},{8,24},{16,0},{24,8},{1,17},{9,25},{17,1},{25,9},{2,18},{10... | collective-permute-start | bytes 196616 | tf_op jit(solution)/shard_map/ppermute | solution.py:19
  128.7 6.0 %collective-permute-start.23 = (f32[1,1,1,27,16,128]{5,4,3,2,1,0:T(8,128)S(1)}, f32[1,1,1,27,16,128]{5,4,3,2,1,0:T(8,128)S(1)}, u32[]{:S(2)}, u32[]{:S(2)}) collective-permute-start(f32[1,1,1,27,16,128]{5,4,3,2,1,0:T(8,128)S(1)} %get-tuple-element.44), channel_id=1, source_target_pairs={{0,4},{1,5},{2,6},{3,7},{4,0},{5,1},{6,2},{7,3},{8,12},{9,13},{10,... | collective-permute-start | bytes 663560 | tf_op jit(solution)/shard_map/ppermute | solution.py:19
  129.6 7.9 %collective-permute-start.26 = (f32[1,1,1,27,16,128]{5,4,3,2,1,0:T(8,128)S(1)}, f32[1,1,1,27,16,128]{5,4,3,2,1,0:T(8,128)S(1)}, u32[]{:S(2)}, u32[]{:S(2)}) collective-permute-start(f32[1,1,1,27,16,128]{5,4,3,2,1,0:T(8,128)S(1)} %get-tuple-element.43), channel_id=1, source_target_pairs={{0,2},{1,3},{2,0},{3,1},{4,6},{5,7},{6,4},{7,5},{8,10},{9,11},{10,... | collective-permute-start | bytes 663560 | tf_op jit(solution)/shard_map/ppermute | solution.py:19
  134.7 10.3 %collective-permute-start.24 = (f32[2,1,1,27,16,128]{5,4,3,0,2,1:T(8,128)S(1)}, f32[2,1,1,27,16,128]{5,4,3,0,2,1:T(8,128)S(1)}, u32[]{:S(2)}, u32[]{:S(2)}) collective-permute-start(f32[2,1,1,27,16,128]{5,4,3,0,2,1:T(8,128)S(1)} %maximum_bitcast_fusion.2), channel_id=1, source_target_pairs={{0,2},{1,3},{2,0},{3,1},{4,6},{5,7},{6,4},{7,5},{8,10},{9,11},{10,... | collective-permute-start | bytes 1327112 | tf_op jit(solution)/shard_map/ppermute | solution.py:19
  137.6 8.4 %collective-permute-start.27 = (f32[1,1,2,27,16,128]{5,4,3,2,1,0:T(8,128)S(1)}, f32[1,1,2,27,16,128]{5,4,3,2,1,0:T(8,128)S(1)}, u32[]{:S(2)}, u32[]{:S(2)}) collective-permute-start(f32[1,1,2,27,16,128]{5,4,3,2,1,0:T(8,128)S(1)} %maximum_bitcast_fusion.3), channel_id=1, source_target_pairs={{0,4},{1,5},{2,6},{3,7},{4,0},{5,1},{6,2},{7,3},{8,12},{9,13},{10,... | collective-permute-start | bytes 1327112 | tf_op jit(solution)/shard_map/ppermute | solution.py:19
  145.2 2.5 %collective-permute-start.25 = (f32[4,27,16,128]{3,2,1,0:T(8,128)S(1)}, f32[4,27,16,128]{3,2,1,0:T(8,128)S(1)}, u32[]{:S(2)}, u32[]{:S(2)}) collective-permute-start(f32[4,27,16,128]{3,2,1,0:T(8,128)S(1)} %bitcast.156), channel_id=1, source_target_pairs={{0,1},{1,0},{2,3},{3,2},{4,5},{5,4},{6,7},{7,6},{8,9},{9,8},{10,11... | collective-permute-start | bytes 2654216 | tf_op jit(solution)/shard_map/ppermute | solution.py:19
  146.0 2.9 %collective-permute-start.28 = (f32[4,27,16,128]{3,2,1,0:T(8,128)S(1)}, f32[4,27,16,128]{3,2,1,0:T(8,128)S(1)}, u32[]{:S(2)}, u32[]{:S(2)}) collective-permute-start(f32[4,27,16,128]{3,2,1,0:T(8,128)S(1)} %bitcast.158), channel_id=1, source_target_pairs={{0,1},{1,0},{2,3},{3,2},{4,5},{5,4},{6,7},{7,6},{8,9},{9,8},{10,11... | collective-permute-start | bytes 2654216 | tf_op jit(solution)/shard_map/ppermute | solution.py:19
  176.9 3.9 %collective-permute-start.29 = (f32[4,54,16,128]{3,2,1,0:T(8,128)}, f32[4,54,16,128]{3,2,1,0:T(8,128)S(1)}, u32[]{:S(2)}, u32[]{:S(2)}) collective-permute-start(f32[4,54,16,128]{3,2,1,0:T(8,128)} %get-tuple-element.29), channel_id=1, source_target_pairs={{0,1},{1,0},{2,3},{3,2},{4,5},{5,4},{6,7},{7,6},{8,9},{9,8},{10,11... | collective-permute-start | bytes 5308424 | tf_op jit(solution)/shard_map/ppermute | solution.py:19
  182.8 12.3 %collective-permute-start.30 = (f32[2,1,27,16,128]{4,3,2,0,1:T(8,128)S(1)}, f32[2,1,27,16,128]{4,3,2,0,1:T(8,128)S(1)}, u32[]{:S(2)}, u32[]{:S(2)}) collective-permute-start(f32[2,1,27,16,128]{4,3,2,0,1:T(8,128)S(1)} %slice_bitcast_fusion.2), channel_id=1, source_target_pairs={{0,2},{1,3},{2,0},{3,1},{4,6},{5,7},{6,4},{7,5},{8,10},{9,11},{10,... | collective-permute-start | bytes 1327112 | tf_op jit(solution)/shard_map/ppermute | solution.py:19
  183.8 12.5 %collective-permute-start.32 = (f32[1,2,27,16,128]{4,3,2,1,0:T(8,128)S(1)}, f32[1,2,27,16,128]{4,3,2,1,0:T(8,128)S(1)}, u32[]{:S(2)}, u32[]{:S(2)}) collective-permute-start(f32[1,2,27,16,128]{4,3,2,1,0:T(8,128)S(1)} %slice_bitcast_fusion), channel_id=1, source_target_pairs={{0,4},{1,5},{2,6},{3,7},{4,0},{5,1},{6,2},{7,3},{8,12},{9,13},{10,... | collective-permute-start | bytes 1327112 | tf_op jit(solution)/shard_map/ppermute | solution.py:19
  195.2 6.7 %collective-permute-start.31 = (f32[1,1,27,16,128]{4,3,2,1,0:T(8,128)S(1)}, f32[1,1,27,16,128]{4,3,2,1,0:T(8,128)S(1)}, u32[]{:S(2)}, u32[]{:S(2)}) collective-permute-start(f32[1,1,27,16,128]{4,3,2,1,0:T(8,128)S(1)} %slice_bitcast_fusion.10), channel_id=1, source_target_pairs={{0,4},{1,5},{2,6},{3,7},{4,0},{5,1},{6,2},{7,3},{8,12},{9,13},{10,... | collective-permute-start | bytes 663560 | tf_op jit(solution)/shard_map/ppermute | solution.py:19
  196.4 6.4 %collective-permute-start.33 = (f32[1,1,27,16,128]{4,3,2,1,0:T(8,128)S(1)}, f32[1,1,27,16,128]{4,3,2,1,0:T(8,128)S(1)}, u32[]{:S(2)}, u32[]{:S(2)}) collective-permute-start(f32[1,1,27,16,128]{4,3,2,1,0:T(8,128)S(1)} %slice_bitcast_fusion.8), channel_id=1, source_target_pairs={{0,2},{1,3},{2,0},{3,1},{4,6},{5,7},{6,4},{7,5},{8,10},{9,11},{10,... | collective-permute-start | bytes 663560 | tf_op jit(solution)/shard_map/ppermute | solution.py:19
  205.8 10.7 %collective-permute-start.34 = (f32[36,16,128]{2,1,0:T(8,128)}, f32[36,16,128]{2,1,0:T(8,128)S(1)}, u32[]{:S(2)}, u32[]{:S(2)}) collective-permute-start(f32[36,16,128]{2,1,0:T(8,128)} %get-tuple-element.30), channel_id=1, source_target_pairs={{0,8},{8,0},{16,24},{24,16},{1,9},{9,1},{17,25},{25,17},{2,10},{10... | collective-permute-start | bytes 884744 | tf_op jit(solution)/shard_map/ppermute | solution.py:19
  206.5 10.0 %collective-permute-start.35 = (f32[12,16,128]{2,1,0:T(8,128)}, f32[12,16,128]{2,1,0:T(8,128)S(1)}, u32[]{:S(2)}, u32[]{:S(2)}) collective-permute-start(f32[12,16,128]{2,1,0:T(8,128)} %get-tuple-element.31), channel_id=1, source_target_pairs={{0,24},{8,16},{16,8},{24,0},{1,25},{9,17},{17,9},{25,1},{2,26},{10... | collective-permute-start | bytes 294920 | tf_op jit(solution)/shard_map/ppermute | solution.py:19
  208.0 8.4 %collective-permute-start.36 = (f32[8,16,128]{2,1,0:T(8,128)}, f32[8,16,128]{2,1,0:T(8,128)S(1)}, u32[]{:S(2)}, u32[]{:S(2)}) collective-permute-start(f32[8,16,128]{2,1,0:T(8,128)} %get-tuple-element.32), channel_id=1, source_target_pairs={{0,16},{8,24},{16,0},{24,8},{1,17},{9,25},{17,1},{25,9},{2,18},{10... | collective-permute-start | bytes 196616 | tf_op jit(solution)/shard_map/ppermute | solution.py:19
  221.4 23.5 %copy-start.8 = (f32[32,16,128]{2,1,0:T(8,128)}, f32[32,16,128]{2,1,0:T(8,128)S(1)}, u32[]{:S(2)}) copy-start(f32[32,16,128]{2,1,0:T(8,128)S(1)} %fusion.8.refs_0_) | copy-start | bytes 786436
  221.4 9.3 %collective-permute-start.37 = (f32[32,16,128]{2,1,0:T(8,128)S(1)}, f32[32,16,128]{2,1,0:T(8,128)S(1)}, u32[]{:S(2)}, u32[]{:S(2)}) collective-permute-start(f32[32,16,128]{2,1,0:T(8,128)S(1)} %fusion.8.refs_0_), channel_id=1, source_target_pairs={{0,8},{8,0},{16,24},{24,16},{1,9},{9,1},{17,25},{25,17},{2,10},{10... | collective-permute-start | bytes 786440 | tf_op jit(solution)/shard_map/ppermute | solution.py:19
  222.2 18.5 %collective-permute-start.38 = (f32[32,16,128]{2,1,0:T(8,128)S(1)}, f32[32,16,128]{2,1,0:T(8,128)S(1)}, u32[]{:S(2)}, u32[]{:S(2)}) collective-permute-start(f32[32,16,128]{2,1,0:T(8,128)S(1)} %fusion.8.refs_0_), channel_id=1, source_target_pairs={{0,16},{8,24},{16,0},{24,8},{1,17},{9,25},{17,1},{25,9},{2,18},{10... | collective-permute-start | bytes 786440 | tf_op jit(solution)/shard_map/ppermute | solution.py:19
  224.5 20.5 %collective-permute-start.39 = (f32[32,16,128]{2,1,0:T(8,128)S(1)}, f32[32,16,128]{2,1,0:T(8,128)S(1)}, u32[]{:S(2)}, u32[]{:S(2)}) collective-permute-start(f32[32,16,128]{2,1,0:T(8,128)S(1)} %fusion.8.refs_0_), channel_id=1, source_target_pairs={{0,24},{8,16},{16,8},{24,0},{1,25},{9,17},{17,9},{25,1},{2,26},{10... | collective-permute-start | bytes 786440 | tf_op jit(solution)/shard_map/ppermute | solution.py:19
  230.7 14.2 %copy-start.14 = (f32[32,16,128]{2,1,0:T(8,128)}, f32[32,16,128]{2,1,0:T(8,128)S(1)}, u32[]{:S(2)}) copy-start(f32[32,16,128]{2,1,0:T(8,128)S(1)} %collective-permute-done.37.refs_1_) | copy-start | bytes 786436
  (17 other events, 27.6 us)

commit v6 on v5

--- a/solution.py
+++ b/solution.py
@@ -299,7 +299,7 @@
         to_c[over + k] = edge[skip + k]
 
 
-def update_kernel(rad, place, a, b, fy, fz, fc, old, count, new):
+def update_kernel(rad, place, a, b, fy, fz, fc, old_a, old_b, count, new_a, new_b):
     yh, zh = place[0], place[1]
     rows, width, hz = a.shape
     group = hz // rad
@@ -319,7 +319,7 @@
 
     for o in range(2 * rims):
         h, k = o // rims, o % rims
-        row = h * rows + half + k
+        old, new, row = (old_a, old_b)[h], (new_a, new_b)[h], half + k
         rim = (a, b)[h][half + k] + fz[2 * rims + o]
         rim = rim + part(fy, hy, o - skip, over) + part(fc, over, o - skip, over)
         new[row] = old[row] * rim / total
@@ -328,21 +328,62 @@
             y = o * group + m
             moved = jnp.where(inside, pltpu.roll(edge, (begin - rad * m + hz) % hz, 1), 0.0)
             value = row_of(a, b, y, half) + part(fy, 0, y - start, hy) + moved
-            row = h * rows + y - h * half
+            row = y - h * half
             new[row] = old[row] * value / total
+
+
+def last_pack_kernel(rad, place, a, b, to_y, to_z, to_c):
+    rows, _, hz = a.shape
+    group = hz // rad
+    half = rows * group // (group + 1)
+    rims, own = half // group, 2 * half - rad
+    for side in range(2):
+
+        @pl.when(place[0] == side)
+        def _():
+            outer = own * (1 - side)
+            for k in range(rad):
+                to_y[k] = row_of(a, b, outer + k, half)
+            for ref, first in ((to_z, rad * side // group), (to_c, outer // group)):
+                for k in range(ref.shape[0]):
+                    o = first + k
+                    ref[k] = (a if o < rims else b)[half + o % rims]
+
+
+def last_update_kernel(rad, place, a, b, fy, fz, fc, old_a, old_b, count, new):
+    rows, width, hz = a.shape
+    group = hz // rad
+    half = rows * group // (group + 1)
+    own = new.shape[1]
+    begin = (hz - rad) * (1 - place[1])
+    inside = (lane_of((width, hz)) >= begin) & (lane_of((width, hz)) < begin + rad)
+    total = count[...]
+    for side in range(2):
+
+        @pl.when(place[0] == side)
+        def _():
+            first = (own - rad) * (1 - side)
+            for k in range(own):
+                y = rad * side + k
+                value, edge = row_of(a, b, y, half), fz[k // group]
+                if first <= k < first + rad:
+                    value = value + fy[k - first]
+                    edge = edge + fc[(k - first) // group]
+                moved = pltpu.roll(edge, (begin - rad * (k % group) + hz) % hz, 1)
+                value = value + jnp.where(inside, moved, 0.0)
+                new[:, k, :] = row_of(old_a, old_b, y, half) * value / total
 
 
 def assemble_kernel(where, *refs):
     pieces, out = refs[:-1], refs[-1]
-    hy, width, hz = pieces[0].shape
+    _, hy, hz = pieces[0].shape
     for r, piece in enumerate(pieces):
         for owner in range(len(pieces)):
             oz, oy = owner >> 1, (owner ^ (owner >> 1)) & 1
 
             @pl.when(where[0] == owner ^ r)
             def _():
-                for y in range(hy):
-                    out[:, oy * hy + y, oz * hz : (oz + 1) * hz] = piece[y]
+                out[:, oy * hy : (oy + 1) * hy, oz * hz : (oz + 1) * hz] = piece[...]
 
 
 VMEM = pl.BlockSpec(memory_space=pltpu.VMEM)
@@ -410,8 +451,8 @@
     rim = lax.dynamic_slice_in_dim(window, jnp.where(zh == 0, hz, hz - rad), rad, axis=2)
     rim = rim.reshape(2 * rims, group, width, rad).transpose(0, 2, 1, 3).reshape(2 * rims, width, hz)
     parts = [main[:half], rim[:rims], main[half:], rim[rims:]]
-    estimate = jnp.concatenate(parts, axis=0)
-    wide = gather([jnp.concatenate(parts[:2], axis=0), jnp.concatenate(parts[2:], axis=0)])
+    estimate = [jnp.concatenate(parts[:2], axis=0), jnp.concatenate(parts[2:], axis=0)]
+    wide = gather(estimate)
     notes = gather([note])
 
     nx = nspace * width
@@ -457,28 +498,34 @@
     over = hy // group
     for step in range(ITERS):
         if step:
-            wide = gather([estimate[:rows], estimate[rows:]])
+            wide = gather(estimate)
         blurred = ahead(wide, () if step else tuple(pieces[1:3]), (mxu if step else 0, plane))
         a, b = scatter_sum(*back(blurred))
+        last = step == ITERS - 1
+        if last:
+            sizes, scratch = (rad, over, rad // group), []
+            results = [(width, hy, hz)]
+        else:
+            sizes, scratch = (hy + over, 4 * rims, 2 * over), [(2 * rims, width, hz)]
+            results = [(rows, width, hz)] * 2
         to_y, to_z, to_c = call(
-            functools.partial(pack_kernel, rad),
-            [(hy + over, width, hz), (4 * rims, width, hz), (2 * over, width, hz)],
-            [(2 * rims, width, hz)],
+            functools.partial(last_pack_kernel if last else pack_kernel, rad),
+            [(size, width, hz) for size in sizes],
+            scratch,
             1,
             (plane, 4 * plane * 4 * rows),
             place_yz, a, b,
         )
         estimate = call(
-            functools.partial(update_kernel, rad),
-            [(2 * rows, width, hz)],
+            functools.partial(last_update_kernel if last else update_kernel, rad),
+            results,
             [],
             1,
             (plane, 4 * plane * 8 * rows),
-            place_yz, a, b, swap(to_y, "view", 1), swap(to_z, "view", 3), swap(to_c, "view", 2), estimate, count,
-        )[0]
-
-    main = jnp.concatenate([estimate[:half], estimate[rows : rows + half]], axis=0)
-    own = lax.dynamic_slice_in_dim(main, rad * yh, hy, axis=0)
+            place_yz, a, b, swap(to_y, "view", 1), swap(to_z, "view", 3), swap(to_c, "view", 2), *estimate, count,
+        )
+
+    own = estimate[0]
     parts = [own] + [swap(own, "view", r) for r in range(1, nview)]
     return call(
         assemble_kernel,

time: 249 us -> 244 us (0.980)
    concatenate x2, other arithmetic: 0.88 us -> 3.4 us  [the longest x1 1.75 us: body(): jnp.concatenate(parts[:2], axis=0)]
    unnamed x53 -> x45, local copies, waits for them, and re-layouts: 5.91 us -> 5.47 us
  transfers between devices with their start and end apart: 40 -> 40, of which waited for: 22 -> 21; matrix products, arithmetic and copies ran while one was open for 7% -> 8% of each run, Pallas kernels for 7% -> 7%
where the time goes in v6:
time: 244 us; the launch traced here: 243 us
  waiting for transfers between devices  103 us (42%)
  Pallas kernels  70.4 us (29%)
  starting transfers between devices  37.8 us (15%)
  other arithmetic  18.7 us (8%)
  local copies, waits for them, and re-layouts  12.7 us (5%)
    ppermute x40, waiting for transfers between devices, swap(): return lax.ppermute(value, axis, [(i, i ^ mask) for i in range(count)])  103 us
    pallas_call x9, Pallas kernels, call(): pl.pallas_call(kernel, out_shape=[jax.ShapeDtypeStruct(shape, F32) for sh...  65.2 us
    ppermute x40, starting transfers between devices, swap(): return lax.ppermute(value, axis, [(i, i ^ mask) for i in range(count)])  37.8 us
    unnamed x45, local copies, waits for them, and re-layouts  5.47 us
    pallas_call x1, Pallas kernels, body(): pl.pallas_call(functools.partial(bands_kernel, rad), out_shape=[jax.Shape...  5.2 us
  transfers between devices with their start and end apart: 40, of which 21 were waited for; matrix products, arithmetic and copies ran while one was open for 8% of the time, Pallas kernels for 7%

profile of v6, /device:TPU:8, one launch (start us, length us, event | category | flops | bytes accessed | tf_op | source)
XLA Modules:
  0.0 243.4 jit_solution(10794403834337686138)
XLA Ops:
  2.4 3.0 %collective-permute-start.1 = (f32[2,128]{1,0:T(2,128)S(1)}, f32[2,128]{1,0:T(2,128)S(1)}, u32[]{:S(2)}, u32[]{:S(2)}) collective-permute-start(f32[2,128]{1,0:T(2,128)S(1)} %select_maximum_fusion), channel_id=1, source_target_pairs={{0,16},{8,24},{16,0},{24,8},{1,17},{9,25},{17,1},{25,9},{2,18},{10... | collective-permute-start | bytes 3080 | tf_op jit(solution)/shard_map/ppermute | solution.py:19
  8.0 1.6 pad_maximum_fusion.5
  9.6 1.5 collective-permute-start.9
  12.2 1.7 pad_maximum_fusion.4
  13.9 1.5 collective-permute-start.6
  15.4 1.4 constant_dynamic-slice_fusion
  17.4 1.3 collective-permute-start.12
  18.8 2.2 collective-permute-start.13
  24.6 1.6 collective-permute-start.3
  26.2 7.1 %collective-permute-done.10 = f32[1,1,2,27,16,128]{5,4,3,2,1,0:T(8,128)S(1)} collective-permute-done((f32[1,1,2,27,16,128]{5,4,3,2,1,0:T(8,128)S(1)}, f32[1,1,2,27,16,128]{5,4,3,2,1,0:T(8,128)S(1)}, u32[]{:S(2)}, u32[]{:S(2)}) %collective-permute-start.10) | collective-permute-done | bytes 442400 | tf_op jit(solution)/shard_map/ppermute | solution.py:19
  36.7 2.9 %collective-permute-done.4 = f32[2,1,1,1,16,128]{5,4,0,3,2,1:T(8,128)S(1)} collective-permute-done((f32[2,1,1,1,16,128]{5,4,0,3,2,1:T(8,128)S(1)}, f32[2,1,1,1,16,128]{5,4,0,3,2,1:T(8,128)S(1)}, u32[]{:S(2)}, u32[]{:S(2)}) %collective-permute-start.4) | collective-permute-done | bytes 16416 | tf_op jit(solution)/shard_map/ppermute | solution.py:19
  41.4 5.2 %shard_map.55 = (bf16[128,384]{1,0:T(8,128)(2,1)}, f32[128,128]{1,0:T(8,128)}, bf16[8,512,128]{2,1,0:T(8,128)(2,1)}, bf16[8,384,256]{2,1,0:T(8,128)(2,1)}) custom-call(s32[3]{0:T(128)} %pad_add_fusion.place, s32[8]{0:T(128)} %and_select_fusion.slab, f32[8,96]{1,0:T(8,128)} %slice_divide_fusion.kern), custom_call_target="tpu_custom_call" | custom-call | flops 4194304 | bytes 2097152 | tf_op jit(solution)/shard_map/pallas_call | solution.py:459
  46.6 8.9 %collective-permute-done.13.refs_1_.refs_2_ = f32[2,16,32,128]{3,2,1,0:T(8,128)S(1)} collective-permute-done((f32[2,16,32,128]{3,2,1,0:T(8,128)}, f32[2,16,32,128]{3,2,1,0:T(8,128)S(1)}, u32[]{:S(2)}, u32[]{:S(2)}) %collective-permute-start.13) | collective-permute-done | bytes 524320 | tf_op jit(solution)/shard_map/ppermute | solution.py:19
  56.4 12.5 %shard_map.56.blurred = f32[32,128,128]{2,1,0:T(8,128)} custom-call(s32[3]{0:T(128)} %pad_add_fusion.place, f32[8,32]{1,0:T(8,128)} %fusion.18.ky, bf16[128,384]{1,0:T(8,128)(2,1)} %get-tuple-element.23.wx, bf16[8,512,128]{2,1,0:T(8,128)(2,1)} %get-tuple-element.24.kz, f32[4,27,16,128]{3,2,1,0:T(8,128)} %bitcast.18.a0, ...), custom_call_target="tpu_custom_call" | custom-call | bytes 2048 | tf_op jit(solution)/shard_map/pallas_call | solution.py:396
  69.7 14.5 %shard_map.57 = (f32[4,54,16,128]{3,2,1,0:T(8,128)}, f32[4,54,16,128]{3,2,1,0:T(8,128)}) custom-call(s32[3]{0:T(128)} %pad_add_fusion.place, f32[8,32]{1,0:T(8,128)} %fusion.18.ky, f32[128,128]{1,0:T(8,128)} %get-tuple-element.21.bxt, f32[4,1,16,128]{3,2,1,0:T(8,128)} %bitcast.164, f32[4,1,16,128]{3,2,1,0:T(8,128)} %copy-done.15, ...), custom_call_target="tpu_custom_call" | custom-call | flops 339738624 | bytes 7733248 | tf_op jit(solution)/shard_map/pallas_call | solution.py:396
  84.1 3.9 %collective-permute-done.15 = f32[4,54,16,128]{3,2,1,0:T(8,128)S(1)} collective-permute-done((f32[4,54,16,128]{3,2,1,0:T(8,128)}, f32[4,54,16,128]{3,2,1,0:T(8,128)S(1)}, u32[]{:S(2)}, u32[]{:S(2)}) %collective-permute-start.15) | collective-permute-done | bytes 1769504 | tf_op jit(solution)/shard_map/ppermute | solution.py:19
  88.0 1.8 add.85
  90.7 11.6 %collective-permute-done.18 = f32[1,2,27,16,128]{4,3,2,1,0:T(8,128)S(1)} collective-permute-done((f32[1,2,27,16,128]{4,3,2,1,0:T(8,128)S(1)}, f32[1,2,27,16,128]{4,3,2,1,0:T(8,128)S(1)}, u32[]{:S(2)}, u32[]{:S(2)}) %collective-permute-start.18) | collective-permute-done | bytes 442400 | tf_op jit(solution)/shard_map/ppermute | solution.py:19
  103.1 1.2 collective-permute-start.17
  104.3 4.8 %collective-permute-done.19 = f32[1,1,27,16,128]{4,3,2,1,0:T(8,128)S(1)} collective-permute-done((f32[1,1,27,16,128]{4,3,2,1,0:T(8,128)S(1)}, f32[1,1,27,16,128]{4,3,2,1,0:T(8,128)S(1)}, u32[]{:S(2)}, u32[]{:S(2)}) %collective-permute-start.19) | collective-permute-done | bytes 221216 | tf_op jit(solution)/shard_map/ppermute | solution.py:19
  110.5 2.5 %shard_map.58 = (f32[36,16,128]{2,1,0:T(8,128)}, f32[12,16,128]{2,1,0:T(8,128)}, f32[8,16,128]{2,1,0:T(8,128)}) custom-call(s32[3]{0:T(128)} %pad_add_fusion.place, f32[27,16,128]{2,1,0:T(8,128)} %fusion.15.a, f32[27,16,128]{2,1,0:T(8,128)} %fusion.13.b), custom_call_target="tpu_custom_call" | custom-call | flops 2048 | bytes 884736 | tf_op jit(solution)/shard_map/pallas_call | solution.py:396
  113.0 3.8 %collective-permute-start.21 = (f32[12,16,128]{2,1,0:T(8,128)}, f32[12,16,128]{2,1,0:T(8,128)S(1)}, u32[]{:S(2)}, u32[]{:S(2)}) collective-permute-start(f32[12,16,128]{2,1,0:T(8,128)} %get-tuple-element.28), channel_id=1, source_target_pairs={{0,24},{8,16},{16,8},{24,0},{1,25},{9,17},{17,9},{25,1},{2,26},{10... | collective-permute-start | bytes 294920 | tf_op jit(solution)/shard_map/ppermute | solution.py:19
  117.4 8.2 %collective-permute-done.22.fc = f32[8,16,128]{2,1,0:T(8,128)S(1)} collective-permute-done((f32[8,16,128]{2,1,0:T(8,128)}, f32[8,16,128]{2,1,0:T(8,128)S(1)}, u32[]{:S(2)}, u32[]{:S(2)}) %collective-permute-start.22) | collective-permute-done | bytes 65568 | tf_op jit(solution)/shard_map/ppermute | solution.py:19
  126.3 2.4 shard_map.59
  130.6 4.3 %collective-permute-done.26 = f32[1,1,1,27,16,128]{5,4,3,2,1,0:T(8,128)S(1)} collective-permute-done((f32[1,1,1,27,16,128]{5,4,3,2,1,0:T(8,128)}, f32[1,1,1,27,16,128]{5,4,3,2,1,0:T(8,128)S(1)}, u32[]{:S(2)}, u32[]{:S(2)}) %collective-permute-start.26) | collective-permute-done | bytes 221216 | tf_op jit(solution)/shard_map/ppermute | solution.py:19
  137.9 1.6 collective-permute-start.24
  139.4 5.9 %collective-permute-done.27 = f32[1,1,2,27,16,128]{5,4,3,2,1,0:T(8,128)S(1)} collective-permute-done((f32[1,1,2,27,16,128]{5,4,3,2,1,0:T(8,128)S(1)}, f32[1,1,2,27,16,128]{5,4,3,2,1,0:T(8,128)S(1)}, u32[]{:S(2)}, u32[]{:S(2)}) %collective-permute-start.27) | collective-permute-done | bytes 442400 | tf_op jit(solution)/shard_map/ppermute | solution.py:19
  146.5 1.4 collective-permute-done.28.b1
  147.9 1.3 collective-permute-done.25.a1
  150.1 12.5 %shard_map.60.blurred = f32[32,128,128]{2,1,0:T(8,128)} custom-call(s32[3]{0:T(128)} %pad_add_fusion.place, f32[8,32]{1,0:T(8,128)} %fusion.18.ky, bf16[128,384]{1,0:T(8,128)(2,1)} %get-tuple-element.23.wx, bf16[8,512,128]{2,1,0:T(8,128)(2,1)} %get-tuple-element.24.kz, f32[4,27,16,128]{3,2,1,0:T(8,128)} %bitcast.157, f32[4,27,16,128]{3,2,1,0:T(8,128)} %copy-done.9, ...), custom_call_target="tpu_custom_call" | custom-call | flops 339738624 | bytes 2048 | tf_op jit(solution)/shard_map/pallas_call | solution.py:396
  162.6 14.5 %shard_map.61 = (f32[4,54,16,128]{3,2,1,0:T(8,128)}, f32[4,54,16,128]{3,2,1,0:T(8,128)}) custom-call(s32[3]{0:T(128)} %pad_add_fusion.place, f32[8,32]{1,0:T(8,128)} %fusion.18.ky, f32[128,128]{1,0:T(8,128)} %get-tuple-element.21.bxt, f32[4,1,16,128]{3,2,1,0:T(8,128)} %bitcast.165, f32[4,1,16,128]{3,2,1,0:T(8,128)} %copy-done.15, ...), custom_call_target="tpu_custom_call" | custom-call | flops 339738624 | bytes 7733248 | tf_op jit(solution)/shard_map/pallas_call | solution.py:396
  177.2 3.8 %collective-permute-done.29 = f32[4,54,16,128]{3,2,1,0:T(8,128)S(1)} collective-permute-done((f32[4,54,16,128]{3,2,1,0:T(8,128)}, f32[4,54,16,128]{3,2,1,0:T(8,128)S(1)}, u32[]{:S(2)}, u32[]{:S(2)}) %collective-permute-start.29) | collective-permute-done | bytes 1769504 | tf_op jit(solution)/shard_map/ppermute | solution.py:19
  180.9 1.8 add.90
  183.9 1.2 collective-permute-start.30
  185.1 10.1 %collective-permute-done.32 = f32[1,2,27,16,128]{4,3,2,1,0:T(8,128)S(1)} collective-permute-done((f32[1,2,27,16,128]{4,3,2,1,0:T(8,128)S(1)}, f32[1,2,27,16,128]{4,3,2,1,0:T(8,128)S(1)}, u32[]{:S(2)}, u32[]{:S(2)}) %collective-permute-start.32) | collective-permute-done | bytes 442400 | tf_op jit(solution)/shard_map/ppermute | solution.py:19
  195.3 1.3 collective-permute-start.33
  197.6 4.4 %collective-permute-done.33 = f32[1,1,27,16,128]{4,3,2,1,0:T(8,128)S(1)} collective-permute-done((f32[1,1,27,16,128]{4,3,2,1,0:T(8,128)S(1)}, f32[1,1,27,16,128]{4,3,2,1,0:T(8,128)S(1)}, u32[]{:S(2)}, u32[]{:S(2)}) %collective-permute-start.33) | collective-permute-done | bytes 221216 | tf_op jit(solution)/shard_map/ppermute | solution.py:19
  203.9 1.8 shard_map.62
  205.6 1.4 collective-permute-start.34
  207.0 1.7 collective-permute-start.35
  208.8 1.2 collective-permute-start.36
  210.0 3.6 %collective-permute-done.36.fc = f32[2,16,128]{2,1,0:T(8,128)S(1)} collective-permute-done((f32[2,16,128]{2,1,0:T(8,128)}, f32[2,16,128]{2,1,0:T(8,128)S(1)}, u32[]{:S(2)}, u32[]{:S(2)}) %collective-permute-start.36) | collective-permute-done | bytes 16416 | tf_op jit(solution)/shard_map/ppermute | solution.py:19
  214.9 2.4 shard_map.63.refs_0_
  219.0 1.7 collective-permute-start.39
  220.7 6.6 %collective-permute-done.37.refs_1_ = f32[16,32,128]{2,1,0:T(8,128)S(1)} collective-permute-done((f32[16,32,128]{2,1,0:T(8,128)}, f32[16,32,128]{2,1,0:T(8,128)S(1)}, u32[]{:S(2)}, u32[]{:S(2)}) %collective-permute-start.37) | collective-permute-done | bytes 262176 | tf_op jit(solution)/shard_map/ppermute | solution.py:19
  227.3 8.1 %collective-permute-done.38.refs_2_ = f32[16,32,128]{2,1,0:T(8,128)S(1)} collective-permute-done((f32[16,32,128]{2,1,0:T(8,128)}, f32[16,32,128]{2,1,0:T(8,128)S(1)}, u32[]{:S(2)}, u32[]{:S(2)}) %collective-permute-start.38) | collective-permute-done | bytes 262176 | tf_op jit(solution)/shard_map/ppermute | solution.py:19
  235.4 5.0 %collective-permute-done.39.refs_3_ = f32[16,32,128]{2,1,0:T(8,128)S(1)} collective-permute-done((f32[16,32,128]{2,1,0:T(8,128)}, f32[16,32,128]{2,1,0:T(8,128)S(1)}, u32[]{:S(2)}, u32[]{:S(2)}) %collective-permute-start.39) | collective-permute-done | bytes 262176 | tf_op jit(solution)/shard_map/ppermute | solution.py:19
  241.1 2.3 shard_map.64
  (150 shorter events, 36.2 us)
Async XLA Ops:
  0.0 5.9 %copy-start = (f32[16,64,256]{2,1,0:T(8,128)S(1)}, f32[16,64,256]{2,1,0:T(8,128)}, u32[]{:S(2)}) copy-start(f32[16,64,256]{2,1,0:T(8,128)} %param.5) | copy-start | bytes 3145732
  2.4 15.0 %collective-permute-start = (f32[2,128]{1,0:T(2,128)S(1)}, f32[2,128]{1,0:T(2,128)S(1)}, u32[]{:S(2)}, u32[]{:S(2)}) collective-permute-start(f32[2,128]{1,0:T(2,128)S(1)} %select_maximum_fusion), channel_id=1, source_target_pairs={{0,8},{8,0},{16,24},{24,16},{1,9},{9,1},{17,25},{25,17},{2,10},{10... | collective-permute-start | bytes 3080 | tf_op jit(solution)/shard_map/ppermute | solution.py:19
  2.4 16.4 %collective-permute-start.1 = (f32[2,128]{1,0:T(2,128)S(1)}, f32[2,128]{1,0:T(2,128)S(1)}, u32[]{:S(2)}, u32[]{:S(2)}) collective-permute-start(f32[2,128]{1,0:T(2,128)S(1)} %select_maximum_fusion), channel_id=1, source_target_pairs={{0,16},{8,24},{16,0},{24,8},{1,17},{9,25},{17,1},{25,9},{2,18},{10... | collective-permute-start | bytes 3080 | tf_op jit(solution)/shard_map/ppermute | solution.py:19
  5.4 15.6 %collective-permute-start.2 = (f32[2,128]{1,0:T(2,128)S(1)}, f32[2,128]{1,0:T(2,128)S(1)}, u32[]{:S(2)}, u32[]{:S(2)}) collective-permute-start(f32[2,128]{1,0:T(2,128)S(1)} %select_maximum_fusion), channel_id=1, source_target_pairs={{0,24},{8,16},{16,8},{24,0},{1,25},{9,17},{17,9},{25,1},{2,26},{10... | collective-permute-start | bytes 3080 | tf_op jit(solution)/shard_map/ppermute | solution.py:19
  7.0 8.5 %copy-start.6 = (f32[2,16,64,256]{3,2,1,0:T(8,128)S(1)}, f32[2,16,64,256]{3,2,1,0:T(8,128)}, u32[]{:S(2)}) copy-start(f32[2,16,64,256]{3,2,1,0:T(8,128)} %param.6) | copy-start | bytes 6291460
  9.6 11.7 %collective-permute-start.9 = (f32[1,1,1,27,16,128]{5,4,3,2,1,0:T(8,128)S(1)}, f32[1,1,1,27,16,128]{5,4,3,2,1,0:T(8,128)}, u32[]{:S(2)}, u32[]{:S(2)}) collective-permute-start(f32[1,1,1,27,16,128]{5,4,3,2,1,0:T(8,128)S(1)} %get-tuple-element.50), channel_id=1, source_target_pairs={{0,2},{1,3},{2,0},{3,1},{4,6},{5,7},{6,4},{7,5},{8,10},{9,11},{10,... | collective-permute-start | bytes 663560 | tf_op jit(solution)/shard_map/ppermute | solution.py:19
  13.9 9.0 %collective-permute-start.6 = (f32[1,1,1,27,16,128]{5,4,3,2,1,0:T(8,128)}, f32[1,1,1,27,16,128]{5,4,3,2,1,0:T(8,128)}, u32[]{:S(2)}, u32[]{:S(2)}) collective-permute-start(f32[1,1,1,27,16,128]{5,4,3,2,1,0:T(8,128)} %get-tuple-element.52), channel_id=1, source_target_pairs={{0,4},{1,5},{2,6},{3,7},{4,0},{5,1},{6,2},{7,3},{8,12},{9,13},{10,... | collective-permute-start | bytes 663560 | tf_op jit(solution)/shard_map/ppermute | solution.py:19
  17.4 23.3 %collective-permute-start.12 = (f32[2,16,32,128]{3,2,1,0:T(8,128)}, f32[2,16,32,128]{3,2,1,0:T(8,128)S(1)}, u32[]{:S(2)}, u32[]{:S(2)}) collective-permute-start(f32[2,16,32,128]{3,2,1,0:T(8,128)} %get-tuple-element.39), channel_id=1, source_target_pairs={{0,8},{8,0},{16,24},{24,16},{1,9},{9,1},{17,25},{25,17},{2,10},{10... | collective-permute-start | bytes 1572872 | tf_op jit(solution)/shard_map/ppermute | solution.py:19
  18.8 36.8 %collective-permute-start.13 = (f32[2,16,32,128]{3,2,1,0:T(8,128)}, f32[2,16,32,128]{3,2,1,0:T(8,128)S(1)}, u32[]{:S(2)}, u32[]{:S(2)}) collective-permute-start(f32[2,16,32,128]{3,2,1,0:T(8,128)} %get-tuple-element.38), channel_id=1, source_target_pairs={{0,16},{8,24},{16,0},{24,8},{1,17},{9,25},{17,1},{25,9},{2,18},{10... | collective-permute-start | bytes 1572872 | tf_op jit(solution)/shard_map/ppermute | solution.py:19
  22.3 11.0 %collective-permute-start.10 = (f32[1,1,2,27,16,128]{5,4,3,2,1,0:T(8,128)S(1)}, f32[1,1,2,27,16,128]{5,4,3,2,1,0:T(8,128)S(1)}, u32[]{:S(2)}, u32[]{:S(2)}) collective-permute-start(f32[1,1,2,27,16,128]{5,4,3,2,1,0:T(8,128)S(1)} %maximum_bitcast_fusion.1), channel_id=1, source_target_pairs={{0,4},{1,5},{2,6},{3,7},{4,0},{5,1},{6,2},{7,3},{8,12},{9,13},{10,... | collective-permute-start | bytes 1327112 | tf_op jit(solution)/shard_map/ppermute | solution.py:19
  23.9 10.0 %collective-permute-start.7 = (f32[2,1,1,27,16,128]{5,4,3,0,2,1:T(8,128)S(1)}, f32[2,1,1,27,16,128]{5,4,3,0,2,1:T(8,128)S(1)}, u32[]{:S(2)}, u32[]{:S(2)}) collective-permute-start(f32[2,1,1,27,16,128]{5,4,3,0,2,1:T(8,128)S(1)} %maximum_bitcast_fusion), channel_id=1, source_target_pairs={{0,2},{1,3},{2,0},{3,1},{4,6},{5,7},{6,4},{7,5},{8,10},{9,11},{10,... | collective-permute-start | bytes 1327112 | tf_op jit(solution)/shard_map/ppermute | solution.py:19
  24.6 11.0 %collective-permute-start.3 = (f32[1,1,1,1,16,128]{4,5,3,2,1,0:T(8,128)S(1)}, f32[1,1,1,1,16,128]{4,5,3,2,1,0:T(8,128)S(1)}, u32[]{:S(2)}, u32[]{:S(2)}) collective-permute-start(f32[1,1,1,1,16,128]{4,5,3,2,1,0:T(8,128)S(1)} %pad_bitcast_fusion), channel_id=1, source_target_pairs={{0,4},{1,5},{2,6},{3,7},{4,0},{5,1},{6,2},{7,3},{8,12},{9,13},{10,... | collective-permute-start | bytes 24584 | tf_op jit(solution)/shard_map/ppermute | solution.py:19
  33.3 1.7 copy-start.3
  33.4 22.2 %collective-permute-start.11 = (f32[4,27,16,128]{3,2,1,0:T(8,128)S(1)}, f32[4,27,16,128]{3,2,1,0:T(8,128)}, u32[]{:S(2)}, u32[]{:S(2)}) collective-permute-start(f32[4,27,16,128]{3,2,1,0:T(8,128)S(1)} %bitcast.144), channel_id=1, source_target_pairs={{0,1},{1,0},{2,3},{3,2},{4,5},{5,4},{6,7},{7,6},{8,9},{9,8},{10,11... | collective-permute-start | bytes 2654216 | tf_op jit(solution)/shard_map/ppermute | solution.py:19
  35.0 20.6 %collective-permute-start.8 = (f32[4,27,16,128]{3,2,1,0:T(8,128)}, f32[4,27,16,128]{3,2,1,0:T(8,128)}, u32[]{:S(2)}, u32[]{:S(2)}) collective-permute-start(f32[4,27,16,128]{3,2,1,0:T(8,128)} %bitcast.18.a0), channel_id=1, source_target_pairs={{0,1},{1,0},{2,3},{3,2},{4,5},{5,4},{6,7},{7,6},{8,9},{9,8},{10,11... | collective-permute-start | bytes 2654216 | tf_op jit(solution)/shard_map/ppermute | solution.py:19
  35.7 3.8 %collective-permute-start.4 = (f32[2,1,1,1,16,128]{5,4,0,3,2,1:T(8,128)S(1)}, f32[2,1,1,1,16,128]{5,4,0,3,2,1:T(8,128)S(1)}, u32[]{:S(2)}, u32[]{:S(2)}) collective-permute-start(f32[2,1,1,1,16,128]{5,4,0,3,2,1:T(8,128)S(1)} %get-tuple-element.54), channel_id=1, source_target_pairs={{0,2},{1,3},{2,0},{3,1},{4,6},{5,7},{6,4},{7,5},{8,10},{9,11},{10,... | collective-permute-start | bytes 49160 | tf_op jit(solution)/shard_map/ppermute | solution.py:19
  39.5 29.4 %collective-permute-start.14 = (f32[2,16,32,128]{3,2,1,0:T(8,128)}, f32[2,16,32,128]{3,2,1,0:T(8,128)S(1)}, u32[]{:S(2)}, u32[]{:S(2)}) collective-permute-start(f32[2,16,32,128]{3,2,1,0:T(8,128)} %get-tuple-element.37), channel_id=1, source_target_pairs={{0,24},{8,16},{16,8},{24,0},{1,25},{9,17},{17,9},{25,1},{2,26},{10... | collective-permute-start | bytes 1572872 | tf_op jit(solution)/shard_map/ppermute | solution.py:19
  40.7 28.2 %copy-start.10 = (f32[2,2,1,1,16,128]{5,4,3,2,1,0:T(8,128)}, f32[2,2,1,1,16,128]{5,4,3,2,1,0:T(8,128)S(1)}, u32[]{:S(2)}) copy-start(f32[2,2,1,1,16,128]{5,4,3,2,1,0:T(8,128)S(1)} %pad_maximum_fusion.6) | copy-start | bytes 98308
  40.7 14.9 %copy-start.1 = (f32[2,16,32,128]{3,2,1,0:T(8,128)}, f32[2,16,32,128]{3,2,1,0:T(8,128)S(1)}, u32[]{:S(2)}) copy-start(f32[2,16,32,128]{3,2,1,0:T(8,128)S(1)} %collective-permute-done.12.refs_0_.refs_1_) | copy-start | bytes 1572868
  40.7 28.2 %collective-permute-start.5 = (f32[4,1,16,128]{3,2,1,0:T(8,128)S(1)}, f32[4,1,16,128]{3,2,1,0:T(8,128)S(1)}, u32[]{:S(2)}, u32[]{:S(2)}) collective-permute-start(f32[4,1,16,128]{3,2,1,0:T(8,128)S(1)} %bitcast.163), channel_id=1, source_target_pairs={{0,1},{1,0},{2,3},{3,2},{4,5},{5,4},{6,7},{7,6},{8,9},{9,8},{10,11... | collective-permute-start | bytes 98312 | tf_op jit(solution)/shard_map/ppermute | solution.py:19
  84.1 3.9 %collective-permute-start.15 = (f32[4,54,16,128]{3,2,1,0:T(8,128)}, f32[4,54,16,128]{3,2,1,0:T(8,128)S(1)}, u32[]{:S(2)}, u32[]{:S(2)}) collective-permute-start(f32[4,54,16,128]{3,2,1,0:T(8,128)} %get-tuple-element.26), channel_id=1, source_target_pairs={{0,1},{1,0},{2,3},{3,2},{4,5},{5,4},{6,7},{7,6},{8,9},{9,8},{10,11... | collective-permute-start | bytes 5308424 | tf_op jit(solution)/shard_map/ppermute | solution.py:19
  90.0 12.3 %collective-permute-start.18 = (f32[1,2,27,16,128]{4,3,2,1,0:T(8,128)S(1)}, f32[1,2,27,16,128]{4,3,2,1,0:T(8,128)S(1)}, u32[]{:S(2)}, u32[]{:S(2)}) collective-permute-start(f32[1,2,27,16,128]{4,3,2,1,0:T(8,128)S(1)} %slice_bitcast_fusion.4), channel_id=1, source_target_pairs={{0,4},{1,5},{2,6},{3,7},{4,0},{5,1},{6,2},{7,3},{8,12},{9,13},{10,... | collective-permute-start | bytes 1327112 | tf_op jit(solution)/shard_map/ppermute | solution.py:19
  90.1 12.8 %collective-permute-start.16 = (f32[2,1,27,16,128]{4,3,2,0,1:T(8,128)S(1)}, f32[2,1,27,16,128]{4,3,2,0,1:T(8,128)S(1)}, u32[]{:S(2)}, u32[]{:S(2)}) collective-permute-start(f32[2,1,27,16,128]{4,3,2,0,1:T(8,128)S(1)} %slice_bitcast_fusion.6), channel_id=1, source_target_pairs={{0,2},{1,3},{2,0},{3,1},{4,6},{5,7},{6,4},{7,5},{8,10},{9,11},{10,... | collective-permute-start | bytes 1327112 | tf_op jit(solution)/shard_map/ppermute | solution.py:19
  102.4 6.7 %collective-permute-start.19 = (f32[1,1,27,16,128]{4,3,2,1,0:T(8,128)S(1)}, f32[1,1,27,16,128]{4,3,2,1,0:T(8,128)S(1)}, u32[]{:S(2)}, u32[]{:S(2)}) collective-permute-start(f32[1,1,27,16,128]{4,3,2,1,0:T(8,128)S(1)} %slice_bitcast_fusion.12), channel_id=1, source_target_pairs={{0,2},{1,3},{2,0},{3,1},{4,6},{5,7},{6,4},{7,5},{8,10},{9,11},{10,... | collective-permute-start | bytes 663560 | tf_op jit(solution)/shard_map/ppermute | solution.py:19
  103.1 6.7 %collective-permute-start.17 = (f32[1,1,27,16,128]{4,3,2,1,0:T(8,128)S(1)}, f32[1,1,27,16,128]{4,3,2,1,0:T(8,128)S(1)}, u32[]{:S(2)}, u32[]{:S(2)}) collective-permute-start(f32[1,1,27,16,128]{4,3,2,1,0:T(8,128)S(1)} %slice_bitcast_fusion.14), channel_id=1, source_target_pairs={{0,4},{1,5},{2,6},{3,7},{4,0},{5,1},{6,2},{7,3},{8,12},{9,13},{10,... | collective-permute-start | bytes 663560 | tf_op jit(solution)/shard_map/ppermute | solution.py:19
  113.0 12.6 %collective-permute-start.20 = (f32[36,16,128]{2,1,0:T(8,128)}, f32[36,16,128]{2,1,0:T(8,128)S(1)}, u32[]{:S(2)}, u32[]{:S(2)}) collective-permute-start(f32[36,16,128]{2,1,0:T(8,128)} %get-tuple-element.27), channel_id=1, source_target_pairs={{0,8},{8,0},{16,24},{24,16},{1,9},{9,1},{17,25},{25,17},{2,10},{10... | collective-permute-start | bytes 884744 | tf_op jit(solution)/shard_map/ppermute | solution.py:19
  113.0 12.6 %collective-permute-start.21 = (f32[12,16,128]{2,1,0:T(8,128)}, f32[12,16,128]{2,1,0:T(8,128)S(1)}, u32[]{:S(2)}, u32[]{:S(2)}) collective-permute-start(f32[12,16,128]{2,1,0:T(8,128)} %get-tuple-element.28), channel_id=1, source_target_pairs={{0,24},{8,16},{16,8},{24,0},{1,25},{9,17},{17,9},{25,1},{2,26},{10... | collective-permute-start | bytes 294920 | tf_op jit(solution)/shard_map/ppermute | solution.py:19
  116.8 8.7 %collective-permute-start.22 = (f32[8,16,128]{2,1,0:T(8,128)}, f32[8,16,128]{2,1,0:T(8,128)S(1)}, u32[]{:S(2)}, u32[]{:S(2)}) collective-permute-start(f32[8,16,128]{2,1,0:T(8,128)} %get-tuple-element.29), channel_id=1, source_target_pairs={{0,16},{8,24},{16,0},{24,8},{1,17},{9,25},{17,1},{25,9},{2,18},{10... | collective-permute-start | bytes 196616 | tf_op jit(solution)/shard_map/ppermute | solution.py:19
  128.8 6.1 %collective-permute-start.26 = (f32[1,1,1,27,16,128]{5,4,3,2,1,0:T(8,128)}, f32[1,1,1,27,16,128]{5,4,3,2,1,0:T(8,128)S(1)}, u32[]{:S(2)}, u32[]{:S(2)}) collective-permute-start(f32[1,1,1,27,16,128]{5,4,3,2,1,0:T(8,128)} %bitcast.161), channel_id=1, source_target_pairs={{0,2},{1,3},{2,0},{3,1},{4,6},{5,7},{6,4},{7,5},{8,10},{9,11},{10,... | collective-permute-start | bytes 663560 | tf_op jit(solution)/shard_map/ppermute | solution.py:19
  129.7 7.2 %collective-permute-start.23 = (f32[1,1,1,27,16,128]{5,4,3,2,1,0:T(8,128)}, f32[1,1,1,27,16,128]{5,4,3,2,1,0:T(8,128)S(1)}, u32[]{:S(2)}, u32[]{:S(2)}) collective-permute-start(f32[1,1,1,27,16,128]{5,4,3,2,1,0:T(8,128)} %bitcast.159), channel_id=1, source_target_pairs={{0,4},{1,5},{2,6},{3,7},{4,0},{5,1},{6,2},{7,3},{8,12},{9,13},{10,... | collective-permute-start | bytes 663560 | tf_op jit(solution)/shard_map/ppermute | solution.py:19
  135.9 9.4 %collective-permute-start.27 = (f32[1,1,2,27,16,128]{5,4,3,2,1,0:T(8,128)S(1)}, f32[1,1,2,27,16,128]{5,4,3,2,1,0:T(8,128)S(1)}, u32[]{:S(2)}, u32[]{:S(2)}) collective-permute-start(f32[1,1,2,27,16,128]{5,4,3,2,1,0:T(8,128)S(1)} %maximum_bitcast_fusion.3), channel_id=1, source_target_pairs={{0,4},{1,5},{2,6},{3,7},{4,0},{5,1},{6,2},{7,3},{8,12},{9,13},{10,... | collective-permute-start | bytes 1327112 | tf_op jit(solution)/shard_map/ppermute | solution.py:19
  137.9 8.4 %collective-permute-start.24 = (f32[2,1,1,27,16,128]{5,4,3,0,2,1:T(8,128)S(1)}, f32[2,1,1,27,16,128]{5,4,3,0,2,1:T(8,128)S(1)}, u32[]{:S(2)}, u32[]{:S(2)}) collective-permute-start(f32[2,1,1,27,16,128]{5,4,3,0,2,1:T(8,128)S(1)} %maximum_bitcast_fusion.2), channel_id=1, source_target_pairs={{0,2},{1,3},{2,0},{3,1},{4,6},{5,7},{6,4},{7,5},{8,10},{9,11},{10,... | collective-permute-start | bytes 1327112 | tf_op jit(solution)/shard_map/ppermute | solution.py:19
  145.4 2.5 %collective-permute-start.28 = (f32[4,27,16,128]{3,2,1,0:T(8,128)S(1)}, f32[4,27,16,128]{3,2,1,0:T(8,128)S(1)}, u32[]{:S(2)}, u32[]{:S(2)}) collective-permute-start(f32[4,27,16,128]{3,2,1,0:T(8,128)S(1)} %bitcast.154), channel_id=1, source_target_pairs={{0,1},{1,0},{2,3},{3,2},{4,5},{5,4},{6,7},{7,6},{8,9},{9,8},{10,11... | collective-permute-start | bytes 2654216 | tf_op jit(solution)/shard_map/ppermute | solution.py:19
  146.4 2.8 %copy-start.5 = (f32[2,2,1,27,16,128]{5,4,3,1,0,2:T(8,128)}, f32[2,2,1,27,16,128]{5,4,3,1,0,2:T(8,128)S(1)}, u32[]{:S(2)}) copy-start(f32[2,2,1,27,16,128]{5,4,3,1,0,2:T(8,128)S(1)} %copy.39) | copy-start | bytes 2654212
  146.4 2.8 %collective-permute-start.25 = (f32[4,27,16,128]{3,2,1,0:T(8,128)S(1)}, f32[4,27,16,128]{3,2,1,0:T(8,128)S(1)}, u32[]{:S(2)}, u32[]{:S(2)}) collective-permute-start(f32[4,27,16,128]{3,2,1,0:T(8,128)S(1)} %bitcast.156), channel_id=1, source_target_pairs={{0,1},{1,0},{2,3},{3,2},{4,5},{5,4},{6,7},{7,6},{8,9},{9,8},{10,11... | collective-permute-start | bytes 2654216 | tf_op jit(solution)/shard_map/ppermute | solution.py:19
  177.0 3.9 %collective-permute-start.29 = (f32[4,54,16,128]{3,2,1,0:T(8,128)}, f32[4,54,16,128]{3,2,1,0:T(8,128)S(1)}, u32[]{:S(2)}, u32[]{:S(2)}) collective-permute-start(f32[4,54,16,128]{3,2,1,0:T(8,128)} %get-tuple-element.33), channel_id=1, source_target_pairs={{0,1},{1,0},{2,3},{3,2},{4,5},{5,4},{6,7},{7,6},{8,9},{9,8},{10,11... | collective-permute-start | bytes 5308424 | tf_op jit(solution)/shard_map/ppermute | solution.py:19
  182.9 12.3 %collective-permute-start.32 = (f32[1,2,27,16,128]{4,3,2,1,0:T(8,128)S(1)}, f32[1,2,27,16,128]{4,3,2,1,0:T(8,128)S(1)}, u32[]{:S(2)}, u32[]{:S(2)}) collective-permute-start(f32[1,2,27,16,128]{4,3,2,1,0:T(8,128)S(1)} %slice_bitcast_fusion), channel_id=1, source_target_pairs={{0,4},{1,5},{2,6},{3,7},{4,0},{5,1},{6,2},{7,3},{8,12},{9,13},{10,... | collective-permute-start | bytes 1327112 | tf_op jit(solution)/shard_map/ppermute | solution.py:19
  183.9 12.6 %collective-permute-start.30 = (f32[2,1,27,16,128]{4,3,2,0,1:T(8,128)S(1)}, f32[2,1,27,16,128]{4,3,2,0,1:T(8,128)S(1)}, u32[]{:S(2)}, u32[]{:S(2)}) collective-permute-start(f32[2,1,27,16,128]{4,3,2,0,1:T(8,128)S(1)} %slice_bitcast_fusion.2), channel_id=1, source_target_pairs={{0,2},{1,3},{2,0},{3,1},{4,6},{5,7},{6,4},{7,5},{8,10},{9,11},{10,... | collective-permute-start | bytes 1327112 | tf_op jit(solution)/shard_map/ppermute | solution.py:19
  195.3 6.7 %collective-permute-start.33 = (f32[1,1,27,16,128]{4,3,2,1,0:T(8,128)S(1)}, f32[1,1,27,16,128]{4,3,2,1,0:T(8,128)S(1)}, u32[]{:S(2)}, u32[]{:S(2)}) collective-permute-start(f32[1,1,27,16,128]{4,3,2,1,0:T(8,128)S(1)} %slice_bitcast_fusion.8), channel_id=1, source_target_pairs={{0,2},{1,3},{2,0},{3,1},{4,6},{5,7},{6,4},{7,5},{8,10},{9,11},{10,... | collective-permute-start | bytes 663560 | tf_op jit(solution)/shard_map/ppermute | solution.py:19
  196.7 6.4 %collective-permute-start.31 = (f32[1,1,27,16,128]{4,3,2,1,0:T(8,128)S(1)}, f32[1,1,27,16,128]{4,3,2,1,0:T(8,128)S(1)}, u32[]{:S(2)}, u32[]{:S(2)}) collective-permute-start(f32[1,1,27,16,128]{4,3,2,1,0:T(8,128)S(1)} %slice_bitcast_fusion.10), channel_id=1, source_target_pairs={{0,4},{1,5},{2,6},{3,7},{4,0},{5,1},{6,2},{7,3},{8,12},{9,13},{10,... | collective-permute-start | bytes 663560 | tf_op jit(solution)/shard_map/ppermute | solution.py:19
  205.6 8.0 %collective-permute-start.34 = (f32[16,16,128]{2,1,0:T(8,128)}, f32[16,16,128]{2,1,0:T(8,128)S(1)}, u32[]{:S(2)}, u32[]{:S(2)}) collective-permute-start(f32[16,16,128]{2,1,0:T(8,128)} %get-tuple-element.34), channel_id=1, source_target_pairs={{0,8},{8,0},{16,24},{24,16},{1,9},{9,1},{17,25},{25,17},{2,10},{10... | collective-permute-start | bytes 393224 | tf_op jit(solution)/shard_map/ppermute | solution.py:19
  207.0 6.6 %collective-permute-start.35 = (f32[4,16,128]{2,1,0:T(8,128)}, f32[4,16,128]{2,1,0:T(8,128)S(1)}, u32[]{:S(2)}, u32[]{:S(2)}) collective-permute-start(f32[4,16,128]{2,1,0:T(8,128)} %get-tuple-element.35), channel_id=1, source_target_pairs={{0,24},{8,16},{16,8},{24,0},{1,25},{9,17},{17,9},{25,1},{2,26},{10... | collective-permute-start | bytes 98312 | tf_op jit(solution)/shard_map/ppermute | solution.py:19
  208.8 4.8 %collective-permute-start.36 = (f32[2,16,128]{2,1,0:T(8,128)}, f32[2,16,128]{2,1,0:T(8,128)S(1)}, u32[]{:S(2)}, u32[]{:S(2)}) collective-permute-start(f32[2,16,128]{2,1,0:T(8,128)} %get-tuple-element.36), channel_id=1, source_target_pairs={{0,16},{8,24},{16,0},{24,8},{1,17},{9,25},{17,1},{25,9},{2,18},{10... | collective-permute-start | bytes 49160 | tf_op jit(solution)/shard_map/ppermute | solution.py:19
  217.2 10.0 %collective-permute-start.37 = (f32[16,32,128]{2,1,0:T(8,128)}, f32[16,32,128]{2,1,0:T(8,128)S(1)}, u32[]{:S(2)}, u32[]{:S(2)}) collective-permute-start(f32[16,32,128]{2,1,0:T(8,128)} %shard_map.63.refs_0_), channel_id=1, source_target_pairs={{0,8},{8,0},{16,24},{24,16},{1,9},{9,1},{17,25},{25,17},{2,10},{10... | collective-permute-start | bytes 786440 | tf_op jit(solution)/shard_map/ppermute | solution.py:19
  218.2 17.2 %collective-permute-start.38 = (f32[16,32,128]{2,1,0:T(8,128)}, f32[16,32,128]{2,1,0:T(8,128)S(1)}, u32[]{:S(2)}, u32[]{:S(2)}) collective-permute-start(f32[16,32,128]{2,1,0:T(8,128)} %shard_map.63.refs_0_), channel_id=1, source_target_pairs={{0,16},{8,24},{16,0},{24,8},{1,17},{9,25},{17,1},{25,9},{2,18},{10... | collective-permute-start | bytes 786440 | tf_op jit(solution)/shard_map/ppermute | solution.py:19
  219.0 21.4 %collective-permute-start.39 = (f32[16,32,128]{2,1,0:T(8,128)}, f32[16,32,128]{2,1,0:T(8,128)S(1)}, u32[]{:S(2)}, u32[]{:S(2)}) collective-permute-start(f32[16,32,128]{2,1,0:T(8,128)} %shard_map.63.refs_0_), channel_id=1, source_target_pairs={{0,24},{8,16},{16,8},{24,0},{1,25},{9,17},{17,9},{25,1},{2,26},{10... | collective-permute-start | bytes 786440 | tf_op jit(solution)/shard_map/ppermute | solution.py:19
  227.3 13.1 %copy-start.12 = (f32[16,32,128]{2,1,0:T(8,128)}, f32[16,32,128]{2,1,0:T(8,128)S(1)}, u32[]{:S(2)}) copy-start(f32[16,32,128]{2,1,0:T(8,128)S(1)} %collective-permute-done.37.refs_1_) | copy-start | bytes 786436
  235.4 5.0 %copy-start.13 = (f32[16,32,128]{2,1,0:T(8,128)}, f32[16,32,128]{2,1,0:T(8,128)S(1)}, u32[]{:S(2)}) copy-start(f32[16,32,128]{2,1,0:T(8,128)S(1)} %collective-permute-done.38.refs_2_) | copy-start | bytes 786436
  (13 other events, 10.2 us)

commit v7 on v6

--- a/solution.py
+++ b/solution.py
@@ -27,10 +27,9 @@
 
 def scatter_sum(kept, sent):
     bits = lax.axis_size("space").bit_length() - 1
-    blocks = kept + swap(sent, "space", 1)
-    middle = blocks.shape[1] // 2
     out = []
-    for part, order in zip((blocks[:, :middle], blocks[:, middle:]), orders(bits)):
+    for part, other, order in zip(kept, sent, orders(bits)):
+        part = part + swap(other, "space", 1)
         left = list(range(1, bits))
         for bit in order:
             low = 1 << left.index(bit)
@@ -191,7 +190,7 @@
 
 
 def back_kernel(rad, npieces, place, ky, bxt, note0, note1, kz, blurred, *refs):
-    pieces, (kept, sent, r, ya, yb, gm, gh, wxt) = refs[:npieces], refs[npieces:]
+    pieces, outs, (r, ya, yb, gm, gh, wxt) = refs[:npieces], refs[npieces : npieces + 4], refs[npieces + 4 :]
     yh = place[0]
     hy, nvi, hz = blurred.shape
     wy = gm.shape[0]
@@ -251,7 +250,9 @@
     lax.fori_loop(0, nviews // 2, views, 0)
 
     def store(out, row):
-        for c, ref in enumerate((kept, sent)):
+        h, row = divmod(row, half + rims)
+        for c in range(2):
+            ref = outs[2 * c + h]
             for k in range(ref.shape[0]):
                 first = (c * ref.shape[0] + k) * width
                 ref[k, row] = out[first : first + width]
@@ -488,7 +489,7 @@
     def back(blurred):
         return call(
             functools.partial(back_kernel, rad, nview),
-            [(nspace // 2, 2 * rows, width, hz)] * 2,
+            [(nspace // 2, rows, width, hz)] * 4,
             [(hy, nvi, hz), (hy + 2 * rad, width, hz), (hy + 2 * rad, width, hz), (wy, nvi, hz), (2 * rims, nvi, hz), pltpu.VMEM((nx, 3 * nvi), BF16)],
             2,
             (mxu, 4 * plane * (nspace * 2 * rows + 2 * hy * nviews)),
@@ -500,7 +501,8 @@
         if step:
             wide = gather(estimate)
         blurred = ahead(wide, () if step else tuple(pieces[1:3]), (mxu if step else 0, plane))
-        a, b = scatter_sum(*back(blurred))
+        sums = back(blurred)
+        a, b = scatter_sum(sums[:2], sums[2:])
         last = step == ITERS - 1
         if last:
             sizes, scratch = (rad, over, rad // group), []

time: 244 us -> 240 us (0.984)
  waiting for transfers between devices: 103 us -> 99.4 us
    ppermute x40 -> x42, waiting for transfers between devices: 103 us -> 99.4 us  [swap(): return lax.ppermute(value, axis, [(i, i ^ mask) for i in range(count)])]
    ppermute x40 -> x42, starting transfers between devices: 37.8 us -> 38.9 us  [swap(): return lax.ppermute(value, axis, [(i, i ^ mask) for i in range(count)])]
    unnamed x45 -> x49, local copies, waits for them, and re-layouts: 5.47 us -> 5.44 us
  transfers between devices with their start and end apart: 40 -> 42, of which waited for: 21 -> 21; matrix products, arithmetic and copies ran while one was open for 8% -> 9% of each run, Pallas kernels for 7% -> 7%
where the time goes in v7:
time: 240 us; the launch traced here: 239 us
  waiting for transfers between devices  99.4 us (41%)
  Pallas kernels  69.9 us (29%)
  starting transfers between devices  38.9 us (16%)
  other arithmetic  17.8 us (7%)
  local copies, waits for them, and re-layouts  12.6 us (5%)
    ppermute x42, waiting for transfers between devices, swap(): return lax.ppermute(value, axis, [(i, i ^ mask) for i in range(count)])  99.4 us
    pallas_call x9, Pallas kernels, call(): pl.pallas_call(kernel, out_shape=[jax.ShapeDtypeStruct(shape, F32) for sh...  64.7 us
    ppermute x42, starting transfers between devices, swap(): return lax.ppermute(value, axis, [(i, i ^ mask) for i in range(count)])  38.9 us
    unnamed x49, local copies, waits for them, and re-layouts  5.44 us
    pallas_call x1, Pallas kernels, body(): pl.pallas_call(functools.partial(bands_kernel, rad), out_shape=[jax.Shape...  5.22 us
  transfers between devices with their start and end apart: 42, of which 21 were waited for; matrix products, arithmetic and copies ran while one was open for 9% of the time, Pallas kernels for 7%

profile of v7, /device:TPU:8, one launch (start us, length us, event | category | flops | bytes accessed | tf_op | source)
XLA Modules:
  0.0 239.0 jit_solution(15144825374661757730)
XLA Ops:
  2.4 3.0 %collective-permute-start.1 = (f32[2,128]{1,0:T(2,128)S(1)}, f32[2,128]{1,0:T(2,128)S(1)}, u32[]{:S(2)}, u32[]{:S(2)}) collective-permute-start(f32[2,128]{1,0:T(2,128)S(1)} %select_maximum_fusion), channel_id=1, source_target_pairs={{0,16},{8,24},{16,0},{24,8},{1,17},{9,25},{17,1},{25,9},{2,18},{10... | collective-permute-start | bytes 3080 | tf_op jit(solution)/shard_map/ppermute | solution.py:19
  8.0 1.7 pad_maximum_fusion.5
  9.7 1.5 collective-permute-start.9
  12.2 1.7 pad_maximum_fusion.4
  13.9 1.5 collective-permute-start.6
  15.5 1.4 constant_dynamic-slice_fusion
  17.5 1.3 collective-permute-start.12
  18.8 2.2 collective-permute-start.13
  24.7 1.6 collective-permute-start.3
  26.3 7.1 %collective-permute-done.10 = f32[1,1,2,27,16,128]{5,4,3,2,1,0:T(8,128)S(1)} collective-permute-done((f32[1,1,2,27,16,128]{5,4,3,2,1,0:T(8,128)S(1)}, f32[1,1,2,27,16,128]{5,4,3,2,1,0:T(8,128)S(1)}, u32[]{:S(2)}, u32[]{:S(2)}) %collective-permute-start.10) | collective-permute-done | bytes 442400 | tf_op jit(solution)/shard_map/ppermute | solution.py:19
  36.8 2.9 %collective-permute-done.4 = f32[2,1,1,1,16,128]{5,4,0,3,2,1:T(8,128)S(1)} collective-permute-done((f32[2,1,1,1,16,128]{5,4,0,3,2,1:T(8,128)S(1)}, f32[2,1,1,1,16,128]{5,4,0,3,2,1:T(8,128)S(1)}, u32[]{:S(2)}, u32[]{:S(2)}) %collective-permute-start.4) | collective-permute-done | bytes 16416 | tf_op jit(solution)/shard_map/ppermute | solution.py:19
  41.6 5.2 %shard_map.55 = (bf16[128,384]{1,0:T(8,128)(2,1)}, f32[128,128]{1,0:T(8,128)}, bf16[8,512,128]{2,1,0:T(8,128)(2,1)}, bf16[8,384,256]{2,1,0:T(8,128)(2,1)}) custom-call(s32[3]{0:T(128)} %pad_add_fusion.place, s32[8]{0:T(128)} %and_select_fusion.slab, f32[8,96]{1,0:T(8,128)} %slice_divide_fusion.kern), custom_call_target="tpu_custom_call" | custom-call | flops 4194304 | bytes 2097152 | tf_op jit(solution)/shard_map/pallas_call | solution.py:460
  46.8 8.9 %collective-permute-done.13.refs_1_.refs_2_ = f32[2,16,32,128]{3,2,1,0:T(8,128)S(1)} collective-permute-done((f32[2,16,32,128]{3,2,1,0:T(8,128)}, f32[2,16,32,128]{3,2,1,0:T(8,128)S(1)}, u32[]{:S(2)}, u32[]{:S(2)}) %collective-permute-start.13) | collective-permute-done | bytes 524320 | tf_op jit(solution)/shard_map/ppermute | solution.py:19
  56.4 12.5 %shard_map.56.blurred = f32[32,128,128]{2,1,0:T(8,128)} custom-call(s32[3]{0:T(128)} %pad_add_fusion.place, f32[8,32]{1,0:T(8,128)} %fusion.18.ky, bf16[128,384]{1,0:T(8,128)(2,1)} %get-tuple-element.27.wx, bf16[8,512,128]{2,1,0:T(8,128)(2,1)} %get-tuple-element.28.kz, f32[4,27,16,128]{3,2,1,0:T(8,128)} %bitcast.18.a0, ...), custom_call_target="tpu_custom_call" | custom-call | bytes 2048 | tf_op jit(solution)/shard_map/pallas_call | solution.py:397
  69.8 14.2 %shard_map.57 = (f32[4,27,16,128]{3,2,1,0:T(8,128)}, f32[4,27,16,128]{3,2,1,0:T(8,128)}, f32[4,27,16,128]{3,2,1,0:T(8,128)}, f32[4,27,16,128]{3,2,1,0:T(8,128)}) custom-call(s32[3]{0:T(128)} %pad_add_fusion.place, f32[8,32]{1,0:T(8,128)} %fusion.18.ky, f32[128,128]{1,0:T(8,128)} %get-tuple-element.25.bxt, f32[4,1,16,128]{3,2,1,0:T(8,128)} %bitcast.164, ...), custom_call_target="tpu_custom_call" | custom-call | flops 339738624 | bytes 7733248 | tf_op jit(solution)/shard_map/pallas_call | solution.py:397
  84.4 2.1 collective-permute-done.18
  86.6 1.3 add.94
  88.7 11.4 %collective-permute-done.19 = f32[1,2,27,16,128]{4,3,2,1,0:T(8,128)S(1)} collective-permute-done((f32[1,2,27,16,128]{4,3,2,1,0:T(8,128)S(1)}, f32[1,2,27,16,128]{4,3,2,1,0:T(8,128)S(1)}, u32[]{:S(2)}, u32[]{:S(2)}) %collective-permute-start.19) | collective-permute-done | bytes 442400 | tf_op jit(solution)/shard_map/ppermute | solution.py:19
  100.9 1.4 collective-permute-start.17
  102.3 4.7 %collective-permute-done.20 = f32[1,1,27,16,128]{4,3,2,1,0:T(8,128)S(1)} collective-permute-done((f32[1,1,27,16,128]{4,3,2,1,0:T(8,128)S(1)}, f32[1,1,27,16,128]{4,3,2,1,0:T(8,128)S(1)}, u32[]{:S(2)}, u32[]{:S(2)}) %collective-permute-start.20) | collective-permute-done | bytes 221216 | tf_op jit(solution)/shard_map/ppermute | solution.py:19
  108.4 2.5 %shard_map.58 = (f32[36,16,128]{2,1,0:T(8,128)}, f32[12,16,128]{2,1,0:T(8,128)}, f32[8,16,128]{2,1,0:T(8,128)}) custom-call(s32[3]{0:T(128)} %pad_add_fusion.place, f32[27,16,128]{2,1,0:T(8,128)} %fusion.15.a, f32[27,16,128]{2,1,0:T(8,128)} %fusion.13.b), custom_call_target="tpu_custom_call" | custom-call | flops 2048 | bytes 884736 | tf_op jit(solution)/shard_map/pallas_call | solution.py:397
  110.9 3.8 %collective-permute-start.22 = (f32[12,16,128]{2,1,0:T(8,128)}, f32[12,16,128]{2,1,0:T(8,128)S(1)}, u32[]{:S(2)}, u32[]{:S(2)}) collective-permute-start(f32[12,16,128]{2,1,0:T(8,128)} %get-tuple-element.34), channel_id=1, source_target_pairs={{0,24},{8,16},{16,8},{24,0},{1,25},{9,17},{17,9},{25,1},{2,26},{10... | collective-permute-start | bytes 294920 | tf_op jit(solution)/shard_map/ppermute | solution.py:19
  115.2 8.2 %collective-permute-done.23.fc = f32[8,16,128]{2,1,0:T(8,128)S(1)} collective-permute-done((f32[8,16,128]{2,1,0:T(8,128)}, f32[8,16,128]{2,1,0:T(8,128)S(1)}, u32[]{:S(2)}, u32[]{:S(2)}) %collective-permute-start.23) | collective-permute-done | bytes 65568 | tf_op jit(solution)/shard_map/ppermute | solution.py:19
  124.2 2.4 %shard_map.59 = (f32[27,16,128]{2,1,0:T(8,128)}, f32[27,16,128]{2,1,0:T(8,128)}) custom-call(s32[3]{0:T(128)} %pad_add_fusion.place, f32[27,16,128]{2,1,0:T(8,128)} %fusion.15.a, f32[27,16,128]{2,1,0:T(8,128)} %fusion.13.b, f32[36,16,128]{2,1,0:T(8,128)} %copy-done.13, f32[12,16,128]{2,1,0:T(8,128)} %copy-done.19, f32[8,16,128]{2,1,0:T(8,128)} %copy-done.20, ...), custom_call_target="tpu_custom_call" | custom-call | flops 2048 | bytes 1769472 | tf_op jit(solution)/shard_map/pallas_call | solution.py:397
  128.4 4.4 %collective-permute-done.27 = f32[1,1,1,27,16,128]{5,4,3,2,1,0:T(8,128)S(1)} collective-permute-done((f32[1,1,1,27,16,128]{5,4,3,2,1,0:T(8,128)}, f32[1,1,1,27,16,128]{5,4,3,2,1,0:T(8,128)S(1)}, u32[]{:S(2)}, u32[]{:S(2)}) %collective-permute-start.27) | collective-permute-done | bytes 221216 | tf_op jit(solution)/shard_map/ppermute | solution.py:19
  135.8 1.6 collective-permute-start.25
  137.4 5.8 %collective-permute-done.28 = f32[1,1,2,27,16,128]{5,4,3,2,1,0:T(8,128)S(1)} collective-permute-done((f32[1,1,2,27,16,128]{5,4,3,2,1,0:T(8,128)S(1)}, f32[1,1,2,27,16,128]{5,4,3,2,1,0:T(8,128)S(1)}, u32[]{:S(2)}, u32[]{:S(2)}) %collective-permute-start.28) | collective-permute-done | bytes 442400 | tf_op jit(solution)/shard_map/ppermute | solution.py:19
  144.4 1.4 collective-permute-done.29.b1
  145.7 1.3 collective-permute-done.26.a1
  147.9 12.5 %shard_map.60.blurred = f32[32,128,128]{2,1,0:T(8,128)} custom-call(s32[3]{0:T(128)} %pad_add_fusion.place, f32[8,32]{1,0:T(8,128)} %fusion.18.ky, bf16[128,384]{1,0:T(8,128)(2,1)} %get-tuple-element.27.wx, bf16[8,512,128]{2,1,0:T(8,128)(2,1)} %get-tuple-element.28.kz, f32[4,27,16,128]{3,2,1,0:T(8,128)} %bitcast.149, f32[4,27,16,128]{3,2,1,0:T(8,128)} %copy-done.9, ...), custom_call_target="tpu_custom_call" | custom-call | flops 339738624 | bytes 2048 | tf_op jit(solution)/shard_map/pallas_call | solution.py:397
  160.5 14.2 %shard_map.61 = (f32[4,27,16,128]{3,2,1,0:T(8,128)}, f32[4,27,16,128]{3,2,1,0:T(8,128)}, f32[4,27,16,128]{3,2,1,0:T(8,128)}, f32[4,27,16,128]{3,2,1,0:T(8,128)}) custom-call(s32[3]{0:T(128)} %pad_add_fusion.place, f32[8,32]{1,0:T(8,128)} %fusion.18.ky, f32[128,128]{1,0:T(8,128)} %get-tuple-element.25.bxt, f32[4,1,16,128]{3,2,1,0:T(8,128)} %bitcast.165, ...), custom_call_target="tpu_custom_call" | custom-call | flops 339738624 | bytes 7733248 | tf_op jit(solution)/shard_map/pallas_call | solution.py:397
  175.2 2.1 collective-permute-done.33
  177.3 1.3 add.100
  179.7 1.3 collective-permute-start.31
  181.0 9.9 %collective-permute-done.34 = f32[1,2,27,16,128]{4,3,2,1,0:T(8,128)S(1)} collective-permute-done((f32[1,2,27,16,128]{4,3,2,1,0:T(8,128)S(1)}, f32[1,2,27,16,128]{4,3,2,1,0:T(8,128)S(1)}, u32[]{:S(2)}, u32[]{:S(2)}) %collective-permute-start.34) | collective-permute-done | bytes 442400 | tf_op jit(solution)/shard_map/ppermute | solution.py:19
  191.0 1.4 collective-permute-start.35
  193.3 4.4 %collective-permute-done.35 = f32[1,1,27,16,128]{4,3,2,1,0:T(8,128)S(1)} collective-permute-done((f32[1,1,27,16,128]{4,3,2,1,0:T(8,128)S(1)}, f32[1,1,27,16,128]{4,3,2,1,0:T(8,128)S(1)}, u32[]{:S(2)}, u32[]{:S(2)}) %collective-permute-start.35) | collective-permute-done | bytes 221216 | tf_op jit(solution)/shard_map/ppermute | solution.py:19
  199.6 1.7 shard_map.62
  201.3 1.4 collective-permute-start.36
  202.7 1.7 collective-permute-start.37
  204.4 1.3 collective-permute-start.38
  205.7 3.5 %collective-permute-done.38.fc = f32[2,16,128]{2,1,0:T(8,128)S(1)} collective-permute-done((f32[2,16,128]{2,1,0:T(8,128)}, f32[2,16,128]{2,1,0:T(8,128)S(1)}, u32[]{:S(2)}, u32[]{:S(2)}) %collective-permute-start.38) | collective-permute-done | bytes 16416 | tf_op jit(solution)/shard_map/ppermute | solution.py:19
  210.5 2.4 shard_map.63.refs_0_
  214.7 1.7 collective-permute-start.41
  216.4 6.7 %collective-permute-done.39.refs_1_ = f32[16,32,128]{2,1,0:T(8,128)S(1)} collective-permute-done((f32[16,32,128]{2,1,0:T(8,128)}, f32[16,32,128]{2,1,0:T(8,128)S(1)}, u32[]{:S(2)}, u32[]{:S(2)}) %collective-permute-start.39) | collective-permute-done | bytes 262176 | tf_op jit(solution)/shard_map/ppermute | solution.py:19
  223.1 7.9 %collective-permute-done.40.refs_2_ = f32[16,32,128]{2,1,0:T(8,128)S(1)} collective-permute-done((f32[16,32,128]{2,1,0:T(8,128)}, f32[16,32,128]{2,1,0:T(8,128)S(1)}, u32[]{:S(2)}, u32[]{:S(2)}) %collective-permute-start.40) | collective-permute-done | bytes 262176 | tf_op jit(solution)/shard_map/ppermute | solution.py:19
  231.0 5.0 %collective-permute-done.41.refs_3_ = f32[16,32,128]{2,1,0:T(8,128)S(1)} collective-permute-done((f32[16,32,128]{2,1,0:T(8,128)}, f32[16,32,128]{2,1,0:T(8,128)S(1)}, u32[]{:S(2)}, u32[]{:S(2)}) %collective-permute-start.41) | collective-permute-done | bytes 262176 | tf_op jit(solution)/shard_map/ppermute | solution.py:19
  236.7 2.3 shard_map.64
  (158 shorter events, 37.0 us)
Async XLA Ops:
  0.0 5.9 %copy-start = (f32[16,64,256]{2,1,0:T(8,128)S(1)}, f32[16,64,256]{2,1,0:T(8,128)}, u32[]{:S(2)}) copy-start(f32[16,64,256]{2,1,0:T(8,128)} %param.5) | copy-start | bytes 3145732
  2.4 15.1 %collective-permute-start = (f32[2,128]{1,0:T(2,128)S(1)}, f32[2,128]{1,0:T(2,128)S(1)}, u32[]{:S(2)}, u32[]{:S(2)}) collective-permute-start(f32[2,128]{1,0:T(2,128)S(1)} %select_maximum_fusion), channel_id=1, source_target_pairs={{0,8},{8,0},{16,24},{24,16},{1,9},{9,1},{17,25},{25,17},{2,10},{10... | collective-permute-start | bytes 3080 | tf_op jit(solution)/shard_map/ppermute | solution.py:19
  2.4 16.4 %collective-permute-start.1 = (f32[2,128]{1,0:T(2,128)S(1)}, f32[2,128]{1,0:T(2,128)S(1)}, u32[]{:S(2)}, u32[]{:S(2)}) collective-permute-start(f32[2,128]{1,0:T(2,128)S(1)} %select_maximum_fusion), channel_id=1, source_target_pairs={{0,16},{8,24},{16,0},{24,8},{1,17},{9,25},{17,1},{25,9},{2,18},{10... | collective-permute-start | bytes 3080 | tf_op jit(solution)/shard_map/ppermute | solution.py:19
  5.4 15.6 %collective-permute-start.2 = (f32[2,128]{1,0:T(2,128)S(1)}, f32[2,128]{1,0:T(2,128)S(1)}, u32[]{:S(2)}, u32[]{:S(2)}) collective-permute-start(f32[2,128]{1,0:T(2,128)S(1)} %select_maximum_fusion), channel_id=1, source_target_pairs={{0,24},{8,16},{16,8},{24,0},{1,25},{9,17},{17,9},{25,1},{2,26},{10... | collective-permute-start | bytes 3080 | tf_op jit(solution)/shard_map/ppermute | solution.py:19
  6.2 9.3 %copy-start.6 = (f32[2,16,64,256]{3,2,1,0:T(8,128)S(1)}, f32[2,16,64,256]{3,2,1,0:T(8,128)}, u32[]{:S(2)}) copy-start(f32[2,16,64,256]{3,2,1,0:T(8,128)} %param.6) | copy-start | bytes 6291460
  9.7 11.7 %collective-permute-start.9 = (f32[1,1,1,27,16,128]{5,4,3,2,1,0:T(8,128)S(1)}, f32[1,1,1,27,16,128]{5,4,3,2,1,0:T(8,128)}, u32[]{:S(2)}, u32[]{:S(2)}) collective-permute-start(f32[1,1,1,27,16,128]{5,4,3,2,1,0:T(8,128)S(1)} %get-tuple-element.54), channel_id=1, source_target_pairs={{0,2},{1,3},{2,0},{3,1},{4,6},{5,7},{6,4},{7,5},{8,10},{9,11},{10,... | collective-permute-start | bytes 663560 | tf_op jit(solution)/shard_map/ppermute | solution.py:19
  13.9 9.0 %collective-permute-start.6 = (f32[1,1,1,27,16,128]{5,4,3,2,1,0:T(8,128)}, f32[1,1,1,27,16,128]{5,4,3,2,1,0:T(8,128)}, u32[]{:S(2)}, u32[]{:S(2)}) collective-permute-start(f32[1,1,1,27,16,128]{5,4,3,2,1,0:T(8,128)} %get-tuple-element.56), channel_id=1, source_target_pairs={{0,4},{1,5},{2,6},{3,7},{4,0},{5,1},{6,2},{7,3},{8,12},{9,13},{10,... | collective-permute-start | bytes 663560 | tf_op jit(solution)/shard_map/ppermute | solution.py:19
  17.5 23.3 %collective-permute-start.12 = (f32[2,16,32,128]{3,2,1,0:T(8,128)}, f32[2,16,32,128]{3,2,1,0:T(8,128)S(1)}, u32[]{:S(2)}, u32[]{:S(2)}) collective-permute-start(f32[2,16,32,128]{3,2,1,0:T(8,128)} %get-tuple-element.47), channel_id=1, source_target_pairs={{0,8},{8,0},{16,24},{24,16},{1,9},{9,1},{17,25},{25,17},{2,10},{10... | collective-permute-start | bytes 1572872 | tf_op jit(solution)/shard_map/ppermute | solution.py:19
  18.8 36.8 %collective-permute-start.13 = (f32[2,16,32,128]{3,2,1,0:T(8,128)}, f32[2,16,32,128]{3,2,1,0:T(8,128)S(1)}, u32[]{:S(2)}, u32[]{:S(2)}) collective-permute-start(f32[2,16,32,128]{3,2,1,0:T(8,128)} %get-tuple-element.46), channel_id=1, source_target_pairs={{0,16},{8,24},{16,0},{24,8},{1,17},{9,25},{17,1},{25,9},{2,18},{10... | collective-permute-start | bytes 1572872 | tf_op jit(solution)/shard_map/ppermute | solution.py:19
  22.4 11.0 %collective-permute-start.10 = (f32[1,1,2,27,16,128]{5,4,3,2,1,0:T(8,128)S(1)}, f32[1,1,2,27,16,128]{5,4,3,2,1,0:T(8,128)S(1)}, u32[]{:S(2)}, u32[]{:S(2)}) collective-permute-start(f32[1,1,2,27,16,128]{5,4,3,2,1,0:T(8,128)S(1)} %maximum_bitcast_fusion.1), channel_id=1, source_target_pairs={{0,4},{1,5},{2,6},{3,7},{4,0},{5,1},{6,2},{7,3},{8,12},{9,13},{10,... | collective-permute-start | bytes 1327112 | tf_op jit(solution)/shard_map/ppermute | solution.py:19
  24.0 10.0 %collective-permute-start.7 = (f32[2,1,1,27,16,128]{5,4,3,0,2,1:T(8,128)S(1)}, f32[2,1,1,27,16,128]{5,4,3,0,2,1:T(8,128)S(1)}, u32[]{:S(2)}, u32[]{:S(2)}) collective-permute-start(f32[2,1,1,27,16,128]{5,4,3,0,2,1:T(8,128)S(1)} %maximum_bitcast_fusion), channel_id=1, source_target_pairs={{0,2},{1,3},{2,0},{3,1},{4,6},{5,7},{6,4},{7,5},{8,10},{9,11},{10,... | collective-permute-start | bytes 1327112 | tf_op jit(solution)/shard_map/ppermute | solution.py:19
  24.7 11.1 %collective-permute-start.3 = (f32[1,1,1,1,16,128]{4,5,3,2,1,0:T(8,128)S(1)}, f32[1,1,1,1,16,128]{4,5,3,2,1,0:T(8,128)S(1)}, u32[]{:S(2)}, u32[]{:S(2)}) collective-permute-start(f32[1,1,1,1,16,128]{4,5,3,2,1,0:T(8,128)S(1)} %pad_bitcast_fusion), channel_id=1, source_target_pairs={{0,4},{1,5},{2,6},{3,7},{4,0},{5,1},{6,2},{7,3},{8,12},{9,13},{10,... | collective-permute-start | bytes 24584 | tf_op jit(solution)/shard_map/ppermute | solution.py:19
  33.4 22.2 %copy-start.3 = (f32[1,2,2,27,16,128]{5,4,3,2,1,0:T(8,128)}, f32[1,2,2,27,16,128]{5,4,3,2,1,0:T(8,128)S(1)}, u32[]{:S(2)}) copy-start(f32[1,2,2,27,16,128]{5,4,3,2,1,0:T(8,128)S(1)} %pad_maximum_fusion.1) | copy-start | bytes 2654212
  33.4 22.2 %collective-permute-start.11 = (f32[4,27,16,128]{3,2,1,0:T(8,128)S(1)}, f32[4,27,16,128]{3,2,1,0:T(8,128)}, u32[]{:S(2)}, u32[]{:S(2)}) collective-permute-start(f32[4,27,16,128]{3,2,1,0:T(8,128)S(1)} %bitcast.144), channel_id=1, source_target_pairs={{0,1},{1,0},{2,3},{3,2},{4,5},{5,4},{6,7},{7,6},{8,9},{9,8},{10,11... | collective-permute-start | bytes 2654216 | tf_op jit(solution)/shard_map/ppermute | solution.py:19
  35.1 20.5 %collective-permute-start.8 = (f32[4,27,16,128]{3,2,1,0:T(8,128)}, f32[4,27,16,128]{3,2,1,0:T(8,128)}, u32[]{:S(2)}, u32[]{:S(2)}) collective-permute-start(f32[4,27,16,128]{3,2,1,0:T(8,128)} %bitcast.18.a0), channel_id=1, source_target_pairs={{0,1},{1,0},{2,3},{3,2},{4,5},{5,4},{6,7},{7,6},{8,9},{9,8},{10,11... | collective-permute-start | bytes 2654216 | tf_op jit(solution)/shard_map/ppermute | solution.py:19
  35.9 3.8 %collective-permute-start.4 = (f32[2,1,1,1,16,128]{5,4,0,3,2,1:T(8,128)S(1)}, f32[2,1,1,1,16,128]{5,4,0,3,2,1:T(8,128)S(1)}, u32[]{:S(2)}, u32[]{:S(2)}) collective-permute-start(f32[2,1,1,1,16,128]{5,4,0,3,2,1:T(8,128)S(1)} %get-tuple-element.58), channel_id=1, source_target_pairs={{0,2},{1,3},{2,0},{3,1},{4,6},{5,7},{6,4},{7,5},{8,10},{9,11},{10,... | collective-permute-start | bytes 49160 | tf_op jit(solution)/shard_map/ppermute | solution.py:19
  39.6 29.3 %collective-permute-start.14 = (f32[2,16,32,128]{3,2,1,0:T(8,128)}, f32[2,16,32,128]{3,2,1,0:T(8,128)S(1)}, u32[]{:S(2)}, u32[]{:S(2)}) collective-permute-start(f32[2,16,32,128]{3,2,1,0:T(8,128)} %get-tuple-element.45), channel_id=1, source_target_pairs={{0,24},{8,16},{16,8},{24,0},{1,25},{9,17},{17,9},{25,1},{2,26},{10... | collective-permute-start | bytes 1572872 | tf_op jit(solution)/shard_map/ppermute | solution.py:19
  40.8 28.2 %copy-start.12 = (f32[2,2,1,1,16,128]{5,4,3,2,1,0:T(8,128)}, f32[2,2,1,1,16,128]{5,4,3,2,1,0:T(8,128)S(1)}, u32[]{:S(2)}) copy-start(f32[2,2,1,1,16,128]{5,4,3,2,1,0:T(8,128)S(1)} %pad_maximum_fusion.6) | copy-start | bytes 98308
  40.8 14.8 %copy-start.1 = (f32[2,16,32,128]{3,2,1,0:T(8,128)}, f32[2,16,32,128]{3,2,1,0:T(8,128)S(1)}, u32[]{:S(2)}) copy-start(f32[2,16,32,128]{3,2,1,0:T(8,128)S(1)} %collective-permute-done.12.refs_0_.refs_1_) | copy-start | bytes 1572868
  40.8 28.1 %collective-permute-start.5 = (f32[4,1,16,128]{3,2,1,0:T(8,128)S(1)}, f32[4,1,16,128]{3,2,1,0:T(8,128)S(1)}, u32[]{:S(2)}, u32[]{:S(2)}) collective-permute-start(f32[4,1,16,128]{3,2,1,0:T(8,128)S(1)} %bitcast.163), channel_id=1, source_target_pairs={{0,1},{1,0},{2,3},{3,2},{4,5},{5,4},{6,7},{7,6},{8,9},{9,8},{10,11... | collective-permute-start | bytes 98312 | tf_op jit(solution)/shard_map/ppermute | solution.py:19
  83.9 2.6 %collective-permute-start.18 = (f32[4,27,16,128]{3,2,1,0:T(8,128)}, f32[4,27,16,128]{3,2,1,0:T(8,128)S(1)}, u32[]{:S(2)}, u32[]{:S(2)}) collective-permute-start(f32[4,27,16,128]{3,2,1,0:T(8,128)} %get-tuple-element.32), channel_id=1, source_target_pairs={{0,1},{1,0},{2,3},{3,2},{4,5},{5,4},{6,7},{7,6},{8,9},{9,8},{10,11... | collective-permute-start | bytes 2654216 | tf_op jit(solution)/shard_map/ppermute | solution.py:19
  83.9 4.0 %collective-permute-start.15 = (f32[4,27,16,128]{3,2,1,0:T(8,128)}, f32[4,27,16,128]{3,2,1,0:T(8,128)S(1)}, u32[]{:S(2)}, u32[]{:S(2)}) collective-permute-start(f32[4,27,16,128]{3,2,1,0:T(8,128)} %get-tuple-element.30), channel_id=1, source_target_pairs={{0,1},{1,0},{2,3},{3,2},{4,5},{5,4},{6,7},{7,6},{8,9},{9,8},{10,11... | collective-permute-start | bytes 2654216 | tf_op jit(solution)/shard_map/ppermute | solution.py:19
  87.9 12.3 %collective-permute-start.19 = (f32[1,2,27,16,128]{4,3,2,1,0:T(8,128)S(1)}, f32[1,2,27,16,128]{4,3,2,1,0:T(8,128)S(1)}, u32[]{:S(2)}, u32[]{:S(2)}) collective-permute-start(f32[1,2,27,16,128]{4,3,2,1,0:T(8,128)S(1)} %slice_bitcast_fusion.4), channel_id=1, source_target_pairs={{0,4},{1,5},{2,6},{3,7},{4,0},{5,1},{6,2},{7,3},{8,12},{9,13},{10,... | collective-permute-start | bytes 1327112 | tf_op jit(solution)/shard_map/ppermute | solution.py:19
  88.1 12.7 %collective-permute-start.16 = (f32[2,1,27,16,128]{4,3,2,0,1:T(8,128)S(1)}, f32[2,1,27,16,128]{4,3,2,0,1:T(8,128)S(1)}, u32[]{:S(2)}, u32[]{:S(2)}) collective-permute-start(f32[2,1,27,16,128]{4,3,2,0,1:T(8,128)S(1)} %slice_bitcast_fusion.6), channel_id=1, source_target_pairs={{0,2},{1,3},{2,0},{3,1},{4,6},{5,7},{6,4},{7,5},{8,10},{9,11},{10,... | collective-permute-start | bytes 1327112 | tf_op jit(solution)/shard_map/ppermute | solution.py:19
  100.2 6.7 %collective-permute-start.20 = (f32[1,1,27,16,128]{4,3,2,1,0:T(8,128)S(1)}, f32[1,1,27,16,128]{4,3,2,1,0:T(8,128)S(1)}, u32[]{:S(2)}, u32[]{:S(2)}) collective-permute-start(f32[1,1,27,16,128]{4,3,2,1,0:T(8,128)S(1)} %slice_bitcast_fusion.12), channel_id=1, source_target_pairs={{0,2},{1,3},{2,0},{3,1},{4,6},{5,7},{6,4},{7,5},{8,10},{9,11},{10,... | collective-permute-start | bytes 663560 | tf_op jit(solution)/shard_map/ppermute | solution.py:19
  100.9 6.7 %collective-permute-start.17 = (f32[1,1,27,16,128]{4,3,2,1,0:T(8,128)S(1)}, f32[1,1,27,16,128]{4,3,2,1,0:T(8,128)S(1)}, u32[]{:S(2)}, u32[]{:S(2)}) collective-permute-start(f32[1,1,27,16,128]{4,3,2,1,0:T(8,128)S(1)} %slice_bitcast_fusion.14), channel_id=1, source_target_pairs={{0,4},{1,5},{2,6},{3,7},{4,0},{5,1},{6,2},{7,3},{8,12},{9,13},{10,... | collective-permute-start | bytes 663560 | tf_op jit(solution)/shard_map/ppermute | solution.py:19
  110.9 12.6 %collective-permute-start.21 = (f32[36,16,128]{2,1,0:T(8,128)}, f32[36,16,128]{2,1,0:T(8,128)S(1)}, u32[]{:S(2)}, u32[]{:S(2)}) collective-permute-start(f32[36,16,128]{2,1,0:T(8,128)} %get-tuple-element.33), channel_id=1, source_target_pairs={{0,8},{8,0},{16,24},{24,16},{1,9},{9,1},{17,25},{25,17},{2,10},{10... | collective-permute-start | bytes 884744 | tf_op jit(solution)/shard_map/ppermute | solution.py:19
  110.9 12.6 %collective-permute-start.22 = (f32[12,16,128]{2,1,0:T(8,128)}, f32[12,16,128]{2,1,0:T(8,128)S(1)}, u32[]{:S(2)}, u32[]{:S(2)}) collective-permute-start(f32[12,16,128]{2,1,0:T(8,128)} %get-tuple-element.34), channel_id=1, source_target_pairs={{0,24},{8,16},{16,8},{24,0},{1,25},{9,17},{17,9},{25,1},{2,26},{10... | collective-permute-start | bytes 294920 | tf_op jit(solution)/shard_map/ppermute | solution.py:19
  114.7 8.7 %collective-permute-start.23 = (f32[8,16,128]{2,1,0:T(8,128)}, f32[8,16,128]{2,1,0:T(8,128)S(1)}, u32[]{:S(2)}, u32[]{:S(2)}) collective-permute-start(f32[8,16,128]{2,1,0:T(8,128)} %get-tuple-element.35), channel_id=1, source_target_pairs={{0,16},{8,24},{16,0},{24,8},{1,17},{9,25},{17,1},{25,9},{2,18},{10... | collective-permute-start | bytes 196616 | tf_op jit(solution)/shard_map/ppermute | solution.py:19
  126.7 6.1 %collective-permute-start.27 = (f32[1,1,1,27,16,128]{5,4,3,2,1,0:T(8,128)}, f32[1,1,1,27,16,128]{5,4,3,2,1,0:T(8,128)S(1)}, u32[]{:S(2)}, u32[]{:S(2)}) collective-permute-start(f32[1,1,1,27,16,128]{5,4,3,2,1,0:T(8,128)} %bitcast.161), channel_id=1, source_target_pairs={{0,2},{1,3},{2,0},{3,1},{4,6},{5,7},{6,4},{7,5},{8,10},{9,11},{10,... | collective-permute-start | bytes 663560 | tf_op jit(solution)/shard_map/ppermute | solution.py:19
  127.6 7.2 %collective-permute-start.24 = (f32[1,1,1,27,16,128]{5,4,3,2,1,0:T(8,128)}, f32[1,1,1,27,16,128]{5,4,3,2,1,0:T(8,128)S(1)}, u32[]{:S(2)}, u32[]{:S(2)}) collective-permute-start(f32[1,1,1,27,16,128]{5,4,3,2,1,0:T(8,128)} %bitcast.159), channel_id=1, source_target_pairs={{0,4},{1,5},{2,6},{3,7},{4,0},{5,1},{6,2},{7,3},{8,12},{9,13},{10,... | collective-permute-start | bytes 663560 | tf_op jit(solution)/shard_map/ppermute | solution.py:19
  133.8 9.4 %collective-permute-start.28 = (f32[1,1,2,27,16,128]{5,4,3,2,1,0:T(8,128)S(1)}, f32[1,1,2,27,16,128]{5,4,3,2,1,0:T(8,128)S(1)}, u32[]{:S(2)}, u32[]{:S(2)}) collective-permute-start(f32[1,1,2,27,16,128]{5,4,3,2,1,0:T(8,128)S(1)} %maximum_bitcast_fusion.3), channel_id=1, source_target_pairs={{0,4},{1,5},{2,6},{3,7},{4,0},{5,1},{6,2},{7,3},{8,12},{9,13},{10,... | collective-permute-start | bytes 1327112 | tf_op jit(solution)/shard_map/ppermute | solution.py:19
  135.8 8.4 %collective-permute-start.25 = (f32[2,1,1,27,16,128]{5,4,3,0,2,1:T(8,128)S(1)}, f32[2,1,1,27,16,128]{5,4,3,0,2,1:T(8,128)S(1)}, u32[]{:S(2)}, u32[]{:S(2)}) collective-permute-start(f32[2,1,1,27,16,128]{5,4,3,0,2,1:T(8,128)S(1)} %maximum_bitcast_fusion.2), channel_id=1, source_target_pairs={{0,2},{1,3},{2,0},{3,1},{4,6},{5,7},{6,4},{7,5},{8,10},{9,11},{10,... | collective-permute-start | bytes 1327112 | tf_op jit(solution)/shard_map/ppermute | solution.py:19
  143.3 2.5 %collective-permute-start.29 = (f32[4,27,16,128]{3,2,1,0:T(8,128)S(1)}, f32[4,27,16,128]{3,2,1,0:T(8,128)S(1)}, u32[]{:S(2)}, u32[]{:S(2)}) collective-permute-start(f32[4,27,16,128]{3,2,1,0:T(8,128)S(1)} %bitcast.146), channel_id=1, source_target_pairs={{0,1},{1,0},{2,3},{3,2},{4,5},{5,4},{6,7},{7,6},{8,9},{9,8},{10,11... | collective-permute-start | bytes 2654216 | tf_op jit(solution)/shard_map/ppermute | solution.py:19
  144.3 2.7 %collective-permute-start.26 = (f32[4,27,16,128]{3,2,1,0:T(8,128)S(1)}, f32[4,27,16,128]{3,2,1,0:T(8,128)S(1)}, u32[]{:S(2)}, u32[]{:S(2)}) collective-permute-start(f32[4,27,16,128]{3,2,1,0:T(8,128)S(1)} %bitcast.148), channel_id=1, source_target_pairs={{0,1},{1,0},{2,3},{3,2},{4,5},{5,4},{6,7},{7,6},{8,9},{9,8},{10,11... | collective-permute-start | bytes 2654216 | tf_op jit(solution)/shard_map/ppermute | solution.py:19
  174.6 2.6 %collective-permute-start.33 = (f32[4,27,16,128]{3,2,1,0:T(8,128)}, f32[4,27,16,128]{3,2,1,0:T(8,128)S(1)}, u32[]{:S(2)}, u32[]{:S(2)}) collective-permute-start(f32[4,27,16,128]{3,2,1,0:T(8,128)} %get-tuple-element.41), channel_id=1, source_target_pairs={{0,1},{1,0},{2,3},{3,2},{4,5},{5,4},{6,7},{7,6},{8,9},{9,8},{10,11... | collective-permute-start | bytes 2654216 | tf_op jit(solution)/shard_map/ppermute | solution.py:19
  174.8 4.8 %collective-permute-start.30 = (f32[4,27,16,128]{3,2,1,0:T(8,128)}, f32[4,27,16,128]{3,2,1,0:T(8,128)S(1)}, u32[]{:S(2)}, u32[]{:S(2)}) collective-permute-start(f32[4,27,16,128]{3,2,1,0:T(8,128)} %get-tuple-element.39), channel_id=1, source_target_pairs={{0,1},{1,0},{2,3},{3,2},{4,5},{5,4},{6,7},{7,6},{8,9},{9,8},{10,11... | collective-permute-start | bytes 2654216 | tf_op jit(solution)/shard_map/ppermute | solution.py:19
  178.6 12.3 %collective-permute-start.34 = (f32[1,2,27,16,128]{4,3,2,1,0:T(8,128)S(1)}, f32[1,2,27,16,128]{4,3,2,1,0:T(8,128)S(1)}, u32[]{:S(2)}, u32[]{:S(2)}) collective-permute-start(f32[1,2,27,16,128]{4,3,2,1,0:T(8,128)S(1)} %slice_bitcast_fusion), channel_id=1, source_target_pairs={{0,4},{1,5},{2,6},{3,7},{4,0},{5,1},{6,2},{7,3},{8,12},{9,13},{10,... | collective-permute-start | bytes 1327112 | tf_op jit(solution)/shard_map/ppermute | solution.py:19
  179.7 12.6 %collective-permute-start.31 = (f32[2,1,27,16,128]{4,3,2,0,1:T(8,128)S(1)}, f32[2,1,27,16,128]{4,3,2,0,1:T(8,128)S(1)}, u32[]{:S(2)}, u32[]{:S(2)}) collective-permute-start(f32[2,1,27,16,128]{4,3,2,0,1:T(8,128)S(1)} %slice_bitcast_fusion.2), channel_id=1, source_target_pairs={{0,2},{1,3},{2,0},{3,1},{4,6},{5,7},{6,4},{7,5},{8,10},{9,11},{10,... | collective-permute-start | bytes 1327112 | tf_op jit(solution)/shard_map/ppermute | solution.py:19
  191.0 6.7 %collective-permute-start.35 = (f32[1,1,27,16,128]{4,3,2,1,0:T(8,128)S(1)}, f32[1,1,27,16,128]{4,3,2,1,0:T(8,128)S(1)}, u32[]{:S(2)}, u32[]{:S(2)}) collective-permute-start(f32[1,1,27,16,128]{4,3,2,1,0:T(8,128)S(1)} %slice_bitcast_fusion.8), channel_id=1, source_target_pairs={{0,2},{1,3},{2,0},{3,1},{4,6},{5,7},{6,4},{7,5},{8,10},{9,11},{10,... | collective-permute-start | bytes 663560 | tf_op jit(solution)/shard_map/ppermute | solution.py:19
  192.4 6.4 %collective-permute-start.32 = (f32[1,1,27,16,128]{4,3,2,1,0:T(8,128)S(1)}, f32[1,1,27,16,128]{4,3,2,1,0:T(8,128)S(1)}, u32[]{:S(2)}, u32[]{:S(2)}) collective-permute-start(f32[1,1,27,16,128]{4,3,2,1,0:T(8,128)S(1)} %slice_bitcast_fusion.10), channel_id=1, source_target_pairs={{0,4},{1,5},{2,6},{3,7},{4,0},{5,1},{6,2},{7,3},{8,12},{9,13},{10,... | collective-permute-start | bytes 663560 | tf_op jit(solution)/shard_map/ppermute | solution.py:19
  201.3 7.9 %collective-permute-start.36 = (f32[16,16,128]{2,1,0:T(8,128)}, f32[16,16,128]{2,1,0:T(8,128)S(1)}, u32[]{:S(2)}, u32[]{:S(2)}) collective-permute-start(f32[16,16,128]{2,1,0:T(8,128)} %get-tuple-element.42), channel_id=1, source_target_pairs={{0,8},{8,0},{16,24},{24,16},{1,9},{9,1},{17,25},{25,17},{2,10},{10... | collective-permute-start | bytes 393224 | tf_op jit(solution)/shard_map/ppermute | solution.py:19
  202.7 6.5 %collective-permute-start.37 = (f32[4,16,128]{2,1,0:T(8,128)}, f32[4,16,128]{2,1,0:T(8,128)S(1)}, u32[]{:S(2)}, u32[]{:S(2)}) collective-permute-start(f32[4,16,128]{2,1,0:T(8,128)} %get-tuple-element.43), channel_id=1, source_target_pairs={{0,24},{8,16},{16,8},{24,0},{1,25},{9,17},{17,9},{25,1},{2,26},{10... | collective-permute-start | bytes 98312 | tf_op jit(solution)/shard_map/ppermute | solution.py:19
  204.4 4.8 %collective-permute-start.38 = (f32[2,16,128]{2,1,0:T(8,128)}, f32[2,16,128]{2,1,0:T(8,128)S(1)}, u32[]{:S(2)}, u32[]{:S(2)}) collective-permute-start(f32[2,16,128]{2,1,0:T(8,128)} %get-tuple-element.44), channel_id=1, source_target_pairs={{0,16},{8,24},{16,0},{24,8},{1,17},{9,25},{17,1},{25,9},{2,18},{10... | collective-permute-start | bytes 49160 | tf_op jit(solution)/shard_map/ppermute | solution.py:19
  212.9 10.2 %collective-permute-start.39 = (f32[16,32,128]{2,1,0:T(8,128)}, f32[16,32,128]{2,1,0:T(8,128)S(1)}, u32[]{:S(2)}, u32[]{:S(2)}) collective-permute-start(f32[16,32,128]{2,1,0:T(8,128)} %shard_map.63.refs_0_), channel_id=1, source_target_pairs={{0,8},{8,0},{16,24},{24,16},{1,9},{9,1},{17,25},{25,17},{2,10},{10... | collective-permute-start | bytes 786440 | tf_op jit(solution)/shard_map/ppermute | solution.py:19
  213.8 17.2 %collective-permute-start.40 = (f32[16,32,128]{2,1,0:T(8,128)}, f32[16,32,128]{2,1,0:T(8,128)S(1)}, u32[]{:S(2)}, u32[]{:S(2)}) collective-permute-start(f32[16,32,128]{2,1,0:T(8,128)} %shard_map.63.refs_0_), channel_id=1, source_target_pairs={{0,16},{8,24},{16,0},{24,8},{1,17},{9,25},{17,1},{25,9},{2,18},{10... | collective-permute-start | bytes 786440 | tf_op jit(solution)/shard_map/ppermute | solution.py:19
  214.7 21.3 %collective-permute-start.41 = (f32[16,32,128]{2,1,0:T(8,128)}, f32[16,32,128]{2,1,0:T(8,128)S(1)}, u32[]{:S(2)}, u32[]{:S(2)}) collective-permute-start(f32[16,32,128]{2,1,0:T(8,128)} %shard_map.63.refs_0_), channel_id=1, source_target_pairs={{0,24},{8,16},{16,8},{24,0},{1,25},{9,17},{17,9},{25,1},{2,26},{10... | collective-permute-start | bytes 786440 | tf_op jit(solution)/shard_map/ppermute | solution.py:19
  223.1 12.9 %copy-start.14 = (f32[16,32,128]{2,1,0:T(8,128)}, f32[16,32,128]{2,1,0:T(8,128)S(1)}, u32[]{:S(2)}) copy-start(f32[16,32,128]{2,1,0:T(8,128)S(1)} %collective-permute-done.39.refs_1_) | copy-start | bytes 786436
  (17 other events, 29.9 us)

commit v8 on v7

--- a/solution.py
+++ b/solution.py
@@ -9,7 +9,7 @@
 
 ITERS = 2
 LANES = 128
-BLOCK = 8
+BLOCK = 16
 F32, BF16 = jnp.float32, jnp.bfloat16
 PARAMS = pltpu.CompilerParams(vmem_limit_bytes=58 * 1024 * 1024)
 

time: 240 us -> 238 us (level)
  no operation moved by 1% of the time
where the time goes in v8:
time: 238 us
  waiting for transfers between devices  99.4 us (42%)
  Pallas kernels  68.6 us (29%)
  starting transfers between devices  38.9 us (16%)
  other arithmetic  17.8 us (7%)
  local copies, waits for them, and re-layouts  12.6 us (5%)
    ppermute x42, waiting for transfers between devices, swap(): return lax.ppermute(value, axis, [(i, i ^ mask) for i in range(count)])  99.4 us
    pallas_call x9, Pallas kernels, call(): pl.pallas_call(kernel, out_shape=[jax.ShapeDtypeStruct(shape, F32) for sh...  63.3 us
    ppermute x42, starting transfers between devices, swap(): return lax.ppermute(value, axis, [(i, i ^ mask) for i in range(count)])  38.9 us
    unnamed x49, local copies, waits for them, and re-layouts  5.44 us
    pallas_call x1, Pallas kernels, body(): pl.pallas_call(functools.partial(bands_kernel, rad), out_shape=[jax.Shape...  5.22 us
  transfers between devices with their start and end apart: 42, of which 21 were waited for; matrix products, arithmetic and copies ran while one was open for 9% of the time, Pallas kernels for 7%

profile of v8, /device:TPU:8, one launch (start us, length us, event | category | flops | bytes accessed | tf_op | source)
XLA Modules:
  0.0 237.7 jit_solution(8742982245005002304)
XLA Ops:
  2.4 3.0 %collective-permute-start.1 = (f32[2,128]{1,0:T(2,128)S(1)}, f32[2,128]{1,0:T(2,128)S(1)}, u32[]{:S(2)}, u32[]{:S(2)}) collective-permute-start(f32[2,128]{1,0:T(2,128)S(1)} %select_maximum_fusion), channel_id=1, source_target_pairs={{0,16},{8,24},{16,0},{24,8},{1,17},{9,25},{17,1},{25,9},{2,18},{10... | collective-permute-start | bytes 3080 | tf_op jit(solution)/shard_map/ppermute | solution.py:19
  8.0 1.7 pad_maximum_fusion.5
  9.7 1.5 collective-permute-start.9
  12.2 1.7 pad_maximum_fusion.4
  13.9 1.5 collective-permute-start.6
  15.5 1.4 constant_dynamic-slice_fusion
  17.5 1.3 collective-permute-start.12
  18.8 2.2 collective-permute-start.13
  24.7 1.6 collective-permute-start.3
  26.3 7.1 %collective-permute-done.10 = f32[1,1,2,27,16,128]{5,4,3,2,1,0:T(8,128)S(1)} collective-permute-done((f32[1,1,2,27,16,128]{5,4,3,2,1,0:T(8,128)S(1)}, f32[1,1,2,27,16,128]{5,4,3,2,1,0:T(8,128)S(1)}, u32[]{:S(2)}, u32[]{:S(2)}) %collective-permute-start.10) | collective-permute-done | bytes 442400 | tf_op jit(solution)/shard_map/ppermute | solution.py:19
  36.8 2.9 %collective-permute-done.4 = f32[2,1,1,1,16,128]{5,4,0,3,2,1:T(8,128)S(1)} collective-permute-done((f32[2,1,1,1,16,128]{5,4,0,3,2,1:T(8,128)S(1)}, f32[2,1,1,1,16,128]{5,4,0,3,2,1:T(8,128)S(1)}, u32[]{:S(2)}, u32[]{:S(2)}) %collective-permute-start.4) | collective-permute-done | bytes 16416 | tf_op jit(solution)/shard_map/ppermute | solution.py:19
  41.6 5.2 %shard_map.55 = (bf16[128,384]{1,0:T(8,128)(2,1)}, f32[128,128]{1,0:T(8,128)}, bf16[8,512,128]{2,1,0:T(8,128)(2,1)}, bf16[8,384,256]{2,1,0:T(8,128)(2,1)}) custom-call(s32[3]{0:T(128)} %pad_add_fusion.place, s32[8]{0:T(128)} %and_select_fusion.slab, f32[8,96]{1,0:T(8,128)} %slice_divide_fusion.kern), custom_call_target="tpu_custom_call" | custom-call | flops 4194304 | bytes 2097152 | tf_op jit(solution)/shard_map/pallas_call | solution.py:460
  46.8 8.9 %collective-permute-done.13.refs_1_.refs_2_ = f32[2,16,32,128]{3,2,1,0:T(8,128)S(1)} collective-permute-done((f32[2,16,32,128]{3,2,1,0:T(8,128)}, f32[2,16,32,128]{3,2,1,0:T(8,128)S(1)}, u32[]{:S(2)}, u32[]{:S(2)}) %collective-permute-start.13) | collective-permute-done | bytes 524320 | tf_op jit(solution)/shard_map/ppermute | solution.py:19
  56.4 11.8 %shard_map.56.blurred = f32[32,128,128]{2,1,0:T(8,128)} custom-call(s32[3]{0:T(128)} %pad_add_fusion.place, f32[8,32]{1,0:T(8,128)} %fusion.18.ky, bf16[128,384]{1,0:T(8,128)(2,1)} %get-tuple-element.27.wx, bf16[8,512,128]{2,1,0:T(8,128)(2,1)} %get-tuple-element.28.kz, f32[4,27,16,128]{3,2,1,0:T(8,128)} %bitcast.18.a0, ...), custom_call_target="tpu_custom_call" | custom-call | bytes 2048 | tf_op jit(solution)/shard_map/pallas_call | solution.py:397
  69.1 14.2 %shard_map.57 = (f32[4,27,16,128]{3,2,1,0:T(8,128)}, f32[4,27,16,128]{3,2,1,0:T(8,128)}, f32[4,27,16,128]{3,2,1,0:T(8,128)}, f32[4,27,16,128]{3,2,1,0:T(8,128)}) custom-call(s32[3]{0:T(128)} %pad_add_fusion.place, f32[8,32]{1,0:T(8,128)} %fusion.18.ky, f32[128,128]{1,0:T(8,128)} %get-tuple-element.25.bxt, f32[4,1,16,128]{3,2,1,0:T(8,128)} %bitcast.164, ...), custom_call_target="tpu_custom_call" | custom-call | flops 339738624 | bytes 7733248 | tf_op jit(solution)/shard_map/pallas_call | solution.py:397
  83.8 2.1 collective-permute-done.18
  85.9 1.3 add.94
  88.1 11.4 %collective-permute-done.19 = f32[1,2,27,16,128]{4,3,2,1,0:T(8,128)S(1)} collective-permute-done((f32[1,2,27,16,128]{4,3,2,1,0:T(8,128)S(1)}, f32[1,2,27,16,128]{4,3,2,1,0:T(8,128)S(1)}, u32[]{:S(2)}, u32[]{:S(2)}) %collective-permute-start.19) | collective-permute-done | bytes 442400 | tf_op jit(solution)/shard_map/ppermute | solution.py:19
  100.3 1.4 collective-permute-start.17
  101.6 4.7 %collective-permute-done.20 = f32[1,1,27,16,128]{4,3,2,1,0:T(8,128)S(1)} collective-permute-done((f32[1,1,27,16,128]{4,3,2,1,0:T(8,128)S(1)}, f32[1,1,27,16,128]{4,3,2,1,0:T(8,128)S(1)}, u32[]{:S(2)}, u32[]{:S(2)}) %collective-permute-start.20) | collective-permute-done | bytes 221216 | tf_op jit(solution)/shard_map/ppermute | solution.py:19
  107.7 2.5 %shard_map.58 = (f32[36,16,128]{2,1,0:T(8,128)}, f32[12,16,128]{2,1,0:T(8,128)}, f32[8,16,128]{2,1,0:T(8,128)}) custom-call(s32[3]{0:T(128)} %pad_add_fusion.place, f32[27,16,128]{2,1,0:T(8,128)} %fusion.15.a, f32[27,16,128]{2,1,0:T(8,128)} %fusion.13.b), custom_call_target="tpu_custom_call" | custom-call | flops 2048 | bytes 884736 | tf_op jit(solution)/shard_map/pallas_call | solution.py:397
  110.2 3.8 %collective-permute-start.22 = (f32[12,16,128]{2,1,0:T(8,128)}, f32[12,16,128]{2,1,0:T(8,128)S(1)}, u32[]{:S(2)}, u32[]{:S(2)}) collective-permute-start(f32[12,16,128]{2,1,0:T(8,128)} %get-tuple-element.34), channel_id=1, source_target_pairs={{0,24},{8,16},{16,8},{24,0},{1,25},{9,17},{17,9},{25,1},{2,26},{10... | collective-permute-start | bytes 294920 | tf_op jit(solution)/shard_map/ppermute | solution.py:19
  114.6 8.2 %collective-permute-done.23.fc = f32[8,16,128]{2,1,0:T(8,128)S(1)} collective-permute-done((f32[8,16,128]{2,1,0:T(8,128)}, f32[8,16,128]{2,1,0:T(8,128)S(1)}, u32[]{:S(2)}, u32[]{:S(2)}) %collective-permute-start.23) | collective-permute-done | bytes 65568 | tf_op jit(solution)/shard_map/ppermute | solution.py:19
  123.6 2.4 %shard_map.59 = (f32[27,16,128]{2,1,0:T(8,128)}, f32[27,16,128]{2,1,0:T(8,128)}) custom-call(s32[3]{0:T(128)} %pad_add_fusion.place, f32[27,16,128]{2,1,0:T(8,128)} %fusion.15.a, f32[27,16,128]{2,1,0:T(8,128)} %fusion.13.b, f32[36,16,128]{2,1,0:T(8,128)} %copy-done.13, f32[12,16,128]{2,1,0:T(8,128)} %copy-done.19, f32[8,16,128]{2,1,0:T(8,128)} %copy-done.20, ...), custom_call_target="tpu_custom_call" | custom-call | flops 2048 | bytes 1769472 | tf_op jit(solution)/shard_map/pallas_call | solution.py:397
  127.8 4.4 %collective-permute-done.27 = f32[1,1,1,27,16,128]{5,4,3,2,1,0:T(8,128)S(1)} collective-permute-done((f32[1,1,1,27,16,128]{5,4,3,2,1,0:T(8,128)}, f32[1,1,1,27,16,128]{5,4,3,2,1,0:T(8,128)S(1)}, u32[]{:S(2)}, u32[]{:S(2)}) %collective-permute-start.27) | collective-permute-done | bytes 221216 | tf_op jit(solution)/shard_map/ppermute | solution.py:19
  135.1 1.6 collective-permute-start.25
  136.7 5.8 %collective-permute-done.28 = f32[1,1,2,27,16,128]{5,4,3,2,1,0:T(8,128)S(1)} collective-permute-done((f32[1,1,2,27,16,128]{5,4,3,2,1,0:T(8,128)S(1)}, f32[1,1,2,27,16,128]{5,4,3,2,1,0:T(8,128)S(1)}, u32[]{:S(2)}, u32[]{:S(2)}) %collective-permute-start.28) | collective-permute-done | bytes 442400 | tf_op jit(solution)/shard_map/ppermute | solution.py:19
  143.7 1.4 collective-permute-done.29.b1
  145.1 1.3 collective-permute-done.26.a1
  147.3 11.8 %shard_map.60.blurred = f32[32,128,128]{2,1,0:T(8,128)} custom-call(s32[3]{0:T(128)} %pad_add_fusion.place, f32[8,32]{1,0:T(8,128)} %fusion.18.ky, bf16[128,384]{1,0:T(8,128)(2,1)} %get-tuple-element.27.wx, bf16[8,512,128]{2,1,0:T(8,128)(2,1)} %get-tuple-element.28.kz, f32[4,27,16,128]{3,2,1,0:T(8,128)} %bitcast.149, f32[4,27,16,128]{3,2,1,0:T(8,128)} %copy-done.9, ...), custom_call_target="tpu_custom_call" | custom-call | flops 339738624 | bytes 2048 | tf_op jit(solution)/shard_map/pallas_call | solution.py:397
  159.1 14.2 %shard_map.61 = (f32[4,27,16,128]{3,2,1,0:T(8,128)}, f32[4,27,16,128]{3,2,1,0:T(8,128)}, f32[4,27,16,128]{3,2,1,0:T(8,128)}, f32[4,27,16,128]{3,2,1,0:T(8,128)}) custom-call(s32[3]{0:T(128)} %pad_add_fusion.place, f32[8,32]{1,0:T(8,128)} %fusion.18.ky, f32[128,128]{1,0:T(8,128)} %get-tuple-element.25.bxt, f32[4,1,16,128]{3,2,1,0:T(8,128)} %bitcast.165, ...), custom_call_target="tpu_custom_call" | custom-call | flops 339738624 | bytes 7733248 | tf_op jit(solution)/shard_map/pallas_call | solution.py:397
  173.8 2.1 collective-permute-done.33
  175.9 1.3 add.100
  178.4 1.3 collective-permute-start.31
  179.6 9.9 %collective-permute-done.34 = f32[1,2,27,16,128]{4,3,2,1,0:T(8,128)S(1)} collective-permute-done((f32[1,2,27,16,128]{4,3,2,1,0:T(8,128)S(1)}, f32[1,2,27,16,128]{4,3,2,1,0:T(8,128)S(1)}, u32[]{:S(2)}, u32[]{:S(2)}) %collective-permute-start.34) | collective-permute-done | bytes 442400 | tf_op jit(solution)/shard_map/ppermute | solution.py:19
  189.6 1.4 collective-permute-start.35
  191.9 4.4 %collective-permute-done.35 = f32[1,1,27,16,128]{4,3,2,1,0:T(8,128)S(1)} collective-permute-done((f32[1,1,27,16,128]{4,3,2,1,0:T(8,128)S(1)}, f32[1,1,27,16,128]{4,3,2,1,0:T(8,128)S(1)}, u32[]{:S(2)}, u32[]{:S(2)}) %collective-permute-start.35) | collective-permute-done | bytes 221216 | tf_op jit(solution)/shard_map/ppermute | solution.py:19
  198.2 1.7 shard_map.62
  200.0 1.4 collective-permute-start.36
  201.4 1.7 collective-permute-start.37
  203.1 1.3 collective-permute-start.38
  204.4 3.5 %collective-permute-done.38.fc = f32[2,16,128]{2,1,0:T(8,128)S(1)} collective-permute-done((f32[2,16,128]{2,1,0:T(8,128)}, f32[2,16,128]{2,1,0:T(8,128)S(1)}, u32[]{:S(2)}, u32[]{:S(2)}) %collective-permute-start.38) | collective-permute-done | bytes 16416 | tf_op jit(solution)/shard_map/ppermute | solution.py:19
  209.2 2.4 shard_map.63.refs_0_
  213.4 1.7 collective-permute-start.41
  215.0 6.7 %collective-permute-done.39.refs_1_ = f32[16,32,128]{2,1,0:T(8,128)S(1)} collective-permute-done((f32[16,32,128]{2,1,0:T(8,128)}, f32[16,32,128]{2,1,0:T(8,128)S(1)}, u32[]{:S(2)}, u32[]{:S(2)}) %collective-permute-start.39) | collective-permute-done | bytes 262176 | tf_op jit(solution)/shard_map/ppermute | solution.py:19
  221.7 7.9 %collective-permute-done.40.refs_2_ = f32[16,32,128]{2,1,0:T(8,128)S(1)} collective-permute-done((f32[16,32,128]{2,1,0:T(8,128)}, f32[16,32,128]{2,1,0:T(8,128)S(1)}, u32[]{:S(2)}, u32[]{:S(2)}) %collective-permute-start.40) | collective-permute-done | bytes 262176 | tf_op jit(solution)/shard_map/ppermute | solution.py:19
  229.6 5.0 %collective-permute-done.41.refs_3_ = f32[16,32,128]{2,1,0:T(8,128)S(1)} collective-permute-done((f32[16,32,128]{2,1,0:T(8,128)}, f32[16,32,128]{2,1,0:T(8,128)S(1)}, u32[]{:S(2)}, u32[]{:S(2)}) %collective-permute-start.41) | collective-permute-done | bytes 262176 | tf_op jit(solution)/shard_map/ppermute | solution.py:19
  235.3 2.3 shard_map.64
  (158 shorter events, 37.1 us)
Async XLA Ops:
  0.0 5.9 %copy-start = (f32[16,64,256]{2,1,0:T(8,128)S(1)}, f32[16,64,256]{2,1,0:T(8,128)}, u32[]{:S(2)}) copy-start(f32[16,64,256]{2,1,0:T(8,128)} %param.5) | copy-start | bytes 3145732
  2.4 15.1 %collective-permute-start = (f32[2,128]{1,0:T(2,128)S(1)}, f32[2,128]{1,0:T(2,128)S(1)}, u32[]{:S(2)}, u32[]{:S(2)}) collective-permute-start(f32[2,128]{1,0:T(2,128)S(1)} %select_maximum_fusion), channel_id=1, source_target_pairs={{0,8},{8,0},{16,24},{24,16},{1,9},{9,1},{17,25},{25,17},{2,10},{10... | collective-permute-start | bytes 3080 | tf_op jit(solution)/shard_map/ppermute | solution.py:19
  2.4 16.4 %collective-permute-start.1 = (f32[2,128]{1,0:T(2,128)S(1)}, f32[2,128]{1,0:T(2,128)S(1)}, u32[]{:S(2)}, u32[]{:S(2)}) collective-permute-start(f32[2,128]{1,0:T(2,128)S(1)} %select_maximum_fusion), channel_id=1, source_target_pairs={{0,16},{8,24},{16,0},{24,8},{1,17},{9,25},{17,1},{25,9},{2,18},{10... | collective-permute-start | bytes 3080 | tf_op jit(solution)/shard_map/ppermute | solution.py:19
  5.4 15.6 %collective-permute-start.2 = (f32[2,128]{1,0:T(2,128)S(1)}, f32[2,128]{1,0:T(2,128)S(1)}, u32[]{:S(2)}, u32[]{:S(2)}) collective-permute-start(f32[2,128]{1,0:T(2,128)S(1)} %select_maximum_fusion), channel_id=1, source_target_pairs={{0,24},{8,16},{16,8},{24,0},{1,25},{9,17},{17,9},{25,1},{2,26},{10... | collective-permute-start | bytes 3080 | tf_op jit(solution)/shard_map/ppermute | solution.py:19
  6.2 9.3 %copy-start.6 = (f32[2,16,64,256]{3,2,1,0:T(8,128)S(1)}, f32[2,16,64,256]{3,2,1,0:T(8,128)}, u32[]{:S(2)}) copy-start(f32[2,16,64,256]{3,2,1,0:T(8,128)} %param.6) | copy-start | bytes 6291460
  9.7 11.7 %collective-permute-start.9 = (f32[1,1,1,27,16,128]{5,4,3,2,1,0:T(8,128)S(1)}, f32[1,1,1,27,16,128]{5,4,3,2,1,0:T(8,128)}, u32[]{:S(2)}, u32[]{:S(2)}) collective-permute-start(f32[1,1,1,27,16,128]{5,4,3,2,1,0:T(8,128)S(1)} %get-tuple-element.54), channel_id=1, source_target_pairs={{0,2},{1,3},{2,0},{3,1},{4,6},{5,7},{6,4},{7,5},{8,10},{9,11},{10,... | collective-permute-start | bytes 663560 | tf_op jit(solution)/shard_map/ppermute | solution.py:19
  13.9 9.0 %collective-permute-start.6 = (f32[1,1,1,27,16,128]{5,4,3,2,1,0:T(8,128)}, f32[1,1,1,27,16,128]{5,4,3,2,1,0:T(8,128)}, u32[]{:S(2)}, u32[]{:S(2)}) collective-permute-start(f32[1,1,1,27,16,128]{5,4,3,2,1,0:T(8,128)} %get-tuple-element.56), channel_id=1, source_target_pairs={{0,4},{1,5},{2,6},{3,7},{4,0},{5,1},{6,2},{7,3},{8,12},{9,13},{10,... | collective-permute-start | bytes 663560 | tf_op jit(solution)/shard_map/ppermute | solution.py:19
  17.5 23.3 %collective-permute-start.12 = (f32[2,16,32,128]{3,2,1,0:T(8,128)}, f32[2,16,32,128]{3,2,1,0:T(8,128)S(1)}, u32[]{:S(2)}, u32[]{:S(2)}) collective-permute-start(f32[2,16,32,128]{3,2,1,0:T(8,128)} %get-tuple-element.47), channel_id=1, source_target_pairs={{0,8},{8,0},{16,24},{24,16},{1,9},{9,1},{17,25},{25,17},{2,10},{10... | collective-permute-start | bytes 1572872 | tf_op jit(solution)/shard_map/ppermute | solution.py:19
  18.8 36.8 %collective-permute-start.13 = (f32[2,16,32,128]{3,2,1,0:T(8,128)}, f32[2,16,32,128]{3,2,1,0:T(8,128)S(1)}, u32[]{:S(2)}, u32[]{:S(2)}) collective-permute-start(f32[2,16,32,128]{3,2,1,0:T(8,128)} %get-tuple-element.46), channel_id=1, source_target_pairs={{0,16},{8,24},{16,0},{24,8},{1,17},{9,25},{17,1},{25,9},{2,18},{10... | collective-permute-start | bytes 1572872 | tf_op jit(solution)/shard_map/ppermute | solution.py:19
  22.4 11.0 %collective-permute-start.10 = (f32[1,1,2,27,16,128]{5,4,3,2,1,0:T(8,128)S(1)}, f32[1,1,2,27,16,128]{5,4,3,2,1,0:T(8,128)S(1)}, u32[]{:S(2)}, u32[]{:S(2)}) collective-permute-start(f32[1,1,2,27,16,128]{5,4,3,2,1,0:T(8,128)S(1)} %maximum_bitcast_fusion.1), channel_id=1, source_target_pairs={{0,4},{1,5},{2,6},{3,7},{4,0},{5,1},{6,2},{7,3},{8,12},{9,13},{10,... | collective-permute-start | bytes 1327112 | tf_op jit(solution)/shard_map/ppermute | solution.py:19
  24.0 10.0 %collective-permute-start.7 = (f32[2,1,1,27,16,128]{5,4,3,0,2,1:T(8,128)S(1)}, f32[2,1,1,27,16,128]{5,4,3,0,2,1:T(8,128)S(1)}, u32[]{:S(2)}, u32[]{:S(2)}) collective-permute-start(f32[2,1,1,27,16,128]{5,4,3,0,2,1:T(8,128)S(1)} %maximum_bitcast_fusion), channel_id=1, source_target_pairs={{0,2},{1,3},{2,0},{3,1},{4,6},{5,7},{6,4},{7,5},{8,10},{9,11},{10,... | collective-permute-start | bytes 1327112 | tf_op jit(solution)/shard_map/ppermute | solution.py:19
  24.7 11.1 %collective-permute-start.3 = (f32[1,1,1,1,16,128]{4,5,3,2,1,0:T(8,128)S(1)}, f32[1,1,1,1,16,128]{4,5,3,2,1,0:T(8,128)S(1)}, u32[]{:S(2)}, u32[]{:S(2)}) collective-permute-start(f32[1,1,1,1,16,128]{4,5,3,2,1,0:T(8,128)S(1)} %pad_bitcast_fusion), channel_id=1, source_target_pairs={{0,4},{1,5},{2,6},{3,7},{4,0},{5,1},{6,2},{7,3},{8,12},{9,13},{10,... | collective-permute-start | bytes 24584 | tf_op jit(solution)/shard_map/ppermute | solution.py:19
  33.4 22.2 %copy-start.3 = (f32[1,2,2,27,16,128]{5,4,3,2,1,0:T(8,128)}, f32[1,2,2,27,16,128]{5,4,3,2,1,0:T(8,128)S(1)}, u32[]{:S(2)}) copy-start(f32[1,2,2,27,16,128]{5,4,3,2,1,0:T(8,128)S(1)} %pad_maximum_fusion.1) | copy-start | bytes 2654212
  33.4 22.2 %collective-permute-start.11 = (f32[4,27,16,128]{3,2,1,0:T(8,128)S(1)}, f32[4,27,16,128]{3,2,1,0:T(8,128)}, u32[]{:S(2)}, u32[]{:S(2)}) collective-permute-start(f32[4,27,16,128]{3,2,1,0:T(8,128)S(1)} %bitcast.144), channel_id=1, source_target_pairs={{0,1},{1,0},{2,3},{3,2},{4,5},{5,4},{6,7},{7,6},{8,9},{9,8},{10,11... | collective-permute-start | bytes 2654216 | tf_op jit(solution)/shard_map/ppermute | solution.py:19
  35.1 20.5 %collective-permute-start.8 = (f32[4,27,16,128]{3,2,1,0:T(8,128)}, f32[4,27,16,128]{3,2,1,0:T(8,128)}, u32[]{:S(2)}, u32[]{:S(2)}) collective-permute-start(f32[4,27,16,128]{3,2,1,0:T(8,128)} %bitcast.18.a0), channel_id=1, source_target_pairs={{0,1},{1,0},{2,3},{3,2},{4,5},{5,4},{6,7},{7,6},{8,9},{9,8},{10,11... | collective-permute-start | bytes 2654216 | tf_op jit(solution)/shard_map/ppermute | solution.py:19
  35.9 3.8 %collective-permute-start.4 = (f32[2,1,1,1,16,128]{5,4,0,3,2,1:T(8,128)S(1)}, f32[2,1,1,1,16,128]{5,4,0,3,2,1:T(8,128)S(1)}, u32[]{:S(2)}, u32[]{:S(2)}) collective-permute-start(f32[2,1,1,1,16,128]{5,4,0,3,2,1:T(8,128)S(1)} %get-tuple-element.58), channel_id=1, source_target_pairs={{0,2},{1,3},{2,0},{3,1},{4,6},{5,7},{6,4},{7,5},{8,10},{9,11},{10,... | collective-permute-start | bytes 49160 | tf_op jit(solution)/shard_map/ppermute | solution.py:19
  39.6 28.6 %collective-permute-start.14 = (f32[2,16,32,128]{3,2,1,0:T(8,128)}, f32[2,16,32,128]{3,2,1,0:T(8,128)S(1)}, u32[]{:S(2)}, u32[]{:S(2)}) collective-permute-start(f32[2,16,32,128]{3,2,1,0:T(8,128)} %get-tuple-element.45), channel_id=1, source_target_pairs={{0,24},{8,16},{16,8},{24,0},{1,25},{9,17},{17,9},{25,1},{2,26},{10... | collective-permute-start | bytes 1572872 | tf_op jit(solution)/shard_map/ppermute | solution.py:19
  40.8 27.5 %copy-start.12 = (f32[2,2,1,1,16,128]{5,4,3,2,1,0:T(8,128)}, f32[2,2,1,1,16,128]{5,4,3,2,1,0:T(8,128)S(1)}, u32[]{:S(2)}) copy-start(f32[2,2,1,1,16,128]{5,4,3,2,1,0:T(8,128)S(1)} %pad_maximum_fusion.6) | copy-start | bytes 98308
  40.8 14.8 %copy-start.1 = (f32[2,16,32,128]{3,2,1,0:T(8,128)}, f32[2,16,32,128]{3,2,1,0:T(8,128)S(1)}, u32[]{:S(2)}) copy-start(f32[2,16,32,128]{3,2,1,0:T(8,128)S(1)} %collective-permute-done.12.refs_0_.refs_1_) | copy-start | bytes 1572868
  40.8 27.4 %collective-permute-start.5 = (f32[4,1,16,128]{3,2,1,0:T(8,128)S(1)}, f32[4,1,16,128]{3,2,1,0:T(8,128)S(1)}, u32[]{:S(2)}, u32[]{:S(2)}) collective-permute-start(f32[4,1,16,128]{3,2,1,0:T(8,128)S(1)} %bitcast.163), channel_id=1, source_target_pairs={{0,1},{1,0},{2,3},{3,2},{4,5},{5,4},{6,7},{7,6},{8,9},{9,8},{10,11... | collective-permute-start | bytes 98312 | tf_op jit(solution)/shard_map/ppermute | solution.py:19
  83.3 2.6 %collective-permute-start.18 = (f32[4,27,16,128]{3,2,1,0:T(8,128)}, f32[4,27,16,128]{3,2,1,0:T(8,128)S(1)}, u32[]{:S(2)}, u32[]{:S(2)}) collective-permute-start(f32[4,27,16,128]{3,2,1,0:T(8,128)} %get-tuple-element.32), channel_id=1, source_target_pairs={{0,1},{1,0},{2,3},{3,2},{4,5},{5,4},{6,7},{7,6},{8,9},{9,8},{10,11... | collective-permute-start | bytes 2654216 | tf_op jit(solution)/shard_map/ppermute | solution.py:19
  83.3 4.0 %collective-permute-start.15 = (f32[4,27,16,128]{3,2,1,0:T(8,128)}, f32[4,27,16,128]{3,2,1,0:T(8,128)S(1)}, u32[]{:S(2)}, u32[]{:S(2)}) collective-permute-start(f32[4,27,16,128]{3,2,1,0:T(8,128)} %get-tuple-element.30), channel_id=1, source_target_pairs={{0,1},{1,0},{2,3},{3,2},{4,5},{5,4},{6,7},{7,6},{8,9},{9,8},{10,11... | collective-permute-start | bytes 2654216 | tf_op jit(solution)/shard_map/ppermute | solution.py:19
  87.2 12.3 %collective-permute-start.19 = (f32[1,2,27,16,128]{4,3,2,1,0:T(8,128)S(1)}, f32[1,2,27,16,128]{4,3,2,1,0:T(8,128)S(1)}, u32[]{:S(2)}, u32[]{:S(2)}) collective-permute-start(f32[1,2,27,16,128]{4,3,2,1,0:T(8,128)S(1)} %slice_bitcast_fusion.4), channel_id=1, source_target_pairs={{0,4},{1,5},{2,6},{3,7},{4,0},{5,1},{6,2},{7,3},{8,12},{9,13},{10,... | collective-permute-start | bytes 1327112 | tf_op jit(solution)/shard_map/ppermute | solution.py:19
  87.5 12.7 %collective-permute-start.16 = (f32[2,1,27,16,128]{4,3,2,0,1:T(8,128)S(1)}, f32[2,1,27,16,128]{4,3,2,0,1:T(8,128)S(1)}, u32[]{:S(2)}, u32[]{:S(2)}) collective-permute-start(f32[2,1,27,16,128]{4,3,2,0,1:T(8,128)S(1)} %slice_bitcast_fusion.6), channel_id=1, source_target_pairs={{0,2},{1,3},{2,0},{3,1},{4,6},{5,7},{6,4},{7,5},{8,10},{9,11},{10,... | collective-permute-start | bytes 1327112 | tf_op jit(solution)/shard_map/ppermute | solution.py:19
  99.6 6.7 %collective-permute-start.20 = (f32[1,1,27,16,128]{4,3,2,1,0:T(8,128)S(1)}, f32[1,1,27,16,128]{4,3,2,1,0:T(8,128)S(1)}, u32[]{:S(2)}, u32[]{:S(2)}) collective-permute-start(f32[1,1,27,16,128]{4,3,2,1,0:T(8,128)S(1)} %slice_bitcast_fusion.12), channel_id=1, source_target_pairs={{0,2},{1,3},{2,0},{3,1},{4,6},{5,7},{6,4},{7,5},{8,10},{9,11},{10,... | collective-permute-start | bytes 663560 | tf_op jit(solution)/shard_map/ppermute | solution.py:19
  100.3 6.7 %collective-permute-start.17 = (f32[1,1,27,16,128]{4,3,2,1,0:T(8,128)S(1)}, f32[1,1,27,16,128]{4,3,2,1,0:T(8,128)S(1)}, u32[]{:S(2)}, u32[]{:S(2)}) collective-permute-start(f32[1,1,27,16,128]{4,3,2,1,0:T(8,128)S(1)} %slice_bitcast_fusion.14), channel_id=1, source_target_pairs={{0,4},{1,5},{2,6},{3,7},{4,0},{5,1},{6,2},{7,3},{8,12},{9,13},{10,... | collective-permute-start | bytes 663560 | tf_op jit(solution)/shard_map/ppermute | solution.py:19
  110.2 12.6 %collective-permute-start.21 = (f32[36,16,128]{2,1,0:T(8,128)}, f32[36,16,128]{2,1,0:T(8,128)S(1)}, u32[]{:S(2)}, u32[]{:S(2)}) collective-permute-start(f32[36,16,128]{2,1,0:T(8,128)} %get-tuple-element.33), channel_id=1, source_target_pairs={{0,8},{8,0},{16,24},{24,16},{1,9},{9,1},{17,25},{25,17},{2,10},{10... | collective-permute-start | bytes 884744 | tf_op jit(solution)/shard_map/ppermute | solution.py:19
  110.2 12.6 %collective-permute-start.22 = (f32[12,16,128]{2,1,0:T(8,128)}, f32[12,16,128]{2,1,0:T(8,128)S(1)}, u32[]{:S(2)}, u32[]{:S(2)}) collective-permute-start(f32[12,16,128]{2,1,0:T(8,128)} %get-tuple-element.34), channel_id=1, source_target_pairs={{0,24},{8,16},{16,8},{24,0},{1,25},{9,17},{17,9},{25,1},{2,26},{10... | collective-permute-start | bytes 294920 | tf_op jit(solution)/shard_map/ppermute | solution.py:19
  114.0 8.7 %collective-permute-start.23 = (f32[8,16,128]{2,1,0:T(8,128)}, f32[8,16,128]{2,1,0:T(8,128)S(1)}, u32[]{:S(2)}, u32[]{:S(2)}) collective-permute-start(f32[8,16,128]{2,1,0:T(8,128)} %get-tuple-element.35), channel_id=1, source_target_pairs={{0,16},{8,24},{16,0},{24,8},{1,17},{9,25},{17,1},{25,9},{2,18},{10... | collective-permute-start | bytes 196616 | tf_op jit(solution)/shard_map/ppermute | solution.py:19
  126.0 6.1 %collective-permute-start.27 = (f32[1,1,1,27,16,128]{5,4,3,2,1,0:T(8,128)}, f32[1,1,1,27,16,128]{5,4,3,2,1,0:T(8,128)S(1)}, u32[]{:S(2)}, u32[]{:S(2)}) collective-permute-start(f32[1,1,1,27,16,128]{5,4,3,2,1,0:T(8,128)} %bitcast.161), channel_id=1, source_target_pairs={{0,2},{1,3},{2,0},{3,1},{4,6},{5,7},{6,4},{7,5},{8,10},{9,11},{10,... | collective-permute-start | bytes 663560 | tf_op jit(solution)/shard_map/ppermute | solution.py:19
  126.9 7.2 %collective-permute-start.24 = (f32[1,1,1,27,16,128]{5,4,3,2,1,0:T(8,128)}, f32[1,1,1,27,16,128]{5,4,3,2,1,0:T(8,128)S(1)}, u32[]{:S(2)}, u32[]{:S(2)}) collective-permute-start(f32[1,1,1,27,16,128]{5,4,3,2,1,0:T(8,128)} %bitcast.159), channel_id=1, source_target_pairs={{0,4},{1,5},{2,6},{3,7},{4,0},{5,1},{6,2},{7,3},{8,12},{9,13},{10,... | collective-permute-start | bytes 663560 | tf_op jit(solution)/shard_map/ppermute | solution.py:19
  133.1 9.4 %collective-permute-start.28 = (f32[1,1,2,27,16,128]{5,4,3,2,1,0:T(8,128)S(1)}, f32[1,1,2,27,16,128]{5,4,3,2,1,0:T(8,128)S(1)}, u32[]{:S(2)}, u32[]{:S(2)}) collective-permute-start(f32[1,1,2,27,16,128]{5,4,3,2,1,0:T(8,128)S(1)} %maximum_bitcast_fusion.3), channel_id=1, source_target_pairs={{0,4},{1,5},{2,6},{3,7},{4,0},{5,1},{6,2},{7,3},{8,12},{9,13},{10,... | collective-permute-start | bytes 1327112 | tf_op jit(solution)/shard_map/ppermute | solution.py:19
  135.1 8.4 %collective-permute-start.25 = (f32[2,1,1,27,16,128]{5,4,3,0,2,1:T(8,128)S(1)}, f32[2,1,1,27,16,128]{5,4,3,0,2,1:T(8,128)S(1)}, u32[]{:S(2)}, u32[]{:S(2)}) collective-permute-start(f32[2,1,1,27,16,128]{5,4,3,0,2,1:T(8,128)S(1)} %maximum_bitcast_fusion.2), channel_id=1, source_target_pairs={{0,2},{1,3},{2,0},{3,1},{4,6},{5,7},{6,4},{7,5},{8,10},{9,11},{10,... | collective-permute-start | bytes 1327112 | tf_op jit(solution)/shard_map/ppermute | solution.py:19
  142.6 2.5 %collective-permute-start.29 = (f32[4,27,16,128]{3,2,1,0:T(8,128)S(1)}, f32[4,27,16,128]{3,2,1,0:T(8,128)S(1)}, u32[]{:S(2)}, u32[]{:S(2)}) collective-permute-start(f32[4,27,16,128]{3,2,1,0:T(8,128)S(1)} %bitcast.146), channel_id=1, source_target_pairs={{0,1},{1,0},{2,3},{3,2},{4,5},{5,4},{6,7},{7,6},{8,9},{9,8},{10,11... | collective-permute-start | bytes 2654216 | tf_op jit(solution)/shard_map/ppermute | solution.py:19
  143.6 2.7 %collective-permute-start.26 = (f32[4,27,16,128]{3,2,1,0:T(8,128)S(1)}, f32[4,27,16,128]{3,2,1,0:T(8,128)S(1)}, u32[]{:S(2)}, u32[]{:S(2)}) collective-permute-start(f32[4,27,16,128]{3,2,1,0:T(8,128)S(1)} %bitcast.148), channel_id=1, source_target_pairs={{0,1},{1,0},{2,3},{3,2},{4,5},{5,4},{6,7},{7,6},{8,9},{9,8},{10,11... | collective-permute-start | bytes 2654216 | tf_op jit(solution)/shard_map/ppermute | solution.py:19
  173.3 2.6 %collective-permute-start.33 = (f32[4,27,16,128]{3,2,1,0:T(8,128)}, f32[4,27,16,128]{3,2,1,0:T(8,128)S(1)}, u32[]{:S(2)}, u32[]{:S(2)}) collective-permute-start(f32[4,27,16,128]{3,2,1,0:T(8,128)} %get-tuple-element.41), channel_id=1, source_target_pairs={{0,1},{1,0},{2,3},{3,2},{4,5},{5,4},{6,7},{7,6},{8,9},{9,8},{10,11... | collective-permute-start | bytes 2654216 | tf_op jit(solution)/shard_map/ppermute | solution.py:19
  173.4 4.8 %collective-permute-start.30 = (f32[4,27,16,128]{3,2,1,0:T(8,128)}, f32[4,27,16,128]{3,2,1,0:T(8,128)S(1)}, u32[]{:S(2)}, u32[]{:S(2)}) collective-permute-start(f32[4,27,16,128]{3,2,1,0:T(8,128)} %get-tuple-element.39), channel_id=1, source_target_pairs={{0,1},{1,0},{2,3},{3,2},{4,5},{5,4},{6,7},{7,6},{8,9},{9,8},{10,11... | collective-permute-start | bytes 2654216 | tf_op jit(solution)/shard_map/ppermute | solution.py:19
  177.3 12.3 %collective-permute-start.34 = (f32[1,2,27,16,128]{4,3,2,1,0:T(8,128)S(1)}, f32[1,2,27,16,128]{4,3,2,1,0:T(8,128)S(1)}, u32[]{:S(2)}, u32[]{:S(2)}) collective-permute-start(f32[1,2,27,16,128]{4,3,2,1,0:T(8,128)S(1)} %slice_bitcast_fusion), channel_id=1, source_target_pairs={{0,4},{1,5},{2,6},{3,7},{4,0},{5,1},{6,2},{7,3},{8,12},{9,13},{10,... | collective-permute-start | bytes 1327112 | tf_op jit(solution)/shard_map/ppermute | solution.py:19
  178.4 12.6 %collective-permute-start.31 = (f32[2,1,27,16,128]{4,3,2,0,1:T(8,128)S(1)}, f32[2,1,27,16,128]{4,3,2,0,1:T(8,128)S(1)}, u32[]{:S(2)}, u32[]{:S(2)}) collective-permute-start(f32[2,1,27,16,128]{4,3,2,0,1:T(8,128)S(1)} %slice_bitcast_fusion.2), channel_id=1, source_target_pairs={{0,2},{1,3},{2,0},{3,1},{4,6},{5,7},{6,4},{7,5},{8,10},{9,11},{10,... | collective-permute-start | bytes 1327112 | tf_op jit(solution)/shard_map/ppermute | solution.py:19
  189.6 6.7 %collective-permute-start.35 = (f32[1,1,27,16,128]{4,3,2,1,0:T(8,128)S(1)}, f32[1,1,27,16,128]{4,3,2,1,0:T(8,128)S(1)}, u32[]{:S(2)}, u32[]{:S(2)}) collective-permute-start(f32[1,1,27,16,128]{4,3,2,1,0:T(8,128)S(1)} %slice_bitcast_fusion.8), channel_id=1, source_target_pairs={{0,2},{1,3},{2,0},{3,1},{4,6},{5,7},{6,4},{7,5},{8,10},{9,11},{10,... | collective-permute-start | bytes 663560 | tf_op jit(solution)/shard_map/ppermute | solution.py:19
  191.1 6.4 %collective-permute-start.32 = (f32[1,1,27,16,128]{4,3,2,1,0:T(8,128)S(1)}, f32[1,1,27,16,128]{4,3,2,1,0:T(8,128)S(1)}, u32[]{:S(2)}, u32[]{:S(2)}) collective-permute-start(f32[1,1,27,16,128]{4,3,2,1,0:T(8,128)S(1)} %slice_bitcast_fusion.10), channel_id=1, source_target_pairs={{0,4},{1,5},{2,6},{3,7},{4,0},{5,1},{6,2},{7,3},{8,12},{9,13},{10,... | collective-permute-start | bytes 663560 | tf_op jit(solution)/shard_map/ppermute | solution.py:19
  200.0 7.9 %collective-permute-start.36 = (f32[16,16,128]{2,1,0:T(8,128)}, f32[16,16,128]{2,1,0:T(8,128)S(1)}, u32[]{:S(2)}, u32[]{:S(2)}) collective-permute-start(f32[16,16,128]{2,1,0:T(8,128)} %get-tuple-element.42), channel_id=1, source_target_pairs={{0,8},{8,0},{16,24},{24,16},{1,9},{9,1},{17,25},{25,17},{2,10},{10... | collective-permute-start | bytes 393224 | tf_op jit(solution)/shard_map/ppermute | solution.py:19
  201.4 6.5 %collective-permute-start.37 = (f32[4,16,128]{2,1,0:T(8,128)}, f32[4,16,128]{2,1,0:T(8,128)S(1)}, u32[]{:S(2)}, u32[]{:S(2)}) collective-permute-start(f32[4,16,128]{2,1,0:T(8,128)} %get-tuple-element.43), channel_id=1, source_target_pairs={{0,24},{8,16},{16,8},{24,0},{1,25},{9,17},{17,9},{25,1},{2,26},{10... | collective-permute-start | bytes 98312 | tf_op jit(solution)/shard_map/ppermute | solution.py:19
  203.1 4.8 %collective-permute-start.38 = (f32[2,16,128]{2,1,0:T(8,128)}, f32[2,16,128]{2,1,0:T(8,128)S(1)}, u32[]{:S(2)}, u32[]{:S(2)}) collective-permute-start(f32[2,16,128]{2,1,0:T(8,128)} %get-tuple-element.44), channel_id=1, source_target_pairs={{0,16},{8,24},{16,0},{24,8},{1,17},{9,25},{17,1},{25,9},{2,18},{10... | collective-permute-start | bytes 49160 | tf_op jit(solution)/shard_map/ppermute | solution.py:19
  211.5 10.2 %collective-permute-start.39 = (f32[16,32,128]{2,1,0:T(8,128)}, f32[16,32,128]{2,1,0:T(8,128)S(1)}, u32[]{:S(2)}, u32[]{:S(2)}) collective-permute-start(f32[16,32,128]{2,1,0:T(8,128)} %shard_map.63.refs_0_), channel_id=1, source_target_pairs={{0,8},{8,0},{16,24},{24,16},{1,9},{9,1},{17,25},{25,17},{2,10},{10... | collective-permute-start | bytes 786440 | tf_op jit(solution)/shard_map/ppermute | solution.py:19
  212.4 17.2 %collective-permute-start.40 = (f32[16,32,128]{2,1,0:T(8,128)}, f32[16,32,128]{2,1,0:T(8,128)S(1)}, u32[]{:S(2)}, u32[]{:S(2)}) collective-permute-start(f32[16,32,128]{2,1,0:T(8,128)} %shard_map.63.refs_0_), channel_id=1, source_target_pairs={{0,16},{8,24},{16,0},{24,8},{1,17},{9,25},{17,1},{25,9},{2,18},{10... | collective-permute-start | bytes 786440 | tf_op jit(solution)/shard_map/ppermute | solution.py:19
  213.4 21.3 %collective-permute-start.41 = (f32[16,32,128]{2,1,0:T(8,128)}, f32[16,32,128]{2,1,0:T(8,128)S(1)}, u32[]{:S(2)}, u32[]{:S(2)}) collective-permute-start(f32[16,32,128]{2,1,0:T(8,128)} %shard_map.63.refs_0_), channel_id=1, source_target_pairs={{0,24},{8,16},{16,8},{24,0},{1,25},{9,17},{17,9},{25,1},{2,26},{10... | collective-permute-start | bytes 786440 | tf_op jit(solution)/shard_map/ppermute | solution.py:19
  221.7 12.9 %copy-start.14 = (f32[16,32,128]{2,1,0:T(8,128)}, f32[16,32,128]{2,1,0:T(8,128)S(1)}, u32[]{:S(2)}) copy-start(f32[16,32,128]{2,1,0:T(8,128)S(1)} %collective-permute-done.39.refs_1_) | copy-start | bytes 786436
  (17 other events, 29.9 us)
